TPU v7x, 32 devices: a whole 2x2x4 slice. The times are simulated.
32 devices in a mesh: grp: 4 (over y, core), sub: 8 (over z, x).
Axes of the slice: x: 2, y: 2, z: 4, core: 2. Of those that a mesh axis runs over, the one named last changes fastest.
Arguments:
- source: float32 [16, 64, 512], P('grp', 'sub'), may hold values from -6 to 6
- fine_coefficients: float32 [27, 16, 64, 512], P(None, 'grp', 'sub'), may hold values from -0.2 to 7, as said below
- middle_coefficients: float32 [27, 8, 32, 256], P(None, 'grp', 'sub'), may hold values from -0.2 to 7, as said below
- coarse_coefficients: float32 [27, 4, 16, 128], P(None, 'grp'), may hold values from -0.2 to 7, as said below
Outputs:
- fine_iterate: float32 [16, 64, 512], P('grp', 'sub')
- middle_iterate: float32 [8, 32, 256], P('grp', 'sub')
- coarse_iterate: float32 [4, 16, 128], P('grp')
Inputs may be any that keep to these rules, and one draw needn't show every extreme that they name: `fine_coefficients`: entries other than entry 13 are at most 0; entry 13 of each cell exceeds the sum of the magnitudes of that cell's other 26 entries. `middle_coefficients`: entries other than entry 13 are at most 0; entry 13 of each cell exceeds the sum of the magnitudes of that cell's other 26 entries. `coarse_coefficients`: entries other than entry 13 are at most 0; entry 13 of each cell exceeds the sum of the magnitudes of that cell's other 26 entries.
All inputs are finite; a program needn't handle non-finite values.
Results may differ from a plain program's by a relative error of at most 0.00002.
Values sent between devices are 32-bit elements; how exact they have to be, the bound alone decides.
No kernel may reach another device: no remote copies, remote signals or barrier semaphores. Data moves between devices by JAX's collectives and lax.ppermute only.
A program may use at most 64 MiB of HBM per device.

v0:
```python
import jax
import jax.numpy as jnp
from jax import lax
from jax.sharding import PartitionSpec as P

NU0 = 3
NU1 = 3
NB = 16


JACOBI_WEIGHT = 0.8
CENTER_TERM = 13


def padded_2(shard, sides, width):
    for axis, dim in sides:
        size, length = (lax.axis_size(axis), shard.shape[dim])
        up = [(i, (i + 1) % size) for i in range(size - 1)]
        down = [(j, i) for i, j in up]
        last = lax.slice_in_dim(shard, length - width, length, axis=dim)
        first = lax.slice_in_dim(shard, 0, width, axis=dim)
        before = lax.ppermute(last, axis, up)
        after = lax.ppermute(first, axis, down)
        shard = jnp.concatenate([before, shard, after], axis=dim)
    return shard


def stencil_sum(coefficients, padded):
    extent_x, extent_y, extent_z = coefficients.shape[1:]
    accumulated = jnp.zeros(coefficients.shape[1:], jnp.float32)
    for term_index in range(27):
        offset_x = term_index // 9
        offset_y = term_index // 3 % 3
        offset_z = term_index % 3
        accumulated = (
            accumulated
            + coefficients[term_index]
            * padded[
                offset_x : offset_x + extent_x,
                offset_y : offset_y + extent_y,
                offset_z : offset_z + extent_z,
            ]
        )
    return accumulated


def blocked_apply(coefficients, field):
    padded = padded_2(field, (("grp", 0), ("sub", 1)), 1)
    padded = jnp.pad(padded, ((0, 0), (0, 0), (1, 1)))
    return stencil_sum(coefficients, padded)


def local_apply(coefficients, field):
    return stencil_sum(coefficients, jnp.pad(field, 1))


def relax_sweeps(coefficients, source, sweeps, operate):
    diagonal = coefficients[CENTER_TERM]
    start_value = JACOBI_WEIGHT * source / diagonal

    def one_sweep(sweep_index, current):
        return current + JACOBI_WEIGHT * (source - operate(coefficients, current)) / diagonal

    return lax.fori_loop(0, sweeps - 1, one_sweep, start_value)


def restrict(residual):
    extent_x, extent_y, extent_z = residual.shape
    blocks = residual.reshape(extent_x // 2, 2, extent_y // 2, 2, extent_z // 2, 2)
    return 0.5 * jnp.sum(blocks, axis=(1, 3, 5))


def body(source, fine_coefficients, middle_coefficients, coarse_coefficients):
    fine_iterate = relax_sweeps(fine_coefficients, source, NU0, blocked_apply)
    fine_residual = source - blocked_apply(fine_coefficients, fine_iterate)
    middle_source = restrict(fine_residual)
    middle_iterate = relax_sweeps(middle_coefficients, middle_source, NU1, blocked_apply)
    middle_residual = middle_source - blocked_apply(middle_coefficients, middle_iterate)
    coarse_source = lax.all_gather(restrict(middle_residual), "sub", axis=1, tiled=True)
    whole_coefficients, whole_source = (
        lax.all_gather(coarse_coefficients, "grp", axis=1, tiled=True),
        lax.all_gather(coarse_source, "grp", axis=0, tiled=True),
    )
    whole_iterate = relax_sweeps(whole_coefficients, whole_source, NB, local_apply)
    plane_count = coarse_source.shape[0]
    coarse_iterate = lax.dynamic_slice_in_dim(
        whole_iterate, lax.axis_index("grp") * plane_count, plane_count, 0
    )
    return (fine_iterate, middle_iterate, coarse_iterate)


def solution(mesh):
    placed = (
        P("grp", "sub", None),
        P(None, "grp", "sub", None),
        P(None, "grp", "sub", None),
        P(None, "grp", None, None),
    )
    return jax.shard_map(
        body,
        mesh=mesh,
        in_specs=placed,
        out_specs=(P("grp", "sub", None), P("grp", "sub", None), P("grp", None, None)),
        check_vma=False,
    )
```

profile of v0, /device:TPU:0, one launch (start us, length us, event | category | flops | bytes accessed | tf_op | source)
XLA Modules:
  0.0 152.8 jit_solution(4776674581897182209)
XLA Ops:
  2.4 33.7 %while.36 = (s32[]{:T(128)}, f32[4,8,512]{2,1,0:T(8,128)S(1)}, f32[27,4,8,512]{3,2,1,0:T(8,128)}, f32[4,8,512]{2,1,0:T(8,128)}, f32[4,8,512]{2,1,0:T(8,128)S(1)}, /*index=5*/s32[]{:T(128)}) while((s32[]{:T(128)}, f32[4,8,512]{2,1,0:T(8,128)S(1)}, f32[27,4,8,512]{3,2,1,0:T(8,128)}, f32[4,8,512]{2,1,0:T(8,128)}, f32[4,8,512]{2,1,0:T(8,128)S(1)}, ...), condition=%wide.region_1.2_spmd, body=%wide.region_0.1_spmd.sunk | while | flops 1311682 | bytes 4285125 | solution.py:64
  2.4 2.5 %collective-permute-start = (f32[1,8,512]{2,1,0:T(8,128)S(1)}, f32[1,8,512]{2,1,0:T(8,128)S(1)}, u32[]{:S(2)}, u32[]{:S(2)}) collective-permute-start(f32[1,8,512]{2,1,0:T(8,128)S(1)} %get-tuple-element.340), channel_id=1, source_target_pairs={{0,8},{8,16},{16,24},{1,9},{9,17},{17,25},{2,10},{10,18},{18,26},{... | collective-permute-start | bytes 49160 | tf_op jit(solution)/shard_map/while/body/eval_jaxpr/ppermute | solution.py:22
  6.3 3.9 %collective-permute-done.1 = f32[1,8,512]{2,1,0:T(8,128)S(1)} collective-permute-done((f32[1,8,512]{2,1,0:T(8,128)S(1)}, f32[1,8,512]{2,1,0:T(8,128)S(1)}, u32[]{:S(2)}, u32[]{:S(2)}) %collective-permute-start.1) | collective-permute-done | bytes 16416 | tf_op jit(solution)/shard_map/while/body/eval_jaxpr/ppermute | solution.py:23
  11.5 4.5 %collective-permute-start.3 = (f32[6,1,512]{2,1,0:T(1,128)S(1)}, f32[6,1,512]{2,1,0:T(1,128)S(1)}, u32[]{:S(2)}, u32[]{:S(2)}) collective-permute-start(f32[6,1,512]{2,1,0:T(1,128)S(1)} %get-tuple-element.343), channel_id=1, source_target_pairs={{0,1},{1,2},{2,3},{3,4},{4,5},{5,6},{6,7},{8,9},{9,10},{10,11},{11... | collective-permute-start | bytes 36872 | tf_op jit(solution)/shard_map/while/body/eval_jaxpr/ppermute | solution.py:22
  19.4 3.2 %collective-permute-start = (f32[1,8,512]{2,1,0:T(8,128)S(1)}, f32[1,8,512]{2,1,0:T(8,128)S(1)}, u32[]{:S(2)}, u32[]{:S(2)}) collective-permute-start(f32[1,8,512]{2,1,0:T(8,128)S(1)} %get-tuple-element.340), channel_id=1, source_target_pairs={{0,8},{8,16},{16,24},{1,9},{9,17},{17,25},{2,10},{10,18},{18,26},{... | collective-permute-start | bytes 49160 | tf_op jit(solution)/shard_map/while/body/eval_jaxpr/ppermute | solution.py:22
  27.7 4.9 %collective-permute-start.3 = (f32[6,1,512]{2,1,0:T(1,128)S(1)}, f32[6,1,512]{2,1,0:T(1,128)S(1)}, u32[]{:S(2)}, u32[]{:S(2)}) collective-permute-start(f32[6,1,512]{2,1,0:T(1,128)S(1)} %get-tuple-element.343), channel_id=1, source_target_pairs={{0,1},{1,2},{2,3},{3,4},{4,5},{5,6},{6,7},{8,9},{9,10},{10,11},{11... | collective-permute-start | bytes 36872 | tf_op jit(solution)/shard_map/while/body/eval_jaxpr/ppermute | solution.py:22
  36.1 3.5 %collective-permute-start.8 = (f32[1,8,512]{2,1,0:T(8,128)S(1)}, f32[1,8,512]{2,1,0:T(8,128)S(1)}, u32[]{:S(2)}, u32[]{:S(2)}) collective-permute-start(f32[1,8,512]{2,1,0:T(8,128)S(1)} %get-tuple-element.242), channel_id=1, source_target_pairs={{0,8},{8,16},{16,24},{1,9},{9,17},{17,25},{2,10},{10,18},{18,26},{... | collective-permute-start | bytes 49160 | tf_op jit(solution)/shard_map/ppermute | solution.py:22
  43.1 5.1 %collective-permute-start.10 = (f32[6,1,512]{2,1,0:T(1,128)S(1)}, f32[6,1,512]{2,1,0:T(1,128)S(1)}, u32[]{:S(2)}, u32[]{:S(2)}) collective-permute-start(f32[6,1,512]{2,1,0:T(1,128)S(1)} %get-tuple-element.239), channel_id=1, source_target_pairs={{0,1},{1,2},{2,3},{3,4},{4,5},{5,6},{6,7},{8,9},{9,10},{10,11},{11... | collective-permute-start | bytes 36872 | tf_op jit(solution)/shard_map/ppermute | solution.py:22
  49.6 5.4 %collective-permute-done.11 = f32[6,1,512]{2,1,0:T(1,128)S(1)} collective-permute-done((f32[6,1,512]{2,1,0:T(1,128)S(1)}, f32[6,1,512]{2,1,0:T(1,128)S(1)}, u32[]{:S(2)}, u32[]{:S(2)}) %collective-permute-start.11) | collective-permute-done | bytes 12320 | tf_op jit(solution)/shard_map/ppermute | solution.py:23
  57.0 5.5 %reshape.22 = f32[2,2,4,2,256,2]{5,4,3,2,1,0:T(8,128)} reshape(f32[4,8,512]{2,1,0:T(8,128)S(1)} %fusion.145) | data formatting | bytes 131072 | tf_op jit(solution)/shard_map/reshape | solution.py:69
  62.5 2.5 %reduce_sum.21 = f32[2,4,256]{2,1,0:T(4,128)S(1)} reduce(f32[2,2,4,2,256,2]{5,4,3,2,1,0:T(8,128)} %reshape.22, f32[]{:T(128)} %constant.76.clone.1), dimensions={1,3,5}, to_apply=%region_2.3 | reduce | flops 14336 | bytes 73732 | tf_op jit(solution)/shard_map/reduce_sum | solution.py:70
  65.1 30.7 %while.37 = (s32[]{:T(128)}, f32[2,4,256]{2,1,0:T(4,128)S(1)}, f32[27,2,4,256]{3,2,1,0:T(4,128)S(1)}, f32[2,4,256]{2,1,0:T(4,128)S(1)}, f32[2,4,256]{2,1,0:T(4,128)S(1)}, /*index=5*/s32[]{:T(128)}) while((s32[]{:T(128)}, f32[2,4,256]{2,1,0:T(4,128)S(1)}, f32[27,2,4,256]{3,2,1,0:T(4,128)S(1)}, f32[2,4,256]{2,1,0:T(4,128)S(1)}, ...), condition=%wide.region_4.5_spmd, body=%wide.region_3.4_spmd.sunk | while | flops 182658 | bytes 631205 | solution.py:64
  65.1 3.4 %collective-permute-start.4 = (f32[1,4,256]{2,1,0:T(4,128)S(1)}, f32[1,4,256]{2,1,0:T(4,128)S(1)}, u32[]{:S(2)}, u32[]{:S(2)}) collective-permute-start(f32[1,4,256]{2,1,0:T(4,128)S(1)} %get-tuple-element.349), channel_id=1, source_target_pairs={{0,8},{8,16},{16,24},{1,9},{9,17},{17,25},{2,10},{10,18},{18,26},{... | collective-permute-start | bytes 12296 | tf_op jit(solution)/shard_map/while/body/eval_jaxpr/ppermute | solution.py:22
  69.8 2.4 %collective-permute-done.5 = f32[1,4,256]{2,1,0:T(4,128)S(1)} collective-permute-done((f32[1,4,256]{2,1,0:T(4,128)S(1)}, f32[1,4,256]{2,1,0:T(4,128)S(1)}, u32[]{:S(2)}, u32[]{:S(2)}) %collective-permute-start.5) | collective-permute-done | bytes 4128 | tf_op jit(solution)/shard_map/while/body/eval_jaxpr/ppermute | solution.py:23
  73.5 5.4 %collective-permute-start.7 = (f32[4,1,256]{2,1,0:T(1,128)S(1)}, f32[4,1,256]{2,1,0:T(1,128)S(1)}, u32[]{:S(2)}, u32[]{:S(2)}) collective-permute-start(f32[4,1,256]{2,1,0:T(1,128)S(1)} %get-tuple-element.352), channel_id=1, source_target_pairs={{0,1},{1,2},{2,3},{3,4},{4,5},{5,6},{6,7},{8,9},{9,10},{10,11},{11... | collective-permute-start | bytes 12296 | tf_op jit(solution)/shard_map/while/body/eval_jaxpr/ppermute | solution.py:22
  80.5 3.4 %collective-permute-start.4 = (f32[1,4,256]{2,1,0:T(4,128)S(1)}, f32[1,4,256]{2,1,0:T(4,128)S(1)}, u32[]{:S(2)}, u32[]{:S(2)}) collective-permute-start(f32[1,4,256]{2,1,0:T(4,128)S(1)} %get-tuple-element.349), channel_id=1, source_target_pairs={{0,8},{8,16},{16,24},{1,9},{9,17},{17,25},{2,10},{10,18},{18,26},{... | collective-permute-start | bytes 12296 | tf_op jit(solution)/shard_map/while/body/eval_jaxpr/ppermute | solution.py:22
  88.7 5.4 %collective-permute-start.7 = (f32[4,1,256]{2,1,0:T(1,128)S(1)}, f32[4,1,256]{2,1,0:T(1,128)S(1)}, u32[]{:S(2)}, u32[]{:S(2)}) collective-permute-start(f32[4,1,256]{2,1,0:T(1,128)S(1)} %get-tuple-element.352), channel_id=1, source_target_pairs={{0,1},{1,2},{2,3},{3,4},{4,5},{5,6},{6,7},{8,9},{9,10},{10,11},{11... | collective-permute-start | bytes 12296 | tf_op jit(solution)/shard_map/while/body/eval_jaxpr/ppermute | solution.py:22
  95.8 3.4 %collective-permute-start.12 = (f32[1,4,256]{2,1,0:T(4,128)S(1)}, f32[1,4,256]{2,1,0:T(4,128)S(1)}, u32[]{:S(2)}, u32[]{:S(2)}) collective-permute-start(f32[1,4,256]{2,1,0:T(4,128)S(1)} %get-tuple-element.246), channel_id=1, source_target_pairs={{0,8},{8,16},{16,24},{1,9},{9,17},{17,25},{2,10},{10,18},{18,26},{... | collective-permute-start | bytes 12296 | tf_op jit(solution)/shard_map/ppermute | solution.py:22
  99.2 9.8 %all_gather.11 = f32[27,4,16,128]{3,2,1,0:T(8,128)S(1)} all-gather(f32[27,1,16,128]{3,2,1,0:T(8,128)S(1)} %copy-done.3), channel_id=1, replica_groups=mesh['grp'=4,'sub'=8] {'grp'}, dimensions={1}, use_global_device_ids=true | all-gather | bytes 1105920 | tf_op jit(solution)/shard_map/all_gather | solution.py:81
  112.1 5.1 %collective-permute-start.14 = (f32[4,1,256]{2,1,0:T(1,128)S(1)}, f32[4,1,256]{2,1,0:T(1,128)S(1)}, u32[]{:S(2)}, u32[]{:S(2)}) collective-permute-start(f32[4,1,256]{2,1,0:T(1,128)S(1)} %get-tuple-element.243), channel_id=1, source_target_pairs={{0,1},{1,2},{2,3},{3,4},{4,5},{5,6},{6,7},{8,9},{9,10},{10,11},{11... | collective-permute-start | bytes 12296 | tf_op jit(solution)/shard_map/ppermute | solution.py:22
  118.5 4.9 %collective-permute-done.15 = f32[4,1,256]{2,1,0:T(1,128)S(1)} collective-permute-done((f32[4,1,256]{2,1,0:T(1,128)S(1)}, f32[4,1,256]{2,1,0:T(1,128)S(1)}, u32[]{:S(2)}, u32[]{:S(2)}) %collective-permute-start.15) | collective-permute-done | bytes 4128 | tf_op jit(solution)/shard_map/ppermute | solution.py:23
  124.0 19.4 %all-gather.2 = f32[8,2,128]{2,1,0:T(2,128)S(1)} all-gather(f32[1,2,128]{2,1,0:T(2,128)S(1)} %multiply_bitcast_fusion), channel_id=2, replica_groups=mesh['grp'=4,'sub'=8] {'sub'}, dimensions={0}, use_global_device_ids=true | all-gather | bytes 9216 | tf_op jit(solution)/shard_map/all_gather | solution.py:79
  143.4 5.4 %all-gather.1 = f32[64,128]{1,0:T(8,128)S(1)} all-gather(f32[16,128]{1,0:T(8,128)S(1)} %bitcast.540), channel_id=3, replica_groups=mesh['grp'=4,'sub'=8] {'grp'}, dimensions={0}, use_global_device_ids=true | all-gather | bytes 40960 | tf_op jit(solution)/shard_map/all_gather | solution.py:82
  148.7 3.5 %while.38 = (s32[]{:T(128)}, f32[4,16,128]{2,1,0:T(8,128)S(1)}, f32[27,4,16,128]{3,2,1,0:T(8,128)S(1)}, f32[4,16,128]{2,1,0:T(8,128)S(1)}, f32[4,16,128]{2,1,0:T(8,128)S(1)}, /*index=5*/s32[]{:T(128)}) while((s32[]{:T(128)}, f32[4,16,128]{2,1,0:T(8,128)S(1)}, f32[27,4,16,128]{3,2,1,0:T(8,128)S(1)}, f32[4,16,128]{2,1,0:T(8,128)S(1)}, ...), condition=%wide.region_8.9_spmd, body=%wide.region_7.8_spmd.sunk | while | flops 466946 | bytes 1081413 | solution.py:64
  (126 shorter events, 41.9 us)
Async XLA Ops:
  2.4 3.8 %collective-permute-start = (f32[1,8,512]{2,1,0:T(8,128)S(1)}, f32[1,8,512]{2,1,0:T(8,128)S(1)}, u32[]{:S(2)}, u32[]{:S(2)}) collective-permute-start(f32[1,8,512]{2,1,0:T(8,128)S(1)} %get-tuple-element.340), channel_id=1, source_target_pairs={{0,8},{8,16},{16,24},{1,9},{9,17},{17,25},{2,10},{10,18},{18,26},{... | collective-permute-start | bytes 49160 | tf_op jit(solution)/shard_map/while/body/eval_jaxpr/ppermute | solution.py:22
  4.9 5.2 %collective-permute-start.1 = (f32[1,8,512]{2,1,0:T(8,128)S(1)}, f32[1,8,512]{2,1,0:T(8,128)S(1)}, u32[]{:S(2)}, u32[]{:S(2)}) collective-permute-start(f32[1,8,512]{2,1,0:T(8,128)S(1)} %get-tuple-element.341), channel_id=1, source_target_pairs={{8,0},{16,8},{24,16},{9,1},{17,9},{25,17},{10,2},{18,10},{26,18},{... | collective-permute-start | bytes 49160 | tf_op jit(solution)/shard_map/while/body/eval_jaxpr/ppermute | solution.py:23
  10.2 5.9 %collective-permute-start.2 = (f32[6,1,512]{2,1,0:T(1,128)S(1)}, f32[6,1,512]{2,1,0:T(1,128)S(1)}, u32[]{:S(2)}, u32[]{:S(2)}) collective-permute-start(f32[6,1,512]{2,1,0:T(1,128)S(1)} %get-tuple-element.342), channel_id=1, source_target_pairs={{1,0},{2,1},{3,2},{4,3},{5,4},{6,5},{7,6},{9,8},{10,9},{11,10},{12... | collective-permute-start | bytes 36872 | tf_op jit(solution)/shard_map/while/body/eval_jaxpr/ppermute | solution.py:23
  11.5 5.9 %collective-permute-start.3 = (f32[6,1,512]{2,1,0:T(1,128)S(1)}, f32[6,1,512]{2,1,0:T(1,128)S(1)}, u32[]{:S(2)}, u32[]{:S(2)}) collective-permute-start(f32[6,1,512]{2,1,0:T(1,128)S(1)} %get-tuple-element.343), channel_id=1, source_target_pairs={{0,1},{1,2},{2,3},{3,4},{4,5},{5,6},{6,7},{8,9},{9,10},{10,11},{11... | collective-permute-start | bytes 36872 | tf_op jit(solution)/shard_map/while/body/eval_jaxpr/ppermute | solution.py:22
  19.4 4.6 %collective-permute-start = (f32[1,8,512]{2,1,0:T(8,128)S(1)}, f32[1,8,512]{2,1,0:T(8,128)S(1)}, u32[]{:S(2)}, u32[]{:S(2)}) collective-permute-start(f32[1,8,512]{2,1,0:T(8,128)S(1)} %get-tuple-element.340), channel_id=1, source_target_pairs={{0,8},{8,16},{16,24},{1,9},{9,17},{17,25},{2,10},{10,18},{18,26},{... | collective-permute-start | bytes 49160 | tf_op jit(solution)/shard_map/while/body/eval_jaxpr/ppermute | solution.py:22
  22.7 3.7 %collective-permute-start.1 = (f32[1,8,512]{2,1,0:T(8,128)S(1)}, f32[1,8,512]{2,1,0:T(8,128)S(1)}, u32[]{:S(2)}, u32[]{:S(2)}) collective-permute-start(f32[1,8,512]{2,1,0:T(8,128)S(1)} %get-tuple-element.341), channel_id=1, source_target_pairs={{8,0},{16,8},{24,16},{9,1},{17,9},{25,17},{10,2},{18,10},{26,18},{... | collective-permute-start | bytes 49160 | tf_op jit(solution)/shard_map/while/body/eval_jaxpr/ppermute | solution.py:23
  26.4 6.2 %collective-permute-start.2 = (f32[6,1,512]{2,1,0:T(1,128)S(1)}, f32[6,1,512]{2,1,0:T(1,128)S(1)}, u32[]{:S(2)}, u32[]{:S(2)}) collective-permute-start(f32[6,1,512]{2,1,0:T(1,128)S(1)} %get-tuple-element.342), channel_id=1, source_target_pairs={{1,0},{2,1},{3,2},{4,3},{5,4},{6,5},{7,6},{9,8},{10,9},{11,10},{12... | collective-permute-start | bytes 36872 | tf_op jit(solution)/shard_map/while/body/eval_jaxpr/ppermute | solution.py:23
  27.7 6.3 %collective-permute-start.3 = (f32[6,1,512]{2,1,0:T(1,128)S(1)}, f32[6,1,512]{2,1,0:T(1,128)S(1)}, u32[]{:S(2)}, u32[]{:S(2)}) collective-permute-start(f32[6,1,512]{2,1,0:T(1,128)S(1)} %get-tuple-element.343), channel_id=1, source_target_pairs={{0,1},{1,2},{2,3},{3,4},{4,5},{5,6},{6,7},{8,9},{9,10},{10,11},{11... | collective-permute-start | bytes 36872 | tf_op jit(solution)/shard_map/while/body/eval_jaxpr/ppermute | solution.py:22
  36.1 4.8 %collective-permute-start.8 = (f32[1,8,512]{2,1,0:T(8,128)S(1)}, f32[1,8,512]{2,1,0:T(8,128)S(1)}, u32[]{:S(2)}, u32[]{:S(2)}) collective-permute-start(f32[1,8,512]{2,1,0:T(8,128)S(1)} %get-tuple-element.242), channel_id=1, source_target_pairs={{0,8},{8,16},{16,24},{1,9},{9,17},{17,25},{2,10},{10,18},{18,26},{... | collective-permute-start | bytes 49160 | tf_op jit(solution)/shard_map/ppermute | solution.py:22
  39.6 3.5 %collective-permute-start.9 = (f32[1,8,512]{2,1,0:T(8,128)S(1)}, f32[1,8,512]{2,1,0:T(8,128)S(1)}, u32[]{:S(2)}, u32[]{:S(2)}) collective-permute-start(f32[1,8,512]{2,1,0:T(8,128)S(1)} %get-tuple-element.241), channel_id=1, source_target_pairs={{8,0},{16,8},{24,16},{9,1},{17,9},{25,17},{10,2},{18,10},{26,18},{... | collective-permute-start | bytes 49160 | tf_op jit(solution)/shard_map/ppermute | solution.py:23
  43.1 6.5 %collective-permute-start.10 = (f32[6,1,512]{2,1,0:T(1,128)S(1)}, f32[6,1,512]{2,1,0:T(1,128)S(1)}, u32[]{:S(2)}, u32[]{:S(2)}) collective-permute-start(f32[6,1,512]{2,1,0:T(1,128)S(1)} %get-tuple-element.239), channel_id=1, source_target_pairs={{0,1},{1,2},{2,3},{3,4},{4,5},{5,6},{6,7},{8,9},{9,10},{10,11},{11... | collective-permute-start | bytes 36872 | tf_op jit(solution)/shard_map/ppermute | solution.py:22
  48.2 6.8 %collective-permute-start.11 = (f32[6,1,512]{2,1,0:T(1,128)S(1)}, f32[6,1,512]{2,1,0:T(1,128)S(1)}, u32[]{:S(2)}, u32[]{:S(2)}) collective-permute-start(f32[6,1,512]{2,1,0:T(1,128)S(1)} %get-tuple-element.240), channel_id=1, source_target_pairs={{1,0},{2,1},{3,2},{4,3},{5,4},{6,5},{7,6},{9,8},{10,9},{11,10},{12... | collective-permute-start | bytes 36872 | tf_op jit(solution)/shard_map/ppermute | solution.py:23
  65.1 4.7 %collective-permute-start.4 = (f32[1,4,256]{2,1,0:T(4,128)S(1)}, f32[1,4,256]{2,1,0:T(4,128)S(1)}, u32[]{:S(2)}, u32[]{:S(2)}) collective-permute-start(f32[1,4,256]{2,1,0:T(4,128)S(1)} %get-tuple-element.349), channel_id=1, source_target_pairs={{0,8},{8,16},{16,24},{1,9},{9,17},{17,25},{2,10},{10,18},{18,26},{... | collective-permute-start | bytes 12296 | tf_op jit(solution)/shard_map/while/body/eval_jaxpr/ppermute | solution.py:22
  68.5 3.7 %collective-permute-start.5 = (f32[1,4,256]{2,1,0:T(4,128)S(1)}, f32[1,4,256]{2,1,0:T(4,128)S(1)}, u32[]{:S(2)}, u32[]{:S(2)}) collective-permute-start(f32[1,4,256]{2,1,0:T(4,128)S(1)} %get-tuple-element.350), channel_id=1, source_target_pairs={{8,0},{16,8},{24,16},{9,1},{17,9},{25,17},{10,2},{18,10},{26,18},{... | collective-permute-start | bytes 12296 | tf_op jit(solution)/shard_map/while/body/eval_jaxpr/ppermute | solution.py:23
  72.2 6.8 %collective-permute-start.6 = (f32[4,1,256]{2,1,0:T(1,128)S(1)}, f32[4,1,256]{2,1,0:T(1,128)S(1)}, u32[]{:S(2)}, u32[]{:S(2)}) collective-permute-start(f32[4,1,256]{2,1,0:T(1,128)S(1)} %get-tuple-element.351), channel_id=1, source_target_pairs={{1,0},{2,1},{3,2},{4,3},{5,4},{6,5},{7,6},{9,8},{10,9},{11,10},{12... | collective-permute-start | bytes 12296 | tf_op jit(solution)/shard_map/while/body/eval_jaxpr/ppermute | solution.py:23
  73.5 6.8 %collective-permute-start.7 = (f32[4,1,256]{2,1,0:T(1,128)S(1)}, f32[4,1,256]{2,1,0:T(1,128)S(1)}, u32[]{:S(2)}, u32[]{:S(2)}) collective-permute-start(f32[4,1,256]{2,1,0:T(1,128)S(1)} %get-tuple-element.352), channel_id=1, source_target_pairs={{0,1},{1,2},{2,3},{3,4},{4,5},{5,6},{6,7},{8,9},{9,10},{10,11},{11... | collective-permute-start | bytes 12296 | tf_op jit(solution)/shard_map/while/body/eval_jaxpr/ppermute | solution.py:22
  80.5 4.7 %collective-permute-start.4 = (f32[1,4,256]{2,1,0:T(4,128)S(1)}, f32[1,4,256]{2,1,0:T(4,128)S(1)}, u32[]{:S(2)}, u32[]{:S(2)}) collective-permute-start(f32[1,4,256]{2,1,0:T(4,128)S(1)} %get-tuple-element.349), channel_id=1, source_target_pairs={{0,8},{8,16},{16,24},{1,9},{9,17},{17,25},{2,10},{10,18},{18,26},{... | collective-permute-start | bytes 12296 | tf_op jit(solution)/shard_map/while/body/eval_jaxpr/ppermute | solution.py:22
  84.0 3.5 %collective-permute-start.5 = (f32[1,4,256]{2,1,0:T(4,128)S(1)}, f32[1,4,256]{2,1,0:T(4,128)S(1)}, u32[]{:S(2)}, u32[]{:S(2)}) collective-permute-start(f32[1,4,256]{2,1,0:T(4,128)S(1)} %get-tuple-element.350), channel_id=1, source_target_pairs={{8,0},{16,8},{24,16},{9,1},{17,9},{25,17},{10,2},{18,10},{26,18},{... | collective-permute-start | bytes 12296 | tf_op jit(solution)/shard_map/while/body/eval_jaxpr/ppermute | solution.py:23
  87.5 6.8 %collective-permute-start.6 = (f32[4,1,256]{2,1,0:T(1,128)S(1)}, f32[4,1,256]{2,1,0:T(1,128)S(1)}, u32[]{:S(2)}, u32[]{:S(2)}) collective-permute-start(f32[4,1,256]{2,1,0:T(1,128)S(1)} %get-tuple-element.351), channel_id=1, source_target_pairs={{1,0},{2,1},{3,2},{4,3},{5,4},{6,5},{7,6},{9,8},{10,9},{11,10},{12... | collective-permute-start | bytes 12296 | tf_op jit(solution)/shard_map/while/body/eval_jaxpr/ppermute | solution.py:23
  88.7 6.8 %collective-permute-start.7 = (f32[4,1,256]{2,1,0:T(1,128)S(1)}, f32[4,1,256]{2,1,0:T(1,128)S(1)}, u32[]{:S(2)}, u32[]{:S(2)}) collective-permute-start(f32[4,1,256]{2,1,0:T(1,128)S(1)} %get-tuple-element.352), channel_id=1, source_target_pairs={{0,1},{1,2},{2,3},{3,4},{4,5},{5,6},{6,7},{8,9},{9,10},{10,11},{11... | collective-permute-start | bytes 12296 | tf_op jit(solution)/shard_map/while/body/eval_jaxpr/ppermute | solution.py:22
  95.8 14.5 %collective-permute-start.12 = (f32[1,4,256]{2,1,0:T(4,128)S(1)}, f32[1,4,256]{2,1,0:T(4,128)S(1)}, u32[]{:S(2)}, u32[]{:S(2)}) collective-permute-start(f32[1,4,256]{2,1,0:T(4,128)S(1)} %get-tuple-element.246), channel_id=1, source_target_pairs={{0,8},{8,16},{16,24},{1,9},{9,17},{17,25},{2,10},{10,18},{18,26},{... | collective-permute-start | bytes 12296 | tf_op jit(solution)/shard_map/ppermute | solution.py:22
  109.0 3.0 %collective-permute-start.13 = (f32[1,4,256]{2,1,0:T(4,128)S(1)}, f32[1,4,256]{2,1,0:T(4,128)S(1)}, u32[]{:S(2)}, u32[]{:S(2)}) collective-permute-start(f32[1,4,256]{2,1,0:T(4,128)S(1)} %get-tuple-element.245), channel_id=1, source_target_pairs={{8,0},{16,8},{24,16},{9,1},{17,9},{25,17},{10,2},{18,10},{26,18},{... | collective-permute-start | bytes 12296 | tf_op jit(solution)/shard_map/ppermute | solution.py:23
  112.1 6.4 %collective-permute-start.14 = (f32[4,1,256]{2,1,0:T(1,128)S(1)}, f32[4,1,256]{2,1,0:T(1,128)S(1)}, u32[]{:S(2)}, u32[]{:S(2)}) collective-permute-start(f32[4,1,256]{2,1,0:T(1,128)S(1)} %get-tuple-element.243), channel_id=1, source_target_pairs={{0,1},{1,2},{2,3},{3,4},{4,5},{5,6},{6,7},{8,9},{9,10},{10,11},{11... | collective-permute-start | bytes 12296 | tf_op jit(solution)/shard_map/ppermute | solution.py:22
  117.2 6.2 %collective-permute-start.15 = (f32[4,1,256]{2,1,0:T(1,128)S(1)}, f32[4,1,256]{2,1,0:T(1,128)S(1)}, u32[]{:S(2)}, u32[]{:S(2)}) collective-permute-start(f32[4,1,256]{2,1,0:T(1,128)S(1)} %get-tuple-element.244), channel_id=1, source_target_pairs={{1,0},{2,1},{3,2},{4,3},{5,4},{6,5},{7,6},{9,8},{10,9},{11,10},{12... | collective-permute-start | bytes 12296 | tf_op jit(solution)/shard_map/ppermute | solution.py:23
  (4 other events, 155.2 us)
where the time goes:
time: 154 us; the launch traced here: 153 us
  starting transfers between devices  65.5 us (43%)
  blocking collectives  34.6 us (22%)
  waiting for transfers between devices  30.4 us (20%)
  other arithmetic  13.2 us (9%)
  local copies, waits for them, and re-layouts  7.48 us (5%)
    ppermute x12, starting transfers between devices, padded_2(): before = lax.ppermute(last, axis, up)  50 us
    ppermute x12, waiting for transfers between devices, padded_2(): after = lax.ppermute(first, axis, down)  24.9 us
    all_gather x1, blocking collectives, body(): lax.all_gather(restrict(middle_residual), 'sub', axis=1, tiled=True)  19.4 us
    ppermute x12, starting transfers between devices, padded_2(): after = lax.ppermute(first, axis, down)  15.5 us
    all_gather x1, blocking collectives, body(): lax.all_gather(coarse_coefficients, 'grp', axis=1, tiled=True)  9.8 us
    add x19, other arithmetic, one_sweep(): current + JACOBI_WEIGHT * (source - operate(coefficients, current)) / dia...  6.83 us
    reshape x1, local copies, waits for them, and re-layouts, restrict(): residual.reshape(extent_x // 2, 2, extent_y // 2, 2, extent_z // 2, 2)  5.5 us
    ppermute x12, waiting for transfers between devices, padded_2(): before = lax.ppermute(last, axis, up)  5.44 us
  transfers between devices with their start and end apart: 24, of which 13 were waited for; matrix products, arithmetic and copies ran while one was open for 0% of the time, Pallas kernels for 0%

commit v1 on v0

v1 whole, which is shorter than its diff:
```python
import functools

import jax
import jax.numpy as jnp
from jax import lax
from jax.experimental import pallas as pl
from jax.experimental.pallas import tpu as pltpu
from jax.sharding import PartitionSpec as P

NU0 = 3
NB = 16
WEIGHT = 0.8
CENTER = 13
LANES = 128
ROWS = 8
BASE = 8


def shape(*dims):
    return jax.ShapeDtypeStruct(dims, jnp.float32)


def call(kernel, outs, args, scratch=(), in_specs=None, grid=None):
    vmem = pl.BlockSpec(memory_space=pltpu.VMEM)
    return pl.pallas_call(
        kernel,
        out_shape=outs,
        in_specs=in_specs or [vmem] * len(args),
        out_specs=jax.tree.map(lambda _: vmem, outs),
        scratch_shapes=list(scratch),
        compiler_params=pltpu.CompilerParams(vmem_limit_bytes=48 << 20),
    )(*args)


def even(axis):
    return lax.rem(lax.axis_index(axis), 2) == 0


def pick(condition, a, b):
    return jnp.where(jnp.broadcast_to(condition, a.shape), a, b)


def shifted(values):
    extent = values.shape[-1]
    lane = lax.broadcasted_iota(jnp.int32, values.shape, values.ndim - 1)
    before = pltpu.roll(values, 1, values.ndim - 1)
    after = pltpu.roll(values, extent - 1, values.ndim - 1)
    return (
        jnp.where(lane == 0, 0.0, before),
        values,
        jnp.where(lane == extent - 1, 0.0, after),
    )


def place(padded, plane, row, values):
    for z, part in enumerate(shifted(values)):
        padded[z, plane, row : row + values.shape[0], :] = part


def stencil(padded, coefficient, first, planes, row, lanes):
    sums = [None] * planes
    for p in range(planes + 2):
        near = [
            [padded[z, first + p, row - 1 + y : row - 1 + y + ROWS, lanes] for z in range(3)]
            for y in range(3)
        ]
        for x in range(3):
            if not 0 <= p - x < planes:
                continue
            for y in range(3):
                for z in range(3):
                    term = coefficient(9 * x + 3 * y + z, p - x, lanes) * near[y][z]
                    sums[p - x] = term if sums[p - x] is None else sums[p - x] + term
    return sums


def lane_tiles(extent):
    return [slice(l, l + LANES) for l in range(0, extent, LANES)]


def paired_lanes(values):
    extent = values.shape[-1]
    row = lax.broadcasted_iota(jnp.int32, (extent, extent // 2), 0)
    column = lax.broadcasted_iota(jnp.int32, (extent, extent // 2), 1)
    pairs = jnp.where(lax.shift_right_logical(row, 1) == column, 1.0, 0.0)
    return lax.dot_general(
        values,
        pairs,
        (((1,), (0,)), ((), ())),
        precision=lax.Precision.HIGHEST,
        preferred_element_type=jnp.float32,
    )


def paired_rows(values):
    return values + pltpu.roll(values, values.shape[0] - 1, 0)


def put_edges(v, to_x, to_zx):
    last = v.shape[1] - 1
    for x in range(v.shape[0]):
        first_row, last_row = v[x, 0:1, :], v[x, last : last + 1, :]
        to_x[x : x + 1, :] = pick(even("sub"), last_row, first_row)
        to_zx[x : x + 1, :] = pick(even("sub"), first_row, last_row)


def start_kernel(f, center, v, to_x, to_zx):
    v[...] = WEIGHT * f[...] / center[0]
    put_edges(v, to_x, to_zx)


def faces_kernel(v, from_x, from_zx, to_core, to_y):
    planes, rows, _ = v.shape
    before = pick(even("sub"), from_zx[...], from_x[...])
    after = pick(even("sub"), from_x[...], from_zx[...])
    for ref, swap in ((to_core, False), (to_y, True)):
        def choose(a, b):
            return pick(even("grp"), b, a) if swap else pick(even("grp"), a, b)

        ref[0:rows, :] = choose(v[planes - 1], v[0])
        ref[rows : rows + 1, :] = choose(before[planes - 1 :], before[0:1])
        ref[rows + 1 : rows + 2, :] = choose(after[planes - 1 :], after[0:1])


def fill_fine(groups, padded, v, from_x, from_zx, from_core, from_y):
    planes, rows, _ = v.shape
    group = lax.axis_index("grp")
    for x in range(planes):
        place(padded, x + 1, BASE, v[x])
    befores = shifted(pick(even("sub"), from_zx[...], from_x[...]))
    afters = shifted(pick(even("sub"), from_x[...], from_zx[...]))
    for z in range(3):
        for x in range(planes):
            padded[z, x + 1, BASE - 1 : BASE, :] = befores[z][x : x + 1]
            padded[z, x + 1, BASE + rows : BASE + rows + 1, :] = afters[z][x : x + 1]
    low = pick(even("grp"), from_y[...], from_core[...])
    high = pick(even("grp"), from_core[...], from_y[...])
    low = pick(group == 0, jnp.zeros_like(low), low)
    high = pick(group == groups - 1, jnp.zeros_like(high), high)
    for plane, face in ((0, low), (planes + 1, high)):
        for z, part in enumerate(shifted(face)):
            padded[z, plane, BASE : BASE + rows, :] = part[0:rows]
            padded[z, plane, BASE - 1 : BASE, :] = part[rows : rows + 1]
            padded[z, plane, BASE + rows : BASE + rows + 1, :] = part[rows + 1 : rows + 2]


def sweep_kernel(groups, v, f, c, from_x, from_zx, from_core, from_y, out, to_x, to_zx, padded):
    planes, rows, extent = v.shape
    fill_fine(groups, padded, v, from_x, from_zx, from_core, from_y)
    for lanes in lane_tiles(extent):
        sums = stencil(padded, lambda k, x, l: c[k, x, :, l], 0, planes, BASE, lanes)
        for x in range(planes):
            out[x, :, lanes] = v[x, :, lanes] + WEIGHT * (f[x, :, lanes] - sums[x]) / c[CENTER, x, :, lanes]
    put_edges(out, to_x, to_zx)


def residual_kernel(groups, v, f, c, from_x, from_zx, from_core, from_y, center, source, to_x, to_zx, padded, held):
    planes, rows, extent = v.shape
    fill_fine(groups, padded, v, from_x, from_zx, from_core, from_y)
    for lanes in lane_tiles(extent):
        sums = stencil(padded, lambda k, x, l: c[k, x, :, l], 0, planes, BASE, lanes)
        r = [f[x, :, lanes] - sums[x] for x in range(planes)]
        for x in range(planes // 2):
            held[x * rows : (x + 1) * rows, lanes] = r[2 * x] + r[2 * x + 1]
    total = 0.5 * paired_rows(paired_lanes(held[...]))
    half = rows // 2
    for x in range(planes // 2):
        for y in range(half):
            row = x * rows + 2 * y
            source[x, y : y + 1, :] = total[row : row + 1]
    for x in range(planes // 2):
        mine = source[x]
        iterate = WEIGHT * mine / center[0, x]
        first = (mine[0:1], mine[1:2], iterate[2:3])
        last = (mine[half - 2 : half - 1], mine[half - 1 : half], iterate[half - 3 : half - 2])
        for i in range(3):
            row = 4 * x + i
            to_x[row : row + 1, :] = pick(even("sub"), last[i], first[i])
            to_zx[row : row + 1, :] = pick(even("sub"), first[i], last[i])


def middle_faces_kernel(source, from_x, from_zx, out):
    planes, half, _ = source.shape
    before = pick(even("sub"), from_zx[...], from_x[...])
    after = pick(even("sub"), from_x[...], from_zx[...])
    for x in range(planes):
        row = x * ROWS
        out[row : row + 2, :] = before[4 * x : 4 * x + 2]
        out[row + 2 : row + 2 + half, :] = source[x]
        out[row + 2 + half : row + ROWS, :] = after[4 * x : 4 * x + 2]
        extra = planes * ROWS + 2 * x
        out[extra : extra + 1, :] = before[4 * x + 2 : 4 * x + 3]
        out[extra + 1 : extra + 2, :] = after[4 * x + 2 : 4 * x + 3]


def coefficient_edges_kernel(c, to_x, to_zx):
    rows = c.shape[2]
    first, last = c[:, :, 0:2, :], c[:, :, rows - 2 : rows, :]
    to_x[...] = pick(even("sub"), last, first)
    to_zx[...] = pick(even("sub"), first, last)


def coefficient_pack_kernel(c, from_x, from_zx, coarse, out):
    _, planes, rows, extent = c.shape
    tiles = extent // LANES
    before = pick(even("sub"), from_zx[...], from_x[...])
    after = pick(even("sub"), from_x[...], from_zx[...])
    for x in range(planes):
        for l, lanes in enumerate(lane_tiles(extent)):
            row = (x * tiles + l) * ROWS
            out[:, row : row + 2, :] = before[:, x, :, lanes]
            out[:, row + 2 : row + 2 + rows, :] = c[:, x, :, lanes]
            out[:, row + 2 + rows : row + ROWS, :] = after[:, x, :, lanes]
    row = planes * tiles * ROWS
    for x in range(coarse.shape[1]):
        out[:, row : row + coarse.shape[2], :] = coarse[:, x]
        row += coarse.shape[2]


def middle_kernel(groups, subs, planes, *refs):
    packed, parts = refs[0], refs[1 : 1 + groups]
    iterate, coarse, padded, held = refs[1 + groups :]
    extent = packed.shape[-1]
    tiles = extent // LANES
    own = ROWS - 4
    group, sub = lax.axis_index("grp"), lax.axis_index("sub")
    total = groups * planes
    y = lax.broadcasted_iota(jnp.int32, (ROWS, extent), 0) + sub * own - 2
    inside = (y >= 0) & (y < subs * own)

    for plane in (0, total + 1):
        for z in range(3):
            padded[z, plane, :, :] = jnp.zeros(padded.shape[2:], jnp.float32)

    def owner_of(j):
        return jnp.bitwise_xor(group, j)

    def part_row(x, l):
        return (x * tiles + l.start // LANES) * ROWS

    for j in range(groups):
        o = owner_of(j)
        for x in range(planes):
            at = o * planes + x + 1
            extra = planes * ROWS + 2 * x
            for lanes in lane_tiles(extent):
                row = part_row(x, lanes)
                f = packed[o, x * ROWS : (x + 1) * ROWS, lanes]
                held[lanes.start // LANES] = WEIGHT * f / parts[j][CENTER, row : row + ROWS, :]
            v = jnp.concatenate([held[l] for l in range(tiles)], axis=1)
            place(padded, at, BASE, jnp.where(inside, v, 0.0))
            place(padded, at, BASE - 1, packed[o, extra : extra + 1, :])
            place(padded, at, BASE + ROWS, packed[o, extra + 1 : extra + 2, :])

    def sums_of(j, lanes):
        return stencil(
            padded,
            lambda k, x, l: parts[j][k, part_row(x, l) : part_row(x, l) + ROWS, :],
            owner_of(j) * planes,
            planes,
            BASE,
            lanes,
        )

    for _ in range(2):
        fresh = []
        for j in range(groups):
            o = owner_of(j)
            columns = [[] for _ in range(planes)]
            for lanes in lane_tiles(extent):
                sums = sums_of(j, lanes)
                for x in range(planes):
                    row = part_row(x, lanes)
                    f = packed[o, x * ROWS : (x + 1) * ROWS, lanes]
                    v = padded[1, o * planes + x + 1, BASE : BASE + ROWS, lanes]
                    v = v + WEIGHT * (f - sums[x]) / parts[j][CENTER, row : row + ROWS, :]
                    columns[x].append(v)
            fresh.append([jnp.concatenate(c, axis=1) for c in columns])
        for j in range(groups):
            for x in range(planes):
                place(padded, owner_of(j) * planes + x + 1, BASE, jnp.where(inside, fresh[j][x], 0.0))

    for x in range(planes):
        iterate[x] = padded[1, group * planes + x + 1, BASE + 2 : BASE + 2 + own, :]

    stacked = []
    for j in range(groups):
        o = owner_of(j)
        columns = [[] for _ in range(planes // 2)]
        for lanes in lane_tiles(extent):
            sums = sums_of(j, lanes)
            r = [packed[o, x * ROWS : (x + 1) * ROWS, lanes] - sums[x] for x in range(planes)]
            for x in range(planes // 2):
                columns[x].append(r[2 * x] + r[2 * x + 1])
        stacked += [jnp.concatenate(c, axis=1) for c in columns]
    result = 0.5 * paired_rows(paired_lanes(jnp.concatenate(stacked, axis=0)))
    place_of = lax.broadcasted_iota(jnp.int32, (ROWS, result.shape[1]), 0)
    for j in range(groups):
        for x in range(planes // 2):
            at = owner_of(j) * (planes // 2) + x
            tile = result[(j * (planes // 2) + x) * ROWS :][:ROWS]
            value = pltpu.roll(tile, ROWS - 2, 0)
            for i in range(1, own // 2):
                value = jnp.where(place_of == i, pltpu.roll(tile, ROWS - 2 - i, 0), value)
            for s in range(subs):
                coarse[s, at] = value[: own // 2]


def coarse_kernel(groups, subs, planes, start, *refs):
    gathered, parts = refs[0], refs[1 : 1 + groups]
    out, padded, right = refs[1 + groups :]
    _, rows, extent = right.shape
    each = rows // subs
    group = lax.axis_index("grp")

    def owner_of(j):
        return jnp.bitwise_xor(group, j)

    for plane in range(groups * planes + 2):
        for z in range(3):
            padded[z, plane, :, :] = jnp.zeros(padded.shape[2:], jnp.float32)
    for s in range(subs):
        for x in range(groups * planes):
            right[x, s * each : (s + 1) * each, :] = gathered[s, x]

    def row_of(x, t):
        return start + x * rows + t * ROWS

    tiles = rows // ROWS
    for j in range(groups):
        for x in range(planes):
            at = owner_of(j) * planes + x
            for t in range(tiles):
                row = row_of(x, t)
                v = WEIGHT * right[at, t * ROWS : (t + 1) * ROWS, :] / parts[j][CENTER, row : row + ROWS, :]
                place(padded, at + 1, BASE + t * ROWS, v)

    def sweep(_, carry):
        fresh = []
        for j in range(groups):
            for t in range(tiles):
                sums = stencil(
                    padded,
                    lambda k, x, l: parts[j][k, row_of(x, t) : row_of(x, t) + ROWS, :],
                    owner_of(j) * planes,
                    planes,
                    BASE + t * ROWS,
                    slice(0, extent),
                )
                for x in range(planes):
                    at = owner_of(j) * planes + x
                    row = row_of(x, t)
                    v = padded[1, at + 1, BASE + t * ROWS : BASE + (t + 1) * ROWS, :]
                    f = right[at, t * ROWS : (t + 1) * ROWS, :]
                    v = v + WEIGHT * (f - sums[x]) / parts[j][CENTER, row : row + ROWS, :]
                    fresh.append((at + 1, BASE + t * ROWS, v))
        for plane, row, v in fresh:
            place(padded, plane, row, v)
        return carry

    lax.fori_loop(0, NB - 1, sweep, 0)
    for x in range(planes):
        out[x] = padded[1, group * planes + x + 1, BASE : BASE + rows, :]


def swaps(pairs):
    return [p for a, b in pairs for p in ((a, b), (b, a))]


def body(source, fine, middle, coarse):
    groups, subs = lax.axis_size("grp"), lax.axis_size("sub")
    _, planes, rows, extent = fine.shape
    _, middle_planes, middle_rows, middle_extent = middle.shape
    _, coarse_planes, coarse_rows, coarse_extent = coarse.shape

    x_pairs = swaps([(i, i + 1) for i in range(0, subs, 2)])
    zx_pairs = swaps([(i, i + 1) for i in range(1, subs - 1, 2)])
    core_pairs = swaps([(i, i + 1) for i in range(0, groups, 2)])
    y_pairs = swaps([(i, (i + 1) % groups) for i in range(1, groups, 2)])

    def along_sub(pair):
        to_x, to_zx = pair
        from_zx = lax.ppermute(to_zx, "sub", zx_pairs)
        return lax.ppermute(to_x, "sub", x_pairs), from_zx

    def exchange(v, edges):
        halo = along_sub(edges)
        to_core, to_y = call(
            faces_kernel, [shape(rows + 8, extent)] * 2, [v, *halo]
        )
        from_core = lax.ppermute(to_core, "grp", core_pairs)
        from_y = lax.ppermute(to_y, "grp", y_pairs)
        return (*halo, from_core, from_y)

    vmem = pl.BlockSpec(memory_space=pltpu.VMEM)
    v, *edges = call(
        start_kernel,
        [shape(planes, rows, extent), shape(planes, extent), shape(planes, extent)],
        [source, fine[CENTER : CENTER + 1]],
    )
    padded_fine = pltpu.VMEM((3, planes + 2, rows + 16, extent), jnp.float32)

    sent = call(
        coefficient_edges_kernel,
        [shape(27, middle_planes, 2, middle_extent)] * 2,
        [middle],
    )
    middle_center = middle[CENTER : CENTER + 1]
    halo_c = along_sub(sent)
    start = middle_planes * (middle_extent // LANES) * ROWS
    mine = call(
        coefficient_pack_kernel,
        shape(27, start + coarse_planes * coarse_rows, LANES),
        [middle, *halo_c, coarse],
    )
    parts = {0: mine}
    bit = groups // 2
    while bit:
        pairs = [(i, i ^ bit) for i in range(groups)]
        for known in sorted(parts):
            parts[known ^ bit] = lax.ppermute(parts[known], "grp", pairs)
        bit //= 2
    parts = [parts[j] for j in range(groups)]

    for _ in range(NU0 - 1):
        v, *edges = call(
            functools.partial(sweep_kernel, groups),
            [shape(planes, rows, extent), shape(planes, extent), shape(planes, extent)],
            [v, source, fine, *exchange(v, edges)],
            [padded_fine],
        )
    fine_iterate = v
    middle_source, *edges = call(
        functools.partial(residual_kernel, groups),
        [shape(middle_planes, middle_rows, middle_extent)]
        + [shape(4 * middle_planes, middle_extent)] * 2,
        [v, source, fine, *exchange(v, edges), middle_center],
        [padded_fine, pltpu.VMEM((planes // 2 * rows, extent), jnp.float32)],
    )
    packed = call(
        middle_faces_kernel,
        shape(middle_planes * ROWS + 8, middle_extent),
        [middle_source, *along_sub(edges)],
    )
    packed = lax.all_gather(packed, "grp", axis=0, tiled=False)
    middle_iterate, coarse_source = call(
        functools.partial(middle_kernel, groups, subs, middle_planes),
        [
            shape(middle_planes, middle_rows, middle_extent),
            shape(subs, groups * coarse_planes, coarse_rows // subs, coarse_extent),
        ],
        [packed, *parts],
        [
            pltpu.VMEM((3, groups * middle_planes + 2, ROWS + 16, middle_extent), jnp.float32),
            pltpu.VMEM((middle_extent // LANES, ROWS, LANES), jnp.float32),
        ],
    )
    gathered = lax.all_to_all(coarse_source, "sub", 0, 0, tiled=True)
    coarse_iterate = call(
        functools.partial(coarse_kernel, groups, subs, coarse_planes, start),
        shape(coarse_planes, coarse_rows, coarse_extent),
        [gathered, *parts],
        [
            pltpu.VMEM((3, groups * coarse_planes + 2, coarse_rows + 16, coarse_extent), jnp.float32),
            pltpu.VMEM((groups * coarse_planes, coarse_rows, coarse_extent), jnp.float32),
        ],
    )
    return fine_iterate, middle_iterate, coarse_iterate


def solution(mesh):
    placed = (
        P("grp", "sub", None),
        P(None, "grp", "sub", None),
        P(None, "grp", "sub", None),
        P(None, "grp", None, None),
    )
    return jax.shard_map(
        body,
        mesh=mesh,
        in_specs=placed,
        out_specs=(P("grp", "sub", None), P("grp", "sub", None), P("grp", None, None)),
        check_vma=False,
    )
```

time: 154 us -> 96.2 us (0.62)
  starting transfers between devices: 65.5 us -> 33.8 us
  other arithmetic: 13.2 us -> 0 us
  blocking collectives: 34.6 us -> 21.8 us
  Pallas kernels: 0 us -> 7.65 us
  waiting for transfers between devices: 30.4 us -> 25.5 us
    ppermute x24 -> x19, starting transfers between devices: 65.5 us -> 33.8 us  [the longest x5 23.9 us: along_sub(): return (lax.ppermute(to_x, 'sub', x_pairs), from_zx)]
    all_gather x3 -> x1, blocking collectives: 34.6 us -> 5.34 us  [body(): packed = lax.all_gather(packed, 'grp', axis=0, tiled=False)]
    all_to_all x0 -> x1, blocking collectives: none -> 16.5 us  [body(): gathered = lax.all_to_all(coarse_source, 'sub', 0, 0, tiled=True)]
    pallas_call x0 -> x12, Pallas kernels: none -> 7.65 us  [call(): pl.pallas_call(kernel, out_shape=outs, in_specs=in_specs or [vmem] * len(...]
    add x19 -> x0, other arithmetic: 6.83 us -> none  [one_sweep(): current + JACOBI_WEIGHT * (source - operate(coefficients, current)) / dia...]
    reshape x1 -> x0, local copies, waits for them, and re-layouts: 5.5 us -> none  [restrict(): residual.reshape(extent_x // 2, 2, extent_y // 2, 2, extent_z // 2, 2)]
    ppermute x24 -> x19, waiting for transfers between devices: 30.4 us -> 25.5 us  [the longest x3 14.3 us: body(): parts[known ^ bit] = lax.ppermute(parts[known], 'grp', pairs)]
    unnamed x12 -> x14, local copies, waits for them, and re-layouts: 0.05 us -> 4.53 us
  transfers between devices with their start and end apart: 24 -> 19, of which waited for: 13 -> 9; matrix products, arithmetic and copies ran while one was open for 0% -> 2% of each run, Pallas kernels for 0% -> 2%
where the time goes in v1:
time: 96.2 us; the launch traced here: 95.6 us
  starting transfers between devices  33.8 us (35%)
  waiting for transfers between devices  25.5 us (27%)
  blocking collectives  21.8 us (23%)
  Pallas kernels  7.65 us (8%)
  local copies, waits for them, and re-layouts  6.07 us (6%)
    ppermute x5, starting transfers between devices, along_sub(): return (lax.ppermute(to_x, 'sub', x_pairs), from_zx)  23.9 us
    all_to_all x1, blocking collectives, body(): gathered = lax.all_to_all(coarse_source, 'sub', 0, 0, tiled=True)  16.5 us
    ppermute x3, waiting for transfers between devices, body(): parts[known ^ bit] = lax.ppermute(parts[known], 'grp', pairs)  14.3 us
    pallas_call x12, Pallas kernels, call(): pl.pallas_call(kernel, out_shape=outs, in_specs=in_specs or [vmem] * len(...  7.65 us
    ppermute x5, waiting for transfers between devices, along_sub(): return (lax.ppermute(to_x, 'sub', x_pairs), from_zx)  6.28 us
    all_gather x1, blocking collectives, body(): packed = lax.all_gather(packed, 'grp', axis=0, tiled=False)  5.34 us
    ppermute x3, waiting for transfers between devices, exchange(): from_y = lax.ppermute(to_y, 'grp', y_pairs)  4.9 us
    ppermute x3, starting transfers between devices, exchange(): from_y = lax.ppermute(to_y, 'grp', y_pairs)  4.61 us
  transfers between devices with their start and end apart: 19, of which 9 were waited for; matrix products, arithmetic and copies ran while one was open for 2% of the time, Pallas kernels for 2%

profile of v1, /device:TPU:0, one launch (start us, length us, event | category | flops | bytes accessed | tf_op | source)
XLA Modules:
  0.0 95.6 jit_solution(6088948499518481739)
XLA Ops:
  0.7 1.1 %copy-done.4 = f32[27,2,4,256]{3,2,1,0:T(4,128)S(1)} copy-done((f32[27,2,4,256]{3,2,1,0:T(4,128)S(1)}, f32[27,2,4,256]{3,2,1,0:T(4,128)}, u32[]{:S(2)}) %copy-start.4) | copy-done | bytes 221208
  1.8 3.0 %collective-permute-start.14 = (f32[27,2,2,256]{3,2,1,0:T(2,128)S(1)}, f32[27,2,2,256]{3,2,1,0:T(2,128)S(1)}, u32[]{:S(2)}, u32[]{:S(2)}) collective-permute-start(f32[27,2,2,256]{3,2,1,0:T(2,128)S(1)} %get-tuple-element.43), channel_id=1, source_target_pairs={{0,1},{1,0},{2,3},{3,2},{4,5},{5,4},{6,7},{7,6},{8,9},{9,8},{10,11... | collective-permute-start | bytes 331784 | tf_op jit(solution)/shard_map/ppermute | solution.py:384
  5.5 2.4 %collective-permute-done.14.from_x = f32[27,2,2,256]{3,2,1,0:T(2,128)S(1)} collective-permute-done((f32[27,2,2,256]{3,2,1,0:T(2,128)S(1)}, f32[27,2,2,256]{3,2,1,0:T(2,128)S(1)}, u32[]{:S(2)}, u32[]{:S(2)}) %collective-permute-start.14) | collective-permute-done | bytes 110624 | tf_op jit(solution)/shard_map/ppermute | solution.py:384
  8.9 1.8 %collective-permute-start.17 = (f32[27,48,128]{2,1,0:T(8,128)S(1)}, f32[27,48,128]{2,1,0:T(8,128)S(1)}, u32[]{:S(2)}, u32[]{:S(2)}) collective-permute-start(f32[27,48,128]{2,1,0:T(8,128)S(1)} %shard_map.76.refs_1_), channel_id=1, source_target_pairs={{0,16},{8,24},{16,0},{24,8},{1,17},{9,25},{17,1},{25,9},{2,18},{10... | collective-permute-start | bytes 1990664 | tf_op jit(solution)/shard_map/ppermute | solution.py:421
  10.8 14.3 %collective-permute-done.17.refs_3_ = f32[27,48,128]{2,1,0:T(8,128)S(1)} collective-permute-done((f32[27,48,128]{2,1,0:T(8,128)S(1)}, f32[27,48,128]{2,1,0:T(8,128)S(1)}, u32[]{:S(2)}, u32[]{:S(2)}) %collective-permute-start.17) | collective-permute-done | bytes 663584 | tf_op jit(solution)/shard_map/ppermute | solution.py:421
  26.8 4.4 %collective-permute-start = (f32[4,512]{1,0:T(4,128)S(1)}, f32[4,512]{1,0:T(4,128)S(1)}, u32[]{:S(2)}, u32[]{:S(2)}) collective-permute-start(f32[4,512]{1,0:T(4,128)S(1)} %get-tuple-element.26), channel_id=1, source_target_pairs={{0,1},{1,0},{2,3},{3,2},{4,5},{5,4},{6,7},{7,6},{8,9},{9,8},{10,11... | collective-permute-start | bytes 24584 | tf_op jit(solution)/shard_map/ppermute | solution.py:384
  31.9 1.0 %collective-permute-done.from_x = f32[4,512]{1,0:T(4,128)S(1)} collective-permute-done((f32[4,512]{1,0:T(4,128)S(1)}, f32[4,512]{1,0:T(4,128)S(1)}, u32[]{:S(2)}, u32[]{:S(2)}) %collective-permute-start) | collective-permute-done | bytes 8224 | tf_op jit(solution)/shard_map/ppermute | solution.py:384
  32.9 1.4 %collective-permute-start.3 = (f32[16,512]{1,0:T(8,128)S(1)}, f32[16,512]{1,0:T(8,128)S(1)}, u32[]{:S(2)}, u32[]{:S(2)}) collective-permute-start(f32[16,512]{1,0:T(8,128)S(1)} %get-tuple-element.29), channel_id=1, source_target_pairs={{8,16},{16,8},{24,0},{0,24},{9,17},{17,9},{25,1},{1,25},{10,18},{1... | collective-permute-start | bytes 98312 | tf_op jit(solution)/shard_map/ppermute | solution.py:392
  34.4 2.0 %collective-permute-done.3.from_y = f32[16,512]{1,0:T(8,128)S(1)} collective-permute-done((f32[16,512]{1,0:T(8,128)S(1)}, f32[16,512]{1,0:T(8,128)S(1)}, u32[]{:S(2)}, u32[]{:S(2)}) %collective-permute-start.3) | collective-permute-done | bytes 32800 | tf_op jit(solution)/shard_map/ppermute | solution.py:392
  37.5 4.9 %collective-permute-start.4 = (f32[4,512]{1,0:T(4,128)S(1)}, f32[4,512]{1,0:T(4,128)S(1)}, u32[]{:S(2)}, u32[]{:S(2)}) collective-permute-start(f32[4,512]{1,0:T(4,128)S(1)} %get-tuple-element.31), channel_id=1, source_target_pairs={{0,1},{1,0},{2,3},{3,2},{4,5},{5,4},{6,7},{7,6},{8,9},{9,8},{10,11... | collective-permute-start | bytes 24584 | tf_op jit(solution)/shard_map/ppermute | solution.py:384
  43.1 1.0 %collective-permute-done.4.from_x = f32[4,512]{1,0:T(4,128)S(1)} collective-permute-done((f32[4,512]{1,0:T(4,128)S(1)}, f32[4,512]{1,0:T(4,128)S(1)}, u32[]{:S(2)}, u32[]{:S(2)}) %collective-permute-start.4) | collective-permute-done | bytes 8224 | tf_op jit(solution)/shard_map/ppermute | solution.py:384
  44.1 1.5 %collective-permute-start.7 = (f32[16,512]{1,0:T(8,128)S(1)}, f32[16,512]{1,0:T(8,128)S(1)}, u32[]{:S(2)}, u32[]{:S(2)}) collective-permute-start(f32[16,512]{1,0:T(8,128)S(1)} %get-tuple-element.34), channel_id=1, source_target_pairs={{8,16},{16,8},{24,0},{0,24},{9,17},{17,9},{25,1},{1,25},{10,18},{1... | collective-permute-start | bytes 98312 | tf_op jit(solution)/shard_map/ppermute | solution.py:392
  45.7 1.9 %collective-permute-done.7.from_y = f32[16,512]{1,0:T(8,128)S(1)} collective-permute-done((f32[16,512]{1,0:T(8,128)S(1)}, f32[16,512]{1,0:T(8,128)S(1)}, u32[]{:S(2)}, u32[]{:S(2)}) %collective-permute-start.7) | collective-permute-done | bytes 32800 | tf_op jit(solution)/shard_map/ppermute | solution.py:392
  47.5 1.0 shard_map.71
  48.5 6.2 %collective-permute-start.8 = (f32[4,512]{1,0:T(4,128)S(1)}, f32[4,512]{1,0:T(4,128)S(1)}, u32[]{:S(2)}, u32[]{:S(2)}) collective-permute-start(f32[4,512]{1,0:T(4,128)S(1)} %get-tuple-element.36), channel_id=1, source_target_pairs={{0,1},{1,0},{2,3},{3,2},{4,5},{5,4},{6,7},{7,6},{8,9},{9,8},{10,11... | collective-permute-start | bytes 24584 | tf_op jit(solution)/shard_map/ppermute | solution.py:384
  55.3 1.0 %collective-permute-done.8.from_x = f32[4,512]{1,0:T(4,128)S(1)} collective-permute-done((f32[4,512]{1,0:T(4,128)S(1)}, f32[4,512]{1,0:T(4,128)S(1)}, u32[]{:S(2)}, u32[]{:S(2)}) %collective-permute-start.8) | collective-permute-done | bytes 8224 | tf_op jit(solution)/shard_map/ppermute | solution.py:384
  57.2 1.6 %collective-permute-start.11 = (f32[16,512]{1,0:T(8,128)S(1)}, f32[16,512]{1,0:T(8,128)S(1)}, u32[]{:S(2)}, u32[]{:S(2)}) collective-permute-start(f32[16,512]{1,0:T(8,128)S(1)} %get-tuple-element.39), channel_id=1, source_target_pairs={{8,16},{16,8},{24,0},{0,24},{9,17},{17,9},{25,1},{1,25},{10,18},{1... | collective-permute-start | bytes 98312 | tf_op jit(solution)/shard_map/ppermute | solution.py:392
  59.6 1.1 %collective-permute-done.11.from_y = f32[16,512]{1,0:T(8,128)S(1)} collective-permute-done((f32[16,512]{1,0:T(8,128)S(1)}, f32[16,512]{1,0:T(8,128)S(1)}, u32[]{:S(2)}, u32[]{:S(2)}) %collective-permute-start.11) | collective-permute-done | bytes 32800 | tf_op jit(solution)/shard_map/ppermute | solution.py:392
  61.3 5.4 %collective-permute-start.12 = (f32[8,256]{1,0:T(8,128)S(1)}, f32[8,256]{1,0:T(8,128)S(1)}, u32[]{:S(2)}, u32[]{:S(2)}) collective-permute-start(f32[8,256]{1,0:T(8,128)S(1)} %get-tuple-element.41), channel_id=1, source_target_pairs={{0,1},{1,0},{2,3},{3,2},{4,5},{5,4},{6,7},{7,6},{8,9},{9,8},{10,11... | collective-permute-start | bytes 24584 | tf_op jit(solution)/shard_map/ppermute | solution.py:384
  67.4 1.0 %collective-permute-done.12.from_x = f32[8,256]{1,0:T(8,128)S(1)} collective-permute-done((f32[8,256]{1,0:T(8,128)S(1)}, f32[8,256]{1,0:T(8,128)S(1)}, u32[]{:S(2)}, u32[]{:S(2)}) %collective-permute-start.12) | collective-permute-done | bytes 8224 | tf_op jit(solution)/shard_map/ppermute | solution.py:384
  68.4 5.3 %all-gather = f32[96,256]{1,0:T(8,128)S(1)} all-gather(f32[24,256]{1,0:T(8,128)S(1)} %shard_map.74), channel_id=2, replica_groups=mesh['grp'=4,'sub'=8] {'grp'}, dimensions={0}, use_global_device_ids=true | all-gather | bytes 122880 | tf_op jit(solution)/shard_map/all_gather | solution.py:445
  73.7 1.7 %shard_map.77 = (f32[2,4,256]{2,1,0:T(4,128)}, f32[8,4,2,128]{3,2,1,0:T(2,128)S(1)}) custom-call(f32[4,24,256]{2,1,0:T(8,128)S(1)} %bitcast.1, f32[27,48,128]{2,1,0:T(8,128)S(1)} %shard_map.76.refs_1_, f32[27,48,128]{2,1,0:T(8,128)S(1)} %collective-permute-done.16.refs_2_, f32[27,48,128]{2,1,0:T(8,128)S(1)} %collective-permute-done.17.refs_3_, ...), custom_call_target="tpu_custom_call" | custom-call | tf_op jit(solution)/shard_map/pallas_call | solution.py:25
  75.4 16.5 %all_to_all.5.refs_0_ = f32[8,4,2,128]{3,2,1,0:T(2,128)S(1)} all-to-all(f32[8,4,2,128]{3,2,1,0:T(2,128)S(1)} %get-tuple-element.46), channel_id=1, replica_groups=mesh['grp'=4,'sub'=8] {'sub'}, dimensions={0} | all-to-all | bytes 65536 | tf_op jit(solution)/shard_map/all_to_all | solution.py:458
  91.9 3.7 %shard_map.78 = f32[1,16,128]{2,1,0:T(8,128)} custom-call(f32[8,4,2,128]{3,2,1,0:T(2,128)S(1)} %all_to_all.5.refs_0_, f32[27,48,128]{2,1,0:T(8,128)S(1)} %shard_map.76.refs_1_, f32[27,48,128]{2,1,0:T(8,128)S(1)} %collective-permute-done.16.refs_2_, f32[27,48,128]{2,1,0:T(8,128)S(1)} %collective-permute-done.17.refs_3_, ...), custom_call_target="tpu_custom_call" | custom-call | tf_op jit(solution)/shard_map/pallas_call | solution.py:25
  (44 shorter events, 9.8 us)
Async XLA Ops:
  0.6 35.7 %copy-start = (f32[27,4,8,512]{3,2,1,0:T(8,128)S(1)}, f32[27,4,8,512]{3,2,1,0:T(8,128)}, u32[]{:S(2)}) copy-start(f32[27,4,8,512]{3,2,1,0:T(8,128)} %c.7) | copy-start | bytes 5308420
  0.6 1.1 %copy-start.4 = (f32[27,2,4,256]{3,2,1,0:T(4,128)S(1)}, f32[27,2,4,256]{3,2,1,0:T(4,128)}, u32[]{:S(2)}) copy-start(f32[27,2,4,256]{3,2,1,0:T(4,128)} %c.9) | copy-start | bytes 663556
  1.8 6.1 %collective-permute-start.14 = (f32[27,2,2,256]{3,2,1,0:T(2,128)S(1)}, f32[27,2,2,256]{3,2,1,0:T(2,128)S(1)}, u32[]{:S(2)}, u32[]{:S(2)}) collective-permute-start(f32[27,2,2,256]{3,2,1,0:T(2,128)S(1)} %get-tuple-element.43), channel_id=1, source_target_pairs={{0,1},{1,0},{2,3},{3,2},{4,5},{5,4},{6,7},{7,6},{8,9},{9,8},{10,11... | collective-permute-start | bytes 331784 | tf_op jit(solution)/shard_map/ppermute | solution.py:384
  4.8 3.1 %collective-permute-start.15 = (f32[27,2,2,256]{3,2,1,0:T(2,128)S(1)}, f32[27,2,2,256]{3,2,1,0:T(2,128)S(1)}, u32[]{:S(2)}, u32[]{:S(2)}) collective-permute-start(f32[27,2,2,256]{3,2,1,0:T(2,128)S(1)} %get-tuple-element.44), channel_id=1, source_target_pairs={{1,2},{2,1},{3,4},{4,3},{5,6},{6,5},{9,10},{10,9},{11,12},{12,11},... | collective-permute-start | bytes 331784 | tf_op jit(solution)/shard_map/ppermute | solution.py:383
  7.9 0.9 copy-start.6
  8.9 16.2 %collective-permute-start.17 = (f32[27,48,128]{2,1,0:T(8,128)S(1)}, f32[27,48,128]{2,1,0:T(8,128)S(1)}, u32[]{:S(2)}, u32[]{:S(2)}) collective-permute-start(f32[27,48,128]{2,1,0:T(8,128)S(1)} %shard_map.76.refs_1_), channel_id=1, source_target_pairs={{0,16},{8,24},{16,0},{24,8},{1,17},{9,25},{17,1},{25,9},{2,18},{10... | collective-permute-start | bytes 1990664 | tf_op jit(solution)/shard_map/ppermute | solution.py:421
  10.8 62.9 %collective-permute-start.16 = (f32[27,48,128]{2,1,0:T(8,128)S(1)}, f32[27,48,128]{2,1,0:T(8,128)S(1)}, u32[]{:S(2)}, u32[]{:S(2)}) collective-permute-start(f32[27,48,128]{2,1,0:T(8,128)S(1)} %shard_map.76.refs_1_), channel_id=1, source_target_pairs={{0,8},{8,0},{16,24},{24,16},{1,9},{9,1},{17,25},{25,17},{2,10},{10... | collective-permute-start | bytes 1990664 | tf_op jit(solution)/shard_map/ppermute | solution.py:421
  25.1 48.6 %collective-permute-start.18 = (f32[27,48,128]{2,1,0:T(8,128)S(1)}, f32[27,48,128]{2,1,0:T(8,128)S(1)}, u32[]{:S(2)}, u32[]{:S(2)}) collective-permute-start(f32[27,48,128]{2,1,0:T(8,128)S(1)} %collective-permute-done.17.refs_3_), channel_id=1, source_target_pairs={{0,8},{8,0},{16,24},{24,16},{1,9},{9,1},{17,25},{25,17},{2,10},{10... | collective-permute-start | bytes 1990664 | tf_op jit(solution)/shard_map/ppermute | solution.py:421
  26.8 20.8 %copy-start.3 = (f32[4,8,512]{2,1,0:T(8,128)S(1)}, f32[4,8,512]{2,1,0:T(8,128)}, u32[]{:S(2)}) copy-start(f32[4,8,512]{2,1,0:T(8,128)} %f.7) | copy-start | bytes 196612
  26.8 6.0 %collective-permute-start = (f32[4,512]{1,0:T(4,128)S(1)}, f32[4,512]{1,0:T(4,128)S(1)}, u32[]{:S(2)}, u32[]{:S(2)}) collective-permute-start(f32[4,512]{1,0:T(4,128)S(1)} %get-tuple-element.26), channel_id=1, source_target_pairs={{0,1},{1,0},{2,3},{3,2},{4,5},{5,4},{6,7},{7,6},{8,9},{9,8},{10,11... | collective-permute-start | bytes 24584 | tf_op jit(solution)/shard_map/ppermute | solution.py:384
  31.2 1.6 %collective-permute-start.1 = (f32[4,512]{1,0:T(4,128)S(1)}, f32[4,512]{1,0:T(4,128)S(1)}, u32[]{:S(2)}, u32[]{:S(2)}) collective-permute-start(f32[4,512]{1,0:T(4,128)S(1)} %get-tuple-element.27), channel_id=1, source_target_pairs={{1,2},{2,1},{3,4},{4,3},{5,6},{6,5},{9,10},{10,9},{11,12},{12,11},... | collective-permute-start | bytes 24584 | tf_op jit(solution)/shard_map/ppermute | solution.py:383
  32.8 1.5 %collective-permute-start.2 = (f32[16,512]{1,0:T(8,128)S(1)}, f32[16,512]{1,0:T(8,128)S(1)}, u32[]{:S(2)}, u32[]{:S(2)}) collective-permute-start(f32[16,512]{1,0:T(8,128)S(1)} %get-tuple-element.28), channel_id=1, source_target_pairs={{0,8},{8,0},{16,24},{24,16},{1,9},{9,1},{17,25},{25,17},{2,10},{10... | collective-permute-start | bytes 98312 | tf_op jit(solution)/shard_map/ppermute | solution.py:391
  32.9 3.4 %collective-permute-start.3 = (f32[16,512]{1,0:T(8,128)S(1)}, f32[16,512]{1,0:T(8,128)S(1)}, u32[]{:S(2)}, u32[]{:S(2)}) collective-permute-start(f32[16,512]{1,0:T(8,128)S(1)} %get-tuple-element.29), channel_id=1, source_target_pairs={{8,16},{16,8},{24,0},{0,24},{9,17},{17,9},{25,1},{1,25},{10,18},{1... | collective-permute-start | bytes 98312 | tf_op jit(solution)/shard_map/ppermute | solution.py:392
  37.5 6.5 %collective-permute-start.4 = (f32[4,512]{1,0:T(4,128)S(1)}, f32[4,512]{1,0:T(4,128)S(1)}, u32[]{:S(2)}, u32[]{:S(2)}) collective-permute-start(f32[4,512]{1,0:T(4,128)S(1)} %get-tuple-element.31), channel_id=1, source_target_pairs={{0,1},{1,0},{2,3},{3,2},{4,5},{5,4},{6,7},{7,6},{8,9},{9,8},{10,11... | collective-permute-start | bytes 24584 | tf_op jit(solution)/shard_map/ppermute | solution.py:384
  42.4 1.6 %collective-permute-start.5 = (f32[4,512]{1,0:T(4,128)S(1)}, f32[4,512]{1,0:T(4,128)S(1)}, u32[]{:S(2)}, u32[]{:S(2)}) collective-permute-start(f32[4,512]{1,0:T(4,128)S(1)} %get-tuple-element.32), channel_id=1, source_target_pairs={{1,2},{2,1},{3,4},{4,3},{5,6},{6,5},{9,10},{10,9},{11,12},{12,11},... | collective-permute-start | bytes 24584 | tf_op jit(solution)/shard_map/ppermute | solution.py:383
  44.0 1.6 %collective-permute-start.6 = (f32[16,512]{1,0:T(8,128)S(1)}, f32[16,512]{1,0:T(8,128)S(1)}, u32[]{:S(2)}, u32[]{:S(2)}) collective-permute-start(f32[16,512]{1,0:T(8,128)S(1)} %get-tuple-element.33), channel_id=1, source_target_pairs={{0,8},{8,0},{16,24},{24,16},{1,9},{9,1},{17,25},{25,17},{2,10},{10... | collective-permute-start | bytes 98312 | tf_op jit(solution)/shard_map/ppermute | solution.py:391
  44.1 3.4 %collective-permute-start.7 = (f32[16,512]{1,0:T(8,128)S(1)}, f32[16,512]{1,0:T(8,128)S(1)}, u32[]{:S(2)}, u32[]{:S(2)}) collective-permute-start(f32[16,512]{1,0:T(8,128)S(1)} %get-tuple-element.34), channel_id=1, source_target_pairs={{8,16},{16,8},{24,0},{0,24},{9,17},{17,9},{25,1},{1,25},{10,18},{1... | collective-permute-start | bytes 98312 | tf_op jit(solution)/shard_map/ppermute | solution.py:392
  48.5 7.8 %collective-permute-start.8 = (f32[4,512]{1,0:T(4,128)S(1)}, f32[4,512]{1,0:T(4,128)S(1)}, u32[]{:S(2)}, u32[]{:S(2)}) collective-permute-start(f32[4,512]{1,0:T(4,128)S(1)} %get-tuple-element.36), channel_id=1, source_target_pairs={{0,1},{1,0},{2,3},{3,2},{4,5},{5,4},{6,7},{7,6},{8,9},{9,8},{10,11... | collective-permute-start | bytes 24584 | tf_op jit(solution)/shard_map/ppermute | solution.py:384
  54.7 1.6 %collective-permute-start.9 = (f32[4,512]{1,0:T(4,128)S(1)}, f32[4,512]{1,0:T(4,128)S(1)}, u32[]{:S(2)}, u32[]{:S(2)}) collective-permute-start(f32[4,512]{1,0:T(4,128)S(1)} %get-tuple-element.37), channel_id=1, source_target_pairs={{1,2},{2,1},{3,4},{4,3},{5,6},{6,5},{9,10},{10,9},{11,12},{12,11},... | collective-permute-start | bytes 24584 | tf_op jit(solution)/shard_map/ppermute | solution.py:383
  56.3 0.8 copy-start.5
  57.2 2.4 %collective-permute-start.10 = (f32[16,512]{1,0:T(8,128)S(1)}, f32[16,512]{1,0:T(8,128)S(1)}, u32[]{:S(2)}, u32[]{:S(2)}) collective-permute-start(f32[16,512]{1,0:T(8,128)S(1)} %get-tuple-element.38), channel_id=1, source_target_pairs={{0,8},{8,0},{16,24},{24,16},{1,9},{9,1},{17,25},{25,17},{2,10},{10... | collective-permute-start | bytes 98312 | tf_op jit(solution)/shard_map/ppermute | solution.py:391
  57.2 3.4 %collective-permute-start.11 = (f32[16,512]{1,0:T(8,128)S(1)}, f32[16,512]{1,0:T(8,128)S(1)}, u32[]{:S(2)}, u32[]{:S(2)}) collective-permute-start(f32[16,512]{1,0:T(8,128)S(1)} %get-tuple-element.39), channel_id=1, source_target_pairs={{8,16},{16,8},{24,0},{0,24},{9,17},{17,9},{25,1},{1,25},{10,18},{1... | collective-permute-start | bytes 98312 | tf_op jit(solution)/shard_map/ppermute | solution.py:392
  61.3 7.0 %collective-permute-start.12 = (f32[8,256]{1,0:T(8,128)S(1)}, f32[8,256]{1,0:T(8,128)S(1)}, u32[]{:S(2)}, u32[]{:S(2)}) collective-permute-start(f32[8,256]{1,0:T(8,128)S(1)} %get-tuple-element.41), channel_id=1, source_target_pairs={{0,1},{1,0},{2,3},{3,2},{4,5},{5,4},{6,7},{7,6},{8,9},{9,8},{10,11... | collective-permute-start | bytes 24584 | tf_op jit(solution)/shard_map/ppermute | solution.py:384
  66.7 1.6 %collective-permute-start.13 = (f32[8,256]{1,0:T(8,128)S(1)}, f32[8,256]{1,0:T(8,128)S(1)}, u32[]{:S(2)}, u32[]{:S(2)}) collective-permute-start(f32[8,256]{1,0:T(8,128)S(1)} %get-tuple-element.42), channel_id=1, source_target_pairs={{1,2},{2,1},{3,4},{4,3},{5,6},{6,5},{9,10},{10,9},{11,12},{12,11},... | collective-permute-start | bytes 24584 | tf_op jit(solution)/shard_map/ppermute | solution.py:383
  (2 other events, 1.7 us)

commit v2 on v1

v2 whole, which is shorter than its diff:
```python
import functools

import jax
import jax.numpy as jnp
from jax import lax
from jax.experimental import pallas as pl
from jax.experimental.pallas import tpu as pltpu
from jax.sharding import PartitionSpec as P

NU0 = 3
NB = 16
WEIGHT = 0.8
CENTER = 13
LANES = 128
ROWS = 8
BASE = 8


def shape(*dims):
    return jax.ShapeDtypeStruct(dims, jnp.float32)


def call(kernel, outs, args, scratch=(), in_specs=None, limit=12, cost=20_000_000):
    vmem = pl.BlockSpec(memory_space=pltpu.VMEM)
    return pl.pallas_call(
        kernel,
        out_shape=outs,
        in_specs=in_specs or [vmem] * len(args),
        out_specs=jax.tree.map(lambda _: vmem, outs),
        scratch_shapes=list(scratch),
        compiler_params=pltpu.CompilerParams(vmem_limit_bytes=limit << 20),
        cost_estimate=pl.CostEstimate(flops=0, bytes_accessed=cost, transcendentals=0),
    )(*args)


def even(axis):
    return lax.rem(lax.axis_index(axis), 2) == 0


def pick(condition, a, b):
    return jnp.where(jnp.broadcast_to(condition, a.shape), a, b)


def shifted(values):
    extent = values.shape[-1]
    lane = lax.broadcasted_iota(jnp.int32, values.shape, values.ndim - 1)
    before = pltpu.roll(values, 1, values.ndim - 1)
    after = pltpu.roll(values, extent - 1, values.ndim - 1)
    return (
        jnp.where(lane == 0, 0.0, before),
        values,
        jnp.where(lane == extent - 1, 0.0, after),
    )


def place(padded, plane, row, values):
    for z, part in enumerate(shifted(values)):
        padded[z, plane, row : row + values.shape[0], :] = part


def stencil(padded, coefficient, first, planes, row, lanes, center=True):
    sums = [None] * planes
    for p in range(planes + 2):
        near = [
            [padded[z, first + p, row - 1 + y : row - 1 + y + ROWS, lanes] for z in range(3)]
            for y in range(3)
        ]
        for x in range(3):
            if not 0 <= p - x < planes:
                continue
            for y in range(3):
                for z in range(3):
                    if not center and 9 * x + 3 * y + z == CENTER:
                        continue
                    term = coefficient(9 * x + 3 * y + z, p - x, lanes) * near[y][z]
                    sums[p - x] = term if sums[p - x] is None else sums[p - x] + term
    return sums


def lane_tiles(extent):
    return [slice(l, l + LANES) for l in range(0, extent, LANES)]


def paired_lanes(values):
    extent = values.shape[-1]
    row = lax.broadcasted_iota(jnp.int32, (extent, extent // 2), 0)
    column = lax.broadcasted_iota(jnp.int32, (extent, extent // 2), 1)
    pairs = jnp.where(lax.shift_right_logical(row, 1) == column, 1.0, 0.0)
    return lax.dot_general(
        values,
        pairs,
        (((1,), (0,)), ((), ())),
        precision=lax.Precision.HIGHEST,
        preferred_element_type=jnp.float32,
    )


def paired_rows(values):
    return values + pltpu.roll(values, values.shape[0] - 1, 0)


def put_edges(v, to_x, to_zx):
    last = v.shape[1] - 1
    for x in range(v.shape[0]):
        first_row, last_row = v[x, 0:1, :], v[x, last : last + 1, :]
        to_x[x : x + 1, :] = pick(even("sub"), last_row, first_row)
        to_zx[x : x + 1, :] = pick(even("sub"), first_row, last_row)


def edges_kernel(v, to_x, to_zx):
    put_edges(v, to_x, to_zx)


def keep_kernel(v, out):
    out[...] = v[...]


def faces_kernel(v, from_x, from_zx, to_core, to_y):
    planes, rows, _ = v.shape
    before = pick(even("sub"), from_zx[0:planes, :], from_x[...])
    after = pick(even("sub"), from_x[...], from_zx[0:planes, :])
    for ref, swap in ((to_core, False), (to_y, True)):
        def choose(a, b):
            return pick(even("grp"), b, a) if swap else pick(even("grp"), a, b)

        ref[0:rows, :] = choose(v[planes - 1], v[0])
        ref[rows : rows + 1, :] = choose(before[planes - 1 :], before[0:1])
        ref[rows + 1 : rows + 2, :] = choose(after[planes - 1 :], after[0:1])


def fill_fine(groups, padded, v, from_x, from_zx, from_core, from_y):
    planes, rows, _ = v.shape
    group = lax.axis_index("grp")
    for x in range(planes):
        place(padded, x + 1, BASE, v[x])
    befores = shifted(pick(even("sub"), from_zx[0:planes, :], from_x[...]))
    afters = shifted(pick(even("sub"), from_x[...], from_zx[0:planes, :]))
    for z in range(3):
        for x in range(planes):
            padded[z, x + 1, BASE - 1 : BASE, :] = befores[z][x : x + 1]
            padded[z, x + 1, BASE + rows : BASE + rows + 1, :] = afters[z][x : x + 1]
    low = pick(even("grp"), from_y[...], from_core[...])
    high = pick(even("grp"), from_core[...], from_y[...])
    low = pick(group == 0, jnp.zeros_like(low), low)
    high = pick(group == groups - 1, jnp.zeros_like(high), high)
    for plane, face in ((0, low), (planes + 1, high)):
        for z, part in enumerate(shifted(face)):
            padded[z, plane, BASE : BASE + rows, :] = part[0:rows]
            padded[z, plane, BASE - 1 : BASE, :] = part[rows : rows + 1]
            padded[z, plane, BASE + rows : BASE + rows + 1, :] = part[rows + 1 : rows + 2]


def sweep_kernel(groups, v, first, c, from_x, from_zx, from_core, from_y, out, to_x, to_zx, padded):
    planes, rows, extent = v.shape
    fill_fine(groups, padded, v, from_x, from_zx, from_core, from_y)
    for lanes in lane_tiles(extent):
        sums = stencil(padded, lambda k, x, l: c[k, x, :, l], 0, planes, BASE, lanes, center=False)
        for x in range(planes):
            out[x, :, lanes] = first[x, :, lanes] + (1.0 - WEIGHT) * v[x, :, lanes] - sums[x]
    put_edges(out, to_x, to_zx)


def residual_kernel(groups, v, first, c, from_x, from_zx, from_core, from_y, center, iterate, to_x, to_zx, padded, held):
    planes, rows, extent = v.shape
    fill_fine(groups, padded, v, from_x, from_zx, from_core, from_y)
    for lanes in lane_tiles(extent):
        sums = stencil(padded, lambda k, x, l: c[k, x, :, l], 0, planes, BASE, lanes, center=False)
        r = []
        for x in range(planes):
            part = first[x, :, lanes] - WEIGHT * v[x, :, lanes] - sums[x]
            r.append((1.0 / WEIGHT) * c[CENTER, x, :, lanes] * part)
        for x in range(planes // 2):
            held[x * rows : (x + 1) * rows, lanes] = r[2 * x] + r[2 * x + 1]
    total = (0.5 * WEIGHT) * paired_rows(paired_lanes(held[...]))
    half = rows // 2
    for x in range(planes // 2):
        for y in range(half):
            row = x * rows + 2 * y
            iterate[x, y : y + 1, :] = total[row : row + 1]
    iterate[...] = iterate[...] / center[...]
    for x in range(planes // 2):
        first, last = iterate[x, 0:3, :], iterate[x, half - 3 : half, :]
        to_x[4 * x : 4 * x + 3, :] = pick(even("sub"), last, first)
        to_zx[4 * x : 4 * x + 3, :] = pick(even("sub"), first, last)


def middle_faces_kernel(mine, from_x, from_zx, out):
    planes, half, _ = mine.shape
    before = pick(even("sub"), from_zx[0 : 4 * planes, :], from_x[...])
    after = pick(even("sub"), from_x[...], from_zx[0 : 4 * planes, :])
    for x in range(planes):
        row = x * ROWS
        out[row : row + 2, :] = before[4 * x + 1 : 4 * x + 3]
        out[row + 2 : row + 2 + half, :] = mine[x]
        out[row + 2 + half : row + ROWS, :] = after[4 * x : 4 * x + 2]
        extra = planes * ROWS + 2 * x
        out[extra : extra + 1, :] = before[4 * x : 4 * x + 1]
        out[extra + 1 : extra + 2, :] = after[4 * x + 2 : 4 * x + 3]


def coefficient_edges_kernel(c, to_x, to_zx):
    rows = c.shape[2]
    first, last = c[:, :, 0:2, :], c[:, :, rows - 2 : rows, :]
    to_x[...] = pick(even("sub"), last, first)
    to_zx[...] = pick(even("sub"), first, last)


def coefficient_scale_kernel(c, out):
    for x in range(c.shape[1]):
        out[:, x] = scaled(c[:, x])


def scaled(c):
    center = c[CENTER : CENTER + 1]
    ratio = WEIGHT * c / jnp.where(center > 0.0, center, 1.0)
    index = lax.broadcasted_iota(jnp.int32, c.shape, 0)
    return jnp.where(index == CENTER, c, ratio)


def coefficient_pack_kernel(known, *refs):
    coarse, (c, from_x, from_zx, _, __, middle_part, whole) = refs[:known], refs[known:]
    _, planes, rows, extent = c.shape
    tiles = extent // LANES
    before = pick(even("sub"), from_zx[...], from_x[...])
    after = pick(even("sub"), from_x[...], from_zx[...])
    for x in range(planes):
        for l, lanes in enumerate(lane_tiles(extent)):
            row = (x * tiles + l) * ROWS
            whole[:, row : row + 2, :] = before[:, x, :, lanes]
            whole[:, row + 2 : row + 2 + rows, :] = c[:, x, :, lanes]
            whole[:, row + 2 + rows : row + ROWS, :] = after[:, x, :, lanes]
    row = planes * tiles * ROWS
    for t in range(0, row, ROWS):
        part = scaled(whole[:, t : t + ROWS, :])
        whole[:, t : t + ROWS, :] = part
        middle_part[:, t : t + ROWS, :] = part
    for ref in coarse:
        for x in range(ref.shape[1]):
            for t in range(0, ref.shape[2], ROWS):
                whole[:, row : row + ROWS, :] = scaled(ref[:, x, t : t + ROWS, :])
                row += ROWS


def middle_kernel(groups, planes, packed, near_core, near_y, far_below, far_above, own, core, other, iterate, coarse, padded, first, fresh):
    extent = packed.shape[-1]
    tiles = extent // LANES
    half = ROWS - 4
    group = lax.axis_index("grp")
    window = 3 * planes

    below = pick(even("grp"), near_y[...], near_core[...])
    above = pick(even("grp"), near_core[...], near_y[...])
    blocks = {-2: far_below[...], -1: below, 0: packed[...], 1: above, 2: far_above[...]}
    for p in range(window + 2):
        away, x = (p - 1) // planes - 1, (p - 1) % planes
        inside = (group + away >= 0) & (group + away < groups)
        block = pick(inside, blocks[away], jnp.zeros_like(blocks[away]))
        extra = planes * ROWS + 2 * x
        for row, count, at in ((x * ROWS, ROWS, BASE), (extra, 1, BASE - 1), (extra + 1, 1, BASE + ROWS)):
            v = block[row : row + count]
            place(padded, p, at, v)
            if count == ROWS and 0 < p <= window:
                first[p - 1] = v

    def work(parts):
        def coefficient(low):
            def get(k, x, lanes):
                w = low + x
                row = (w % planes * tiles + lanes.start // LANES) * ROWS
                return parts[w // planes][k, row : row + ROWS, :]

            return get

        for margin in range(2):
            low, high = planes - 2 + margin, 2 * planes + 2 - margin
            for lanes in lane_tiles(extent):
                sums = stencil(padded, coefficient(low), low, high - low, BASE, lanes, center=False)
                for w in range(low, high):
                    v = padded[1, w + 1, BASE : BASE + ROWS, lanes]
                    fresh[w, :, lanes] = first[w, :, lanes] + (1.0 - WEIGHT) * v - sums[w - low]
            for w in range(low, high):
                place(padded, w + 1, BASE, fresh[w])
        low = planes
        for lanes in lane_tiles(extent):
            sums = stencil(padded, coefficient(low), low, planes, BASE, lanes, center=False)
            for x in range(planes):
                v = fresh[low + x, :, lanes]
                rest = first[low + x, :, lanes] - WEIGHT * v - sums[x]
                fresh[x, :, lanes] = (1.0 / WEIGHT) * coefficient(low)(CENTER, x, lanes) * rest

    @pl.when(even("grp"))
    def _():
        work((other, own, core))

    @pl.when(jnp.logical_not(even("grp")))
    def _():
        work((core, own, other))

    for x in range(planes):
        iterate[x] = padded[1, planes + x + 1, BASE + 2 : BASE + 2 + half, :]
    place_of = lax.broadcasted_iota(jnp.int32, (ROWS, extent // 2), 0)
    for x in range(planes // 2):
        total = 0.5 * paired_rows(paired_lanes(fresh[2 * x] + fresh[2 * x + 1]))
        value = pltpu.roll(total, ROWS - 2, 0)
        for i in range(1, half // 2):
            value = jnp.where(place_of == i, pltpu.roll(total, ROWS - 2 - i, 0), value)
        for device in range(coarse.shape[0]):
            coarse[device, x] = value[: half // 2]


def coarse_order_kernel(planes, rows, start, offsets, own, core, out):
    group = lax.axis_index("grp")
    for ref, flip in ((own, 0), (core, 1)):
        for i, offset in enumerate(offsets):
            owner = jnp.bitwise_xor(group, offset ^ flip)
            for x in range(planes):
                row = start + (i * planes + x) * rows
                out[owner * planes + x] = ref[:, row : row + rows, :]


def coarse_kernel(groups, planes, gathered, c, out, padded, first):
    total, rows, extent = first.shape
    subs = gathered.shape[0] // groups
    each = rows // subs
    for plane in range(total + 2):
        for z in range(3):
            padded[z, plane, :, :] = jnp.zeros(padded.shape[2:], jnp.float32)
    for g in range(groups):
        for s in range(subs):
            for x in range(planes):
                first[g * planes + x, s * each : (s + 1) * each, :] = gathered[g * subs + s, x]
    for p in range(total):
        first[p] = WEIGHT * first[p] / c[p, CENTER]
        place(padded, p + 1, BASE, first[p])

    def sweep(_, carry):
        fresh = []
        for t in range(0, rows, ROWS):
            sums = stencil(
                padded,
                lambda k, x, l: c[x, k, t : t + ROWS, l],
                0,
                total,
                BASE + t,
                slice(0, extent),
                center=False,
            )
            for p in range(total):
                v = padded[1, p + 1, BASE + t : BASE + t + ROWS, :]
                fresh.append((p + 1, BASE + t, first[p, t : t + ROWS, :] + (1.0 - WEIGHT) * v - sums[p]))
        for plane, row, v in fresh:
            place(padded, plane, row, v)
        return carry

    lax.fori_loop(0, NB - 1, sweep, 0)
    for x in range(planes):
        out[x] = padded[1, lax.axis_index("grp") * planes + x + 1, BASE : BASE + rows, :]


def after(value, *others):
    return lax.optimization_barrier((value, *others))[0]


def after_all(values, *others):
    return lax.optimization_barrier((*values, *others))[: len(values)]


def swaps(pairs):
    return [p for a, b in pairs for p in ((a, b), (b, a))]


def body(source, fine, middle, coarse):
    groups, subs = lax.axis_size("grp"), lax.axis_size("sub")
    _, planes, rows, extent = fine.shape
    _, middle_planes, middle_rows, middle_extent = middle.shape
    _, coarse_planes, coarse_rows, coarse_extent = coarse.shape

    x_pairs = swaps([(i, i + 1) for i in range(0, subs, 2)])
    zx_pairs = swaps([(i, i + 1) for i in range(1, subs - 1, 2)])
    core_pairs = swaps([(i, i + 1) for i in range(0, groups, 2)])
    y_pairs = swaps([(i, i + 1) for i in range(1, groups - 1, 2)])
    y_ring = y_pairs + [(groups - 1, 0), (0, groups - 1)]

    def along_sub(pair):
        to_x, to_zx = pair
        from_x = lax.ppermute(to_x, "sub", x_pairs)
        return from_x, lax.ppermute(to_zx, "sub", zx_pairs)

    def along_grp(v, halo):
        to_core, to_y = call(faces_kernel, [shape(rows + 8, extent)] * 2, [v, *halo])
        from_core = lax.ppermute(to_core, "grp", core_pairs)
        from_y = lax.ppermute(to_y, "grp", y_ring)
        return (*halo, from_core, from_y)

    weights = call(coefficient_scale_kernel, shape(*fine.shape), [fine])
    v = WEIGHT * source / fine[CENTER]
    first = v
    to_x, to_zx = call(edges_kernel, [shape(planes, extent), shape(4 * planes, extent)], [v])
    padded_fine = pltpu.VMEM((3, planes + 2, rows + 16, extent), jnp.float32)

    def sweep(v, halo):
        v, *edges = call(
            functools.partial(sweep_kernel, groups),
            [shape(planes, rows, extent), shape(planes, extent), shape(4 * planes, extent)],
            [v, first, weights, *halo],
            [padded_fine],
        )
        return v, along_sub(edges)

    edges_c = call(
        coefficient_edges_kernel,
        [shape(27, middle_planes, 2, middle_extent)] * 2,
        [middle],
    )
    halo = along_sub((to_x, to_zx))
    halo = along_grp(after(v, weights), halo)
    halo_c = along_sub(after_all(edges_c, *halo[2:]))
    v = after(v, *edges_c)
    known = {0: after(coarse, *halo[2:])}
    bit = groups // 2
    while bit > 1:
        for offset in sorted(known):
            known[offset ^ bit] = lax.ppermute(known[offset], "grp", [(i, i ^ bit) for i in range(groups)])
        bit //= 2
    offsets = sorted(known)
    v, halo = sweep(v, halo)
    halo = along_grp(v, halo)
    start = middle_planes * (middle_extent // LANES) * ROWS
    middle_part, own = call(
        functools.partial(coefficient_pack_kernel, len(known)),
        [shape(27, start, LANES), shape(27, start + len(known) * coarse_planes * coarse_rows, LANES)],
        [*(known[o] for o in offsets), middle, *halo_c, *halo[2:]],
    )
    core = lax.ppermute(own, "grp", core_pairs)
    other = lax.ppermute(middle_part, "grp", y_pairs)
    v, halo = sweep(v, halo)
    fine_iterate = call(keep_kernel, shape(planes, rows, extent), [v])
    halo = along_grp(v, halo)
    iterate, *edges = call(
        functools.partial(residual_kernel, groups),
        [shape(middle_planes, middle_rows, middle_extent)]
        + [shape(4 * middle_planes, middle_extent), shape(8 * middle_planes, middle_extent)],
        [v, first, weights, *halo, middle[CENTER]],
        [padded_fine, pltpu.VMEM((planes // 2 * rows, extent), jnp.float32)],
    )
    packed = call(
        middle_faces_kernel,
        shape(middle_planes * ROWS + 8, middle_extent),
        [iterate, *along_sub(edges)],
    )
    near_core = lax.ppermute(packed, "grp", core_pairs)
    if groups == 4:
        far_below = far_above = lax.ppermute(packed, "grp", swaps([(0, 2), (1, 3)]))
        near_y = lax.ppermute(far_below, "grp", core_pairs)
    else:
        near_y = lax.ppermute(packed, "grp", y_pairs)
        up = [(i, i + 2) for i in range(groups - 2)]
        far_below = lax.ppermute(packed, "grp", up)
        far_above = lax.ppermute(packed, "grp", [(j, i) for i, j in up])
    window = pltpu.VMEM((3 * middle_planes, ROWS, middle_extent), jnp.float32)
    middle_iterate, coarse_source = call(
        functools.partial(middle_kernel, groups, middle_planes),
        [
            shape(middle_planes, middle_rows, middle_extent),
            shape(groups * subs, coarse_planes, coarse_rows // subs, coarse_extent),
        ],
        [packed, near_core, near_y, far_below, far_above, own, core, other],
        [
            pltpu.VMEM((3, 3 * middle_planes + 2, ROWS + 16, middle_extent), jnp.float32),
            window,
            window,
        ],
    )
    gathered = lax.all_to_all(coarse_source, ("grp", "sub"), 0, 0, tiled=True)
    total = groups * coarse_planes
    ordered = call(
        functools.partial(coarse_order_kernel, coarse_planes, coarse_rows, start, offsets),
        shape(total, 27, coarse_rows, coarse_extent),
        [own, core],
    )
    coarse_iterate = call(
        functools.partial(coarse_kernel, groups, coarse_planes),
        shape(coarse_planes, coarse_rows, coarse_extent),
        [gathered, ordered],
        [
            pltpu.VMEM((3, total + 2, coarse_rows + 16, coarse_extent), jnp.float32),
            pltpu.VMEM((total, coarse_rows, coarse_extent), jnp.float32),
        ],
    )
    return fine_iterate, middle_iterate, coarse_iterate


def solution(mesh):
    placed = (
        P("grp", "sub", None),
        P(None, "grp", "sub", None),
        P(None, "grp", "sub", None),
        P(None, "grp", None, None),
    )
    return jax.shard_map(
        body,
        mesh=mesh,
        in_specs=placed,
        out_specs=(P("grp", "sub", None), P("grp", "sub", None), P("grp", None, None)),
        check_vma=False,
    )
```

time: 96.2 us -> 73.6 us (0.77)
  blocking collectives: 21.8 us -> 0 us
  starting transfers between devices: 33.8 us -> 42.1 us
  local copies, waits for them, and re-layouts: 6.07 us -> 1.48 us
  waiting for transfers between devices: 25.5 us -> 21 us
    all_to_all x1 -> x0, blocking collectives: 16.5 us -> none  [body(): gathered = lax.all_to_all(coarse_source, 'sub', 0, 0, tiled=True)]
    ppermute x19 -> x22, waiting for transfers between devices: 25.5 us -> 14.5 us  [the longest x3 5.64 us: along_grp(): from_y = lax.ppermute(to_y, 'grp', y_ring)]
    all_to_all x0 -> x1, waiting for transfers between devices: none -> 6.47 us  [body(): gathered = lax.all_to_all(coarse_source, ('grp', 'sub'), 0, 0, tiled=True)]
    all_gather x1 -> x0, blocking collectives: 5.34 us -> none  [body(): packed = lax.all_gather(packed, 'grp', axis=0, tiled=False)]
    all_to_all x0 -> x1, starting transfers between devices: none -> 4.75 us  [body(): gathered = lax.all_to_all(coarse_source, ('grp', 'sub'), 0, 0, tiled=True)]
    ppermute x19 -> x22, starting transfers between devices: 33.8 us -> 37.4 us  [the longest x5 24.2 us: along_sub(): from_x = lax.ppermute(to_x, 'sub', x_pairs)]
    unnamed x14 -> x6, local copies, waits for them, and re-layouts: 4.53 us -> 1.48 us
    slice x2 -> x0, local copies, waits for them, and re-layouts: 1.54 us -> none  [the longest x1 0.85 us: body(): fine[CENTER:CENTER + 1]]
  transfers between devices with their start and end apart: 19 -> 23, of which waited for: 9 -> 10; matrix products, arithmetic and copies ran while one was open for 2% -> 0% of each run, Pallas kernels for 2% -> 3%
where the time goes in v2:
time: 73.6 us; the launch traced here: 73.3 us
  starting transfers between devices  42.1 us (57%)
  waiting for transfers between devices  21 us (29%)
  Pallas kernels  6.96 us (9%)
  local copies, waits for them, and re-layouts  1.48 us (2%)
  other arithmetic  0.89 us (1%)
  between operations  0.8 us (1%)
    ppermute x5, starting transfers between devices, along_sub(): from_x = lax.ppermute(to_x, 'sub', x_pairs)  24.2 us
    pallas_call x15, Pallas kernels, call(): pl.pallas_call(kernel, out_shape=outs, in_specs=in_specs or [vmem] * len(...  6.96 us
    all_to_all x1, waiting for transfers between devices, body(): gathered = lax.all_to_all(coarse_source, ('grp', 'sub'), 0, 0, tiled=True)  6.47 us
    ppermute x3, waiting for transfers between devices, along_grp(): from_y = lax.ppermute(to_y, 'grp', y_ring)  5.64 us
    ppermute x5, waiting for transfers between devices, along_sub(): from_x = lax.ppermute(to_x, 'sub', x_pairs)  4.9 us
    all_to_all x1, starting transfers between devices, body(): gathered = lax.all_to_all(coarse_source, ('grp', 'sub'), 0, 0, tiled=True)  4.75 us
    ppermute x3, starting transfers between devices, along_grp(): from_y = lax.ppermute(to_y, 'grp', y_ring)  4.61 us
    ppermute x5, starting transfers between devices, along_sub(): return (from_x, lax.ppermute(to_zx, 'sub', zx_pairs))  3.31 us
  transfers between devices with their start and end apart: 23, of which 10 were waited for; matrix products, arithmetic and copies ran while one was open for 0% of the time, Pallas kernels for 3%

profile of v2, /device:TPU:0, one launch (start us, length us, event | category | flops | bytes accessed | tf_op | source)
XLA Modules:
  0.0 73.3 jit_solution(5400847658255022517)
XLA Ops:
  0.6 0.9 %bitcast_divide_fusion.v.first = f32[4,8,512]{2,1,0:T(8,128)S(1)} fusion(f32[27,4,8,512]{3,2,1,0:T(8,128)} %c.3, f32[4,8,512]{2,1,0:T(8,128)} %param.4), kind=kLoop, calls=%fused_computation | loop fusion | flops 32768 | bytes 196608 | tf_op jit(solution)/shard_map/div | solution.py:396
  2.2 5.8 %collective-permute-start = (f32[4,512]{1,0:T(4,128)S(1)}, f32[4,512]{1,0:T(4,128)S(1)}, u32[]{:S(2)}, u32[]{:S(2)}) collective-permute-start(f32[4,512]{1,0:T(4,128)S(1)} %get-tuple-element.34), channel_id=1, source_target_pairs={{0,1},{1,0},{2,3},{3,2},{4,5},{5,4},{6,7},{7,6},{8,9},{9,8},{10,11... | collective-permute-start | bytes 24584 | tf_op jit(solution)/shard_map/ppermute | solution.py:386
  8.0 1.5 %copy-done = f32[27,4,8,512]{3,2,1,0:T(8,128)S(1)} copy-done((f32[27,4,8,512]{3,2,1,0:T(8,128)S(1)}, f32[27,4,8,512]{3,2,1,0:T(8,128)}, u32[]{:S(2)}) %copy-start) | copy-done | bytes 1769496
  9.8 1.6 %collective-permute-start.3 = (f32[16,512]{1,0:T(8,128)S(1)}, f32[16,512]{1,0:T(8,128)S(1)}, u32[]{:S(2)}, u32[]{:S(2)}) collective-permute-start(f32[16,512]{1,0:T(8,128)S(1)} %get-tuple-element.38), channel_id=1, source_target_pairs={{8,16},{16,8},{24,0},{0,24},{9,17},{17,9},{25,1},{1,25},{10,18},{1... | collective-permute-start | bytes 98312 | tf_op jit(solution)/shard_map/ppermute | solution.py:392
  11.4 1.8 %collective-permute-done.3.from_y = f32[16,512]{1,0:T(8,128)S(1)} collective-permute-done((f32[16,512]{1,0:T(8,128)S(1)}, f32[16,512]{1,0:T(8,128)S(1)}, u32[]{:S(2)}, u32[]{:S(2)}) %collective-permute-start.3) | collective-permute-done | bytes 32800 | tf_op jit(solution)/shard_map/ppermute | solution.py:392
  13.2 1.5 %collective-permute-start.17 = (f32[27,1,16,128]{3,2,1,0:T(8,128)S(1)}, f32[27,1,16,128]{3,2,1,0:T(8,128)S(1)}, u32[]{:S(2)}, u32[]{:S(2)}) collective-permute-start(f32[27,1,16,128]{3,2,1,0:T(8,128)S(1)} %copy-done.2), channel_id=1, source_target_pairs={{0,16},{8,24},{16,0},{24,8},{1,17},{9,25},{17,1},{25,9},{2,18},{10... | collective-permute-start | bytes 663560 | tf_op jit(solution)/shard_map/ppermute | solution.py:423
  14.8 2.0 %collective-permute-start.18 = (f32[27,2,2,256]{3,2,1,0:T(2,128)S(1)}, f32[27,2,2,256]{3,2,1,0:T(2,128)S(1)}, u32[]{:S(2)}, u32[]{:S(2)}) collective-permute-start(f32[27,2,2,256]{3,2,1,0:T(2,128)S(1)} %get-tuple-element.53), channel_id=1, source_target_pairs={{0,1},{1,0},{2,3},{3,2},{4,5},{5,4},{6,7},{7,6},{8,9},{9,8},{10,11... | collective-permute-start | bytes 331784 | tf_op jit(solution)/shard_map/ppermute | solution.py:386
  18.5 5.6 %collective-permute-start.4 = (f32[4,512]{1,0:T(4,128)S(1)}, f32[4,512]{1,0:T(4,128)S(1)}, u32[]{:S(2)}, u32[]{:S(2)}) collective-permute-start(f32[4,512]{1,0:T(4,128)S(1)} %get-tuple-element.40), channel_id=1, source_target_pairs={{0,1},{1,0},{2,3},{3,2},{4,5},{5,4},{6,7},{7,6},{8,9},{9,8},{10,11... | collective-permute-start | bytes 24584 | tf_op jit(solution)/shard_map/ppermute | solution.py:386
  24.1 1.6 %collective-permute-done.4.from_x = f32[4,512]{1,0:T(4,128)S(1)} collective-permute-done((f32[4,512]{1,0:T(4,128)S(1)}, f32[4,512]{1,0:T(4,128)S(1)}, u32[]{:S(2)}, u32[]{:S(2)}) %collective-permute-start.4) | collective-permute-done | bytes 8224 | tf_op jit(solution)/shard_map/ppermute | solution.py:386
  27.0 2.2 %collective-permute-done.7.from_y.refs_6_ = f32[16,512]{1,0:T(8,128)S(1)} collective-permute-done((f32[16,512]{1,0:T(8,128)S(1)}, f32[16,512]{1,0:T(8,128)S(1)}, u32[]{:S(2)}, u32[]{:S(2)}) %collective-permute-start.7) | collective-permute-done | bytes 32800 | tf_op jit(solution)/shard_map/ppermute | solution.py:392
  31.7 6.2 %collective-permute-start.8 = (f32[4,512]{1,0:T(4,128)S(1)}, f32[4,512]{1,0:T(4,128)S(1)}, u32[]{:S(2)}, u32[]{:S(2)}) collective-permute-start(f32[4,512]{1,0:T(4,128)S(1)} %get-tuple-element.45), channel_id=1, source_target_pairs={{0,1},{1,0},{2,3},{3,2},{4,5},{5,4},{6,7},{7,6},{8,9},{9,8},{10,11... | collective-permute-start | bytes 24584 | tf_op jit(solution)/shard_map/ppermute | solution.py:386
  38.0 1.6 %collective-permute-done.8.from_x = f32[4,512]{1,0:T(4,128)S(1)} collective-permute-done((f32[4,512]{1,0:T(4,128)S(1)}, f32[4,512]{1,0:T(4,128)S(1)}, u32[]{:S(2)}, u32[]{:S(2)}) %collective-permute-start.8) | collective-permute-done | bytes 8224 | tf_op jit(solution)/shard_map/ppermute | solution.py:386
  39.6 0.8 %collective-permute-start.10 = (f32[16,512]{1,0:T(8,128)S(1)}, f32[16,512]{1,0:T(8,128)S(1)}, u32[]{:S(2)}, u32[]{:S(2)}) collective-permute-start(f32[16,512]{1,0:T(8,128)S(1)} %get-tuple-element.47), channel_id=1, source_target_pairs={{0,8},{8,0},{16,24},{24,16},{1,9},{9,1},{17,25},{25,17},{2,10},{10... | collective-permute-start | bytes 98312 | tf_op jit(solution)/shard_map/ppermute | solution.py:391
  40.4 2.4 %collective-permute-start.11 = (f32[16,512]{1,0:T(8,128)S(1)}, f32[16,512]{1,0:T(8,128)S(1)}, u32[]{:S(2)}, u32[]{:S(2)}) collective-permute-start(f32[16,512]{1,0:T(8,128)S(1)} %get-tuple-element.48), channel_id=1, source_target_pairs={{8,16},{16,8},{24,0},{0,24},{9,17},{17,9},{25,1},{1,25},{10,18},{1... | collective-permute-start | bytes 98312 | tf_op jit(solution)/shard_map/ppermute | solution.py:392
  42.7 1.7 %collective-permute-done.11.from_y = f32[16,512]{1,0:T(8,128)S(1)} collective-permute-done((f32[16,512]{1,0:T(8,128)S(1)}, f32[16,512]{1,0:T(8,128)S(1)}, u32[]{:S(2)}, u32[]{:S(2)}) %collective-permute-start.11) | collective-permute-done | bytes 32800 | tf_op jit(solution)/shard_map/ppermute | solution.py:392
  45.7 4.5 %collective-permute-start.12 = (f32[8,256]{1,0:T(8,128)S(1)}, f32[8,256]{1,0:T(8,128)S(1)}, u32[]{:S(2)}, u32[]{:S(2)}) collective-permute-start(f32[8,256]{1,0:T(8,128)S(1)} %get-tuple-element.50), channel_id=1, source_target_pairs={{0,1},{1,0},{2,3},{3,2},{4,5},{5,4},{6,7},{7,6},{8,9},{9,8},{10,11... | collective-permute-start | bytes 24584 | tf_op jit(solution)/shard_map/ppermute | solution.py:386
  50.2 1.6 %collective-permute-done.12.from_x = f32[8,256]{1,0:T(8,128)S(1)} collective-permute-done((f32[8,256]{1,0:T(8,128)S(1)}, f32[8,256]{1,0:T(8,128)S(1)}, u32[]{:S(2)}, u32[]{:S(2)}) %collective-permute-start.12) | collective-permute-done | bytes 8224 | tf_op jit(solution)/shard_map/ppermute | solution.py:386
  51.9 1.7 %collective-permute-start.15 = (f32[24,256]{1,0:T(8,128)S(1)}, f32[24,256]{1,0:T(8,128)S(1)}, u32[]{:S(2)}, u32[]{:S(2)}) collective-permute-start(f32[24,256]{1,0:T(8,128)S(1)} %shard_map.77.packed), channel_id=1, source_target_pairs={{0,16},{16,0},{8,24},{24,8},{1,17},{17,1},{9,25},{25,9},{2,18},{18... | collective-permute-start | bytes 73736 | tf_op jit(solution)/shard_map/ppermute | solution.py:453
  53.6 2.2 %collective-permute-done.15.far_below.far_above = f32[24,256]{1,0:T(8,128)S(1)} collective-permute-done((f32[24,256]{1,0:T(8,128)S(1)}, f32[24,256]{1,0:T(8,128)S(1)}, u32[]{:S(2)}, u32[]{:S(2)}) %collective-permute-start.15) | collective-permute-done | bytes 24608 | tf_op jit(solution)/shard_map/ppermute | solution.py:453
  55.8 1.2 %collective-permute-done.16.near_y = f32[24,256]{1,0:T(8,128)S(1)} collective-permute-done((f32[24,256]{1,0:T(8,128)S(1)}, f32[24,256]{1,0:T(8,128)S(1)}, u32[]{:S(2)}, u32[]{:S(2)}) %collective-permute-start.16) | collective-permute-done | bytes 24608 | tf_op jit(solution)/shard_map/ppermute | solution.py:454
  57.0 1.4 %shard_map.79 = (f32[2,4,256]{2,1,0:T(4,128)}, f32[32,1,2,128]{3,2,1,0:T(2,128)}) custom-call(f32[24,256]{1,0:T(8,128)S(1)} %shard_map.77.packed, f32[24,256]{1,0:T(8,128)S(1)} %collective-permute-done.14.near_core, f32[24,256]{1,0:T(8,128)S(1)} %collective-permute-done.16.near_y, f32[24,256]{1,0:T(8,128)S(1)} %collective-permute-done.15.far_below.far_above, ...), custom_call_target="tpu_custom_call" | custom-call | bytes 20000000 | tf_op jit(solution)/shard_map/pallas_call | solution.py:25
  58.4 4.8 %all-to-all-start = ((f32[32,1,2,128]{3,2,1,0:T(2,128)}), f32[32,1,2,128]{3,2,1,0:T(2,128)S(1)}, u32[]{:S(2)}, u32[]{:S(2)}) async-start(f32[32,1,2,128]{3,2,1,0:T(2,128)} %get-tuple-element.58), calls=%async_computation | async-start | bytes 65536 | tf_op jit(solution)/shard_map/all_to_all | solution.py:474
  63.9 6.5 %all-to-all-done.gathered = f32[32,1,2,128]{3,2,1,0:T(2,128)S(1)} async-done(((f32[32,1,2,128]{3,2,1,0:T(2,128)}), f32[32,1,2,128]{3,2,1,0:T(2,128)S(1)}, u32[]{:S(2)}, u32[]{:S(2)}) %all-to-all-start) | async-done | bytes 32800 | tf_op jit(solution)/shard_map/all_to_all | solution.py:474
  70.3 3.0 %shard_map.81 = f32[1,16,128]{2,1,0:T(8,128)} custom-call(f32[32,1,2,128]{3,2,1,0:T(2,128)S(1)} %all-to-all-done.gathered, f32[4,27,16,128]{3,2,1,0:T(8,128)S(1)} %shard_map.80.c), custom_call_target="tpu_custom_call" | custom-call | bytes 20000000 | tf_op jit(solution)/shard_map/pallas_call | solution.py:25
  (45 shorter events, 8.5 us)
Async XLA Ops:
  1.5 8.1 %collective-permute-start.1 = (f32[16,512]{1,0:T(8,128)S(1)}, f32[16,512]{1,0:T(8,128)S(1)}, u32[]{:S(2)}, u32[]{:S(2)}) collective-permute-start(f32[16,512]{1,0:T(8,128)S(1)} %get-tuple-element.35), channel_id=1, source_target_pairs={{1,2},{2,1},{3,4},{4,3},{5,6},{6,5},{9,10},{10,9},{11,12},{12,11},... | collective-permute-start | bytes 98312 | tf_op jit(solution)/shard_map/ppermute | solution.py:387
  2.2 7.4 %collective-permute-start = (f32[4,512]{1,0:T(4,128)S(1)}, f32[4,512]{1,0:T(4,128)S(1)}, u32[]{:S(2)}, u32[]{:S(2)}) collective-permute-start(f32[4,512]{1,0:T(4,128)S(1)} %get-tuple-element.34), channel_id=1, source_target_pairs={{0,1},{1,0},{2,3},{3,2},{4,5},{5,4},{6,7},{7,6},{8,9},{9,8},{10,11... | collective-permute-start | bytes 24584 | tf_op jit(solution)/shard_map/ppermute | solution.py:386
  9.5 5.2 %copy-start.1 = (f32[27,2,4,256]{3,2,1,0:T(4,128)S(1)}, f32[27,2,4,256]{3,2,1,0:T(4,128)}, u32[]{:S(2)}) copy-start(f32[27,2,4,256]{3,2,1,0:T(4,128)} %refs_2_.1) | copy-start | bytes 663556
  9.7 1.7 %collective-permute-start.2 = (f32[16,512]{1,0:T(8,128)S(1)}, f32[16,512]{1,0:T(8,128)S(1)}, u32[]{:S(2)}, u32[]{:S(2)}) collective-permute-start(f32[16,512]{1,0:T(8,128)S(1)} %get-tuple-element.37), channel_id=1, source_target_pairs={{0,8},{8,0},{16,24},{24,16},{1,9},{9,1},{17,25},{25,17},{2,10},{10... | collective-permute-start | bytes 98312 | tf_op jit(solution)/shard_map/ppermute | solution.py:391
  9.8 3.4 %collective-permute-start.3 = (f32[16,512]{1,0:T(8,128)S(1)}, f32[16,512]{1,0:T(8,128)S(1)}, u32[]{:S(2)}, u32[]{:S(2)}) collective-permute-start(f32[16,512]{1,0:T(8,128)S(1)} %get-tuple-element.38), channel_id=1, source_target_pairs={{8,16},{16,8},{24,0},{0,24},{9,17},{17,9},{25,1},{1,25},{10,18},{1... | collective-permute-start | bytes 98312 | tf_op jit(solution)/shard_map/ppermute | solution.py:392
  13.2 16.0 %collective-permute-start.17 = (f32[27,1,16,128]{3,2,1,0:T(8,128)S(1)}, f32[27,1,16,128]{3,2,1,0:T(8,128)S(1)}, u32[]{:S(2)}, u32[]{:S(2)}) collective-permute-start(f32[27,1,16,128]{3,2,1,0:T(8,128)S(1)} %copy-done.2), channel_id=1, source_target_pairs={{0,16},{8,24},{16,0},{24,8},{1,17},{9,25},{17,1},{25,9},{2,18},{10... | collective-permute-start | bytes 663560 | tf_op jit(solution)/shard_map/ppermute | solution.py:423
  14.8 14.4 %collective-permute-start.18 = (f32[27,2,2,256]{3,2,1,0:T(2,128)S(1)}, f32[27,2,2,256]{3,2,1,0:T(2,128)S(1)}, u32[]{:S(2)}, u32[]{:S(2)}) collective-permute-start(f32[27,2,2,256]{3,2,1,0:T(2,128)S(1)} %get-tuple-element.53), channel_id=1, source_target_pairs={{0,1},{1,0},{2,3},{3,2},{4,5},{5,4},{6,7},{7,6},{8,9},{9,8},{10,11... | collective-permute-start | bytes 331784 | tf_op jit(solution)/shard_map/ppermute | solution.py:386
  16.9 12.4 %collective-permute-start.19 = (f32[27,2,2,256]{3,2,1,0:T(2,128)S(1)}, f32[27,2,2,256]{3,2,1,0:T(2,128)S(1)}, u32[]{:S(2)}, u32[]{:S(2)}) collective-permute-start(f32[27,2,2,256]{3,2,1,0:T(2,128)S(1)} %get-tuple-element.54), channel_id=1, source_target_pairs={{1,2},{2,1},{3,4},{4,3},{5,6},{6,5},{9,10},{10,9},{11,12},{12,11},... | collective-permute-start | bytes 331784 | tf_op jit(solution)/shard_map/ppermute | solution.py:387
  17.8 7.9 %collective-permute-start.5 = (f32[16,512]{1,0:T(8,128)S(1)}, f32[16,512]{1,0:T(8,128)S(1)}, u32[]{:S(2)}, u32[]{:S(2)}) collective-permute-start(f32[16,512]{1,0:T(8,128)S(1)} %get-tuple-element.41), channel_id=1, source_target_pairs={{1,2},{2,1},{3,4},{4,3},{5,6},{6,5},{9,10},{10,9},{11,12},{12,11},... | collective-permute-start | bytes 98312 | tf_op jit(solution)/shard_map/ppermute | solution.py:387
  18.5 7.2 %collective-permute-start.4 = (f32[4,512]{1,0:T(4,128)S(1)}, f32[4,512]{1,0:T(4,128)S(1)}, u32[]{:S(2)}, u32[]{:S(2)}) collective-permute-start(f32[4,512]{1,0:T(4,128)S(1)} %get-tuple-element.40), channel_id=1, source_target_pairs={{0,1},{1,0},{2,3},{3,2},{4,5},{5,4},{6,7},{7,6},{8,9},{9,8},{10,11... | collective-permute-start | bytes 24584 | tf_op jit(solution)/shard_map/ppermute | solution.py:386
  25.8 1.3 %collective-permute-start.6 = (f32[16,512]{1,0:T(8,128)S(1)}, f32[16,512]{1,0:T(8,128)S(1)}, u32[]{:S(2)}, u32[]{:S(2)}) collective-permute-start(f32[16,512]{1,0:T(8,128)S(1)} %get-tuple-element.42), channel_id=1, source_target_pairs={{0,8},{8,0},{16,24},{24,16},{1,9},{9,1},{17,25},{25,17},{2,10},{10... | collective-permute-start | bytes 98312 | tf_op jit(solution)/shard_map/ppermute | solution.py:391
  25.8 3.4 %collective-permute-start.7 = (f32[16,512]{1,0:T(8,128)S(1)}, f32[16,512]{1,0:T(8,128)S(1)}, u32[]{:S(2)}, u32[]{:S(2)}) collective-permute-start(f32[16,512]{1,0:T(8,128)S(1)} %get-tuple-element.43), channel_id=1, source_target_pairs={{8,16},{16,8},{24,0},{0,24},{9,17},{17,9},{25,1},{1,25},{10,18},{1... | collective-permute-start | bytes 98312 | tf_op jit(solution)/shard_map/ppermute | solution.py:392
  29.5 27.4 %collective-permute-start.20 = (f32[27,64,128]{2,1,0:T(8,128)S(1)}, f32[27,64,128]{2,1,0:T(8,128)S(1)}, u32[]{:S(2)}, u32[]{:S(2)}) collective-permute-start(f32[27,64,128]{2,1,0:T(8,128)S(1)} %get-tuple-element.55.own), channel_id=1, source_target_pairs={{0,8},{8,0},{16,24},{24,16},{1,9},{9,1},{17,25},{25,17},{2,10},{10... | collective-permute-start | bytes 2654216 | tf_op jit(solution)/shard_map/ppermute | solution.py:434
  30.1 26.9 %collective-permute-start.21 = (f32[27,32,128]{2,1,0:T(8,128)S(1)}, f32[27,32,128]{2,1,0:T(8,128)S(1)}, u32[]{:S(2)}, u32[]{:S(2)}) collective-permute-start(f32[27,32,128]{2,1,0:T(8,128)S(1)} %get-tuple-element.56), channel_id=1, source_target_pairs={{8,16},{16,8},{9,17},{17,9},{10,18},{18,10},{11,19},{19,11},{12,20... | collective-permute-start | bytes 1327112 | tf_op jit(solution)/shard_map/ppermute | solution.py:435
  31.1 8.5 %collective-permute-start.9 = (f32[16,512]{1,0:T(8,128)S(1)}, f32[16,512]{1,0:T(8,128)S(1)}, u32[]{:S(2)}, u32[]{:S(2)}) collective-permute-start(f32[16,512]{1,0:T(8,128)S(1)} %get-tuple-element.46), channel_id=1, source_target_pairs={{1,2},{2,1},{3,4},{4,3},{5,6},{6,5},{9,10},{10,9},{11,12},{12,11},... | collective-permute-start | bytes 98312 | tf_op jit(solution)/shard_map/ppermute | solution.py:387
  31.7 7.9 %collective-permute-start.8 = (f32[4,512]{1,0:T(4,128)S(1)}, f32[4,512]{1,0:T(4,128)S(1)}, u32[]{:S(2)}, u32[]{:S(2)}) collective-permute-start(f32[4,512]{1,0:T(4,128)S(1)} %get-tuple-element.45), channel_id=1, source_target_pairs={{0,1},{1,0},{2,3},{3,2},{4,5},{5,4},{6,7},{7,6},{8,9},{9,8},{10,11... | collective-permute-start | bytes 24584 | tf_op jit(solution)/shard_map/ppermute | solution.py:386
  39.6 3.1 %collective-permute-start.10 = (f32[16,512]{1,0:T(8,128)S(1)}, f32[16,512]{1,0:T(8,128)S(1)}, u32[]{:S(2)}, u32[]{:S(2)}) collective-permute-start(f32[16,512]{1,0:T(8,128)S(1)} %get-tuple-element.47), channel_id=1, source_target_pairs={{0,8},{8,0},{16,24},{24,16},{1,9},{9,1},{17,25},{25,17},{2,10},{10... | collective-permute-start | bytes 98312 | tf_op jit(solution)/shard_map/ppermute | solution.py:391
  40.4 4.0 %collective-permute-start.11 = (f32[16,512]{1,0:T(8,128)S(1)}, f32[16,512]{1,0:T(8,128)S(1)}, u32[]{:S(2)}, u32[]{:S(2)}) collective-permute-start(f32[16,512]{1,0:T(8,128)S(1)} %get-tuple-element.48), channel_id=1, source_target_pairs={{8,16},{16,8},{24,0},{0,24},{9,17},{17,9},{25,1},{1,25},{10,18},{1... | collective-permute-start | bytes 98312 | tf_op jit(solution)/shard_map/ppermute | solution.py:392
  45.1 6.8 %collective-permute-start.13 = (f32[16,256]{1,0:T(8,128)S(1)}, f32[16,256]{1,0:T(8,128)S(1)}, u32[]{:S(2)}, u32[]{:S(2)}) collective-permute-start(f32[16,256]{1,0:T(8,128)S(1)} %get-tuple-element.51), channel_id=1, source_target_pairs={{1,2},{2,1},{3,4},{4,3},{5,6},{6,5},{9,10},{10,9},{11,12},{12,11},... | collective-permute-start | bytes 49160 | tf_op jit(solution)/shard_map/ppermute | solution.py:387
  45.7 6.1 %collective-permute-start.12 = (f32[8,256]{1,0:T(8,128)S(1)}, f32[8,256]{1,0:T(8,128)S(1)}, u32[]{:S(2)}, u32[]{:S(2)}) collective-permute-start(f32[8,256]{1,0:T(8,128)S(1)} %get-tuple-element.50), channel_id=1, source_target_pairs={{0,1},{1,0},{2,3},{3,2},{4,5},{5,4},{6,7},{7,6},{8,9},{9,8},{10,11... | collective-permute-start | bytes 24584 | tf_op jit(solution)/shard_map/ppermute | solution.py:386
  51.9 3.9 %collective-permute-start.15 = (f32[24,256]{1,0:T(8,128)S(1)}, f32[24,256]{1,0:T(8,128)S(1)}, u32[]{:S(2)}, u32[]{:S(2)}) collective-permute-start(f32[24,256]{1,0:T(8,128)S(1)} %shard_map.77.packed), channel_id=1, source_target_pairs={{0,16},{16,0},{8,24},{24,8},{1,17},{17,1},{9,25},{25,9},{2,18},{18... | collective-permute-start | bytes 73736 | tf_op jit(solution)/shard_map/ppermute | solution.py:453
  53.6 2.2 %collective-permute-start.14 = (f32[24,256]{1,0:T(8,128)S(1)}, f32[24,256]{1,0:T(8,128)S(1)}, u32[]{:S(2)}, u32[]{:S(2)}) collective-permute-start(f32[24,256]{1,0:T(8,128)S(1)} %shard_map.77.packed), channel_id=1, source_target_pairs={{0,8},{8,0},{16,24},{24,16},{1,9},{9,1},{17,25},{25,17},{2,10},{10... | collective-permute-start | bytes 73736 | tf_op jit(solution)/shard_map/ppermute | solution.py:451
  55.8 1.2 %collective-permute-start.16 = (f32[24,256]{1,0:T(8,128)S(1)}, f32[24,256]{1,0:T(8,128)S(1)}, u32[]{:S(2)}, u32[]{:S(2)}) collective-permute-start(f32[24,256]{1,0:T(8,128)S(1)} %collective-permute-done.15.far_below.far_above), channel_id=1, source_target_pairs={{0,8},{8,0},{16,24},{24,16},{1,9},{9,1},{17,25},{25,17},{2,10},{10... | collective-permute-start | bytes 73736 | tf_op jit(solution)/shard_map/ppermute | solution.py:454
  58.4 11.9 %all-to-all-start = ((f32[32,1,2,128]{3,2,1,0:T(2,128)}), f32[32,1,2,128]{3,2,1,0:T(2,128)S(1)}, u32[]{:S(2)}, u32[]{:S(2)}) async-start(f32[32,1,2,128]{3,2,1,0:T(2,128)} %get-tuple-element.58), calls=%async_computation | async-start | bytes 65536 | tf_op jit(solution)/shard_map/all_to_all | solution.py:474
  (2 other events, 5.2 us)

commit v3 on v2

--- a/solution.py
+++ b/solution.py
@@ -39,6 +39,12 @@
 
 def pick(condition, a, b):
     return jnp.where(jnp.broadcast_to(condition, a.shape), a, b)
+
+
+def sides(from_x, from_zx):
+    sub, subs = lax.axis_index("sub"), lax.axis_size("sub")
+    from_zx = pick((sub == 0) | (sub == subs - 1), jnp.zeros_like(from_zx), from_zx)
+    return pick(even("sub"), from_zx, from_x), pick(even("sub"), from_x, from_zx)
 
 
 def shifted(values):
@@ -117,8 +123,7 @@
 
 def faces_kernel(v, from_x, from_zx, to_core, to_y):
     planes, rows, _ = v.shape
-    before = pick(even("sub"), from_zx[0:planes, :], from_x[...])
-    after = pick(even("sub"), from_x[...], from_zx[0:planes, :])
+    before, after = sides(from_x[...], from_zx[0:planes, :])
     for ref, swap in ((to_core, False), (to_y, True)):
         def choose(a, b):
             return pick(even("grp"), b, a) if swap else pick(even("grp"), a, b)
@@ -133,8 +138,7 @@
     group = lax.axis_index("grp")
     for x in range(planes):
         place(padded, x + 1, BASE, v[x])
-    befores = shifted(pick(even("sub"), from_zx[0:planes, :], from_x[...]))
-    afters = shifted(pick(even("sub"), from_x[...], from_zx[0:planes, :]))
+    befores, afters = map(shifted, sides(from_x[...], from_zx[0:planes, :]))
     for z in range(3):
         for x in range(planes):
             padded[z, x + 1, BASE - 1 : BASE, :] = befores[z][x : x + 1]
@@ -186,8 +190,7 @@
 
 def middle_faces_kernel(mine, from_x, from_zx, out):
     planes, half, _ = mine.shape
-    before = pick(even("sub"), from_zx[0 : 4 * planes, :], from_x[...])
-    after = pick(even("sub"), from_x[...], from_zx[0 : 4 * planes, :])
+    before, after = sides(from_x[...], from_zx[0 : 4 * planes, :])
     for x in range(planes):
         row = x * ROWS
         out[row : row + 2, :] = before[4 * x + 1 : 4 * x + 3]
@@ -221,8 +224,7 @@
     coarse, (c, from_x, from_zx, _, __, middle_part, whole) = refs[:known], refs[known:]
     _, planes, rows, extent = c.shape
     tiles = extent // LANES
-    before = pick(even("sub"), from_zx[...], from_x[...])
-    after = pick(even("sub"), from_x[...], from_zx[...])
+    before, after = sides(from_x[...], from_zx[...])
     for x in range(planes):
         for l, lanes in enumerate(lane_tiles(extent)):
             row = (x * tiles + l) * ROWS
@@ -376,7 +378,10 @@
     _, coarse_planes, coarse_rows, coarse_extent = coarse.shape
 
     x_pairs = swaps([(i, i + 1) for i in range(0, subs, 2)])
-    zx_pairs = swaps([(i, i + 1) for i in range(1, subs - 1, 2)])
+    zx_pairs = swaps(
+        [(g * subs + i, g * subs + i + 1) for g in range(groups) for i in range(1, subs - 1, 2)]
+        + [(g * subs + i, (g + 1) * subs + i) for g in range(0, groups, 2) for i in (0, subs - 1)]
+    )
     core_pairs = swaps([(i, i + 1) for i in range(0, groups, 2)])
     y_pairs = swaps([(i, i + 1) for i in range(1, groups - 1, 2)])
     y_ring = y_pairs + [(groups - 1, 0), (0, groups - 1)]
@@ -384,7 +389,7 @@
     def along_sub(pair):
         to_x, to_zx = pair
         from_x = lax.ppermute(to_x, "sub", x_pairs)
-        return from_x, lax.ppermute(to_zx, "sub", zx_pairs)
+        return from_x, lax.ppermute(to_zx, ("grp", "sub"), zx_pairs)
 
     def along_grp(v, halo):
         to_core, to_y = call(faces_kernel, [shape(rows + 8, extent)] * 2, [v, *halo])
@@ -413,9 +418,8 @@
         [middle],
     )
     halo = along_sub((to_x, to_zx))
-    halo = along_grp(after(v, weights), halo)
-    halo_c = along_sub(after_all(edges_c, *halo[2:]))
-    v = after(v, *edges_c)
+    halo_c = along_sub(after_all(edges_c, *halo))
+    halo = along_grp(after(v, weights, *edges_c), halo)
     known = {0: after(coarse, *halo[2:])}
     bit = groups // 2
     while bit > 1:

time: 73.6 us -> 64.7 us (0.88)
  starting transfers between devices: 42.1 us -> 32.6 us
  local copies, waits for them, and re-layouts: 1.48 us -> 2.25 us
    ppermute x5, starting transfers between devices: 24.2 us -> 14.2 us  [along_sub(): from_x = lax.ppermute(to_x, 'sub', x_pairs)]
    unnamed x6, local copies, waits for them, and re-layouts: 1.48 us -> 2.25 us
  transfers between devices with their start and end apart: 23 -> 23, of which waited for: 10 -> 10; matrix products, arithmetic and copies ran while one was open for 0% -> 0% of each run, Pallas kernels for 3% -> 4%
where the time goes in v3:
time: 64.7 us; the launch traced here: 64.5 us
  starting transfers between devices  32.6 us (50%)
  waiting for transfers between devices  21 us (32%)
  Pallas kernels  6.98 us (11%)
  local copies, waits for them, and re-layouts  2.25 us (3%)
  other arithmetic  0.89 us (1%)
  between operations  0.77 us (1%)
    ppermute x5, starting transfers between devices, along_sub(): from_x = lax.ppermute(to_x, 'sub', x_pairs)  14.2 us
    pallas_call x15, Pallas kernels, call(): pl.pallas_call(kernel, out_shape=outs, in_specs=in_specs or [vmem] * len(...  6.98 us
    all_to_all x1, waiting for transfers between devices, body(): gathered = lax.all_to_all(coarse_source, ('grp', 'sub'), 0, 0, tiled=True)  6.47 us
    ppermute x3, waiting for transfers between devices, along_grp(): from_y = lax.ppermute(to_y, 'grp', y_ring)  5.64 us
    all_to_all x1, starting transfers between devices, body(): gathered = lax.all_to_all(coarse_source, ('grp', 'sub'), 0, 0, tiled=True)  5.23 us
    ppermute x5, waiting for transfers between devices, along_sub(): from_x = lax.ppermute(to_x, 'sub', x_pairs)  4.89 us
    ppermute x3, starting transfers between devices, along_grp(): from_y = lax.ppermute(to_y, 'grp', y_ring)  4.61 us
    ppermute x5, starting transfers between devices, along_sub(): return (from_x, lax.ppermute(to_zx, ('grp', 'sub'), zx_pairs))  3.18 us
  transfers between devices with their start and end apart: 23, of which 10 were waited for; matrix products, arithmetic and copies ran while one was open for 0% of the time, Pallas kernels for 4%

profile of v3, /device:TPU:0, one launch (start us, length us, event | category | flops | bytes accessed | tf_op | source)
XLA Modules:
  0.0 64.5 jit_solution(9837978840158993557)
XLA Ops:
  0.6 0.9 %bitcast_divide_fusion.v.first = f32[4,8,512]{2,1,0:T(8,128)S(1)} fusion(f32[27,4,8,512]{3,2,1,0:T(8,128)} %c.2, f32[4,8,512]{2,1,0:T(8,128)} %param.4), kind=kLoop, calls=%fused_computation | loop fusion | flops 32768 | bytes 196608 | tf_op jit(solution)/shard_map/div | solution.py:401
  2.1 4.0 %collective-permute-start = (f32[4,512]{1,0:T(4,128)S(1)}, f32[4,512]{1,0:T(4,128)S(1)}, u32[]{:S(2)}, u32[]{:S(2)}) collective-permute-start(f32[4,512]{1,0:T(4,128)S(1)} %get-tuple-element.30), channel_id=1, source_target_pairs={{0,1},{1,0},{2,3},{3,2},{4,5},{5,4},{6,7},{7,6},{8,9},{9,8},{10,11... | collective-permute-start | bytes 24584 | tf_op jit(solution)/shard_map/ppermute | solution.py:391
  6.1 1.5 %copy-done = f32[27,4,8,512]{3,2,1,0:T(8,128)S(1)} copy-done((f32[27,4,8,512]{3,2,1,0:T(8,128)S(1)}, f32[27,4,8,512]{3,2,1,0:T(8,128)}, u32[]{:S(2)}) %copy-start) | copy-done | bytes 1769496
  8.7 1.6 %collective-permute-start.3 = (f32[16,512]{1,0:T(8,128)S(1)}, f32[16,512]{1,0:T(8,128)S(1)}, u32[]{:S(2)}, u32[]{:S(2)}) collective-permute-start(f32[16,512]{1,0:T(8,128)S(1)} %get-tuple-element.36), channel_id=1, source_target_pairs={{8,16},{16,8},{24,0},{0,24},{9,17},{17,9},{25,1},{1,25},{10,18},{1... | collective-permute-start | bytes 98312 | tf_op jit(solution)/shard_map/ppermute | solution.py:397
  10.4 1.8 %collective-permute-done.3.from_y = f32[16,512]{1,0:T(8,128)S(1)} collective-permute-done((f32[16,512]{1,0:T(8,128)S(1)}, f32[16,512]{1,0:T(8,128)S(1)}, u32[]{:S(2)}, u32[]{:S(2)}) %collective-permute-start.3) | collective-permute-done | bytes 32800 | tf_op jit(solution)/shard_map/ppermute | solution.py:397
  12.1 1.5 %collective-permute-start.17 = (f32[27,1,16,128]{3,2,1,0:T(8,128)S(1)}, f32[27,1,16,128]{3,2,1,0:T(8,128)S(1)}, u32[]{:S(2)}, u32[]{:S(2)}) collective-permute-start(f32[27,1,16,128]{3,2,1,0:T(8,128)S(1)} %copy-done.2), channel_id=1, source_target_pairs={{0,16},{8,24},{16,0},{24,8},{1,17},{9,25},{17,1},{25,9},{2,18},{10... | collective-permute-start | bytes 663560 | tf_op jit(solution)/shard_map/ppermute | solution.py:427
  13.7 1.1 %collective-permute-start.18 = (f32[27,2,2,256]{3,2,1,0:T(2,128)S(1)}, f32[27,2,2,256]{3,2,1,0:T(2,128)S(1)}, u32[]{:S(2)}, u32[]{:S(2)}) collective-permute-start(f32[27,2,2,256]{3,2,1,0:T(2,128)S(1)} %get-tuple-element.51), channel_id=1, source_target_pairs={{0,1},{1,0},{2,3},{3,2},{4,5},{5,4},{6,7},{7,6},{8,9},{9,8},{10,11... | collective-permute-start | bytes 331784 | tf_op jit(solution)/shard_map/ppermute | solution.py:391
  15.7 3.3 %collective-permute-start.4 = (f32[4,512]{1,0:T(4,128)S(1)}, f32[4,512]{1,0:T(4,128)S(1)}, u32[]{:S(2)}, u32[]{:S(2)}) collective-permute-start(f32[4,512]{1,0:T(4,128)S(1)} %get-tuple-element.38), channel_id=1, source_target_pairs={{0,1},{1,0},{2,3},{3,2},{4,5},{5,4},{6,7},{7,6},{8,9},{9,8},{10,11... | collective-permute-start | bytes 24584 | tf_op jit(solution)/shard_map/ppermute | solution.py:391
  19.0 1.6 %collective-permute-done.4.from_x = f32[4,512]{1,0:T(4,128)S(1)} collective-permute-done((f32[4,512]{1,0:T(4,128)S(1)}, f32[4,512]{1,0:T(4,128)S(1)}, u32[]{:S(2)}, u32[]{:S(2)}) %collective-permute-start.4) | collective-permute-done | bytes 8224 | tf_op jit(solution)/shard_map/ppermute | solution.py:391
  21.9 2.2 %collective-permute-done.7.from_y.refs_6_ = f32[16,512]{1,0:T(8,128)S(1)} collective-permute-done((f32[16,512]{1,0:T(8,128)S(1)}, f32[16,512]{1,0:T(8,128)S(1)}, u32[]{:S(2)}, u32[]{:S(2)}) %collective-permute-start.7) | collective-permute-done | bytes 32800 | tf_op jit(solution)/shard_map/ppermute | solution.py:397
  26.0 1.9 %collective-permute-start.9 = (f32[16,512]{1,0:T(8,128)S(1)}, f32[16,512]{1,0:T(8,128)S(1)}, u32[]{:S(2)}, u32[]{:S(2)}) collective-permute-start(f32[16,512]{1,0:T(8,128)S(1)} %get-tuple-element.44), channel_id=1, source_target_pairs={{1,2},{2,1},{3,4},{4,3},{5,6},{6,5},{9,10},{10,9},{11,12},{12,11},... | collective-permute-start | bytes 98312 | tf_op jit(solution)/shard_map/ppermute | solution.py:392
  27.9 2.6 %collective-permute-start.8 = (f32[4,512]{1,0:T(4,128)S(1)}, f32[4,512]{1,0:T(4,128)S(1)}, u32[]{:S(2)}, u32[]{:S(2)}) collective-permute-start(f32[4,512]{1,0:T(4,128)S(1)} %get-tuple-element.43), channel_id=1, source_target_pairs={{0,1},{1,0},{2,3},{3,2},{4,5},{5,4},{6,7},{7,6},{8,9},{9,8},{10,11... | collective-permute-start | bytes 24584 | tf_op jit(solution)/shard_map/ppermute | solution.py:391
  30.5 1.6 %collective-permute-done.8.from_x = f32[4,512]{1,0:T(4,128)S(1)} collective-permute-done((f32[4,512]{1,0:T(4,128)S(1)}, f32[4,512]{1,0:T(4,128)S(1)}, u32[]{:S(2)}, u32[]{:S(2)}) %collective-permute-start.8) | collective-permute-done | bytes 8224 | tf_op jit(solution)/shard_map/ppermute | solution.py:391
  32.9 2.4 %collective-permute-start.11 = (f32[16,512]{1,0:T(8,128)S(1)}, f32[16,512]{1,0:T(8,128)S(1)}, u32[]{:S(2)}, u32[]{:S(2)}) collective-permute-start(f32[16,512]{1,0:T(8,128)S(1)} %get-tuple-element.46), channel_id=1, source_target_pairs={{8,16},{16,8},{24,0},{0,24},{9,17},{17,9},{25,1},{1,25},{10,18},{1... | collective-permute-start | bytes 98312 | tf_op jit(solution)/shard_map/ppermute | solution.py:397
  35.3 1.7 %collective-permute-done.11.from_y = f32[16,512]{1,0:T(8,128)S(1)} collective-permute-done((f32[16,512]{1,0:T(8,128)S(1)}, f32[16,512]{1,0:T(8,128)S(1)}, u32[]{:S(2)}, u32[]{:S(2)}) %collective-permute-start.11) | collective-permute-done | bytes 32800 | tf_op jit(solution)/shard_map/ppermute | solution.py:397
  37.8 3.2 %collective-permute-start.12 = (f32[8,256]{1,0:T(8,128)S(1)}, f32[8,256]{1,0:T(8,128)S(1)}, u32[]{:S(2)}, u32[]{:S(2)}) collective-permute-start(f32[8,256]{1,0:T(8,128)S(1)} %get-tuple-element.48), channel_id=1, source_target_pairs={{0,1},{1,0},{2,3},{3,2},{4,5},{5,4},{6,7},{7,6},{8,9},{9,8},{10,11... | collective-permute-start | bytes 24584 | tf_op jit(solution)/shard_map/ppermute | solution.py:391
  40.9 1.6 %collective-permute-done.12.from_x = f32[8,256]{1,0:T(8,128)S(1)} collective-permute-done((f32[8,256]{1,0:T(8,128)S(1)}, f32[8,256]{1,0:T(8,128)S(1)}, u32[]{:S(2)}, u32[]{:S(2)}) %collective-permute-start.12) | collective-permute-done | bytes 8224 | tf_op jit(solution)/shard_map/ppermute | solution.py:391
  42.6 1.7 %collective-permute-start.15 = (f32[24,256]{1,0:T(8,128)S(1)}, f32[24,256]{1,0:T(8,128)S(1)}, u32[]{:S(2)}, u32[]{:S(2)}) collective-permute-start(f32[24,256]{1,0:T(8,128)S(1)} %shard_map.77.packed), channel_id=1, source_target_pairs={{0,16},{16,0},{8,24},{24,8},{1,17},{17,1},{9,25},{25,9},{2,18},{18... | collective-permute-start | bytes 73736 | tf_op jit(solution)/shard_map/ppermute | solution.py:457
  44.3 2.2 %collective-permute-done.15.far_below.far_above = f32[24,256]{1,0:T(8,128)S(1)} collective-permute-done((f32[24,256]{1,0:T(8,128)S(1)}, f32[24,256]{1,0:T(8,128)S(1)}, u32[]{:S(2)}, u32[]{:S(2)}) %collective-permute-start.15) | collective-permute-done | bytes 24608 | tf_op jit(solution)/shard_map/ppermute | solution.py:457
  46.5 1.2 %collective-permute-done.16.near_y = f32[24,256]{1,0:T(8,128)S(1)} collective-permute-done((f32[24,256]{1,0:T(8,128)S(1)}, f32[24,256]{1,0:T(8,128)S(1)}, u32[]{:S(2)}, u32[]{:S(2)}) %collective-permute-start.16) | collective-permute-done | bytes 24608 | tf_op jit(solution)/shard_map/ppermute | solution.py:458
  47.7 1.4 %shard_map.79 = (f32[2,4,256]{2,1,0:T(4,128)}, f32[32,1,2,128]{3,2,1,0:T(2,128)}) custom-call(f32[24,256]{1,0:T(8,128)S(1)} %shard_map.77.packed, f32[24,256]{1,0:T(8,128)S(1)} %collective-permute-done.14.near_core, f32[24,256]{1,0:T(8,128)S(1)} %collective-permute-done.16.near_y, f32[24,256]{1,0:T(8,128)S(1)} %collective-permute-done.15.far_below.far_above, ...), custom_call_target="tpu_custom_call" | custom-call | bytes 20000000 | tf_op jit(solution)/shard_map/pallas_call | solution.py:25
  49.1 5.2 %all-to-all-start = ((f32[32,1,2,128]{3,2,1,0:T(2,128)}), f32[32,1,2,128]{3,2,1,0:T(2,128)S(1)}, u32[]{:S(2)}, u32[]{:S(2)}) async-start(f32[32,1,2,128]{3,2,1,0:T(2,128)} %get-tuple-element.56), calls=%async_computation | async-start | bytes 65536 | tf_op jit(solution)/shard_map/all_to_all | solution.py:478
  55.0 6.5 %all-to-all-done.gathered = f32[32,1,2,128]{3,2,1,0:T(2,128)S(1)} async-done(((f32[32,1,2,128]{3,2,1,0:T(2,128)}), f32[32,1,2,128]{3,2,1,0:T(2,128)S(1)}, u32[]{:S(2)}, u32[]{:S(2)}) %all-to-all-start) | async-done | bytes 32800 | tf_op jit(solution)/shard_map/all_to_all | solution.py:478
  61.5 3.0 %shard_map.81 = f32[1,16,128]{2,1,0:T(8,128)} custom-call(f32[32,1,2,128]{3,2,1,0:T(2,128)S(1)} %all-to-all-done.gathered, f32[4,27,16,128]{3,2,1,0:T(8,128)S(1)} %shard_map.80.c), custom_call_target="tpu_custom_call" | custom-call | bytes 20000000 | tf_op jit(solution)/shard_map/pallas_call | solution.py:25
  (45 shorter events, 8.0 us)
Async XLA Ops:
  1.5 7.1 %collective-permute-start.1 = (f32[16,512]{1,0:T(8,128)S(1)}, f32[16,512]{1,0:T(8,128)S(1)}, u32[]{:S(2)}, u32[]{:S(2)}) collective-permute-start(f32[16,512]{1,0:T(8,128)S(1)} %get-tuple-element.31), channel_id=1, source_target_pairs={{1,2},{2,1},{3,4},{4,3},{5,6},{6,5},{9,10},{10,9},{11,12},{12,11},... | collective-permute-start | bytes 98312 | tf_op jit(solution)/shard_map/ppermute | solution.py:392
  2.1 6.5 %collective-permute-start = (f32[4,512]{1,0:T(4,128)S(1)}, f32[4,512]{1,0:T(4,128)S(1)}, u32[]{:S(2)}, u32[]{:S(2)}) collective-permute-start(f32[4,512]{1,0:T(4,128)S(1)} %get-tuple-element.30), channel_id=1, source_target_pairs={{0,1},{1,0},{2,3},{3,2},{4,5},{5,4},{6,7},{7,6},{8,9},{9,8},{10,11... | collective-permute-start | bytes 24584 | tf_op jit(solution)/shard_map/ppermute | solution.py:391
  7.6 4.6 %copy-start.2 = (f32[27,1,16,128]{3,2,1,0:T(8,128)S(1)}, f32[27,1,16,128]{3,2,1,0:T(8,128)}, u32[]{:S(2)}) copy-start(f32[27,1,16,128]{3,2,1,0:T(8,128)} %refs_0_) | copy-start | bytes 663556
  8.7 1.7 %collective-permute-start.2 = (f32[16,512]{1,0:T(8,128)S(1)}, f32[16,512]{1,0:T(8,128)S(1)}, u32[]{:S(2)}, u32[]{:S(2)}) collective-permute-start(f32[16,512]{1,0:T(8,128)S(1)} %get-tuple-element.35), channel_id=1, source_target_pairs={{0,8},{8,0},{16,24},{24,16},{1,9},{9,1},{17,25},{25,17},{2,10},{10... | collective-permute-start | bytes 98312 | tf_op jit(solution)/shard_map/ppermute | solution.py:396
  8.7 3.4 %collective-permute-start.3 = (f32[16,512]{1,0:T(8,128)S(1)}, f32[16,512]{1,0:T(8,128)S(1)}, u32[]{:S(2)}, u32[]{:S(2)}) collective-permute-start(f32[16,512]{1,0:T(8,128)S(1)} %get-tuple-element.36), channel_id=1, source_target_pairs={{8,16},{16,8},{24,0},{0,24},{9,17},{17,9},{25,1},{1,25},{10,18},{1... | collective-permute-start | bytes 98312 | tf_op jit(solution)/shard_map/ppermute | solution.py:397
  12.1 12.0 %collective-permute-start.17 = (f32[27,1,16,128]{3,2,1,0:T(8,128)S(1)}, f32[27,1,16,128]{3,2,1,0:T(8,128)S(1)}, u32[]{:S(2)}, u32[]{:S(2)}) collective-permute-start(f32[27,1,16,128]{3,2,1,0:T(8,128)S(1)} %copy-done.2), channel_id=1, source_target_pairs={{0,16},{8,24},{16,0},{24,8},{1,17},{9,25},{17,1},{25,9},{2,18},{10... | collective-permute-start | bytes 663560 | tf_op jit(solution)/shard_map/ppermute | solution.py:427
  13.7 10.5 %collective-permute-start.18 = (f32[27,2,2,256]{3,2,1,0:T(2,128)S(1)}, f32[27,2,2,256]{3,2,1,0:T(2,128)S(1)}, u32[]{:S(2)}, u32[]{:S(2)}) collective-permute-start(f32[27,2,2,256]{3,2,1,0:T(2,128)S(1)} %get-tuple-element.51), channel_id=1, source_target_pairs={{0,1},{1,0},{2,3},{3,2},{4,5},{5,4},{6,7},{7,6},{8,9},{9,8},{10,11... | collective-permute-start | bytes 331784 | tf_op jit(solution)/shard_map/ppermute | solution.py:391
  14.8 9.3 %collective-permute-start.19 = (f32[27,2,2,256]{3,2,1,0:T(2,128)S(1)}, f32[27,2,2,256]{3,2,1,0:T(2,128)S(1)}, u32[]{:S(2)}, u32[]{:S(2)}) collective-permute-start(f32[27,2,2,256]{3,2,1,0:T(2,128)S(1)} %get-tuple-element.52), channel_id=1, source_target_pairs={{1,2},{2,1},{3,4},{4,3},{5,6},{6,5},{9,10},{10,9},{11,12},{12,11},... | collective-permute-start | bytes 331784 | tf_op jit(solution)/shard_map/ppermute | solution.py:392
  15.1 5.5 %collective-permute-start.5 = (f32[16,512]{1,0:T(8,128)S(1)}, f32[16,512]{1,0:T(8,128)S(1)}, u32[]{:S(2)}, u32[]{:S(2)}) collective-permute-start(f32[16,512]{1,0:T(8,128)S(1)} %get-tuple-element.39), channel_id=1, source_target_pairs={{1,2},{2,1},{3,4},{4,3},{5,6},{6,5},{9,10},{10,9},{11,12},{12,11},... | collective-permute-start | bytes 98312 | tf_op jit(solution)/shard_map/ppermute | solution.py:392
  15.7 4.9 %collective-permute-start.4 = (f32[4,512]{1,0:T(4,128)S(1)}, f32[4,512]{1,0:T(4,128)S(1)}, u32[]{:S(2)}, u32[]{:S(2)}) collective-permute-start(f32[4,512]{1,0:T(4,128)S(1)} %get-tuple-element.38), channel_id=1, source_target_pairs={{0,1},{1,0},{2,3},{3,2},{4,5},{5,4},{6,7},{7,6},{8,9},{9,8},{10,11... | collective-permute-start | bytes 24584 | tf_op jit(solution)/shard_map/ppermute | solution.py:391
  20.6 1.3 %collective-permute-start.6 = (f32[16,512]{1,0:T(8,128)S(1)}, f32[16,512]{1,0:T(8,128)S(1)}, u32[]{:S(2)}, u32[]{:S(2)}) collective-permute-start(f32[16,512]{1,0:T(8,128)S(1)} %get-tuple-element.40), channel_id=1, source_target_pairs={{0,8},{8,0},{16,24},{24,16},{1,9},{9,1},{17,25},{25,17},{2,10},{10... | collective-permute-start | bytes 98312 | tf_op jit(solution)/shard_map/ppermute | solution.py:396
  20.7 3.4 %collective-permute-start.7 = (f32[16,512]{1,0:T(8,128)S(1)}, f32[16,512]{1,0:T(8,128)S(1)}, u32[]{:S(2)}, u32[]{:S(2)}) collective-permute-start(f32[16,512]{1,0:T(8,128)S(1)} %get-tuple-element.41), channel_id=1, source_target_pairs={{8,16},{16,8},{24,0},{0,24},{9,17},{17,9},{25,1},{1,25},{10,18},{1... | collective-permute-start | bytes 98312 | tf_op jit(solution)/shard_map/ppermute | solution.py:397
  24.5 23.2 %collective-permute-start.20 = (f32[27,64,128]{2,1,0:T(8,128)S(1)}, f32[27,64,128]{2,1,0:T(8,128)S(1)}, u32[]{:S(2)}, u32[]{:S(2)}) collective-permute-start(f32[27,64,128]{2,1,0:T(8,128)S(1)} %get-tuple-element.53.own), channel_id=1, source_target_pairs={{0,8},{8,0},{16,24},{24,16},{1,9},{9,1},{17,25},{25,17},{2,10},{10... | collective-permute-start | bytes 2654216 | tf_op jit(solution)/shard_map/ppermute | solution.py:438
  25.0 22.7 %collective-permute-start.21 = (f32[27,32,128]{2,1,0:T(8,128)S(1)}, f32[27,32,128]{2,1,0:T(8,128)S(1)}, u32[]{:S(2)}, u32[]{:S(2)}) collective-permute-start(f32[27,32,128]{2,1,0:T(8,128)S(1)} %get-tuple-element.54), channel_id=1, source_target_pairs={{8,16},{16,8},{9,17},{17,9},{10,18},{18,10},{11,19},{19,11},{12,20... | collective-permute-start | bytes 1327112 | tf_op jit(solution)/shard_map/ppermute | solution.py:439
  26.0 6.2 %collective-permute-start.9 = (f32[16,512]{1,0:T(8,128)S(1)}, f32[16,512]{1,0:T(8,128)S(1)}, u32[]{:S(2)}, u32[]{:S(2)}) collective-permute-start(f32[16,512]{1,0:T(8,128)S(1)} %get-tuple-element.44), channel_id=1, source_target_pairs={{1,2},{2,1},{3,4},{4,3},{5,6},{6,5},{9,10},{10,9},{11,12},{12,11},... | collective-permute-start | bytes 98312 | tf_op jit(solution)/shard_map/ppermute | solution.py:392
  27.9 4.2 %collective-permute-start.8 = (f32[4,512]{1,0:T(4,128)S(1)}, f32[4,512]{1,0:T(4,128)S(1)}, u32[]{:S(2)}, u32[]{:S(2)}) collective-permute-start(f32[4,512]{1,0:T(4,128)S(1)} %get-tuple-element.43), channel_id=1, source_target_pairs={{0,1},{1,0},{2,3},{3,2},{4,5},{5,4},{6,7},{7,6},{8,9},{9,8},{10,11... | collective-permute-start | bytes 24584 | tf_op jit(solution)/shard_map/ppermute | solution.py:391
  32.1 3.1 %collective-permute-start.10 = (f32[16,512]{1,0:T(8,128)S(1)}, f32[16,512]{1,0:T(8,128)S(1)}, u32[]{:S(2)}, u32[]{:S(2)}) collective-permute-start(f32[16,512]{1,0:T(8,128)S(1)} %get-tuple-element.45), channel_id=1, source_target_pairs={{0,8},{8,0},{16,24},{24,16},{1,9},{9,1},{17,25},{25,17},{2,10},{10... | collective-permute-start | bytes 98312 | tf_op jit(solution)/shard_map/ppermute | solution.py:396
  32.9 4.0 %collective-permute-start.11 = (f32[16,512]{1,0:T(8,128)S(1)}, f32[16,512]{1,0:T(8,128)S(1)}, u32[]{:S(2)}, u32[]{:S(2)}) collective-permute-start(f32[16,512]{1,0:T(8,128)S(1)} %get-tuple-element.46), channel_id=1, source_target_pairs={{8,16},{16,8},{24,0},{0,24},{9,17},{17,9},{25,1},{1,25},{10,18},{1... | collective-permute-start | bytes 98312 | tf_op jit(solution)/shard_map/ppermute | solution.py:397
  37.6 5.0 %collective-permute-start.13 = (f32[16,256]{1,0:T(8,128)S(1)}, f32[16,256]{1,0:T(8,128)S(1)}, u32[]{:S(2)}, u32[]{:S(2)}) collective-permute-start(f32[16,256]{1,0:T(8,128)S(1)} %get-tuple-element.49), channel_id=1, source_target_pairs={{1,2},{2,1},{3,4},{4,3},{5,6},{6,5},{9,10},{10,9},{11,12},{12,11},... | collective-permute-start | bytes 49160 | tf_op jit(solution)/shard_map/ppermute | solution.py:392
  37.8 4.8 %collective-permute-start.12 = (f32[8,256]{1,0:T(8,128)S(1)}, f32[8,256]{1,0:T(8,128)S(1)}, u32[]{:S(2)}, u32[]{:S(2)}) collective-permute-start(f32[8,256]{1,0:T(8,128)S(1)} %get-tuple-element.48), channel_id=1, source_target_pairs={{0,1},{1,0},{2,3},{3,2},{4,5},{5,4},{6,7},{7,6},{8,9},{9,8},{10,11... | collective-permute-start | bytes 24584 | tf_op jit(solution)/shard_map/ppermute | solution.py:391
  42.6 3.9 %collective-permute-start.15 = (f32[24,256]{1,0:T(8,128)S(1)}, f32[24,256]{1,0:T(8,128)S(1)}, u32[]{:S(2)}, u32[]{:S(2)}) collective-permute-start(f32[24,256]{1,0:T(8,128)S(1)} %shard_map.77.packed), channel_id=1, source_target_pairs={{0,16},{16,0},{8,24},{24,8},{1,17},{17,1},{9,25},{25,9},{2,18},{18... | collective-permute-start | bytes 73736 | tf_op jit(solution)/shard_map/ppermute | solution.py:457
  44.3 2.2 %collective-permute-start.14 = (f32[24,256]{1,0:T(8,128)S(1)}, f32[24,256]{1,0:T(8,128)S(1)}, u32[]{:S(2)}, u32[]{:S(2)}) collective-permute-start(f32[24,256]{1,0:T(8,128)S(1)} %shard_map.77.packed), channel_id=1, source_target_pairs={{0,8},{8,0},{16,24},{24,16},{1,9},{9,1},{17,25},{25,17},{2,10},{10... | collective-permute-start | bytes 73736 | tf_op jit(solution)/shard_map/ppermute | solution.py:455
  46.5 1.2 %collective-permute-start.16 = (f32[24,256]{1,0:T(8,128)S(1)}, f32[24,256]{1,0:T(8,128)S(1)}, u32[]{:S(2)}, u32[]{:S(2)}) collective-permute-start(f32[24,256]{1,0:T(8,128)S(1)} %collective-permute-done.15.far_below.far_above), channel_id=1, source_target_pairs={{0,8},{8,0},{16,24},{24,16},{1,9},{9,1},{17,25},{25,17},{2,10},{10... | collective-permute-start | bytes 73736 | tf_op jit(solution)/shard_map/ppermute | solution.py:458
  49.1 12.4 %all-to-all-start = ((f32[32,1,2,128]{3,2,1,0:T(2,128)}), f32[32,1,2,128]{3,2,1,0:T(2,128)S(1)}, u32[]{:S(2)}, u32[]{:S(2)}) async-start(f32[32,1,2,128]{3,2,1,0:T(2,128)} %get-tuple-element.56), calls=%async_computation | async-start | bytes 65536 | tf_op jit(solution)/shard_map/all_to_all | solution.py:478
  (2 other events, 2.4 us)

commit v4 on v3

v4 whole, which is shorter than its diff:
```python
import functools

import jax
import jax.numpy as jnp
from jax import lax
from jax.experimental import pallas as pl
from jax.experimental.pallas import tpu as pltpu
from jax.sharding import PartitionSpec as P

NU0 = 3
NB = 16
WEIGHT = 0.8
CENTER = 13
LANES = 128
ROWS = 8


def shape(*dims):
    return jax.ShapeDtypeStruct(dims, jnp.float32)


def call(kernel, outs, args, scratch=(), out_specs=None):
    vmem = pl.BlockSpec(memory_space=pltpu.VMEM)
    return pl.pallas_call(
        kernel,
        out_shape=outs,
        in_specs=[vmem] * len(args),
        out_specs=out_specs or jax.tree.map(lambda _: vmem, outs),
        scratch_shapes=list(scratch),
        compiler_params=pltpu.CompilerParams(vmem_limit_bytes=12 << 20),
    )(*args)


def even(axis):
    return lax.rem(lax.axis_index(axis), 2) == 0


def pick(condition, a, b):
    return jnp.where(jnp.broadcast_to(condition, a.shape), a, b)


def sides(from_x, from_zx):
    sub, subs = lax.axis_index("sub"), lax.axis_size("sub")
    from_zx = pick((sub == 0) | (sub == subs - 1), jnp.zeros_like(from_zx), from_zx)
    return pick(even("sub"), from_zx, from_x), pick(even("sub"), from_x, from_zx)


def rolled(values):
    extent = values.shape[-1]
    return pltpu.roll(values, 1, 1), values, pltpu.roll(values, extent - 1, 1)


def homed(k, part, first=True, last=True):
    rows, extent = part.shape
    y, z = k // 3 % 3, k % 3
    lane = lax.broadcasted_iota(jnp.int32, part.shape, 1)
    if z == 0 and first:
        part = jnp.where(lane == 0, 0.0, part)
    if z == 2 and last:
        part = jnp.where(lane == extent - 1, 0.0, part)
    if y != 1:
        part = pltpu.roll(part, rows - 1 if y == 0 else 1, 0)
    return part


def neighbours(values, before=None, after=None):
    here = rolled(values)
    if before is None:
        return here, here, here
    row = lax.broadcasted_iota(jnp.int32, values.shape, 0)
    lower = [jnp.where(row == values.shape[0] - 1, b, h) for b, h in zip(rolled(before), here)]
    upper = [jnp.where(row == 0, a, h) for a, h in zip(rolled(after), here)]
    return lower, here, upper


def outer_terms(near, coefficient, lanes):
    sums = [None] * 3
    for x in range(3):
        for y in range(3):
            for z in range(3):
                k = 9 * x + 3 * y + z
                if k == CENTER or near[x] is None:
                    continue
                term = coefficient(k) * near[x][y][z][:, lanes]
                sums[y] = term if sums[y] is None else sums[y] + term
    rows = sums[1].shape[0]
    return sums[1] + (pltpu.roll(sums[0], 1, 0) + pltpu.roll(sums[2], rows - 1, 0))


def lane_tiles(extent):
    return [slice(l, l + LANES) for l in range(0, extent, LANES)]


def paired_lanes(values):
    rows, extent = values.shape
    row = lax.broadcasted_iota(jnp.int32, (extent, extent // 2), 0)
    column = lax.broadcasted_iota(jnp.int32, (extent, extent // 2), 1)
    pairs = jnp.where(lax.shift_right_logical(row, 1) == column, 1.0, 0.0).astype(jnp.bfloat16)
    parts = []
    for _ in range(3):
        part = values.astype(jnp.bfloat16).astype(jnp.float32)
        parts.append(part)
        values = values - part
    if 3 * rows % 16:
        parts.append(jnp.zeros_like(values))
    stacked = jnp.concatenate(parts, axis=0).astype(jnp.bfloat16)
    sums = lax.dot_general(stacked, pairs, (((1,), (0,)), ((), ())), preferred_element_type=jnp.float32)
    return sums[:rows] + (sums[rows : 2 * rows] + sums[2 * rows : 3 * rows])


def paired_rows(values):
    return values + pltpu.roll(values, values.shape[0] - 1, 0)


def put_edges(v, to_x, to_zx):
    last = v.shape[1] - 1
    for x in range(v.shape[0]):
        first_row, last_row = v[x, 0:1, :], v[x, last : last + 1, :]
        to_x[x : x + 1, :] = pick(even("sub"), last_row, first_row)
        to_zx[x : x + 1, :] = pick(even("sub"), first_row, last_row)


def edges_kernel(v, to_x, to_zx):
    put_edges(v, to_x, to_zx)


def faces_kernel(v, from_x, from_zx, to_core, to_y):
    planes, rows, _ = v.shape
    before, after = sides(from_x[...], from_zx[0:planes, :])
    for ref, swap in ((to_core, False), (to_y, True)):
        def choose(a, b):
            return pick(even("grp"), b, a) if swap else pick(even("grp"), a, b)

        ref[0:rows, :] = choose(v[planes - 1], v[0])
        ref[rows : rows + 1, :] = choose(before[planes - 1 :], before[0:1])
        ref[rows + 1 : rows + 2, :] = choose(after[planes - 1 :], after[0:1])


def fine_neighbours(groups, v, from_x, from_zx, from_core, from_y):
    planes, rows, _ = v.shape
    group = lax.axis_index("grp")
    before, after = sides(from_x[...], from_zx[0:planes, :])
    low = pick(even("grp"), from_y[...], from_core[...])
    high = pick(even("grp"), from_core[...], from_y[...])
    low = pick(group == 0, jnp.zeros_like(low), low)
    high = pick(group == groups - 1, jnp.zeros_like(high), high)
    faces = [neighbours(f[0:rows], f[rows : rows + 1], f[rows + 1 : rows + 2]) for f in (low, high)]
    inner = [neighbours(v[x], before[x : x + 1], after[x : x + 1]) for x in range(planes)]
    return [faces[0], *inner, faces[1]]


def sweep_kernel(groups, v, first, c, from_x, from_zx, from_core, from_y, out, to_x, to_zx):
    planes, rows, extent = v.shape
    near = fine_neighbours(groups, v, from_x, from_zx, from_core, from_y)
    for x in range(planes):
        for lanes in lane_tiles(extent):
            sums = outer_terms(near[x : x + 3], lambda k: c[k, x, :, lanes], lanes)
            out[x, :, lanes] = first[x, :, lanes] + (1.0 - WEIGHT) * v[x, :, lanes] - sums
    put_edges(out, to_x, to_zx)


def residual_kernel(
    groups, v, first, c, from_x, from_zx, from_core, from_y, center, iterate, to_x, to_zx, held
):
    planes, rows, extent = v.shape
    near = fine_neighbours(groups, v, from_x, from_zx, from_core, from_y)
    for x in range(0, planes, 2):
        for lanes in lane_tiles(extent):
            total = None
            for p in (x, x + 1):
                sums = outer_terms(near[p : p + 3], lambda k: c[k, p, :, lanes], lanes)
                part = first[p, :, lanes] - WEIGHT * v[p, :, lanes] - sums
                part = (1.0 / WEIGHT) * c[CENTER, p, :, lanes] * part
                total = part if total is None else total + part
            held[x // 2 * rows : (x // 2 + 1) * rows, lanes] = total
    total = (0.5 * WEIGHT) * paired_rows(paired_lanes(held[...]))
    half = rows // 2
    for x in range(planes // 2):
        for y in range(half):
            row = x * rows + 2 * y
            iterate[x, y : y + 1, :] = total[row : row + 1]
    iterate[...] = iterate[...] / center[...]
    for x in range(planes // 2):
        first_rows, last_rows = iterate[x, 0:3, :], iterate[x, half - 3 : half, :]
        to_x[4 * x : 4 * x + 3, :] = pick(even("sub"), last_rows, first_rows)
        to_zx[4 * x : 4 * x + 3, :] = pick(even("sub"), first_rows, last_rows)


def middle_faces_kernel(mine, from_x, from_zx, out):
    planes, half, _ = mine.shape
    before, after = sides(from_x[...], from_zx[0 : 4 * planes, :])
    for x in range(planes):
        row = x * ROWS
        out[row : row + 2, :] = before[4 * x + 1 : 4 * x + 3]
        out[row + 2 : row + 2 + half, :] = mine[x]
        out[row + 2 + half : row + ROWS, :] = after[4 * x : 4 * x + 2]
        extra = planes * ROWS + 2 * x
        out[extra : extra + 1, :] = before[4 * x : 4 * x + 1]
        out[extra + 1 : extra + 2, :] = after[4 * x + 2 : 4 * x + 3]


def coefficient_edges_kernel(c, to_x, to_zx):
    rows = c.shape[2]
    first, last = c[:, :, 0:2, :], c[:, :, rows - 2 : rows, :]
    to_x[...] = pick(even("sub"), last, first)
    to_zx[0:27] = pick(even("sub"), first, last)


def coefficient_scale_kernel(c, out):
    for x in range(c.shape[1]):
        out[:, x] = scaled(c[:, x])
        for k in range(27):
            out[k, x] = homed(k, out[k, x])


def scaled(c):
    center = c[CENTER : CENTER + 1]
    ratio = WEIGHT / jnp.where(center > 0.0, center, 1.0)
    index = lax.broadcasted_iota(jnp.int32, c.shape, 0)
    return c * jnp.where(index == CENTER, 1.0, ratio)


def coefficient_pack_kernel(known, *refs):
    coarse, (c, from_x, from_zx, _, __, middle_part, whole) = refs[:known], refs[known:]
    _, planes, rows, extent = c.shape
    tiles = extent // LANES
    before, after = sides(from_x[...], from_zx[0:27])
    for x in range(planes):
        for l, lanes in enumerate(lane_tiles(extent)):
            row = (x * tiles + l) * ROWS
            whole[:, row : row + 2, :] = before[:, x, :, lanes]
            whole[:, row + 2 : row + 2 + rows, :] = c[:, x, :, lanes]
            whole[:, row + 2 + rows : row + ROWS, :] = after[:, x, :, lanes]
    row = planes * tiles * ROWS
    for t in range(0, row, ROWS):
        part = scaled(whole[:, t : t + ROWS, :])
        l = t // ROWS % tiles
        for k in range(27):
            ready = homed(k, part[k], l == 0, l == tiles - 1)
            whole[k, t : t + ROWS, :] = ready
            middle_part[k, t : t + ROWS, :] = ready
    for ref in coarse:
        for x in range(ref.shape[1]):
            for t in range(0, ref.shape[2], ROWS):
                whole[:, row : row + ROWS, :] = scaled(ref[:, x, t : t + ROWS, :])
                row += ROWS


def middle_kernel(
    groups, planes, packed, near_core, near_y, far_below, far_above, own, core, other, iterate, coarse, held
):
    extent = packed.shape[-1]
    tiles = extent // LANES
    half = ROWS - 4
    group = lax.axis_index("grp")
    window = 3 * planes

    below = pick(even("grp"), near_y[...], near_core[...])
    above = pick(even("grp"), near_core[...], near_y[...])
    blocks = {-2: far_below[...], -1: below, 0: packed[...], 1: above, 2: far_above[...]}
    for away in (-2, -1, 1, 2):
        inside = (group + away >= 0) & (group + away < groups)
        blocks[away] = pick(inside, blocks[away], jnp.zeros_like(blocks[away]))
    first, near = [], []
    for p in range(-1, window + 1):
        block, x = blocks[p // planes - 1], p % planes
        v, extra = block[x * ROWS : (x + 1) * ROWS], planes * ROWS + 2 * x
        first.append(v)
        near.append(neighbours(v, block[extra : extra + 1], block[extra + 1 : extra + 2]))

    def work(parts):
        def terms(forms, w, lanes):
            row = (w % planes * tiles + lanes.start // LANES) * ROWS
            return outer_terms(forms, lambda k: parts[w // planes][k, row : row + ROWS, :], lanes)

        def swept(forms, field, w):
            sums = jnp.concatenate([terms(forms, w, lanes) for lanes in lane_tiles(extent)], axis=1)
            return first[w + 1] + (1.0 - WEIGHT) * field - sums

        low, high = planes - 2, 2 * planes + 2
        once = {w: swept(near[w : w + 3], first[w + 1], w) for w in range(low, high)}
        forms = {w: neighbours(v) for w, v in once.items()}
        low, high = low + 1, high - 1
        twice = {w: swept([forms[w + x] for x in (-1, 0, 1)], once[w], w) for w in range(low, high)}
        forms = {w: neighbours(v) for w, v in twice.items()}
        for x in range(planes):
            w = planes + x
            iterate[x] = twice[w][2 : 2 + half]
            for lanes in lane_tiles(extent):
                row = (x * tiles + lanes.start // LANES) * ROWS
                sums = terms([forms[w + i] for i in (-1, 0, 1)], w, lanes)
                rest = first[w + 1][:, lanes] - WEIGHT * twice[w][:, lanes] - sums
                held[x, :, lanes] = (1.0 / WEIGHT) * own[CENTER, row : row + ROWS, :] * rest

    @pl.when(even("grp"))
    def _():
        work((other, own, core))

    @pl.when(jnp.logical_not(even("grp")))
    def _():
        work((core, own, other))

    place_of = lax.broadcasted_iota(jnp.int32, (ROWS, extent // 2), 0)
    for x in range(planes // 2):
        total = 0.5 * paired_rows(paired_lanes(held[2 * x] + held[2 * x + 1]))
        value = pltpu.roll(total, ROWS - 2, 0)
        for i in range(1, half // 2):
            value = jnp.where(place_of == i, pltpu.roll(total, ROWS - 2 - i, 0), value)
        for device in range(coarse.shape[0]):
            coarse[device, x] = value[: half // 2]


def coarse_order_kernel(planes, rows, start, offsets, own, core, out):
    group = lax.axis_index("grp")
    row_of = lax.broadcasted_iota(jnp.int32, (rows, out.shape[-1]), 0)
    for ref, flip in ((own, 0), (core, 1)):
        for i, offset in enumerate(offsets):
            owner = jnp.bitwise_xor(group, offset ^ flip)
            for x in range(planes):
                row = start + (i * planes + x) * rows
                for k in range(27):
                    part = ref[k, row : row + rows, :]
                    if k // 3 % 3 != 1:
                        outside = 0 if k // 3 % 3 == 0 else rows - 1
                        part = jnp.where(row_of == outside, 0.0, part)
                    out[owner * planes + x, k] = homed(k, part)


def coarse_kernel(groups, planes, gathered, c, fine, middle, out, fine_out, middle_out, first, sems):
    kept = [
        pltpu.make_async_copy(fine, fine_out, sems.at[0]),
        pltpu.make_async_copy(middle, middle_out, sems.at[1]),
    ]
    for copy in kept:
        copy.start()
    total, rows, extent = first.shape
    subs = gathered.shape[0] // groups
    each = rows // subs
    for g in range(groups):
        for s in range(subs):
            for x in range(planes):
                first[g * planes + x, s * each : (s + 1) * each, :] = gathered[g * subs + s, x]
    for p in range(total):
        first[p] = WEIGHT * first[p] / c[p, CENTER]

    def sweep(_, field):
        near = [None, *map(neighbours, field), None]
        every = slice(0, extent)
        fresh = []
        for p in range(total):
            sums = outer_terms(near[p : p + 3], lambda k: c[p, k], every)
            fresh.append(first[p] + (1.0 - WEIGHT) * field[p] - sums)
        return tuple(fresh)

    field = lax.fori_loop(0, NB - 1, sweep, tuple(first[p] for p in range(total)))
    for p in range(total):
        first[p] = field[p]
    for x in range(planes):
        out[x] = first[lax.axis_index("grp") * planes + x]
    for copy in kept:
        copy.wait()


def after(value, *others):
    return lax.optimization_barrier((value, *others))[0]


def after_all(values, *others):
    return lax.optimization_barrier((*values, *others))[: len(values)]


def swaps(pairs):
    return [p for a, b in pairs for p in ((a, b), (b, a))]


def body(source, fine, middle, coarse):
    groups, subs = lax.axis_size("grp"), lax.axis_size("sub")
    _, planes, rows, extent = fine.shape
    _, middle_planes, middle_rows, middle_extent = middle.shape
    _, coarse_planes, coarse_rows, coarse_extent = coarse.shape

    x_pairs = swaps([(i, i + 1) for i in range(0, subs, 2)])
    zx_pairs = swaps(
        [(g * subs + i, g * subs + i + 1) for g in range(groups) for i in range(1, subs - 1, 2)]
        + [(g * subs + i, (g + 1) * subs + i) for g in range(0, groups, 2) for i in (0, subs - 1)]
    )
    core_pairs = swaps([(i, i + 1) for i in range(0, groups, 2)])
    y_pairs = swaps([(i, i + 1) for i in range(1, groups - 1, 2)])
    y_ring = y_pairs + [(groups - 1, 0), (0, groups - 1)]

    def along_sub(pair):
        to_x, to_zx = pair
        from_x = lax.ppermute(to_x, "sub", x_pairs)
        return from_x, lax.ppermute(to_zx, ("grp", "sub"), zx_pairs)

    def along_grp(v, halo):
        to_core, to_y = call(faces_kernel, [shape(rows + 8, extent)] * 2, [v, *halo])
        from_core = lax.ppermute(to_core, "grp", core_pairs)
        from_y = lax.ppermute(to_y, "grp", y_ring)
        return (*halo, from_core, from_y)

    weights = call(coefficient_scale_kernel, shape(*fine.shape), [fine])
    v = WEIGHT * source / fine[CENTER]
    first = v
    to_x, to_zx = call(edges_kernel, [shape(planes, extent), shape(4 * planes, extent)], [v])

    def sweep(v, halo):
        v, *edges = call(
            functools.partial(sweep_kernel, groups),
            [shape(planes, rows, extent), shape(planes, extent), shape(4 * planes, extent)],
            [v, first, weights, *halo],
        )
        return v, along_sub(edges)

    edges_c = call(
        coefficient_edges_kernel,
        [shape(27, middle_planes, 2, middle_extent), shape(28, middle_planes, 2, middle_extent)],
        [middle],
    )
    halo = along_sub((to_x, to_zx))
    halo_c = along_sub(after_all(edges_c, *halo))
    halo = along_grp(after(v, weights, *edges_c), halo)
    known = {0: after(coarse, *halo[2:])}
    bit = groups // 2
    while bit > 1:
        for offset in sorted(known):
            known[offset ^ bit] = lax.ppermute(known[offset], "grp", [(i, i ^ bit) for i in range(groups)])
        bit //= 2
    offsets = sorted(known)
    v, halo = sweep(v, halo)
    halo = along_grp(v, halo)
    start = middle_planes * (middle_extent // LANES) * ROWS
    middle_part, own = call(
        functools.partial(coefficient_pack_kernel, len(known)),
        [shape(27, start, LANES), shape(27, start + len(known) * coarse_planes * coarse_rows, LANES)],
        [*(known[o] for o in offsets), middle, *halo_c, *halo[2:]],
    )
    core = lax.ppermute(own, "grp", core_pairs)
    other = lax.ppermute(middle_part, "grp", y_pairs)
    v, halo = sweep(v, halo)
    fine_iterate = v
    halo = along_grp(v, halo)
    iterate, *edges = call(
        functools.partial(residual_kernel, groups),
        [shape(middle_planes, middle_rows, middle_extent)]
        + [shape(4 * middle_planes, middle_extent), shape(8 * middle_planes, middle_extent)],
        [v, first, weights, *halo, middle[CENTER]],
        [pltpu.VMEM((planes // 2 * rows, extent), jnp.float32)],
    )
    total = groups * coarse_planes
    ordered = call(
        functools.partial(coarse_order_kernel, coarse_planes, coarse_rows, start, offsets),
        shape(total, 27, coarse_rows, coarse_extent),
        [own, core],
    )
    packed = call(
        middle_faces_kernel,
        shape(middle_planes * ROWS + 8, middle_extent),
        [after(iterate, ordered), *along_sub(edges)],
    )
    near_core = lax.ppermute(packed, "grp", core_pairs)
    if groups == 4:
        far_below = far_above = lax.ppermute(packed, "grp", swaps([(0, 2), (1, 3)]))
        near_y = lax.ppermute(packed, "grp", y_ring)
    else:
        near_y = lax.ppermute(packed, "grp", y_pairs)
        up = [(i, i + 2) for i in range(groups - 2)]
        far_below = lax.ppermute(packed, "grp", up)
        far_above = lax.ppermute(packed, "grp", [(j, i) for i, j in up])
    middle_iterate, coarse_source = call(
        functools.partial(middle_kernel, groups, middle_planes),
        [
            shape(middle_planes, middle_rows, middle_extent),
            shape(groups * subs, coarse_planes, coarse_rows // subs, coarse_extent),
        ],
        [packed, near_core, near_y, far_below, far_above, own, core, other],
        [pltpu.VMEM((middle_planes, ROWS, middle_extent), jnp.float32)],
    )
    gathered = lax.all_to_all(coarse_source, ("grp", "sub"), 0, 0, tiled=True)
    vmem, hbm = pl.BlockSpec(memory_space=pltpu.VMEM), pl.BlockSpec(memory_space=pl.ANY)
    coarse_iterate, fine_iterate, middle_iterate = call(
        functools.partial(coarse_kernel, groups, coarse_planes),
        [
            shape(coarse_planes, coarse_rows, coarse_extent),
            shape(*fine_iterate.shape),
            shape(*middle_iterate.shape),
        ],
        [gathered, ordered, fine_iterate, middle_iterate],
        [
            pltpu.VMEM((total, coarse_rows, coarse_extent), jnp.float32),
            pltpu.SemaphoreType.DMA((2,)),
        ],
        out_specs=[vmem, hbm, hbm],
    )
    return fine_iterate, middle_iterate, coarse_iterate


def solution(mesh):
    placed = (
        P("grp", "sub", None),
        P(None, "grp", "sub", None),
        P(None, "grp", "sub", None),
        P(None, "grp", None, None),
    )
    return jax.shard_map(
        body,
        mesh=mesh,
        in_specs=placed,
        out_specs=(P("grp", "sub", None), P("grp", "sub", None), P("grp", None, None)),
        check_vma=False,
    )
```

time: 64.7 us -> 63 us (0.974)
  blocking collectives: 0 us -> 11.3 us
  waiting for transfers between devices: 21 us -> 13.8 us
  starting transfers between devices: 32.6 us -> 28.8 us
  Pallas kernels: 6.98 us -> 5.01 us
    all_to_all x0 -> x1, blocking collectives: none -> 11.3 us  [body(): gathered = lax.all_to_all(coarse_source, ('grp', 'sub'), 0, 0, tiled=True)]
    all_to_all x1 -> x0, waiting for transfers between devices: 6.47 us -> none  [body(): gathered = lax.all_to_all(coarse_source, ('grp', 'sub'), 0, 0, tiled=True)]
    all_to_all x1 -> x0, starting transfers between devices: 5.23 us -> none  [body(): gathered = lax.all_to_all(coarse_source, ('grp', 'sub'), 0, 0, tiled=True)]
    pallas_call x15 -> x14, Pallas kernels: 6.98 us -> 5.01 us  [call(): pl.pallas_call(kernel, out_shape=outs, in_specs=[vmem] * len(args), out_s...]
    ppermute x5, starting transfers between devices: 14.2 us -> 15.6 us  [along_sub(): from_x = lax.ppermute(to_x, 'sub', x_pairs)]
  transfers between devices with their start and end apart: 23 -> 22, of which waited for: 10 -> 9; matrix products, arithmetic and copies ran while one was open for 0% -> 0% of each run, Pallas kernels for 4% -> 3%
where the time goes in v4:
time: 63 us; the launch traced here: 62.8 us
  starting transfers between devices  28.8 us (46%)
  waiting for transfers between devices  13.8 us (22%)
  blocking collectives  11.3 us (18%)
  Pallas kernels  5.01 us (8%)
  local copies, waits for them, and re-layouts  2.21 us (4%)
  other arithmetic  0.89 us (1%)
  between operations  0.77 us (1%)
    ppermute x5, starting transfers between devices, along_sub(): from_x = lax.ppermute(to_x, 'sub', x_pairs)  15.6 us
    all_to_all x1, blocking collectives, body(): gathered = lax.all_to_all(coarse_source, ('grp', 'sub'), 0, 0, tiled=True)  11.3 us
    ppermute x3, waiting for transfers between devices, along_grp(): from_y = lax.ppermute(to_y, 'grp', y_ring)  5.64 us
    pallas_call x14, Pallas kernels, call(): pl.pallas_call(kernel, out_shape=outs, in_specs=[vmem] * len(args), out_s...  5.01 us
    ppermute x5, waiting for transfers between devices, along_sub(): from_x = lax.ppermute(to_x, 'sub', x_pairs)  4.8 us
    ppermute x3, starting transfers between devices, along_grp(): from_y = lax.ppermute(to_y, 'grp', y_ring)  4.61 us
    ppermute x5, starting transfers between devices, along_sub(): return (from_x, lax.ppermute(to_zx, ('grp', 'sub'), zx_pairs))  2.84 us
    unnamed x6, local copies, waits for them, and re-layouts  2.21 us
  transfers between devices with their start and end apart: 22, of which 9 were waited for; matrix products, arithmetic and copies ran while one was open for 0% of the time, Pallas kernels for 3%

profile of v4, /device:TPU:0, one launch (start us, length us, event | category | flops | bytes accessed | tf_op | source)
XLA Modules:
  0.0 62.8 jit_solution(550833921125186609)
XLA Ops:
  0.6 0.9 %bitcast_divide_fusion.v.first = f32[4,8,512]{2,1,0:T(8,128)S(1)} fusion(f32[27,4,8,512]{3,2,1,0:T(8,128)} %c.2, f32[4,8,512]{2,1,0:T(8,128)} %param.4), kind=kLoop, calls=%fused_computation | loop fusion | flops 32768 | bytes 196608 | tf_op jit(solution)/shard_map/div | solution.py:403
  2.1 4.0 %collective-permute-start = (f32[4,512]{1,0:T(4,128)S(1)}, f32[4,512]{1,0:T(4,128)S(1)}, u32[]{:S(2)}, u32[]{:S(2)}) collective-permute-start(f32[4,512]{1,0:T(4,128)S(1)} %get-tuple-element.34), channel_id=1, source_target_pairs={{0,1},{1,0},{2,3},{3,2},{4,5},{5,4},{6,7},{7,6},{8,9},{9,8},{10,11... | collective-permute-start | bytes 24584 | tf_op jit(solution)/shard_map/ppermute | solution.py:393
  6.1 1.5 %copy-done = f32[27,4,8,512]{3,2,1,0:T(8,128)S(1)} copy-done((f32[27,4,8,512]{3,2,1,0:T(8,128)S(1)}, f32[27,4,8,512]{3,2,1,0:T(8,128)}, u32[]{:S(2)}) %copy-start) | copy-done | bytes 1769496
  7.8 0.7 %copy-done.1 = f32[27,2,4,256]{3,2,1,0:T(4,128)S(1)} copy-done((f32[27,2,4,256]{3,2,1,0:T(4,128)S(1)}, f32[27,2,4,256]{3,2,1,0:T(4,128)}, u32[]{:S(2)}) %copy-start.1) | copy-done | bytes 221208
  8.7 1.6 %collective-permute-start.3 = (f32[16,512]{1,0:T(8,128)S(1)}, f32[16,512]{1,0:T(8,128)S(1)}, u32[]{:S(2)}, u32[]{:S(2)}) collective-permute-start(f32[16,512]{1,0:T(8,128)S(1)} %get-tuple-element.40), channel_id=1, source_target_pairs={{8,16},{16,8},{24,0},{0,24},{9,17},{17,9},{25,1},{1,25},{10,18},{1... | collective-permute-start | bytes 98312 | tf_op jit(solution)/shard_map/ppermute | solution.py:399
  10.4 1.8 %collective-permute-done.3.from_y = f32[16,512]{1,0:T(8,128)S(1)} collective-permute-done((f32[16,512]{1,0:T(8,128)S(1)}, f32[16,512]{1,0:T(8,128)S(1)}, u32[]{:S(2)}, u32[]{:S(2)}) %collective-permute-start.3) | collective-permute-done | bytes 32800 | tf_op jit(solution)/shard_map/ppermute | solution.py:399
  12.1 1.5 %collective-permute-start.12 = (f32[27,1,16,128]{3,2,1,0:T(8,128)S(1)}, f32[27,1,16,128]{3,2,1,0:T(8,128)S(1)}, u32[]{:S(2)}, u32[]{:S(2)}) collective-permute-start(f32[27,1,16,128]{3,2,1,0:T(8,128)S(1)} %copy-done.2), channel_id=1, source_target_pairs={{0,16},{8,24},{16,0},{24,8},{1,17},{9,25},{17,1},{25,9},{2,18},{10... | collective-permute-start | bytes 663560 | tf_op jit(solution)/shard_map/ppermute | solution.py:427
  13.8 2.9 %collective-permute-start.13 = (f32[27,2,2,256]{3,2,1,0:T(2,128)S(1)}, f32[27,2,2,256]{3,2,1,0:T(2,128)S(1)}, u32[]{:S(2)}, u32[]{:S(2)}) collective-permute-start(f32[27,2,2,256]{3,2,1,0:T(2,128)S(1)} %get-tuple-element.53), channel_id=1, source_target_pairs={{0,1},{1,0},{2,3},{3,2},{4,5},{5,4},{6,7},{7,6},{8,9},{9,8},{10,11... | collective-permute-start | bytes 331784 | tf_op jit(solution)/shard_map/ppermute | solution.py:393
  17.1 3.0 %collective-permute-start.4 = (f32[4,512]{1,0:T(4,128)S(1)}, f32[4,512]{1,0:T(4,128)S(1)}, u32[]{:S(2)}, u32[]{:S(2)}) collective-permute-start(f32[4,512]{1,0:T(4,128)S(1)} %get-tuple-element.42), channel_id=1, source_target_pairs={{0,1},{1,0},{2,3},{3,2},{4,5},{5,4},{6,7},{7,6},{8,9},{9,8},{10,11... | collective-permute-start | bytes 24584 | tf_op jit(solution)/shard_map/ppermute | solution.py:393
  20.1 1.6 %collective-permute-done.4.from_x = f32[4,512]{1,0:T(4,128)S(1)} collective-permute-done((f32[4,512]{1,0:T(4,128)S(1)}, f32[4,512]{1,0:T(4,128)S(1)}, u32[]{:S(2)}, u32[]{:S(2)}) %collective-permute-start.4) | collective-permute-done | bytes 8224 | tf_op jit(solution)/shard_map/ppermute | solution.py:393
  23.0 2.2 %collective-permute-done.7.from_y.refs_6_ = f32[16,512]{1,0:T(8,128)S(1)} collective-permute-done((f32[16,512]{1,0:T(8,128)S(1)}, f32[16,512]{1,0:T(8,128)S(1)}, u32[]{:S(2)}, u32[]{:S(2)}) %collective-permute-start.7) | collective-permute-done | bytes 32800 | tf_op jit(solution)/shard_map/ppermute | solution.py:399
  27.1 1.9 %collective-permute-start.9 = (f32[16,512]{1,0:T(8,128)S(1)}, f32[16,512]{1,0:T(8,128)S(1)}, u32[]{:S(2)}, u32[]{:S(2)}) collective-permute-start(f32[16,512]{1,0:T(8,128)S(1)} %get-tuple-element.48), channel_id=1, source_target_pairs={{1,2},{2,1},{3,4},{4,3},{5,6},{6,5},{9,10},{10,9},{11,12},{12,11},... | collective-permute-start | bytes 98312 | tf_op jit(solution)/shard_map/ppermute | solution.py:394
  29.0 2.5 %collective-permute-start.8 = (f32[4,512]{1,0:T(4,128)S(1)}, f32[4,512]{1,0:T(4,128)S(1)}, u32[]{:S(2)}, u32[]{:S(2)}) collective-permute-start(f32[4,512]{1,0:T(4,128)S(1)} %get-tuple-element.47), channel_id=1, source_target_pairs={{0,1},{1,0},{2,3},{3,2},{4,5},{5,4},{6,7},{7,6},{8,9},{9,8},{10,11... | collective-permute-start | bytes 24584 | tf_op jit(solution)/shard_map/ppermute | solution.py:393
  31.5 1.6 %collective-permute-done.8.from_x = f32[4,512]{1,0:T(4,128)S(1)} collective-permute-done((f32[4,512]{1,0:T(4,128)S(1)}, f32[4,512]{1,0:T(4,128)S(1)}, u32[]{:S(2)}, u32[]{:S(2)}) %collective-permute-start.8) | collective-permute-done | bytes 8224 | tf_op jit(solution)/shard_map/ppermute | solution.py:393
  33.1 0.8 %collective-permute-start.10 = (f32[16,512]{1,0:T(8,128)S(1)}, f32[16,512]{1,0:T(8,128)S(1)}, u32[]{:S(2)}, u32[]{:S(2)}) collective-permute-start(f32[16,512]{1,0:T(8,128)S(1)} %get-tuple-element.49), channel_id=1, source_target_pairs={{0,8},{8,0},{16,24},{24,16},{1,9},{9,1},{17,25},{25,17},{2,10},{10... | collective-permute-start | bytes 98312 | tf_op jit(solution)/shard_map/ppermute | solution.py:398
  33.9 2.4 %collective-permute-start.11 = (f32[16,512]{1,0:T(8,128)S(1)}, f32[16,512]{1,0:T(8,128)S(1)}, u32[]{:S(2)}, u32[]{:S(2)}) collective-permute-start(f32[16,512]{1,0:T(8,128)S(1)} %get-tuple-element.50), channel_id=1, source_target_pairs={{8,16},{16,8},{24,0},{0,24},{9,17},{17,9},{25,1},{1,25},{10,18},{1... | collective-permute-start | bytes 98312 | tf_op jit(solution)/shard_map/ppermute | solution.py:399
  36.2 1.7 %collective-permute-done.11.from_y = f32[16,512]{1,0:T(8,128)S(1)} collective-permute-done((f32[16,512]{1,0:T(8,128)S(1)}, f32[16,512]{1,0:T(8,128)S(1)}, u32[]{:S(2)}, u32[]{:S(2)}) %collective-permute-start.11) | collective-permute-done | bytes 32800 | tf_op jit(solution)/shard_map/ppermute | solution.py:399
  38.6 3.2 %collective-permute-start.16 = (f32[8,256]{1,0:T(8,128)S(1)}, f32[8,256]{1,0:T(8,128)S(1)}, u32[]{:S(2)}, u32[]{:S(2)}) collective-permute-start(f32[8,256]{1,0:T(8,128)S(1)} %get-tuple-element.57), channel_id=1, source_target_pairs={{0,1},{1,0},{2,3},{3,2},{4,5},{5,4},{6,7},{7,6},{8,9},{9,8},{10,11... | collective-permute-start | bytes 24584 | tf_op jit(solution)/shard_map/ppermute | solution.py:393
  41.9 1.5 %collective-permute-done.16.from_x = f32[8,256]{1,0:T(8,128)S(1)} collective-permute-done((f32[8,256]{1,0:T(8,128)S(1)}, f32[8,256]{1,0:T(8,128)S(1)}, u32[]{:S(2)}, u32[]{:S(2)}) %collective-permute-start.16) | collective-permute-done | bytes 8224 | tf_op jit(solution)/shard_map/ppermute | solution.py:393
  43.4 1.7 %collective-permute-start.20 = (f32[24,256]{1,0:T(8,128)S(1)}, f32[24,256]{1,0:T(8,128)S(1)}, u32[]{:S(2)}, u32[]{:S(2)}) collective-permute-start(f32[24,256]{1,0:T(8,128)S(1)} %shard_map.78.packed), channel_id=1, source_target_pairs={{0,16},{16,0},{8,24},{24,8},{1,17},{17,1},{9,25},{25,9},{2,18},{18... | collective-permute-start | bytes 73736 | tf_op jit(solution)/shard_map/ppermute | solution.py:463
  45.6 1.7 %collective-permute-done.20.far_below.far_above = f32[24,256]{1,0:T(8,128)S(1)} collective-permute-done((f32[24,256]{1,0:T(8,128)S(1)}, f32[24,256]{1,0:T(8,128)S(1)}, u32[]{:S(2)}, u32[]{:S(2)}) %collective-permute-start.20) | collective-permute-done | bytes 24608 | tf_op jit(solution)/shard_map/ppermute | solution.py:463
  47.3 1.0 %collective-permute-done.19.near_y = f32[24,256]{1,0:T(8,128)S(1)} collective-permute-done((f32[24,256]{1,0:T(8,128)S(1)}, f32[24,256]{1,0:T(8,128)S(1)}, u32[]{:S(2)}, u32[]{:S(2)}) %collective-permute-start.19) | collective-permute-done | bytes 24608 | tf_op jit(solution)/shard_map/ppermute | solution.py:464
  49.0 11.3 %all_to_all.5.gathered = f32[32,1,2,128]{3,2,1,0:T(2,128)S(1)} all-to-all(f32[32,1,2,128]{3,2,1,0:T(2,128)S(1)} %get-tuple-element.60), channel_id=1, replica_groups=mesh['grp'=4,'sub'=8] {'grp','sub'}, dimensions={0} | all-to-all | bytes 65536 | tf_op jit(solution)/shard_map/all_to_all | solution.py:479
  60.3 2.5 %shard_map.80 = (f32[1,16,128]{2,1,0:T(8,128)}, f32[4,8,512]{2,1,0:T(8,128)}, f32[2,4,256]{2,1,0:T(4,128)}) custom-call(f32[32,1,2,128]{3,2,1,0:T(2,128)S(1)} %all_to_all.5.gathered, f32[4,27,16,128]{3,2,1,0:T(8,128)S(1)} %shard_map.77.c, f32[4,8,512]{2,1,0:T(8,128)S(1)} %get-tuple-element.46.v.fine, f32[2,4,256]{2,1,0:T(4,128)S(1)} %get-tuple-element.61.middle), custom_call_target="tpu_custom_call" | custom-call | tf_op jit(solution)/shard_map/pallas_call | solution.py:24
  (43 shorter events, 6.6 us)
Async XLA Ops:
  1.5 7.1 %collective-permute-start.1 = (f32[16,512]{1,0:T(8,128)S(1)}, f32[16,512]{1,0:T(8,128)S(1)}, u32[]{:S(2)}, u32[]{:S(2)}) collective-permute-start(f32[16,512]{1,0:T(8,128)S(1)} %get-tuple-element.35), channel_id=1, source_target_pairs={{1,2},{2,1},{3,4},{4,3},{5,6},{6,5},{9,10},{10,9},{11,12},{12,11},... | collective-permute-start | bytes 98312 | tf_op jit(solution)/shard_map/ppermute | solution.py:394
  2.1 6.5 %collective-permute-start = (f32[4,512]{1,0:T(4,128)S(1)}, f32[4,512]{1,0:T(4,128)S(1)}, u32[]{:S(2)}, u32[]{:S(2)}) collective-permute-start(f32[4,512]{1,0:T(4,128)S(1)} %get-tuple-element.34), channel_id=1, source_target_pairs={{0,1},{1,0},{2,3},{3,2},{4,5},{5,4},{6,7},{7,6},{8,9},{9,8},{10,11... | collective-permute-start | bytes 24584 | tf_op jit(solution)/shard_map/ppermute | solution.py:393
  6.1 1.5 %copy-start = (f32[27,4,8,512]{3,2,1,0:T(8,128)S(1)}, f32[27,4,8,512]{3,2,1,0:T(8,128)}, u32[]{:S(2)}) copy-start(f32[27,4,8,512]{3,2,1,0:T(8,128)} %c.2) | copy-start | bytes 5308420
  7.6 4.6 %copy-start.2 = (f32[27,1,16,128]{3,2,1,0:T(8,128)S(1)}, f32[27,1,16,128]{3,2,1,0:T(8,128)}, u32[]{:S(2)}) copy-start(f32[27,1,16,128]{3,2,1,0:T(8,128)} %refs_0_) | copy-start | bytes 663556
  8.7 1.7 %collective-permute-start.2 = (f32[16,512]{1,0:T(8,128)S(1)}, f32[16,512]{1,0:T(8,128)S(1)}, u32[]{:S(2)}, u32[]{:S(2)}) collective-permute-start(f32[16,512]{1,0:T(8,128)S(1)} %get-tuple-element.39), channel_id=1, source_target_pairs={{0,8},{8,0},{16,24},{24,16},{1,9},{9,1},{17,25},{25,17},{2,10},{10... | collective-permute-start | bytes 98312 | tf_op jit(solution)/shard_map/ppermute | solution.py:398
  8.7 3.4 %collective-permute-start.3 = (f32[16,512]{1,0:T(8,128)S(1)}, f32[16,512]{1,0:T(8,128)S(1)}, u32[]{:S(2)}, u32[]{:S(2)}) collective-permute-start(f32[16,512]{1,0:T(8,128)S(1)} %get-tuple-element.40), channel_id=1, source_target_pairs={{8,16},{16,8},{24,0},{0,24},{9,17},{17,9},{25,1},{1,25},{10,18},{1... | collective-permute-start | bytes 98312 | tf_op jit(solution)/shard_map/ppermute | solution.py:399
  12.1 13.1 %collective-permute-start.12 = (f32[27,1,16,128]{3,2,1,0:T(8,128)S(1)}, f32[27,1,16,128]{3,2,1,0:T(8,128)S(1)}, u32[]{:S(2)}, u32[]{:S(2)}) collective-permute-start(f32[27,1,16,128]{3,2,1,0:T(8,128)S(1)} %copy-done.2), channel_id=1, source_target_pairs={{0,16},{8,24},{16,0},{24,8},{1,17},{9,25},{17,1},{25,9},{2,18},{10... | collective-permute-start | bytes 663560 | tf_op jit(solution)/shard_map/ppermute | solution.py:427
  13.7 11.6 %collective-permute-start.14 = (f32[28,2,2,256]{3,2,1,0:T(2,128)S(1)}, f32[28,2,2,256]{3,2,1,0:T(2,128)S(1)}, u32[]{:S(2)}, u32[]{:S(2)}) collective-permute-start(f32[28,2,2,256]{3,2,1,0:T(2,128)S(1)} %get-tuple-element.54), channel_id=1, source_target_pairs={{1,2},{2,1},{3,4},{4,3},{5,6},{6,5},{9,10},{10,9},{11,12},{12,11},... | collective-permute-start | bytes 344072 | tf_op jit(solution)/shard_map/ppermute | solution.py:394
  13.8 11.4 %collective-permute-start.13 = (f32[27,2,2,256]{3,2,1,0:T(2,128)S(1)}, f32[27,2,2,256]{3,2,1,0:T(2,128)S(1)}, u32[]{:S(2)}, u32[]{:S(2)}) collective-permute-start(f32[27,2,2,256]{3,2,1,0:T(2,128)S(1)} %get-tuple-element.53), channel_id=1, source_target_pairs={{0,1},{1,0},{2,3},{3,2},{4,5},{5,4},{6,7},{7,6},{8,9},{9,8},{10,11... | collective-permute-start | bytes 331784 | tf_op jit(solution)/shard_map/ppermute | solution.py:393
  17.0 4.7 %collective-permute-start.5 = (f32[16,512]{1,0:T(8,128)S(1)}, f32[16,512]{1,0:T(8,128)S(1)}, u32[]{:S(2)}, u32[]{:S(2)}) collective-permute-start(f32[16,512]{1,0:T(8,128)S(1)} %get-tuple-element.43), channel_id=1, source_target_pairs={{1,2},{2,1},{3,4},{4,3},{5,6},{6,5},{9,10},{10,9},{11,12},{12,11},... | collective-permute-start | bytes 98312 | tf_op jit(solution)/shard_map/ppermute | solution.py:394
  17.1 4.7 %collective-permute-start.4 = (f32[4,512]{1,0:T(4,128)S(1)}, f32[4,512]{1,0:T(4,128)S(1)}, u32[]{:S(2)}, u32[]{:S(2)}) collective-permute-start(f32[4,512]{1,0:T(4,128)S(1)} %get-tuple-element.42), channel_id=1, source_target_pairs={{0,1},{1,0},{2,3},{3,2},{4,5},{5,4},{6,7},{7,6},{8,9},{9,8},{10,11... | collective-permute-start | bytes 24584 | tf_op jit(solution)/shard_map/ppermute | solution.py:393
  21.8 1.3 %collective-permute-start.6 = (f32[16,512]{1,0:T(8,128)S(1)}, f32[16,512]{1,0:T(8,128)S(1)}, u32[]{:S(2)}, u32[]{:S(2)}) collective-permute-start(f32[16,512]{1,0:T(8,128)S(1)} %get-tuple-element.44), channel_id=1, source_target_pairs={{0,8},{8,0},{16,24},{24,16},{1,9},{9,1},{17,25},{25,17},{2,10},{10... | collective-permute-start | bytes 98312 | tf_op jit(solution)/shard_map/ppermute | solution.py:398
  21.9 3.4 %collective-permute-start.7 = (f32[16,512]{1,0:T(8,128)S(1)}, f32[16,512]{1,0:T(8,128)S(1)}, u32[]{:S(2)}, u32[]{:S(2)}) collective-permute-start(f32[16,512]{1,0:T(8,128)S(1)} %get-tuple-element.45), channel_id=1, source_target_pairs={{8,16},{16,8},{24,0},{0,24},{9,17},{17,9},{25,1},{1,25},{10,18},{1... | collective-permute-start | bytes 98312 | tf_op jit(solution)/shard_map/ppermute | solution.py:399
  25.6 16.2 %collective-permute-start.15 = (f32[27,64,128]{2,1,0:T(8,128)S(1)}, f32[27,64,128]{2,1,0:T(8,128)S(1)}, u32[]{:S(2)}, u32[]{:S(2)}) collective-permute-start(f32[27,64,128]{2,1,0:T(8,128)S(1)} %get-tuple-element.55.own), channel_id=1, source_target_pairs={{0,8},{8,0},{16,24},{24,16},{1,9},{9,1},{17,25},{25,17},{2,10},{10... | collective-permute-start | bytes 2654216 | tf_op jit(solution)/shard_map/ppermute | solution.py:438
  26.1 19.6 %collective-permute-start.21 = (f32[27,32,128]{2,1,0:T(8,128)S(1)}, f32[27,32,128]{2,1,0:T(8,128)S(1)}, u32[]{:S(2)}, u32[]{:S(2)}) collective-permute-start(f32[27,32,128]{2,1,0:T(8,128)S(1)} %get-tuple-element.59), channel_id=1, source_target_pairs={{8,16},{16,8},{9,17},{17,9},{10,18},{18,10},{11,19},{19,11},{12,20... | collective-permute-start | bytes 1327112 | tf_op jit(solution)/shard_map/ppermute | solution.py:439
  27.1 6.0 %collective-permute-start.9 = (f32[16,512]{1,0:T(8,128)S(1)}, f32[16,512]{1,0:T(8,128)S(1)}, u32[]{:S(2)}, u32[]{:S(2)}) collective-permute-start(f32[16,512]{1,0:T(8,128)S(1)} %get-tuple-element.48), channel_id=1, source_target_pairs={{1,2},{2,1},{3,4},{4,3},{5,6},{6,5},{9,10},{10,9},{11,12},{12,11},... | collective-permute-start | bytes 98312 | tf_op jit(solution)/shard_map/ppermute | solution.py:394
  29.0 4.1 %collective-permute-start.8 = (f32[4,512]{1,0:T(4,128)S(1)}, f32[4,512]{1,0:T(4,128)S(1)}, u32[]{:S(2)}, u32[]{:S(2)}) collective-permute-start(f32[4,512]{1,0:T(4,128)S(1)} %get-tuple-element.47), channel_id=1, source_target_pairs={{0,1},{1,0},{2,3},{3,2},{4,5},{5,4},{6,7},{7,6},{8,9},{9,8},{10,11... | collective-permute-start | bytes 24584 | tf_op jit(solution)/shard_map/ppermute | solution.py:393
  33.1 3.1 %collective-permute-start.10 = (f32[16,512]{1,0:T(8,128)S(1)}, f32[16,512]{1,0:T(8,128)S(1)}, u32[]{:S(2)}, u32[]{:S(2)}) collective-permute-start(f32[16,512]{1,0:T(8,128)S(1)} %get-tuple-element.49), channel_id=1, source_target_pairs={{0,8},{8,0},{16,24},{24,16},{1,9},{9,1},{17,25},{25,17},{2,10},{10... | collective-permute-start | bytes 98312 | tf_op jit(solution)/shard_map/ppermute | solution.py:398
  33.9 4.0 %collective-permute-start.11 = (f32[16,512]{1,0:T(8,128)S(1)}, f32[16,512]{1,0:T(8,128)S(1)}, u32[]{:S(2)}, u32[]{:S(2)}) collective-permute-start(f32[16,512]{1,0:T(8,128)S(1)} %get-tuple-element.50), channel_id=1, source_target_pairs={{8,16},{16,8},{24,0},{0,24},{9,17},{17,9},{25,1},{1,25},{10,18},{1... | collective-permute-start | bytes 98312 | tf_op jit(solution)/shard_map/ppermute | solution.py:399
  38.4 5.0 %collective-permute-start.17 = (f32[16,256]{1,0:T(8,128)S(1)}, f32[16,256]{1,0:T(8,128)S(1)}, u32[]{:S(2)}, u32[]{:S(2)}) collective-permute-start(f32[16,256]{1,0:T(8,128)S(1)} %get-tuple-element.58), channel_id=1, source_target_pairs={{1,2},{2,1},{3,4},{4,3},{5,6},{6,5},{9,10},{10,9},{11,12},{12,11},... | collective-permute-start | bytes 49160 | tf_op jit(solution)/shard_map/ppermute | solution.py:394
  38.6 4.8 %collective-permute-start.16 = (f32[8,256]{1,0:T(8,128)S(1)}, f32[8,256]{1,0:T(8,128)S(1)}, u32[]{:S(2)}, u32[]{:S(2)}) collective-permute-start(f32[8,256]{1,0:T(8,128)S(1)} %get-tuple-element.57), channel_id=1, source_target_pairs={{0,1},{1,0},{2,3},{3,2},{4,5},{5,4},{6,7},{7,6},{8,9},{9,8},{10,11... | collective-permute-start | bytes 24584 | tf_op jit(solution)/shard_map/ppermute | solution.py:393
  43.4 3.9 %collective-permute-start.20 = (f32[24,256]{1,0:T(8,128)S(1)}, f32[24,256]{1,0:T(8,128)S(1)}, u32[]{:S(2)}, u32[]{:S(2)}) collective-permute-start(f32[24,256]{1,0:T(8,128)S(1)} %shard_map.78.packed), channel_id=1, source_target_pairs={{0,16},{16,0},{8,24},{24,8},{1,17},{17,1},{9,25},{25,9},{2,18},{18... | collective-permute-start | bytes 73736 | tf_op jit(solution)/shard_map/ppermute | solution.py:463
  45.1 3.3 %collective-permute-start.19 = (f32[24,256]{1,0:T(8,128)S(1)}, f32[24,256]{1,0:T(8,128)S(1)}, u32[]{:S(2)}, u32[]{:S(2)}) collective-permute-start(f32[24,256]{1,0:T(8,128)S(1)} %shard_map.78.packed), channel_id=1, source_target_pairs={{8,16},{16,8},{24,0},{0,24},{9,17},{17,9},{25,1},{1,25},{10,18},{1... | collective-permute-start | bytes 73736 | tf_op jit(solution)/shard_map/ppermute | solution.py:464
  45.1 3.3 %collective-permute-start.18 = (f32[24,256]{1,0:T(8,128)S(1)}, f32[24,256]{1,0:T(8,128)S(1)}, u32[]{:S(2)}, u32[]{:S(2)}) collective-permute-start(f32[24,256]{1,0:T(8,128)S(1)} %shard_map.78.packed), channel_id=1, source_target_pairs={{0,8},{8,0},{16,24},{24,16},{1,9},{9,1},{17,25},{25,17},{2,10},{10... | collective-permute-start | bytes 73736 | tf_op jit(solution)/shard_map/ppermute | solution.py:461
  (1 other events, 0.9 us)

commit v5 on v4

--- a/solution.py
+++ b/solution.py
@@ -203,7 +203,7 @@
     rows = c.shape[2]
     first, last = c[:, :, 0:2, :], c[:, :, rows - 2 : rows, :]
     to_x[...] = pick(even("sub"), last, first)
-    to_zx[0:27] = pick(even("sub"), first, last)
+    to_zx[...] = pick(even("sub"), first, last)
 
 
 def coefficient_scale_kernel(c, out):
@@ -224,7 +224,7 @@
     coarse, (c, from_x, from_zx, _, __, middle_part, whole) = refs[:known], refs[known:]
     _, planes, rows, extent = c.shape
     tiles = extent // LANES
-    before, after = sides(from_x[...], from_zx[0:27])
+    before, after = sides(from_x[...], from_zx[...])
     for x in range(planes):
         for l, lanes in enumerate(lane_tiles(extent)):
             row = (x * tiles + l) * ROWS
@@ -414,7 +414,7 @@
 
     edges_c = call(
         coefficient_edges_kernel,
-        [shape(27, middle_planes, 2, middle_extent), shape(28, middle_planes, 2, middle_extent)],
+        [shape(27, middle_planes, 2, middle_extent)] * 2,
         [middle],
     )
     halo = along_sub((to_x, to_zx))

time: 63 us -> 61.9 us (0.983)
  starting transfers between devices: 28.8 us -> 27.9 us
    ppermute x5, starting transfers between devices: 15.6 us -> 14.3 us  [along_sub(): from_x = lax.ppermute(to_x, 'sub', x_pairs)]
  transfers between devices with their start and end apart: 22 -> 22, of which waited for: 9 -> 9; matrix products, arithmetic and copies ran while one was open for 0% -> 0% of each run, Pallas kernels for 3% -> 2%
where the time goes in v5:
time: 61.9 us; the launch traced here: 61.7 us
  starting transfers between devices  27.9 us (45%)
  waiting for transfers between devices  13.8 us (22%)
  blocking collectives  11.3 us (18%)
  Pallas kernels  4.89 us (8%)
  local copies, waits for them, and re-layouts  2.21 us (4%)
  other arithmetic  0.89 us (1%)
  between operations  0.76 us (1%)
    ppermute x5, starting transfers between devices, along_sub(): from_x = lax.ppermute(to_x, 'sub', x_pairs)  14.3 us
    all_to_all x1, blocking collectives, body(): gathered = lax.all_to_all(coarse_source, ('grp', 'sub'), 0, 0, tiled=True)  11.3 us
    ppermute x3, waiting for transfers between devices, along_grp(): from_y = lax.ppermute(to_y, 'grp', y_ring)  5.64 us
    pallas_call x14, Pallas kernels, call(): pl.pallas_call(kernel, out_shape=outs, in_specs=[vmem] * len(args), out_s...  4.89 us
    ppermute x5, waiting for transfers between devices, along_sub(): from_x = lax.ppermute(to_x, 'sub', x_pairs)  4.8 us
    ppermute x3, starting transfers between devices, along_grp(): from_y = lax.ppermute(to_y, 'grp', y_ring)  4.61 us
    ppermute x5, starting transfers between devices, along_sub(): return (from_x, lax.ppermute(to_zx, ('grp', 'sub'), zx_pairs))  3.18 us
    unnamed x6, local copies, waits for them, and re-layouts  2.21 us
  transfers between devices with their start and end apart: 22, of which 9 were waited for; matrix products, arithmetic and copies ran while one was open for 0% of the time, Pallas kernels for 2%

profile of v5, /device:TPU:0, one launch (start us, length us, event | category | flops | bytes accessed | tf_op | source)
XLA Modules:
  0.0 61.7 jit_solution(8792409732923711183)
XLA Ops:
  0.6 0.9 %bitcast_divide_fusion.v.first = f32[4,8,512]{2,1,0:T(8,128)S(1)} fusion(f32[27,4,8,512]{3,2,1,0:T(8,128)} %c.2, f32[4,8,512]{2,1,0:T(8,128)} %param.4), kind=kLoop, calls=%fused_computation | loop fusion | flops 32768 | bytes 196608 | tf_op jit(solution)/shard_map/div | solution.py:403
  2.1 4.0 %collective-permute-start = (f32[4,512]{1,0:T(4,128)S(1)}, f32[4,512]{1,0:T(4,128)S(1)}, u32[]{:S(2)}, u32[]{:S(2)}) collective-permute-start(f32[4,512]{1,0:T(4,128)S(1)} %get-tuple-element.34), channel_id=1, source_target_pairs={{0,1},{1,0},{2,3},{3,2},{4,5},{5,4},{6,7},{7,6},{8,9},{9,8},{10,11... | collective-permute-start | bytes 24584 | tf_op jit(solution)/shard_map/ppermute | solution.py:393
  6.1 1.5 %copy-done = f32[27,4,8,512]{3,2,1,0:T(8,128)S(1)} copy-done((f32[27,4,8,512]{3,2,1,0:T(8,128)S(1)}, f32[27,4,8,512]{3,2,1,0:T(8,128)}, u32[]{:S(2)}) %copy-start) | copy-done | bytes 1769496
  7.8 0.7 %copy-done.1 = f32[27,2,4,256]{3,2,1,0:T(4,128)S(1)} copy-done((f32[27,2,4,256]{3,2,1,0:T(4,128)S(1)}, f32[27,2,4,256]{3,2,1,0:T(4,128)}, u32[]{:S(2)}) %copy-start.1) | copy-done | bytes 221208
  8.7 1.6 %collective-permute-start.3 = (f32[16,512]{1,0:T(8,128)S(1)}, f32[16,512]{1,0:T(8,128)S(1)}, u32[]{:S(2)}, u32[]{:S(2)}) collective-permute-start(f32[16,512]{1,0:T(8,128)S(1)} %get-tuple-element.40), channel_id=1, source_target_pairs={{8,16},{16,8},{24,0},{0,24},{9,17},{17,9},{25,1},{1,25},{10,18},{1... | collective-permute-start | bytes 98312 | tf_op jit(solution)/shard_map/ppermute | solution.py:399
  10.4 1.8 %collective-permute-done.3.from_y = f32[16,512]{1,0:T(8,128)S(1)} collective-permute-done((f32[16,512]{1,0:T(8,128)S(1)}, f32[16,512]{1,0:T(8,128)S(1)}, u32[]{:S(2)}, u32[]{:S(2)}) %collective-permute-start.3) | collective-permute-done | bytes 32800 | tf_op jit(solution)/shard_map/ppermute | solution.py:399
  12.1 1.5 %collective-permute-start.12 = (f32[27,1,16,128]{3,2,1,0:T(8,128)S(1)}, f32[27,1,16,128]{3,2,1,0:T(8,128)S(1)}, u32[]{:S(2)}, u32[]{:S(2)}) collective-permute-start(f32[27,1,16,128]{3,2,1,0:T(8,128)S(1)} %copy-done.2), channel_id=1, source_target_pairs={{0,16},{8,24},{16,0},{24,8},{1,17},{9,25},{17,1},{25,9},{2,18},{10... | collective-permute-start | bytes 663560 | tf_op jit(solution)/shard_map/ppermute | solution.py:427
  13.7 1.1 %collective-permute-start.13 = (f32[27,2,2,256]{3,2,1,0:T(2,128)S(1)}, f32[27,2,2,256]{3,2,1,0:T(2,128)S(1)}, u32[]{:S(2)}, u32[]{:S(2)}) collective-permute-start(f32[27,2,2,256]{3,2,1,0:T(2,128)S(1)} %get-tuple-element.53), channel_id=1, source_target_pairs={{0,1},{1,0},{2,3},{3,2},{4,5},{5,4},{6,7},{7,6},{8,9},{9,8},{10,11... | collective-permute-start | bytes 331784 | tf_op jit(solution)/shard_map/ppermute | solution.py:393
  15.6 3.3 %collective-permute-start.4 = (f32[4,512]{1,0:T(4,128)S(1)}, f32[4,512]{1,0:T(4,128)S(1)}, u32[]{:S(2)}, u32[]{:S(2)}) collective-permute-start(f32[4,512]{1,0:T(4,128)S(1)} %get-tuple-element.42), channel_id=1, source_target_pairs={{0,1},{1,0},{2,3},{3,2},{4,5},{5,4},{6,7},{7,6},{8,9},{9,8},{10,11... | collective-permute-start | bytes 24584 | tf_op jit(solution)/shard_map/ppermute | solution.py:393
  19.0 1.6 %collective-permute-done.4.from_x = f32[4,512]{1,0:T(4,128)S(1)} collective-permute-done((f32[4,512]{1,0:T(4,128)S(1)}, f32[4,512]{1,0:T(4,128)S(1)}, u32[]{:S(2)}, u32[]{:S(2)}) %collective-permute-start.4) | collective-permute-done | bytes 8224 | tf_op jit(solution)/shard_map/ppermute | solution.py:393
  21.9 2.2 %collective-permute-done.7.from_y.refs_6_ = f32[16,512]{1,0:T(8,128)S(1)} collective-permute-done((f32[16,512]{1,0:T(8,128)S(1)}, f32[16,512]{1,0:T(8,128)S(1)}, u32[]{:S(2)}, u32[]{:S(2)}) %collective-permute-start.7) | collective-permute-done | bytes 32800 | tf_op jit(solution)/shard_map/ppermute | solution.py:399
  25.9 1.9 %collective-permute-start.9 = (f32[16,512]{1,0:T(8,128)S(1)}, f32[16,512]{1,0:T(8,128)S(1)}, u32[]{:S(2)}, u32[]{:S(2)}) collective-permute-start(f32[16,512]{1,0:T(8,128)S(1)} %get-tuple-element.48), channel_id=1, source_target_pairs={{1,2},{2,1},{3,4},{4,3},{5,6},{6,5},{9,10},{10,9},{11,12},{12,11},... | collective-permute-start | bytes 98312 | tf_op jit(solution)/shard_map/ppermute | solution.py:394
  27.8 2.6 %collective-permute-start.8 = (f32[4,512]{1,0:T(4,128)S(1)}, f32[4,512]{1,0:T(4,128)S(1)}, u32[]{:S(2)}, u32[]{:S(2)}) collective-permute-start(f32[4,512]{1,0:T(4,128)S(1)} %get-tuple-element.47), channel_id=1, source_target_pairs={{0,1},{1,0},{2,3},{3,2},{4,5},{5,4},{6,7},{7,6},{8,9},{9,8},{10,11... | collective-permute-start | bytes 24584 | tf_op jit(solution)/shard_map/ppermute | solution.py:393
  30.4 1.6 %collective-permute-done.8.from_x = f32[4,512]{1,0:T(4,128)S(1)} collective-permute-done((f32[4,512]{1,0:T(4,128)S(1)}, f32[4,512]{1,0:T(4,128)S(1)}, u32[]{:S(2)}, u32[]{:S(2)}) %collective-permute-start.8) | collective-permute-done | bytes 8224 | tf_op jit(solution)/shard_map/ppermute | solution.py:393
  32.1 0.8 %collective-permute-start.10 = (f32[16,512]{1,0:T(8,128)S(1)}, f32[16,512]{1,0:T(8,128)S(1)}, u32[]{:S(2)}, u32[]{:S(2)}) collective-permute-start(f32[16,512]{1,0:T(8,128)S(1)} %get-tuple-element.49), channel_id=1, source_target_pairs={{0,8},{8,0},{16,24},{24,16},{1,9},{9,1},{17,25},{25,17},{2,10},{10... | collective-permute-start | bytes 98312 | tf_op jit(solution)/shard_map/ppermute | solution.py:398
  32.9 2.4 %collective-permute-start.11 = (f32[16,512]{1,0:T(8,128)S(1)}, f32[16,512]{1,0:T(8,128)S(1)}, u32[]{:S(2)}, u32[]{:S(2)}) collective-permute-start(f32[16,512]{1,0:T(8,128)S(1)} %get-tuple-element.50), channel_id=1, source_target_pairs={{8,16},{16,8},{24,0},{0,24},{9,17},{17,9},{25,1},{1,25},{10,18},{1... | collective-permute-start | bytes 98312 | tf_op jit(solution)/shard_map/ppermute | solution.py:399
  35.2 1.7 %collective-permute-done.11.from_y = f32[16,512]{1,0:T(8,128)S(1)} collective-permute-done((f32[16,512]{1,0:T(8,128)S(1)}, f32[16,512]{1,0:T(8,128)S(1)}, u32[]{:S(2)}, u32[]{:S(2)}) %collective-permute-start.11) | collective-permute-done | bytes 32800 | tf_op jit(solution)/shard_map/ppermute | solution.py:399
  37.6 3.2 %collective-permute-start.16 = (f32[8,256]{1,0:T(8,128)S(1)}, f32[8,256]{1,0:T(8,128)S(1)}, u32[]{:S(2)}, u32[]{:S(2)}) collective-permute-start(f32[8,256]{1,0:T(8,128)S(1)} %get-tuple-element.57), channel_id=1, source_target_pairs={{0,1},{1,0},{2,3},{3,2},{4,5},{5,4},{6,7},{7,6},{8,9},{9,8},{10,11... | collective-permute-start | bytes 24584 | tf_op jit(solution)/shard_map/ppermute | solution.py:393
  40.8 1.5 %collective-permute-done.16.from_x = f32[8,256]{1,0:T(8,128)S(1)} collective-permute-done((f32[8,256]{1,0:T(8,128)S(1)}, f32[8,256]{1,0:T(8,128)S(1)}, u32[]{:S(2)}, u32[]{:S(2)}) %collective-permute-start.16) | collective-permute-done | bytes 8224 | tf_op jit(solution)/shard_map/ppermute | solution.py:393
  42.4 1.7 %collective-permute-start.20 = (f32[24,256]{1,0:T(8,128)S(1)}, f32[24,256]{1,0:T(8,128)S(1)}, u32[]{:S(2)}, u32[]{:S(2)}) collective-permute-start(f32[24,256]{1,0:T(8,128)S(1)} %shard_map.78.packed), channel_id=1, source_target_pairs={{0,16},{16,0},{8,24},{24,8},{1,17},{17,1},{9,25},{25,9},{2,18},{18... | collective-permute-start | bytes 73736 | tf_op jit(solution)/shard_map/ppermute | solution.py:463
  44.6 1.7 %collective-permute-done.20.far_below.far_above = f32[24,256]{1,0:T(8,128)S(1)} collective-permute-done((f32[24,256]{1,0:T(8,128)S(1)}, f32[24,256]{1,0:T(8,128)S(1)}, u32[]{:S(2)}, u32[]{:S(2)}) %collective-permute-start.20) | collective-permute-done | bytes 24608 | tf_op jit(solution)/shard_map/ppermute | solution.py:463
  46.3 1.0 %collective-permute-done.19.near_y = f32[24,256]{1,0:T(8,128)S(1)} collective-permute-done((f32[24,256]{1,0:T(8,128)S(1)}, f32[24,256]{1,0:T(8,128)S(1)}, u32[]{:S(2)}, u32[]{:S(2)}) %collective-permute-start.19) | collective-permute-done | bytes 24608 | tf_op jit(solution)/shard_map/ppermute | solution.py:464
  47.9 11.3 %all_to_all.5.gathered = f32[32,1,2,128]{3,2,1,0:T(2,128)S(1)} all-to-all(f32[32,1,2,128]{3,2,1,0:T(2,128)S(1)} %get-tuple-element.60), channel_id=1, replica_groups=mesh['grp'=4,'sub'=8] {'grp','sub'}, dimensions={0} | all-to-all | bytes 65536 | tf_op jit(solution)/shard_map/all_to_all | solution.py:479
  59.2 2.5 %shard_map.80 = (f32[1,16,128]{2,1,0:T(8,128)}, f32[4,8,512]{2,1,0:T(8,128)}, f32[2,4,256]{2,1,0:T(4,128)}) custom-call(f32[32,1,2,128]{3,2,1,0:T(2,128)S(1)} %all_to_all.5.gathered, f32[4,27,16,128]{3,2,1,0:T(8,128)S(1)} %shard_map.77.c, f32[4,8,512]{2,1,0:T(8,128)S(1)} %get-tuple-element.46.v.fine, f32[2,4,256]{2,1,0:T(4,128)S(1)} %get-tuple-element.61.middle), custom_call_target="tpu_custom_call" | custom-call | tf_op jit(solution)/shard_map/pallas_call | solution.py:24
  (43 shorter events, 6.8 us)
Async XLA Ops:
  1.5 7.1 %collective-permute-start.1 = (f32[16,512]{1,0:T(8,128)S(1)}, f32[16,512]{1,0:T(8,128)S(1)}, u32[]{:S(2)}, u32[]{:S(2)}) collective-permute-start(f32[16,512]{1,0:T(8,128)S(1)} %get-tuple-element.35), channel_id=1, source_target_pairs={{1,2},{2,1},{3,4},{4,3},{5,6},{6,5},{9,10},{10,9},{11,12},{12,11},... | collective-permute-start | bytes 98312 | tf_op jit(solution)/shard_map/ppermute | solution.py:394
  2.1 6.5 %collective-permute-start = (f32[4,512]{1,0:T(4,128)S(1)}, f32[4,512]{1,0:T(4,128)S(1)}, u32[]{:S(2)}, u32[]{:S(2)}) collective-permute-start(f32[4,512]{1,0:T(4,128)S(1)} %get-tuple-element.34), channel_id=1, source_target_pairs={{0,1},{1,0},{2,3},{3,2},{4,5},{5,4},{6,7},{7,6},{8,9},{9,8},{10,11... | collective-permute-start | bytes 24584 | tf_op jit(solution)/shard_map/ppermute | solution.py:393
  6.1 1.5 %copy-start = (f32[27,4,8,512]{3,2,1,0:T(8,128)S(1)}, f32[27,4,8,512]{3,2,1,0:T(8,128)}, u32[]{:S(2)}) copy-start(f32[27,4,8,512]{3,2,1,0:T(8,128)} %c.2) | copy-start | bytes 5308420
  7.6 4.6 %copy-start.2 = (f32[27,1,16,128]{3,2,1,0:T(8,128)S(1)}, f32[27,1,16,128]{3,2,1,0:T(8,128)}, u32[]{:S(2)}) copy-start(f32[27,1,16,128]{3,2,1,0:T(8,128)} %refs_0_) | copy-start | bytes 663556
  8.7 1.7 %collective-permute-start.2 = (f32[16,512]{1,0:T(8,128)S(1)}, f32[16,512]{1,0:T(8,128)S(1)}, u32[]{:S(2)}, u32[]{:S(2)}) collective-permute-start(f32[16,512]{1,0:T(8,128)S(1)} %get-tuple-element.39), channel_id=1, source_target_pairs={{0,8},{8,0},{16,24},{24,16},{1,9},{9,1},{17,25},{25,17},{2,10},{10... | collective-permute-start | bytes 98312 | tf_op jit(solution)/shard_map/ppermute | solution.py:398
  8.7 3.4 %collective-permute-start.3 = (f32[16,512]{1,0:T(8,128)S(1)}, f32[16,512]{1,0:T(8,128)S(1)}, u32[]{:S(2)}, u32[]{:S(2)}) collective-permute-start(f32[16,512]{1,0:T(8,128)S(1)} %get-tuple-element.40), channel_id=1, source_target_pairs={{8,16},{16,8},{24,0},{0,24},{9,17},{17,9},{25,1},{1,25},{10,18},{1... | collective-permute-start | bytes 98312 | tf_op jit(solution)/shard_map/ppermute | solution.py:399
  12.1 12.0 %collective-permute-start.12 = (f32[27,1,16,128]{3,2,1,0:T(8,128)S(1)}, f32[27,1,16,128]{3,2,1,0:T(8,128)S(1)}, u32[]{:S(2)}, u32[]{:S(2)}) collective-permute-start(f32[27,1,16,128]{3,2,1,0:T(8,128)S(1)} %copy-done.2), channel_id=1, source_target_pairs={{0,16},{8,24},{16,0},{24,8},{1,17},{9,25},{17,1},{25,9},{2,18},{10... | collective-permute-start | bytes 663560 | tf_op jit(solution)/shard_map/ppermute | solution.py:427
  13.7 10.4 %collective-permute-start.13 = (f32[27,2,2,256]{3,2,1,0:T(2,128)S(1)}, f32[27,2,2,256]{3,2,1,0:T(2,128)S(1)}, u32[]{:S(2)}, u32[]{:S(2)}) collective-permute-start(f32[27,2,2,256]{3,2,1,0:T(2,128)S(1)} %get-tuple-element.53), channel_id=1, source_target_pairs={{0,1},{1,0},{2,3},{3,2},{4,5},{5,4},{6,7},{7,6},{8,9},{9,8},{10,11... | collective-permute-start | bytes 331784 | tf_op jit(solution)/shard_map/ppermute | solution.py:393
  14.8 9.3 %collective-permute-start.14 = (f32[27,2,2,256]{3,2,1,0:T(2,128)S(1)}, f32[27,2,2,256]{3,2,1,0:T(2,128)S(1)}, u32[]{:S(2)}, u32[]{:S(2)}) collective-permute-start(f32[27,2,2,256]{3,2,1,0:T(2,128)S(1)} %get-tuple-element.54), channel_id=1, source_target_pairs={{1,2},{2,1},{3,4},{4,3},{5,6},{6,5},{9,10},{10,9},{11,12},{12,11},... | collective-permute-start | bytes 331784 | tf_op jit(solution)/shard_map/ppermute | solution.py:394
  15.1 5.5 %collective-permute-start.5 = (f32[16,512]{1,0:T(8,128)S(1)}, f32[16,512]{1,0:T(8,128)S(1)}, u32[]{:S(2)}, u32[]{:S(2)}) collective-permute-start(f32[16,512]{1,0:T(8,128)S(1)} %get-tuple-element.43), channel_id=1, source_target_pairs={{1,2},{2,1},{3,4},{4,3},{5,6},{6,5},{9,10},{10,9},{11,12},{12,11},... | collective-permute-start | bytes 98312 | tf_op jit(solution)/shard_map/ppermute | solution.py:394
  15.6 4.9 %collective-permute-start.4 = (f32[4,512]{1,0:T(4,128)S(1)}, f32[4,512]{1,0:T(4,128)S(1)}, u32[]{:S(2)}, u32[]{:S(2)}) collective-permute-start(f32[4,512]{1,0:T(4,128)S(1)} %get-tuple-element.42), channel_id=1, source_target_pairs={{0,1},{1,0},{2,3},{3,2},{4,5},{5,4},{6,7},{7,6},{8,9},{9,8},{10,11... | collective-permute-start | bytes 24584 | tf_op jit(solution)/shard_map/ppermute | solution.py:393
  20.6 1.3 %collective-permute-start.6 = (f32[16,512]{1,0:T(8,128)S(1)}, f32[16,512]{1,0:T(8,128)S(1)}, u32[]{:S(2)}, u32[]{:S(2)}) collective-permute-start(f32[16,512]{1,0:T(8,128)S(1)} %get-tuple-element.44), channel_id=1, source_target_pairs={{0,8},{8,0},{16,24},{24,16},{1,9},{9,1},{17,25},{25,17},{2,10},{10... | collective-permute-start | bytes 98312 | tf_op jit(solution)/shard_map/ppermute | solution.py:398
  20.7 3.4 %collective-permute-start.7 = (f32[16,512]{1,0:T(8,128)S(1)}, f32[16,512]{1,0:T(8,128)S(1)}, u32[]{:S(2)}, u32[]{:S(2)}) collective-permute-start(f32[16,512]{1,0:T(8,128)S(1)} %get-tuple-element.45), channel_id=1, source_target_pairs={{8,16},{16,8},{24,0},{0,24},{9,17},{17,9},{25,1},{1,25},{10,18},{1... | collective-permute-start | bytes 98312 | tf_op jit(solution)/shard_map/ppermute | solution.py:399
  24.4 16.3 %collective-permute-start.15 = (f32[27,64,128]{2,1,0:T(8,128)S(1)}, f32[27,64,128]{2,1,0:T(8,128)S(1)}, u32[]{:S(2)}, u32[]{:S(2)}) collective-permute-start(f32[27,64,128]{2,1,0:T(8,128)S(1)} %get-tuple-element.55.own), channel_id=1, source_target_pairs={{0,8},{8,0},{16,24},{24,16},{1,9},{9,1},{17,25},{25,17},{2,10},{10... | collective-permute-start | bytes 2654216 | tf_op jit(solution)/shard_map/ppermute | solution.py:438
  24.9 19.7 %collective-permute-start.21 = (f32[27,32,128]{2,1,0:T(8,128)S(1)}, f32[27,32,128]{2,1,0:T(8,128)S(1)}, u32[]{:S(2)}, u32[]{:S(2)}) collective-permute-start(f32[27,32,128]{2,1,0:T(8,128)S(1)} %get-tuple-element.59), channel_id=1, source_target_pairs={{8,16},{16,8},{9,17},{17,9},{10,18},{18,10},{11,19},{19,11},{12,20... | collective-permute-start | bytes 1327112 | tf_op jit(solution)/shard_map/ppermute | solution.py:439
  25.9 6.2 %collective-permute-start.9 = (f32[16,512]{1,0:T(8,128)S(1)}, f32[16,512]{1,0:T(8,128)S(1)}, u32[]{:S(2)}, u32[]{:S(2)}) collective-permute-start(f32[16,512]{1,0:T(8,128)S(1)} %get-tuple-element.48), channel_id=1, source_target_pairs={{1,2},{2,1},{3,4},{4,3},{5,6},{6,5},{9,10},{10,9},{11,12},{12,11},... | collective-permute-start | bytes 98312 | tf_op jit(solution)/shard_map/ppermute | solution.py:394
  27.8 4.3 %collective-permute-start.8 = (f32[4,512]{1,0:T(4,128)S(1)}, f32[4,512]{1,0:T(4,128)S(1)}, u32[]{:S(2)}, u32[]{:S(2)}) collective-permute-start(f32[4,512]{1,0:T(4,128)S(1)} %get-tuple-element.47), channel_id=1, source_target_pairs={{0,1},{1,0},{2,3},{3,2},{4,5},{5,4},{6,7},{7,6},{8,9},{9,8},{10,11... | collective-permute-start | bytes 24584 | tf_op jit(solution)/shard_map/ppermute | solution.py:393
  32.1 3.1 %collective-permute-start.10 = (f32[16,512]{1,0:T(8,128)S(1)}, f32[16,512]{1,0:T(8,128)S(1)}, u32[]{:S(2)}, u32[]{:S(2)}) collective-permute-start(f32[16,512]{1,0:T(8,128)S(1)} %get-tuple-element.49), channel_id=1, source_target_pairs={{0,8},{8,0},{16,24},{24,16},{1,9},{9,1},{17,25},{25,17},{2,10},{10... | collective-permute-start | bytes 98312 | tf_op jit(solution)/shard_map/ppermute | solution.py:398
  32.9 4.0 %collective-permute-start.11 = (f32[16,512]{1,0:T(8,128)S(1)}, f32[16,512]{1,0:T(8,128)S(1)}, u32[]{:S(2)}, u32[]{:S(2)}) collective-permute-start(f32[16,512]{1,0:T(8,128)S(1)} %get-tuple-element.50), channel_id=1, source_target_pairs={{8,16},{16,8},{24,0},{0,24},{9,17},{17,9},{25,1},{1,25},{10,18},{1... | collective-permute-start | bytes 98312 | tf_op jit(solution)/shard_map/ppermute | solution.py:399
  37.4 5.0 %collective-permute-start.17 = (f32[16,256]{1,0:T(8,128)S(1)}, f32[16,256]{1,0:T(8,128)S(1)}, u32[]{:S(2)}, u32[]{:S(2)}) collective-permute-start(f32[16,256]{1,0:T(8,128)S(1)} %get-tuple-element.58), channel_id=1, source_target_pairs={{1,2},{2,1},{3,4},{4,3},{5,6},{6,5},{9,10},{10,9},{11,12},{12,11},... | collective-permute-start | bytes 49160 | tf_op jit(solution)/shard_map/ppermute | solution.py:394
  37.6 4.8 %collective-permute-start.16 = (f32[8,256]{1,0:T(8,128)S(1)}, f32[8,256]{1,0:T(8,128)S(1)}, u32[]{:S(2)}, u32[]{:S(2)}) collective-permute-start(f32[8,256]{1,0:T(8,128)S(1)} %get-tuple-element.57), channel_id=1, source_target_pairs={{0,1},{1,0},{2,3},{3,2},{4,5},{5,4},{6,7},{7,6},{8,9},{9,8},{10,11... | collective-permute-start | bytes 24584 | tf_op jit(solution)/shard_map/ppermute | solution.py:393
  42.4 3.9 %collective-permute-start.20 = (f32[24,256]{1,0:T(8,128)S(1)}, f32[24,256]{1,0:T(8,128)S(1)}, u32[]{:S(2)}, u32[]{:S(2)}) collective-permute-start(f32[24,256]{1,0:T(8,128)S(1)} %shard_map.78.packed), channel_id=1, source_target_pairs={{0,16},{16,0},{8,24},{24,8},{1,17},{17,1},{9,25},{25,9},{2,18},{18... | collective-permute-start | bytes 73736 | tf_op jit(solution)/shard_map/ppermute | solution.py:463
  44.1 3.3 %collective-permute-start.19 = (f32[24,256]{1,0:T(8,128)S(1)}, f32[24,256]{1,0:T(8,128)S(1)}, u32[]{:S(2)}, u32[]{:S(2)}) collective-permute-start(f32[24,256]{1,0:T(8,128)S(1)} %shard_map.78.packed), channel_id=1, source_target_pairs={{8,16},{16,8},{24,0},{0,24},{9,17},{17,9},{25,1},{1,25},{10,18},{1... | collective-permute-start | bytes 73736 | tf_op jit(solution)/shard_map/ppermute | solution.py:464
  44.1 3.3 %collective-permute-start.18 = (f32[24,256]{1,0:T(8,128)S(1)}, f32[24,256]{1,0:T(8,128)S(1)}, u32[]{:S(2)}, u32[]{:S(2)}) collective-permute-start(f32[24,256]{1,0:T(8,128)S(1)} %shard_map.78.packed), channel_id=1, source_target_pairs={{0,8},{8,0},{16,24},{24,16},{1,9},{9,1},{17,25},{25,17},{2,10},{10... | collective-permute-start | bytes 73736 | tf_op jit(solution)/shard_map/ppermute | solution.py:461
  (1 other events, 0.9 us)

commit v6 on v5

--- a/solution.py
+++ b/solution.py
@@ -419,8 +419,8 @@
     )
     halo = along_sub((to_x, to_zx))
     halo_c = along_sub(after_all(edges_c, *halo))
-    halo = along_grp(after(v, weights, *edges_c), halo)
-    known = {0: after(coarse, *halo[2:])}
+    halo = along_grp(after(v, *edges_c), halo)
+    known = {0: coarse}
     bit = groups // 2
     while bit > 1:
         for offset in sorted(known):

time: 61.9 us -> 61.1 us (0.987)
  starting transfers between devices: 27.9 us -> 27 us
    ppermute x1, starting transfers between devices: 1.52 us -> 3.03 us  [body(): lax.ppermute(known[offset], 'grp', [(i, i ^ bit) for i in range(groups)])]
    ppermute x3, starting transfers between devices: 4.61 us -> 3.16 us  [along_grp(): from_y = lax.ppermute(to_y, 'grp', y_ring)]
    ppermute x5, starting transfers between devices: 3.18 us -> 2.34 us  [along_sub(): return (from_x, lax.ppermute(to_zx, ('grp', 'sub'), zx_pairs))]
    unnamed x6 -> x8, local copies, waits for them, and re-layouts: 2.21 us -> 2.42 us
  transfers between devices with their start and end apart: 22 -> 22, of which waited for: 9 -> 10; matrix products, arithmetic and copies ran while one was open for 0% -> 1% of each run, Pallas kernels for 2% -> 2%
where the time goes in v6:
time: 61.1 us; the launch traced here: 60.9 us
  starting transfers between devices  27 us (44%)
  waiting for transfers between devices  14.1 us (23%)
  blocking collectives  10.7 us (18%)
  Pallas kernels  4.88 us (8%)
  local copies, waits for them, and re-layouts  2.43 us (4%)
  other arithmetic  0.89 us (1%)
  between operations  0.78 us (1%)
    ppermute x5, starting transfers between devices, along_sub(): from_x = lax.ppermute(to_x, 'sub', x_pairs)  13.7 us
    all_to_all x1, blocking collectives, body(): gathered = lax.all_to_all(coarse_source, ('grp', 'sub'), 0, 0, tiled=True)  10.7 us
    ppermute x5, waiting for transfers between devices, along_sub(): from_x = lax.ppermute(to_x, 'sub', x_pairs)  5.41 us
    ppermute x3, waiting for transfers between devices, along_grp(): from_y = lax.ppermute(to_y, 'grp', y_ring)  5.39 us
    pallas_call x14, Pallas kernels, call(): pl.pallas_call(kernel, out_shape=outs, in_specs=[vmem] * len(args), out_s...  4.88 us
    ppermute x3, starting transfers between devices, along_grp(): from_y = lax.ppermute(to_y, 'grp', y_ring)  3.16 us
    ppermute x1, starting transfers between devices, body(): lax.ppermute(known[offset], 'grp', [(i, i ^ bit) for i in range(groups)])  3.03 us
    unnamed x8, local copies, waits for them, and re-layouts  2.42 us
  transfers between devices with their start and end apart: 22, of which 10 were waited for; matrix products, arithmetic and copies ran while one was open for 1% of the time, Pallas kernels for 2%

profile of v6, /device:TPU:0, one launch (start us, length us, event | category | flops | bytes accessed | tf_op | source)
XLA Modules:
  0.0 60.9 jit_solution(8376985454122326400)
XLA Ops:
  0.6 3.0 %collective-permute-start.12 = (f32[27,1,16,128]{3,2,1,0:T(8,128)}, f32[27,1,16,128]{3,2,1,0:T(8,128)S(1)}, u32[]{:S(2)}, u32[]{:S(2)}) collective-permute-start(f32[27,1,16,128]{3,2,1,0:T(8,128)} %refs_0_.1), channel_id=1, source_target_pairs={{0,16},{8,24},{16,0},{24,8},{1,17},{9,25},{17,1},{25,9},{2,18},{10... | collective-permute-start | bytes 663560 | tf_op jit(solution)/shard_map/ppermute | solution.py:427
  3.7 0.9 %bitcast_divide_fusion.v.first = f32[4,8,512]{2,1,0:T(8,128)S(1)} fusion(f32[27,4,8,512]{3,2,1,0:T(8,128)} %c.2, f32[4,8,512]{2,1,0:T(8,128)} %param.4), kind=kLoop, calls=%fused_computation | loop fusion | flops 32768 | bytes 196608 | tf_op jit(solution)/shard_map/div | solution.py:403
  4.7 3.0 %collective-permute-start = (f32[4,512]{1,0:T(4,128)S(1)}, f32[4,512]{1,0:T(4,128)S(1)}, u32[]{:S(2)}, u32[]{:S(2)}) collective-permute-start(f32[4,512]{1,0:T(4,128)S(1)} %get-tuple-element.33), channel_id=1, source_target_pairs={{0,1},{1,0},{2,3},{3,2},{4,5},{5,4},{6,7},{7,6},{8,9},{9,8},{10,11... | collective-permute-start | bytes 24584 | tf_op jit(solution)/shard_map/ppermute | solution.py:393
  7.7 0.9 %copy-done.1 = f32[27,2,4,256]{3,2,1,0:T(4,128)S(1)} copy-done((f32[27,2,4,256]{3,2,1,0:T(4,128)S(1)}, f32[27,2,4,256]{3,2,1,0:T(4,128)}, u32[]{:S(2)}) %copy-start.1) | copy-done | bytes 221208
  9.3 2.0 %collective-permute-start.13 = (f32[27,2,2,256]{3,2,1,0:T(2,128)S(1)}, f32[27,2,2,256]{3,2,1,0:T(2,128)S(1)}, u32[]{:S(2)}, u32[]{:S(2)}) collective-permute-start(f32[27,2,2,256]{3,2,1,0:T(2,128)S(1)} %get-tuple-element.51), channel_id=1, source_target_pairs={{0,1},{1,0},{2,3},{3,2},{4,5},{5,4},{6,7},{7,6},{8,9},{9,8},{10,11... | collective-permute-start | bytes 331784 | tf_op jit(solution)/shard_map/ppermute | solution.py:393
  12.1 1.5 %copy-done = f32[27,4,8,512]{3,2,1,0:T(8,128)S(1)} copy-done((f32[27,4,8,512]{3,2,1,0:T(8,128)S(1)}, f32[27,4,8,512]{3,2,1,0:T(8,128)}, u32[]{:S(2)}) %copy-start) | copy-done | bytes 1769496
  13.8 1.5 %collective-permute-done.3.from_y = f32[16,512]{1,0:T(8,128)S(1)} collective-permute-done((f32[16,512]{1,0:T(8,128)S(1)}, f32[16,512]{1,0:T(8,128)S(1)}, u32[]{:S(2)}, u32[]{:S(2)}) %collective-permute-start.3) | collective-permute-done | bytes 32800 | tf_op jit(solution)/shard_map/ppermute | solution.py:399
  15.8 2.5 %collective-permute-start.4 = (f32[4,512]{1,0:T(4,128)S(1)}, f32[4,512]{1,0:T(4,128)S(1)}, u32[]{:S(2)}, u32[]{:S(2)}) collective-permute-start(f32[4,512]{1,0:T(4,128)S(1)} %get-tuple-element.41), channel_id=1, source_target_pairs={{0,1},{1,0},{2,3},{3,2},{4,5},{5,4},{6,7},{7,6},{8,9},{9,8},{10,11... | collective-permute-start | bytes 24584 | tf_op jit(solution)/shard_map/ppermute | solution.py:393
  18.3 1.6 %collective-permute-done.4.from_x = f32[4,512]{1,0:T(4,128)S(1)} collective-permute-done((f32[4,512]{1,0:T(4,128)S(1)}, f32[4,512]{1,0:T(4,128)S(1)}, u32[]{:S(2)}, u32[]{:S(2)}) %collective-permute-start.4) | collective-permute-done | bytes 8224 | tf_op jit(solution)/shard_map/ppermute | solution.py:393
  21.2 2.2 %collective-permute-done.7.from_y.refs_6_ = f32[16,512]{1,0:T(8,128)S(1)} collective-permute-done((f32[16,512]{1,0:T(8,128)S(1)}, f32[16,512]{1,0:T(8,128)S(1)}, u32[]{:S(2)}, u32[]{:S(2)}) %collective-permute-start.7) | collective-permute-done | bytes 32800 | tf_op jit(solution)/shard_map/ppermute | solution.py:399
  24.3 0.7 %collective-permute-start.21 = (f32[27,32,128]{2,1,0:T(8,128)S(1)}, f32[27,32,128]{2,1,0:T(8,128)S(1)}, u32[]{:S(2)}, u32[]{:S(2)}) collective-permute-start(f32[27,32,128]{2,1,0:T(8,128)S(1)} %get-tuple-element.57), channel_id=1, source_target_pairs={{8,16},{16,8},{9,17},{17,9},{10,18},{18,10},{11,19},{19,11},{12,20... | collective-permute-start | bytes 1327112 | tf_op jit(solution)/shard_map/ppermute | solution.py:439
  25.3 1.9 %collective-permute-start.9 = (f32[16,512]{1,0:T(8,128)S(1)}, f32[16,512]{1,0:T(8,128)S(1)}, u32[]{:S(2)}, u32[]{:S(2)}) collective-permute-start(f32[16,512]{1,0:T(8,128)S(1)} %get-tuple-element.47), channel_id=1, source_target_pairs={{1,2},{2,1},{3,4},{4,3},{5,6},{6,5},{9,10},{10,9},{11,12},{12,11},... | collective-permute-start | bytes 98312 | tf_op jit(solution)/shard_map/ppermute | solution.py:394
  27.2 3.0 %collective-permute-start.8 = (f32[4,512]{1,0:T(4,128)S(1)}, f32[4,512]{1,0:T(4,128)S(1)}, u32[]{:S(2)}, u32[]{:S(2)}) collective-permute-start(f32[4,512]{1,0:T(4,128)S(1)} %get-tuple-element.46), channel_id=1, source_target_pairs={{0,1},{1,0},{2,3},{3,2},{4,5},{5,4},{6,7},{7,6},{8,9},{9,8},{10,11... | collective-permute-start | bytes 24584 | tf_op jit(solution)/shard_map/ppermute | solution.py:393
  30.2 1.6 %collective-permute-done.8.from_x = f32[4,512]{1,0:T(4,128)S(1)} collective-permute-done((f32[4,512]{1,0:T(4,128)S(1)}, f32[4,512]{1,0:T(4,128)S(1)}, u32[]{:S(2)}, u32[]{:S(2)}) %collective-permute-start.8) | collective-permute-done | bytes 8224 | tf_op jit(solution)/shard_map/ppermute | solution.py:393
  31.9 0.8 %collective-permute-start.10 = (f32[16,512]{1,0:T(8,128)S(1)}, f32[16,512]{1,0:T(8,128)S(1)}, u32[]{:S(2)}, u32[]{:S(2)}) collective-permute-start(f32[16,512]{1,0:T(8,128)S(1)} %get-tuple-element.48), channel_id=1, source_target_pairs={{0,8},{8,0},{16,24},{24,16},{1,9},{9,1},{17,25},{25,17},{2,10},{10... | collective-permute-start | bytes 98312 | tf_op jit(solution)/shard_map/ppermute | solution.py:398
  32.6 2.4 %collective-permute-start.11 = (f32[16,512]{1,0:T(8,128)S(1)}, f32[16,512]{1,0:T(8,128)S(1)}, u32[]{:S(2)}, u32[]{:S(2)}) collective-permute-start(f32[16,512]{1,0:T(8,128)S(1)} %get-tuple-element.49), channel_id=1, source_target_pairs={{8,16},{16,8},{24,0},{0,24},{9,17},{17,9},{25,1},{1,25},{10,18},{1... | collective-permute-start | bytes 98312 | tf_op jit(solution)/shard_map/ppermute | solution.py:399
  35.0 1.7 %collective-permute-done.11.from_y = f32[16,512]{1,0:T(8,128)S(1)} collective-permute-done((f32[16,512]{1,0:T(8,128)S(1)}, f32[16,512]{1,0:T(8,128)S(1)}, u32[]{:S(2)}, u32[]{:S(2)}) %collective-permute-start.11) | collective-permute-done | bytes 32800 | tf_op jit(solution)/shard_map/ppermute | solution.py:399
  37.3 3.2 %collective-permute-start.16 = (f32[8,256]{1,0:T(8,128)S(1)}, f32[8,256]{1,0:T(8,128)S(1)}, u32[]{:S(2)}, u32[]{:S(2)}) collective-permute-start(f32[8,256]{1,0:T(8,128)S(1)} %get-tuple-element.55), channel_id=1, source_target_pairs={{0,1},{1,0},{2,3},{3,2},{4,5},{5,4},{6,7},{7,6},{8,9},{9,8},{10,11... | collective-permute-start | bytes 24584 | tf_op jit(solution)/shard_map/ppermute | solution.py:393
  40.6 1.5 %collective-permute-done.16.from_x = f32[8,256]{1,0:T(8,128)S(1)} collective-permute-done((f32[8,256]{1,0:T(8,128)S(1)}, f32[8,256]{1,0:T(8,128)S(1)}, u32[]{:S(2)}, u32[]{:S(2)}) %collective-permute-start.16) | collective-permute-done | bytes 8224 | tf_op jit(solution)/shard_map/ppermute | solution.py:393
  42.1 1.7 %collective-permute-start.20 = (f32[24,256]{1,0:T(8,128)S(1)}, f32[24,256]{1,0:T(8,128)S(1)}, u32[]{:S(2)}, u32[]{:S(2)}) collective-permute-start(f32[24,256]{1,0:T(8,128)S(1)} %shard_map.78.packed), channel_id=1, source_target_pairs={{0,16},{16,0},{8,24},{24,8},{1,17},{17,1},{9,25},{25,9},{2,18},{18... | collective-permute-start | bytes 73736 | tf_op jit(solution)/shard_map/ppermute | solution.py:463
  44.3 1.7 %collective-permute-done.20.far_below.far_above = f32[24,256]{1,0:T(8,128)S(1)} collective-permute-done((f32[24,256]{1,0:T(8,128)S(1)}, f32[24,256]{1,0:T(8,128)S(1)}, u32[]{:S(2)}, u32[]{:S(2)}) %collective-permute-start.20) | collective-permute-done | bytes 24608 | tf_op jit(solution)/shard_map/ppermute | solution.py:463
  46.0 1.0 %collective-permute-done.19.near_y = f32[24,256]{1,0:T(8,128)S(1)} collective-permute-done((f32[24,256]{1,0:T(8,128)S(1)}, f32[24,256]{1,0:T(8,128)S(1)}, u32[]{:S(2)}, u32[]{:S(2)}) %collective-permute-start.19) | collective-permute-done | bytes 24608 | tf_op jit(solution)/shard_map/ppermute | solution.py:464
  47.7 10.7 %all_to_all.5.gathered = f32[32,1,2,128]{3,2,1,0:T(2,128)S(1)} all-to-all(f32[32,1,2,128]{3,2,1,0:T(2,128)S(1)} %get-tuple-element.58), channel_id=1, replica_groups=mesh['grp'=4,'sub'=8] {'grp','sub'}, dimensions={0} | all-to-all | bytes 65536 | tf_op jit(solution)/shard_map/all_to_all | solution.py:479
  58.4 2.5 %shard_map.80 = (f32[1,16,128]{2,1,0:T(8,128)}, f32[4,8,512]{2,1,0:T(8,128)}, f32[2,4,256]{2,1,0:T(4,128)}) custom-call(f32[32,1,2,128]{3,2,1,0:T(2,128)S(1)} %all_to_all.5.gathered, f32[4,27,16,128]{3,2,1,0:T(8,128)S(1)} %shard_map.77.c, f32[4,8,512]{2,1,0:T(8,128)S(1)} %get-tuple-element.45.v.fine, f32[2,4,256]{2,1,0:T(4,128)S(1)} %get-tuple-element.59.middle), custom_call_target="tpu_custom_call" | custom-call | tf_op jit(solution)/shard_map/pallas_call | solution.py:24
  (45 shorter events, 6.6 us)
Async XLA Ops:
  0.6 22.8 %collective-permute-start.12 = (f32[27,1,16,128]{3,2,1,0:T(8,128)}, f32[27,1,16,128]{3,2,1,0:T(8,128)S(1)}, u32[]{:S(2)}, u32[]{:S(2)}) collective-permute-start(f32[27,1,16,128]{3,2,1,0:T(8,128)} %refs_0_.1), channel_id=1, source_target_pairs={{0,16},{8,24},{16,0},{24,8},{1,17},{9,25},{17,1},{25,9},{2,18},{10... | collective-permute-start | bytes 663560 | tf_op jit(solution)/shard_map/ppermute | solution.py:427
  4.6 4.7 %collective-permute-start.1 = (f32[16,512]{1,0:T(8,128)S(1)}, f32[16,512]{1,0:T(8,128)S(1)}, u32[]{:S(2)}, u32[]{:S(2)}) collective-permute-start(f32[16,512]{1,0:T(8,128)S(1)} %get-tuple-element.34), channel_id=1, source_target_pairs={{1,2},{2,1},{3,4},{4,3},{5,6},{6,5},{9,10},{10,9},{11,12},{12,11},... | collective-permute-start | bytes 98312 | tf_op jit(solution)/shard_map/ppermute | solution.py:394
  4.7 4.7 %collective-permute-start = (f32[4,512]{1,0:T(4,128)S(1)}, f32[4,512]{1,0:T(4,128)S(1)}, u32[]{:S(2)}, u32[]{:S(2)}) collective-permute-start(f32[4,512]{1,0:T(4,128)S(1)} %get-tuple-element.33), channel_id=1, source_target_pairs={{0,1},{1,0},{2,3},{3,2},{4,5},{5,4},{6,7},{7,6},{8,9},{9,8},{10,11... | collective-permute-start | bytes 24584 | tf_op jit(solution)/shard_map/ppermute | solution.py:393
  9.3 14.1 %collective-permute-start.13 = (f32[27,2,2,256]{3,2,1,0:T(2,128)S(1)}, f32[27,2,2,256]{3,2,1,0:T(2,128)S(1)}, u32[]{:S(2)}, u32[]{:S(2)}) collective-permute-start(f32[27,2,2,256]{3,2,1,0:T(2,128)S(1)} %get-tuple-element.51), channel_id=1, source_target_pairs={{0,1},{1,0},{2,3},{3,2},{4,5},{5,4},{6,7},{7,6},{8,9},{9,8},{10,11... | collective-permute-start | bytes 331784 | tf_op jit(solution)/shard_map/ppermute | solution.py:393
  11.3 12.1 %collective-permute-start.14 = (f32[27,2,2,256]{3,2,1,0:T(2,128)S(1)}, f32[27,2,2,256]{3,2,1,0:T(2,128)S(1)}, u32[]{:S(2)}, u32[]{:S(2)}) collective-permute-start(f32[27,2,2,256]{3,2,1,0:T(2,128)S(1)} %get-tuple-element.52), channel_id=1, source_target_pairs={{1,2},{2,1},{3,4},{4,3},{5,6},{6,5},{9,10},{10,9},{11,12},{12,11},... | collective-permute-start | bytes 331784 | tf_op jit(solution)/shard_map/ppermute | solution.py:394
  11.4 2.5 %collective-permute-start.2 = (f32[16,512]{1,0:T(8,128)S(1)}, f32[16,512]{1,0:T(8,128)S(1)}, u32[]{:S(2)}, u32[]{:S(2)}) collective-permute-start(f32[16,512]{1,0:T(8,128)S(1)} %get-tuple-element.38), channel_id=1, source_target_pairs={{0,8},{8,0},{16,24},{24,16},{1,9},{9,1},{17,25},{25,17},{2,10},{10... | collective-permute-start | bytes 98312 | tf_op jit(solution)/shard_map/ppermute | solution.py:398
  11.9 3.4 %collective-permute-start.3 = (f32[16,512]{1,0:T(8,128)S(1)}, f32[16,512]{1,0:T(8,128)S(1)}, u32[]{:S(2)}, u32[]{:S(2)}) collective-permute-start(f32[16,512]{1,0:T(8,128)S(1)} %get-tuple-element.39), channel_id=1, source_target_pairs={{8,16},{16,8},{24,0},{0,24},{9,17},{17,9},{25,1},{1,25},{10,18},{1... | collective-permute-start | bytes 98312 | tf_op jit(solution)/shard_map/ppermute | solution.py:399
  13.8 9.7 %copy-start.2 = (f32[27,2,4,256]{3,2,1,0:T(4,128)S(1)}, f32[27,2,4,256]{3,2,1,0:T(4,128)}, u32[]{:S(2)}) copy-start(f32[27,2,4,256]{3,2,1,0:T(4,128)} %refs_2_.1) | copy-start | bytes 663556
  13.8 9.7 %copy-start.3 = (f32[27,1,16,128]{3,2,1,0:T(8,128)S(1)}, f32[27,1,16,128]{3,2,1,0:T(8,128)}, u32[]{:S(2)}) copy-start(f32[27,1,16,128]{3,2,1,0:T(8,128)} %refs_0_.1) | copy-start | bytes 663556
  15.6 4.3 %collective-permute-start.5 = (f32[16,512]{1,0:T(8,128)S(1)}, f32[16,512]{1,0:T(8,128)S(1)}, u32[]{:S(2)}, u32[]{:S(2)}) collective-permute-start(f32[16,512]{1,0:T(8,128)S(1)} %get-tuple-element.42), channel_id=1, source_target_pairs={{1,2},{2,1},{3,4},{4,3},{5,6},{6,5},{9,10},{10,9},{11,12},{12,11},... | collective-permute-start | bytes 98312 | tf_op jit(solution)/shard_map/ppermute | solution.py:394
  15.8 4.1 %collective-permute-start.4 = (f32[4,512]{1,0:T(4,128)S(1)}, f32[4,512]{1,0:T(4,128)S(1)}, u32[]{:S(2)}, u32[]{:S(2)}) collective-permute-start(f32[4,512]{1,0:T(4,128)S(1)} %get-tuple-element.41), channel_id=1, source_target_pairs={{0,1},{1,0},{2,3},{3,2},{4,5},{5,4},{6,7},{7,6},{8,9},{9,8},{10,11... | collective-permute-start | bytes 24584 | tf_op jit(solution)/shard_map/ppermute | solution.py:393
  20.0 1.3 %collective-permute-start.6 = (f32[16,512]{1,0:T(8,128)S(1)}, f32[16,512]{1,0:T(8,128)S(1)}, u32[]{:S(2)}, u32[]{:S(2)}) collective-permute-start(f32[16,512]{1,0:T(8,128)S(1)} %get-tuple-element.43), channel_id=1, source_target_pairs={{0,8},{8,0},{16,24},{24,16},{1,9},{9,1},{17,25},{25,17},{2,10},{10... | collective-permute-start | bytes 98312 | tf_op jit(solution)/shard_map/ppermute | solution.py:398
  20.0 3.4 %collective-permute-start.7 = (f32[16,512]{1,0:T(8,128)S(1)}, f32[16,512]{1,0:T(8,128)S(1)}, u32[]{:S(2)}, u32[]{:S(2)}) collective-permute-start(f32[16,512]{1,0:T(8,128)S(1)} %get-tuple-element.44), channel_id=1, source_target_pairs={{8,16},{16,8},{24,0},{0,24},{9,17},{17,9},{25,1},{1,25},{10,18},{1... | collective-permute-start | bytes 98312 | tf_op jit(solution)/shard_map/ppermute | solution.py:399
  23.8 16.7 %collective-permute-start.15 = (f32[27,64,128]{2,1,0:T(8,128)S(1)}, f32[27,64,128]{2,1,0:T(8,128)S(1)}, u32[]{:S(2)}, u32[]{:S(2)}) collective-permute-start(f32[27,64,128]{2,1,0:T(8,128)S(1)} %get-tuple-element.53.own), channel_id=1, source_target_pairs={{0,8},{8,0},{16,24},{24,16},{1,9},{9,1},{17,25},{25,17},{2,10},{10... | collective-permute-start | bytes 2654216 | tf_op jit(solution)/shard_map/ppermute | solution.py:438
  24.3 20.0 %collective-permute-start.21 = (f32[27,32,128]{2,1,0:T(8,128)S(1)}, f32[27,32,128]{2,1,0:T(8,128)S(1)}, u32[]{:S(2)}, u32[]{:S(2)}) collective-permute-start(f32[27,32,128]{2,1,0:T(8,128)S(1)} %get-tuple-element.57), channel_id=1, source_target_pairs={{8,16},{16,8},{9,17},{17,9},{10,18},{18,10},{11,19},{19,11},{12,20... | collective-permute-start | bytes 1327112 | tf_op jit(solution)/shard_map/ppermute | solution.py:439
  25.3 6.6 %collective-permute-start.9 = (f32[16,512]{1,0:T(8,128)S(1)}, f32[16,512]{1,0:T(8,128)S(1)}, u32[]{:S(2)}, u32[]{:S(2)}) collective-permute-start(f32[16,512]{1,0:T(8,128)S(1)} %get-tuple-element.47), channel_id=1, source_target_pairs={{1,2},{2,1},{3,4},{4,3},{5,6},{6,5},{9,10},{10,9},{11,12},{12,11},... | collective-permute-start | bytes 98312 | tf_op jit(solution)/shard_map/ppermute | solution.py:394
  27.2 4.7 %collective-permute-start.8 = (f32[4,512]{1,0:T(4,128)S(1)}, f32[4,512]{1,0:T(4,128)S(1)}, u32[]{:S(2)}, u32[]{:S(2)}) collective-permute-start(f32[4,512]{1,0:T(4,128)S(1)} %get-tuple-element.46), channel_id=1, source_target_pairs={{0,1},{1,0},{2,3},{3,2},{4,5},{5,4},{6,7},{7,6},{8,9},{9,8},{10,11... | collective-permute-start | bytes 24584 | tf_op jit(solution)/shard_map/ppermute | solution.py:393
  31.9 3.1 %collective-permute-start.10 = (f32[16,512]{1,0:T(8,128)S(1)}, f32[16,512]{1,0:T(8,128)S(1)}, u32[]{:S(2)}, u32[]{:S(2)}) collective-permute-start(f32[16,512]{1,0:T(8,128)S(1)} %get-tuple-element.48), channel_id=1, source_target_pairs={{0,8},{8,0},{16,24},{24,16},{1,9},{9,1},{17,25},{25,17},{2,10},{10... | collective-permute-start | bytes 98312 | tf_op jit(solution)/shard_map/ppermute | solution.py:398
  32.6 4.0 %collective-permute-start.11 = (f32[16,512]{1,0:T(8,128)S(1)}, f32[16,512]{1,0:T(8,128)S(1)}, u32[]{:S(2)}, u32[]{:S(2)}) collective-permute-start(f32[16,512]{1,0:T(8,128)S(1)} %get-tuple-element.49), channel_id=1, source_target_pairs={{8,16},{16,8},{24,0},{0,24},{9,17},{17,9},{25,1},{1,25},{10,18},{1... | collective-permute-start | bytes 98312 | tf_op jit(solution)/shard_map/ppermute | solution.py:399
  37.1 5.0 %collective-permute-start.17 = (f32[16,256]{1,0:T(8,128)S(1)}, f32[16,256]{1,0:T(8,128)S(1)}, u32[]{:S(2)}, u32[]{:S(2)}) collective-permute-start(f32[16,256]{1,0:T(8,128)S(1)} %get-tuple-element.56), channel_id=1, source_target_pairs={{1,2},{2,1},{3,4},{4,3},{5,6},{6,5},{9,10},{10,9},{11,12},{12,11},... | collective-permute-start | bytes 49160 | tf_op jit(solution)/shard_map/ppermute | solution.py:394
  37.3 4.8 %collective-permute-start.16 = (f32[8,256]{1,0:T(8,128)S(1)}, f32[8,256]{1,0:T(8,128)S(1)}, u32[]{:S(2)}, u32[]{:S(2)}) collective-permute-start(f32[8,256]{1,0:T(8,128)S(1)} %get-tuple-element.55), channel_id=1, source_target_pairs={{0,1},{1,0},{2,3},{3,2},{4,5},{5,4},{6,7},{7,6},{8,9},{9,8},{10,11... | collective-permute-start | bytes 24584 | tf_op jit(solution)/shard_map/ppermute | solution.py:393
  42.1 3.9 %collective-permute-start.20 = (f32[24,256]{1,0:T(8,128)S(1)}, f32[24,256]{1,0:T(8,128)S(1)}, u32[]{:S(2)}, u32[]{:S(2)}) collective-permute-start(f32[24,256]{1,0:T(8,128)S(1)} %shard_map.78.packed), channel_id=1, source_target_pairs={{0,16},{16,0},{8,24},{24,8},{1,17},{17,1},{9,25},{25,9},{2,18},{18... | collective-permute-start | bytes 73736 | tf_op jit(solution)/shard_map/ppermute | solution.py:463
  43.8 3.3 %collective-permute-start.19 = (f32[24,256]{1,0:T(8,128)S(1)}, f32[24,256]{1,0:T(8,128)S(1)}, u32[]{:S(2)}, u32[]{:S(2)}) collective-permute-start(f32[24,256]{1,0:T(8,128)S(1)} %shard_map.78.packed), channel_id=1, source_target_pairs={{8,16},{16,8},{24,0},{0,24},{9,17},{17,9},{25,1},{1,25},{10,18},{1... | collective-permute-start | bytes 73736 | tf_op jit(solution)/shard_map/ppermute | solution.py:464
  43.8 3.3 %collective-permute-start.18 = (f32[24,256]{1,0:T(8,128)S(1)}, f32[24,256]{1,0:T(8,128)S(1)}, u32[]{:S(2)}, u32[]{:S(2)}) collective-permute-start(f32[24,256]{1,0:T(8,128)S(1)} %shard_map.78.packed), channel_id=1, source_target_pairs={{0,8},{8,0},{16,24},{24,16},{1,9},{9,1},{17,25},{25,17},{2,10},{10... | collective-permute-start | bytes 73736 | tf_op jit(solution)/shard_map/ppermute | solution.py:461
  (2 other events, 2.4 us)

commit v7 on v5

--- a/solution.py
+++ b/solution.py
@@ -140,8 +140,8 @@
     planes, rows, _ = v.shape
     group = lax.axis_index("grp")
     before, after = sides(from_x[...], from_zx[0:planes, :])
-    low = pick(even("grp"), from_y[...], from_core[...])
-    high = pick(even("grp"), from_core[...], from_y[...])
+    low = pick(even("grp"), from_y[0 : rows + 8, :], from_core[...])
+    high = pick(even("grp"), from_core[...], from_y[0 : rows + 8, :])
     low = pick(group == 0, jnp.zeros_like(low), low)
     high = pick(group == groups - 1, jnp.zeros_like(high), high)
     faces = [neighbours(f[0:rows], f[rows : rows + 1], f[rows + 1 : rows + 2]) for f in (low, high)]
@@ -352,7 +352,7 @@
             fresh.append(first[p] + (1.0 - WEIGHT) * field[p] - sums)
         return tuple(fresh)
 
-    field = lax.fori_loop(0, NB - 1, sweep, tuple(first[p] for p in range(total)))
+    field = lax.fori_loop(0, NB - 1, sweep, tuple(first[p] for p in range(total)), unroll=5)
     for p in range(total):
         first[p] = field[p]
     for x in range(planes):
@@ -394,7 +394,7 @@
         return from_x, lax.ppermute(to_zx, ("grp", "sub"), zx_pairs)
 
     def along_grp(v, halo):
-        to_core, to_y = call(faces_kernel, [shape(rows + 8, extent)] * 2, [v, *halo])
+        to_core, to_y = call(faces_kernel, [shape(rows + 8, extent), shape(2 * rows + 8, extent)], [v, *halo])
         from_core = lax.ppermute(to_core, "grp", core_pairs)
         from_y = lax.ppermute(to_y, "grp", y_ring)
         return (*halo, from_core, from_y)
@@ -402,12 +402,12 @@
     weights = call(coefficient_scale_kernel, shape(*fine.shape), [fine])
     v = WEIGHT * source / fine[CENTER]
     first = v
-    to_x, to_zx = call(edges_kernel, [shape(planes, extent), shape(4 * planes, extent)], [v])
+    to_x, to_zx = call(edges_kernel, [shape(planes, extent), shape(2 * planes, extent)], [v])
 
     def sweep(v, halo):
         v, *edges = call(
             functools.partial(sweep_kernel, groups),
-            [shape(planes, rows, extent), shape(planes, extent), shape(4 * planes, extent)],
+            [shape(planes, rows, extent), shape(planes, extent), shape(2 * planes, extent)],
             [v, first, weights, *halo],
         )
         return v, along_sub(edges)
@@ -420,7 +420,7 @@
     halo = along_sub((to_x, to_zx))
     halo_c = along_sub(after_all(edges_c, *halo))
     halo = along_grp(after(v, weights, *edges_c), halo)
-    known = {0: after(coarse, *halo[2:])}
+    known = {0: after(coarse, first)}
     bit = groups // 2
     while bit > 1:
         for offset in sorted(known):

time: 61.9 us -> 59.7 us (0.964)
  starting transfers between devices: 27.9 us -> 25.5 us
    ppermute x5, starting transfers between devices: 14.3 us -> 11.9 us  [along_sub(): from_x = lax.ppermute(to_x, 'sub', x_pairs)]
    ppermute x3, starting transfers between devices: 4.61 us -> 2.5 us  [along_grp(): from_y = lax.ppermute(to_y, 'grp', y_ring)]
    ppermute x1, starting transfers between devices: 1.52 us -> 3.03 us  [body(): lax.ppermute(known[offset], 'grp', [(i, i ^ bit) for i in range(groups)])]
    ppermute x3, waiting for transfers between devices: 0.58 us -> 1.82 us  [along_grp(): from_core = lax.ppermute(to_core, 'grp', core_pairs)]
    ppermute x3, starting transfers between devices: 0.9 us -> 2.09 us  [along_grp(): from_core = lax.ppermute(to_core, 'grp', core_pairs)]
    ppermute x3, waiting for transfers between devices: 5.64 us -> 4.47 us  [along_grp(): from_y = lax.ppermute(to_y, 'grp', y_ring)]
  transfers between devices with their start and end apart: 22 -> 22, of which waited for: 9 -> 10; matrix products, arithmetic and copies ran while one was open for 0% -> 0% of each run, Pallas kernels for 2% -> 3%
where the time goes in v7:
time: 59.7 us; the launch traced here: 59.5 us
  starting transfers between devices  25.5 us (43%)
  waiting for transfers between devices  14.1 us (24%)
  blocking collectives  11.4 us (19%)
  Pallas kernels  4.65 us (8%)
  local copies, waits for them, and re-layouts  2.21 us (4%)
  other arithmetic  0.89 us (1%)
  between operations  0.77 us (1%)
    ppermute x5, starting transfers between devices, along_sub(): from_x = lax.ppermute(to_x, 'sub', x_pairs)  11.9 us
    all_to_all x1, blocking collectives, body(): gathered = lax.all_to_all(coarse_source, ('grp', 'sub'), 0, 0, tiled=True)  11.4 us
    ppermute x5, waiting for transfers between devices, along_sub(): from_x = lax.ppermute(to_x, 'sub', x_pairs)  5.18 us
    pallas_call x14, Pallas kernels, call(): pl.pallas_call(kernel, out_shape=outs, in_specs=[vmem] * len(args), out_s...  4.65 us
    ppermute x3, waiting for transfers between devices, along_grp(): from_y = lax.ppermute(to_y, 'grp', y_ring)  4.47 us
    ppermute x5, starting transfers between devices, along_sub(): return (from_x, lax.ppermute(to_zx, ('grp', 'sub'), zx_pairs))  3.05 us
    ppermute x1, starting transfers between devices, body(): lax.ppermute(known[offset], 'grp', [(i, i ^ bit) for i in range(groups)])  3.03 us
    ppermute x3, starting transfers between devices, along_grp(): from_y = lax.ppermute(to_y, 'grp', y_ring)  2.5 us
  transfers between devices with their start and end apart: 22, of which 10 were waited for; matrix products, arithmetic and copies ran while one was open for 0% of the time, Pallas kernels for 3%

profile of v7, /device:TPU:0, one launch (start us, length us, event | category | flops | bytes accessed | tf_op | source)
XLA Modules:
  0.0 59.5 jit_solution(11745544813928482895)
XLA Ops:
  0.6 0.9 %bitcast_divide_fusion.v.first = f32[4,8,512]{2,1,0:T(8,128)S(1)} fusion(f32[27,4,8,512]{3,2,1,0:T(8,128)} %c.2, f32[4,8,512]{2,1,0:T(8,128)} %param.4), kind=kLoop, calls=%fused_computation | loop fusion | flops 32768 | bytes 196608 | tf_op jit(solution)/shard_map/div | solution.py:403
  1.5 3.0 %collective-permute-start.12 = (f32[27,1,16,128]{3,2,1,0:T(8,128)}, f32[27,1,16,128]{3,2,1,0:T(8,128)S(1)}, u32[]{:S(2)}, u32[]{:S(2)}) collective-permute-start(f32[27,1,16,128]{3,2,1,0:T(8,128)} %refs_0_), channel_id=1, source_target_pairs={{0,16},{8,24},{16,0},{24,8},{1,17},{9,25},{17,1},{25,9},{2,18},{10... | collective-permute-start | bytes 663560 | tf_op jit(solution)/shard_map/ppermute | solution.py:427
  4.6 3.0 %collective-permute-start = (f32[4,512]{1,0:T(4,128)S(1)}, f32[4,512]{1,0:T(4,128)S(1)}, u32[]{:S(2)}, u32[]{:S(2)}) collective-permute-start(f32[4,512]{1,0:T(4,128)S(1)} %get-tuple-element.34), channel_id=1, source_target_pairs={{0,1},{1,0},{2,3},{3,2},{4,5},{5,4},{6,7},{7,6},{8,9},{9,8},{10,11... | collective-permute-start | bytes 24584 | tf_op jit(solution)/shard_map/ppermute | solution.py:393
  7.7 1.5 %copy-done = f32[27,4,8,512]{3,2,1,0:T(8,128)S(1)} copy-done((f32[27,4,8,512]{3,2,1,0:T(8,128)S(1)}, f32[27,4,8,512]{3,2,1,0:T(8,128)}, u32[]{:S(2)}) %copy-start) | copy-done | bytes 1769496
  10.3 1.2 %collective-permute-start.13 = (f32[27,2,2,256]{3,2,1,0:T(2,128)S(1)}, f32[27,2,2,256]{3,2,1,0:T(2,128)S(1)}, u32[]{:S(2)}, u32[]{:S(2)}) collective-permute-start(f32[27,2,2,256]{3,2,1,0:T(2,128)S(1)} %get-tuple-element.53), channel_id=1, source_target_pairs={{0,1},{1,0},{2,3},{3,2},{4,5},{5,4},{6,7},{7,6},{8,9},{9,8},{10,11... | collective-permute-start | bytes 331784 | tf_op jit(solution)/shard_map/ppermute | solution.py:393
  12.0 1.0 %collective-permute-done.2.from_core = f32[16,512]{1,0:T(8,128)S(1)} collective-permute-done((f32[16,512]{1,0:T(8,128)S(1)}, f32[16,512]{1,0:T(8,128)S(1)}, u32[]{:S(2)}, u32[]{:S(2)}) %collective-permute-start.2) | collective-permute-done | bytes 32800 | tf_op jit(solution)/shard_map/ppermute | solution.py:398
  13.0 0.8 %collective-permute-done.3.from_y = f32[24,512]{1,0:T(8,128)S(1)} collective-permute-done((f32[24,512]{1,0:T(8,128)S(1)}, f32[24,512]{1,0:T(8,128)S(1)}, u32[]{:S(2)}, u32[]{:S(2)}) %collective-permute-start.3) | collective-permute-done | bytes 49184 | tf_op jit(solution)/shard_map/ppermute | solution.py:399
  14.2 3.0 %collective-permute-start.4 = (f32[4,512]{1,0:T(4,128)S(1)}, f32[4,512]{1,0:T(4,128)S(1)}, u32[]{:S(2)}, u32[]{:S(2)}) collective-permute-start(f32[4,512]{1,0:T(4,128)S(1)} %get-tuple-element.42), channel_id=1, source_target_pairs={{0,1},{1,0},{2,3},{3,2},{4,5},{5,4},{6,7},{7,6},{8,9},{9,8},{10,11... | collective-permute-start | bytes 24584 | tf_op jit(solution)/shard_map/ppermute | solution.py:393
  17.2 1.6 %collective-permute-done.4.from_x = f32[4,512]{1,0:T(4,128)S(1)} collective-permute-done((f32[4,512]{1,0:T(4,128)S(1)}, f32[4,512]{1,0:T(4,128)S(1)}, u32[]{:S(2)}, u32[]{:S(2)}) %collective-permute-start.4) | collective-permute-done | bytes 8224 | tf_op jit(solution)/shard_map/ppermute | solution.py:393
  18.9 1.1 %collective-permute-start.6 = (f32[16,512]{1,0:T(8,128)S(1)}, f32[16,512]{1,0:T(8,128)S(1)}, u32[]{:S(2)}, u32[]{:S(2)}) collective-permute-start(f32[16,512]{1,0:T(8,128)S(1)} %get-tuple-element.44), channel_id=1, source_target_pairs={{0,8},{8,0},{16,24},{24,16},{1,9},{9,1},{17,25},{25,17},{2,10},{10... | collective-permute-start | bytes 98312 | tf_op jit(solution)/shard_map/ppermute | solution.py:398
  20.0 0.9 %collective-permute-done.6.from_core.refs_5_ = f32[16,512]{1,0:T(8,128)S(1)} collective-permute-done((f32[16,512]{1,0:T(8,128)S(1)}, f32[16,512]{1,0:T(8,128)S(1)}, u32[]{:S(2)}, u32[]{:S(2)}) %collective-permute-start.6) | collective-permute-done | bytes 32800 | tf_op jit(solution)/shard_map/ppermute | solution.py:398
  20.8 1.6 %collective-permute-done.7.from_y.refs_6_ = f32[24,512]{1,0:T(8,128)S(1)} collective-permute-done((f32[24,512]{1,0:T(8,128)S(1)}, f32[24,512]{1,0:T(8,128)S(1)}, u32[]{:S(2)}, u32[]{:S(2)}) %collective-permute-start.7) | collective-permute-done | bytes 49184 | tf_op jit(solution)/shard_map/ppermute | solution.py:399
  23.8 2.5 %collective-permute-start.9 = (f32[8,512]{1,0:T(8,128)S(1)}, f32[8,512]{1,0:T(8,128)S(1)}, u32[]{:S(2)}, u32[]{:S(2)}) collective-permute-start(f32[8,512]{1,0:T(8,128)S(1)} %get-tuple-element.48), channel_id=1, source_target_pairs={{1,2},{2,1},{3,4},{4,3},{5,6},{6,5},{9,10},{10,9},{11,12},{12,11},... | collective-permute-start | bytes 49160 | tf_op jit(solution)/shard_map/ppermute | solution.py:394
  26.3 1.6 %collective-permute-start.8 = (f32[4,512]{1,0:T(4,128)S(1)}, f32[4,512]{1,0:T(4,128)S(1)}, u32[]{:S(2)}, u32[]{:S(2)}) collective-permute-start(f32[4,512]{1,0:T(4,128)S(1)} %get-tuple-element.47), channel_id=1, source_target_pairs={{0,1},{1,0},{2,3},{3,2},{4,5},{5,4},{6,7},{7,6},{8,9},{9,8},{10,11... | collective-permute-start | bytes 24584 | tf_op jit(solution)/shard_map/ppermute | solution.py:393
  27.9 2.0 %collective-permute-done.8.from_x = f32[4,512]{1,0:T(4,128)S(1)} collective-permute-done((f32[4,512]{1,0:T(4,128)S(1)}, f32[4,512]{1,0:T(4,128)S(1)}, u32[]{:S(2)}, u32[]{:S(2)}) %collective-permute-start.8) | collective-permute-done | bytes 8224 | tf_op jit(solution)/shard_map/ppermute | solution.py:393
  30.8 2.4 %collective-permute-start.11 = (f32[24,512]{1,0:T(8,128)S(1)}, f32[24,512]{1,0:T(8,128)S(1)}, u32[]{:S(2)}, u32[]{:S(2)}) collective-permute-start(f32[24,512]{1,0:T(8,128)S(1)} %get-tuple-element.50), channel_id=1, source_target_pairs={{8,16},{16,8},{24,0},{0,24},{9,17},{17,9},{25,1},{1,25},{10,18},{1... | collective-permute-start | bytes 147464 | tf_op jit(solution)/shard_map/ppermute | solution.py:399
  33.1 2.0 %collective-permute-done.11.from_y = f32[24,512]{1,0:T(8,128)S(1)} collective-permute-done((f32[24,512]{1,0:T(8,128)S(1)}, f32[24,512]{1,0:T(8,128)S(1)}, u32[]{:S(2)}, u32[]{:S(2)}) %collective-permute-start.11) | collective-permute-done | bytes 49184 | tf_op jit(solution)/shard_map/ppermute | solution.py:399
  35.8 3.0 %collective-permute-start.16 = (f32[8,256]{1,0:T(8,128)S(1)}, f32[8,256]{1,0:T(8,128)S(1)}, u32[]{:S(2)}, u32[]{:S(2)}) collective-permute-start(f32[8,256]{1,0:T(8,128)S(1)} %get-tuple-element.57), channel_id=1, source_target_pairs={{0,1},{1,0},{2,3},{3,2},{4,5},{5,4},{6,7},{7,6},{8,9},{9,8},{10,11... | collective-permute-start | bytes 24584 | tf_op jit(solution)/shard_map/ppermute | solution.py:393
  38.9 1.5 %collective-permute-done.16.from_x = f32[8,256]{1,0:T(8,128)S(1)} collective-permute-done((f32[8,256]{1,0:T(8,128)S(1)}, f32[8,256]{1,0:T(8,128)S(1)}, u32[]{:S(2)}, u32[]{:S(2)}) %collective-permute-start.16) | collective-permute-done | bytes 8224 | tf_op jit(solution)/shard_map/ppermute | solution.py:393
  40.5 1.5 %collective-permute-start.20 = (f32[24,256]{1,0:T(8,128)S(1)}, f32[24,256]{1,0:T(8,128)S(1)}, u32[]{:S(2)}, u32[]{:S(2)}) collective-permute-start(f32[24,256]{1,0:T(8,128)S(1)} %shard_map.78.packed), channel_id=1, source_target_pairs={{0,16},{16,0},{8,24},{24,8},{1,17},{17,1},{9,25},{25,9},{2,18},{18... | collective-permute-start | bytes 73736 | tf_op jit(solution)/shard_map/ppermute | solution.py:463
  42.7 1.7 %collective-permute-done.20.far_below.far_above = f32[24,256]{1,0:T(8,128)S(1)} collective-permute-done((f32[24,256]{1,0:T(8,128)S(1)}, f32[24,256]{1,0:T(8,128)S(1)}, u32[]{:S(2)}, u32[]{:S(2)}) %collective-permute-start.20) | collective-permute-done | bytes 24608 | tf_op jit(solution)/shard_map/ppermute | solution.py:463
  44.4 0.9 %collective-permute-done.19.near_y = f32[24,256]{1,0:T(8,128)S(1)} collective-permute-done((f32[24,256]{1,0:T(8,128)S(1)}, f32[24,256]{1,0:T(8,128)S(1)}, u32[]{:S(2)}, u32[]{:S(2)}) %collective-permute-start.19) | collective-permute-done | bytes 24608 | tf_op jit(solution)/shard_map/ppermute | solution.py:464
  45.9 11.4 %all_to_all.5.gathered = f32[32,1,2,128]{3,2,1,0:T(2,128)S(1)} all-to-all(f32[32,1,2,128]{3,2,1,0:T(2,128)S(1)} %get-tuple-element.60), channel_id=1, replica_groups=mesh['grp'=4,'sub'=8] {'grp','sub'}, dimensions={0} | all-to-all | bytes 65536 | tf_op jit(solution)/shard_map/all_to_all | solution.py:479
  57.3 2.2 %shard_map.80 = (f32[1,16,128]{2,1,0:T(8,128)}, f32[4,8,512]{2,1,0:T(8,128)}, f32[2,4,256]{2,1,0:T(4,128)}) custom-call(f32[32,1,2,128]{3,2,1,0:T(2,128)S(1)} %all_to_all.5.gathered, f32[4,27,16,128]{3,2,1,0:T(8,128)S(1)} %shard_map.77.c, f32[4,8,512]{2,1,0:T(8,128)S(1)} %get-tuple-element.46.v.fine, f32[2,4,256]{2,1,0:T(4,128)S(1)} %get-tuple-element.61.middle), custom_call_target="tpu_custom_call" | custom-call | tf_op jit(solution)/shard_map/pallas_call | solution.py:24
  (43 shorter events, 6.4 us)
Async XLA Ops:
  1.5 20.9 %collective-permute-start.12 = (f32[27,1,16,128]{3,2,1,0:T(8,128)}, f32[27,1,16,128]{3,2,1,0:T(8,128)S(1)}, u32[]{:S(2)}, u32[]{:S(2)}) collective-permute-start(f32[27,1,16,128]{3,2,1,0:T(8,128)} %refs_0_), channel_id=1, source_target_pairs={{0,16},{8,24},{16,0},{24,8},{1,17},{9,25},{17,1},{25,9},{2,18},{10... | collective-permute-start | bytes 663560 | tf_op jit(solution)/shard_map/ppermute | solution.py:427
  4.6 5.6 %collective-permute-start.1 = (f32[8,512]{1,0:T(8,128)S(1)}, f32[8,512]{1,0:T(8,128)S(1)}, u32[]{:S(2)}, u32[]{:S(2)}) collective-permute-start(f32[8,512]{1,0:T(8,128)S(1)} %get-tuple-element.35), channel_id=1, source_target_pairs={{1,2},{2,1},{3,4},{4,3},{5,6},{6,5},{9,10},{10,9},{11,12},{12,11},... | collective-permute-start | bytes 49160 | tf_op jit(solution)/shard_map/ppermute | solution.py:394
  4.6 5.5 %collective-permute-start = (f32[4,512]{1,0:T(4,128)S(1)}, f32[4,512]{1,0:T(4,128)S(1)}, u32[]{:S(2)}, u32[]{:S(2)}) collective-permute-start(f32[4,512]{1,0:T(4,128)S(1)} %get-tuple-element.34), channel_id=1, source_target_pairs={{0,1},{1,0},{2,3},{3,2},{4,5},{5,4},{6,7},{7,6},{8,9},{9,8},{10,11... | collective-permute-start | bytes 24584 | tf_op jit(solution)/shard_map/ppermute | solution.py:393
  7.7 1.5 %copy-start = (f32[27,4,8,512]{3,2,1,0:T(8,128)S(1)}, f32[27,4,8,512]{3,2,1,0:T(8,128)}, u32[]{:S(2)}) copy-start(f32[27,4,8,512]{3,2,1,0:T(8,128)} %c.2) | copy-start | bytes 5308420
  10.1 12.4 %copy-start.2 = (f32[27,1,16,128]{3,2,1,0:T(8,128)S(1)}, f32[27,1,16,128]{3,2,1,0:T(8,128)}, u32[]{:S(2)}) copy-start(f32[27,1,16,128]{3,2,1,0:T(8,128)} %refs_0_) | copy-start | bytes 663556
  10.2 3.6 %collective-permute-start.3 = (f32[24,512]{1,0:T(8,128)S(1)}, f32[24,512]{1,0:T(8,128)S(1)}, u32[]{:S(2)}, u32[]{:S(2)}) collective-permute-start(f32[24,512]{1,0:T(8,128)S(1)} %get-tuple-element.40), channel_id=1, source_target_pairs={{8,16},{16,8},{24,0},{0,24},{9,17},{17,9},{25,1},{1,25},{10,18},{1... | collective-permute-start | bytes 147464 | tf_op jit(solution)/shard_map/ppermute | solution.py:399
  10.3 10.5 %collective-permute-start.13 = (f32[27,2,2,256]{3,2,1,0:T(2,128)S(1)}, f32[27,2,2,256]{3,2,1,0:T(2,128)S(1)}, u32[]{:S(2)}, u32[]{:S(2)}) collective-permute-start(f32[27,2,2,256]{3,2,1,0:T(2,128)S(1)} %get-tuple-element.53), channel_id=1, source_target_pairs={{0,1},{1,0},{2,3},{3,2},{4,5},{5,4},{6,7},{7,6},{8,9},{9,8},{10,11... | collective-permute-start | bytes 331784 | tf_op jit(solution)/shard_map/ppermute | solution.py:393
  11.5 9.4 %collective-permute-start.14 = (f32[27,2,2,256]{3,2,1,0:T(2,128)S(1)}, f32[27,2,2,256]{3,2,1,0:T(2,128)S(1)}, u32[]{:S(2)}, u32[]{:S(2)}) collective-permute-start(f32[27,2,2,256]{3,2,1,0:T(2,128)S(1)} %get-tuple-element.54), channel_id=1, source_target_pairs={{1,2},{2,1},{3,4},{4,3},{5,6},{6,5},{9,10},{10,9},{11,12},{12,11},... | collective-permute-start | bytes 331784 | tf_op jit(solution)/shard_map/ppermute | solution.py:394
  11.7 1.2 %collective-permute-start.2 = (f32[16,512]{1,0:T(8,128)S(1)}, f32[16,512]{1,0:T(8,128)S(1)}, u32[]{:S(2)}, u32[]{:S(2)}) collective-permute-start(f32[16,512]{1,0:T(8,128)S(1)} %get-tuple-element.39), channel_id=1, source_target_pairs={{0,8},{8,0},{16,24},{24,16},{1,9},{9,1},{17,25},{25,17},{2,10},{10... | collective-permute-start | bytes 98312 | tf_op jit(solution)/shard_map/ppermute | solution.py:398
  14.1 4.7 %collective-permute-start.5 = (f32[8,512]{1,0:T(8,128)S(1)}, f32[8,512]{1,0:T(8,128)S(1)}, u32[]{:S(2)}, u32[]{:S(2)}) collective-permute-start(f32[8,512]{1,0:T(8,128)S(1)} %get-tuple-element.43), channel_id=1, source_target_pairs={{1,2},{2,1},{3,4},{4,3},{5,6},{6,5},{9,10},{10,9},{11,12},{12,11},... | collective-permute-start | bytes 49160 | tf_op jit(solution)/shard_map/ppermute | solution.py:394
  14.2 4.7 %collective-permute-start.4 = (f32[4,512]{1,0:T(4,128)S(1)}, f32[4,512]{1,0:T(4,128)S(1)}, u32[]{:S(2)}, u32[]{:S(2)}) collective-permute-start(f32[4,512]{1,0:T(4,128)S(1)} %get-tuple-element.42), channel_id=1, source_target_pairs={{0,1},{1,0},{2,3},{3,2},{4,5},{5,4},{6,7},{7,6},{8,9},{9,8},{10,11... | collective-permute-start | bytes 24584 | tf_op jit(solution)/shard_map/ppermute | solution.py:393
  18.8 3.6 %collective-permute-start.7 = (f32[24,512]{1,0:T(8,128)S(1)}, f32[24,512]{1,0:T(8,128)S(1)}, u32[]{:S(2)}, u32[]{:S(2)}) collective-permute-start(f32[24,512]{1,0:T(8,128)S(1)} %get-tuple-element.45), channel_id=1, source_target_pairs={{8,16},{16,8},{24,0},{0,24},{9,17},{17,9},{25,1},{1,25},{10,18},{1... | collective-permute-start | bytes 147464 | tf_op jit(solution)/shard_map/ppermute | solution.py:399
  18.9 1.9 %collective-permute-start.6 = (f32[16,512]{1,0:T(8,128)S(1)}, f32[16,512]{1,0:T(8,128)S(1)}, u32[]{:S(2)}, u32[]{:S(2)}) collective-permute-start(f32[16,512]{1,0:T(8,128)S(1)} %get-tuple-element.44), channel_id=1, source_target_pairs={{0,8},{8,0},{16,24},{24,16},{1,9},{9,1},{17,25},{25,17},{2,10},{10... | collective-permute-start | bytes 98312 | tf_op jit(solution)/shard_map/ppermute | solution.py:398
  22.8 16.1 %collective-permute-start.15 = (f32[27,64,128]{2,1,0:T(8,128)S(1)}, f32[27,64,128]{2,1,0:T(8,128)S(1)}, u32[]{:S(2)}, u32[]{:S(2)}) collective-permute-start(f32[27,64,128]{2,1,0:T(8,128)S(1)} %get-tuple-element.55.own), channel_id=1, source_target_pairs={{0,8},{8,0},{16,24},{24,16},{1,9},{9,1},{17,25},{25,17},{2,10},{10... | collective-permute-start | bytes 2654216 | tf_op jit(solution)/shard_map/ppermute | solution.py:438
  22.8 19.8 %collective-permute-start.21 = (f32[27,32,128]{2,1,0:T(8,128)S(1)}, f32[27,32,128]{2,1,0:T(8,128)S(1)}, u32[]{:S(2)}, u32[]{:S(2)}) collective-permute-start(f32[27,32,128]{2,1,0:T(8,128)S(1)} %get-tuple-element.59), channel_id=1, source_target_pairs={{8,16},{16,8},{9,17},{17,9},{10,18},{18,10},{11,19},{19,11},{12,20... | collective-permute-start | bytes 1327112 | tf_op jit(solution)/shard_map/ppermute | solution.py:439
  23.8 6.1 %collective-permute-start.9 = (f32[8,512]{1,0:T(8,128)S(1)}, f32[8,512]{1,0:T(8,128)S(1)}, u32[]{:S(2)}, u32[]{:S(2)}) collective-permute-start(f32[8,512]{1,0:T(8,128)S(1)} %get-tuple-element.48), channel_id=1, source_target_pairs={{1,2},{2,1},{3,4},{4,3},{5,6},{6,5},{9,10},{10,9},{11,12},{12,11},... | collective-permute-start | bytes 49160 | tf_op jit(solution)/shard_map/ppermute | solution.py:394
  26.3 3.7 %collective-permute-start.8 = (f32[4,512]{1,0:T(4,128)S(1)}, f32[4,512]{1,0:T(4,128)S(1)}, u32[]{:S(2)}, u32[]{:S(2)}) collective-permute-start(f32[4,512]{1,0:T(4,128)S(1)} %get-tuple-element.47), channel_id=1, source_target_pairs={{0,1},{1,0},{2,3},{3,2},{4,5},{5,4},{6,7},{7,6},{8,9},{9,8},{10,11... | collective-permute-start | bytes 24584 | tf_op jit(solution)/shard_map/ppermute | solution.py:393
  30.0 3.2 %collective-permute-start.10 = (f32[16,512]{1,0:T(8,128)S(1)}, f32[16,512]{1,0:T(8,128)S(1)}, u32[]{:S(2)}, u32[]{:S(2)}) collective-permute-start(f32[16,512]{1,0:T(8,128)S(1)} %get-tuple-element.49), channel_id=1, source_target_pairs={{0,8},{8,0},{16,24},{24,16},{1,9},{9,1},{17,25},{25,17},{2,10},{10... | collective-permute-start | bytes 98312 | tf_op jit(solution)/shard_map/ppermute | solution.py:398
  30.8 4.4 %collective-permute-start.11 = (f32[24,512]{1,0:T(8,128)S(1)}, f32[24,512]{1,0:T(8,128)S(1)}, u32[]{:S(2)}, u32[]{:S(2)}) collective-permute-start(f32[24,512]{1,0:T(8,128)S(1)} %get-tuple-element.50), channel_id=1, source_target_pairs={{8,16},{16,8},{24,0},{0,24},{9,17},{17,9},{25,1},{1,25},{10,18},{1... | collective-permute-start | bytes 147464 | tf_op jit(solution)/shard_map/ppermute | solution.py:399
  35.7 4.8 %collective-permute-start.17 = (f32[16,256]{1,0:T(8,128)S(1)}, f32[16,256]{1,0:T(8,128)S(1)}, u32[]{:S(2)}, u32[]{:S(2)}) collective-permute-start(f32[16,256]{1,0:T(8,128)S(1)} %get-tuple-element.58), channel_id=1, source_target_pairs={{1,2},{2,1},{3,4},{4,3},{5,6},{6,5},{9,10},{10,9},{11,12},{12,11},... | collective-permute-start | bytes 49160 | tf_op jit(solution)/shard_map/ppermute | solution.py:394
  35.8 4.6 %collective-permute-start.16 = (f32[8,256]{1,0:T(8,128)S(1)}, f32[8,256]{1,0:T(8,128)S(1)}, u32[]{:S(2)}, u32[]{:S(2)}) collective-permute-start(f32[8,256]{1,0:T(8,128)S(1)} %get-tuple-element.57), channel_id=1, source_target_pairs={{0,1},{1,0},{2,3},{3,2},{4,5},{5,4},{6,7},{7,6},{8,9},{9,8},{10,11... | collective-permute-start | bytes 24584 | tf_op jit(solution)/shard_map/ppermute | solution.py:393
  40.5 3.9 %collective-permute-start.20 = (f32[24,256]{1,0:T(8,128)S(1)}, f32[24,256]{1,0:T(8,128)S(1)}, u32[]{:S(2)}, u32[]{:S(2)}) collective-permute-start(f32[24,256]{1,0:T(8,128)S(1)} %shard_map.78.packed), channel_id=1, source_target_pairs={{0,16},{16,0},{8,24},{24,8},{1,17},{17,1},{9,25},{25,9},{2,18},{18... | collective-permute-start | bytes 73736 | tf_op jit(solution)/shard_map/ppermute | solution.py:463
  42.0 3.3 %collective-permute-start.19 = (f32[24,256]{1,0:T(8,128)S(1)}, f32[24,256]{1,0:T(8,128)S(1)}, u32[]{:S(2)}, u32[]{:S(2)}) collective-permute-start(f32[24,256]{1,0:T(8,128)S(1)} %shard_map.78.packed), channel_id=1, source_target_pairs={{8,16},{16,8},{24,0},{0,24},{9,17},{17,9},{25,1},{1,25},{10,18},{1... | collective-permute-start | bytes 73736 | tf_op jit(solution)/shard_map/ppermute | solution.py:464
  42.0 3.3 %collective-permute-start.18 = (f32[24,256]{1,0:T(8,128)S(1)}, f32[24,256]{1,0:T(8,128)S(1)}, u32[]{:S(2)}, u32[]{:S(2)}) collective-permute-start(f32[24,256]{1,0:T(8,128)S(1)} %shard_map.78.packed), channel_id=1, source_target_pairs={{0,8},{8,0},{16,24},{24,16},{1,9},{9,1},{17,25},{25,17},{2,10},{10... | collective-permute-start | bytes 73736 | tf_op jit(solution)/shard_map/ppermute | solution.py:461
  (1 other events, 0.9 us)

commit v8 on v7

--- a/solution.py
+++ b/solution.py
@@ -11,6 +11,7 @@
 NB = 16
 WEIGHT = 0.8
 CENTER = 13
+EARLY = 18
 LANES = 128
 ROWS = 8
 
@@ -221,7 +222,7 @@
 
 
 def coefficient_pack_kernel(known, *refs):
-    coarse, (c, from_x, from_zx, _, __, middle_part, whole) = refs[:known], refs[known:]
+    coarse, (c, from_x, from_zx, _, __, early, late, whole) = refs[:known], refs[known:]
     _, planes, rows, extent = c.shape
     tiles = extent // LANES
     before, after = sides(from_x[...], from_zx[...])
@@ -238,7 +239,10 @@
         for k in range(27):
             ready = homed(k, part[k], l == 0, l == tiles - 1)
             whole[k, t : t + ROWS, :] = ready
-            middle_part[k, t : t + ROWS, :] = ready
+            if k < EARLY:
+                early[k, t : t + ROWS, :] = ready
+            else:
+                late[k - EARLY, t : t + ROWS, :] = ready
     for ref in coarse:
         for x in range(ref.shape[1]):
             for t in range(0, ref.shape[2], ROWS):
@@ -247,7 +251,7 @@
 
 
 def middle_kernel(
-    groups, planes, packed, near_core, near_y, far_below, far_above, own, core, other, iterate, coarse, held
+    groups, planes, packed, near_core, near_y, far_below, far_above, own, core, early, late, iterate, coarse, held
 ):
     extent = packed.shape[-1]
     tiles = extent // LANES
@@ -271,11 +275,16 @@
     def work(parts):
         def terms(forms, w, lanes):
             row = (w % planes * tiles + lanes.start // LANES) * ROWS
-            return outer_terms(forms, lambda k: parts[w // planes][k, row : row + ROWS, :], lanes)
+            return outer_terms(forms, lambda k: parts[w // planes](k)[row : row + ROWS, :], lanes)
 
         def swept(forms, field, w):
             sums = jnp.concatenate([terms(forms, w, lanes) for lanes in lane_tiles(extent)], axis=1)
-            return first[w + 1] + (1.0 - WEIGHT) * field - sums
+            values = first[w + 1] + (1.0 - WEIGHT) * field - sums
+            away = w // planes - 1
+            if away:
+                inside = (group + away >= 0) & (group + away < groups)
+                values = pick(inside, values, jnp.zeros_like(values))
+            return values
 
         low, high = planes - 2, 2 * planes + 2
         once = {w: swept(near[w : w + 3], first[w + 1], w) for w in range(low, high)}
@@ -292,13 +301,22 @@
                 rest = first[w + 1][:, lanes] - WEIGHT * twice[w][:, lanes] - sums
                 held[x, :, lanes] = (1.0 / WEIGHT) * own[CENTER, row : row + ROWS, :] * rest
 
+    def here(k):
+        return own.at[k]
+
+    def beside(k):
+        return core.at[k]
+
+    def across(k):
+        return early.at[k] if k < EARLY else late.at[k - EARLY]
+
     @pl.when(even("grp"))
     def _():
-        work((other, own, core))
+        work((across, here, beside))
 
     @pl.when(jnp.logical_not(even("grp")))
     def _():
-        work((core, own, other))
+        work((beside, here, across))
 
     place_of = lax.broadcasted_iota(jnp.int32, (ROWS, extent // 2), 0)
     for x in range(planes // 2):
@@ -430,16 +448,17 @@
     v, halo = sweep(v, halo)
     halo = along_grp(v, halo)
     start = middle_planes * (middle_extent // LANES) * ROWS
-    middle_part, own = call(
+    early, late, own = call(
         functools.partial(coefficient_pack_kernel, len(known)),
-        [shape(27, start, LANES), shape(27, start + len(known) * coarse_planes * coarse_rows, LANES)],
+        [shape(EARLY, start, LANES), shape(27 - EARLY, start, LANES), shape(27, start + len(known) * coarse_planes * coarse_rows, LANES)],
         [*(known[o] for o in offsets), middle, *halo_c, *halo[2:]],
     )
     core = lax.ppermute(own, "grp", core_pairs)
-    other = lax.ppermute(middle_part, "grp", y_pairs)
+    early = lax.ppermute(early, "grp", y_ring)
     v, halo = sweep(v, halo)
     fine_iterate = v
     halo = along_grp(v, halo)
+    late = lax.ppermute(after(late, *halo[2:]), "grp", y_ring)
     iterate, *edges = call(
         functools.partial(residual_kernel, groups),
         [shape(middle_planes, middle_rows, middle_extent)]
@@ -473,7 +492,7 @@
             shape(middle_planes, middle_rows, middle_extent),
             shape(groups * subs, coarse_planes, coarse_rows // subs, coarse_extent),
         ],
-        [packed, near_core, near_y, far_below, far_above, own, core, other],
+        [packed, near_core, near_y, far_below, far_above, own, core, early, late],
         [pltpu.VMEM((middle_planes, ROWS, middle_extent), jnp.float32)],
     )
     gathered = lax.all_to_all(coarse_source, ("grp", "sub"), 0, 0, tiled=True)

time: 59.7 us -> 57.7 us (0.966)
  starting transfers between devices: 25.5 us -> 24.2 us
  waiting for transfers between devices: 14.1 us -> 13.5 us
    ppermute x3, starting transfers between devices: 2.5 us -> 0.21 us  [along_grp(): from_y = lax.ppermute(to_y, 'grp', y_ring)]
    ppermute x5, starting transfers between devices: 11.9 us -> 13.5 us  [along_sub(): from_x = lax.ppermute(to_x, 'sub', x_pairs)]
    ppermute x1 -> x2, waiting for transfers between devices: 0.01 us -> 1.5 us  [the longest x1 1.5 us: body(): late = lax.ppermute(after(late, *halo[2:]), 'grp', y_ring)]
    ppermute x5, starting transfers between devices: 3.05 us -> 1.75 us  [along_sub(): return (from_x, lax.ppermute(to_zx, ('grp', 'sub'), zx_pairs))]
    ppermute x1, waiting for transfers between devices: 1.68 us -> 0.89 us  [body(): far_below = far_above = lax.ppermute(packed, 'grp', swaps([(0, 2), (1, 3)]))]
    ppermute x1, waiting for transfers between devices: 0.87 us -> 0.16 us  [body(): near_y = lax.ppermute(packed, 'grp', y_ring)]
  transfers between devices with their start and end apart: 22 -> 23, of which waited for: 10 -> 12; matrix products, arithmetic and copies ran while one was open for 0% -> 0% of each run, Pallas kernels for 3% -> 3%
where the time goes in v8:
time: 57.7 us; the launch traced here: 57.5 us
  starting transfers between devices  24.2 us (42%)
  waiting for transfers between devices  13.5 us (23%)
  blocking collectives  11.3 us (20%)
  Pallas kernels  4.65 us (8%)
  local copies, waits for them, and re-layouts  2.21 us (4%)
  other arithmetic  0.89 us (2%)
  between operations  0.77 us (1%)
    ppermute x5, starting transfers between devices, along_sub(): from_x = lax.ppermute(to_x, 'sub', x_pairs)  13.5 us
    all_to_all x1, blocking collectives, body(): gathered = lax.all_to_all(coarse_source, ('grp', 'sub'), 0, 0, tiled=True)  11.3 us
    ppermute x5, waiting for transfers between devices, along_sub(): from_x = lax.ppermute(to_x, 'sub', x_pairs)  4.8 us
    pallas_call x14, Pallas kernels, call(): pl.pallas_call(kernel, out_shape=outs, in_specs=[vmem] * len(args), out_s...  4.65 us
    ppermute x3, waiting for transfers between devices, along_grp(): from_y = lax.ppermute(to_y, 'grp', y_ring)  4.12 us
    ppermute x1, starting transfers between devices, body(): lax.ppermute(known[offset], 'grp', [(i, i ^ bit) for i in range(groups)])  3.03 us
    ppermute x3, starting transfers between devices, along_grp(): from_core = lax.ppermute(to_core, 'grp', core_pairs)  2.33 us
    unnamed x6, local copies, waits for them, and re-layouts  2.21 us
  transfers between devices with their start and end apart: 23, of which 12 were waited for; matrix products, arithmetic and copies ran while one was open for 0% of the time, Pallas kernels for 3%

profile of v8, /device:TPU:0, one launch (start us, length us, event | category | flops | bytes accessed | tf_op | source)
XLA Modules:
  0.0 57.5 jit_solution(8640364763189413474)
XLA Ops:
  0.6 0.9 %bitcast_divide_fusion.v.first = f32[4,8,512]{2,1,0:T(8,128)S(1)} fusion(f32[27,4,8,512]{3,2,1,0:T(8,128)} %c.2, f32[4,8,512]{2,1,0:T(8,128)} %param.4), kind=kLoop, calls=%fused_computation | loop fusion | flops 32768 | bytes 196608 | tf_op jit(solution)/shard_map/div | solution.py:421
  1.5 3.0 %collective-permute-start.12 = (f32[27,1,16,128]{3,2,1,0:T(8,128)}, f32[27,1,16,128]{3,2,1,0:T(8,128)S(1)}, u32[]{:S(2)}, u32[]{:S(2)}) collective-permute-start(f32[27,1,16,128]{3,2,1,0:T(8,128)} %refs_0_), channel_id=1, source_target_pairs={{0,16},{8,24},{16,0},{24,8},{1,17},{9,25},{17,1},{25,9},{2,18},{10... | collective-permute-start | bytes 663560 | tf_op jit(solution)/shard_map/ppermute | solution.py:445
  4.6 3.0 %collective-permute-start = (f32[4,512]{1,0:T(4,128)S(1)}, f32[4,512]{1,0:T(4,128)S(1)}, u32[]{:S(2)}, u32[]{:S(2)}) collective-permute-start(f32[4,512]{1,0:T(4,128)S(1)} %get-tuple-element.36), channel_id=1, source_target_pairs={{0,1},{1,0},{2,3},{3,2},{4,5},{5,4},{6,7},{7,6},{8,9},{9,8},{10,11... | collective-permute-start | bytes 24584 | tf_op jit(solution)/shard_map/ppermute | solution.py:411
  7.7 1.5 %copy-done = f32[27,4,8,512]{3,2,1,0:T(8,128)S(1)} copy-done((f32[27,4,8,512]{3,2,1,0:T(8,128)S(1)}, f32[27,4,8,512]{3,2,1,0:T(8,128)}, u32[]{:S(2)}) %copy-start) | copy-done | bytes 1769496
  10.3 1.2 %collective-permute-start.13 = (f32[27,2,2,256]{3,2,1,0:T(2,128)S(1)}, f32[27,2,2,256]{3,2,1,0:T(2,128)S(1)}, u32[]{:S(2)}, u32[]{:S(2)}) collective-permute-start(f32[27,2,2,256]{3,2,1,0:T(2,128)S(1)} %get-tuple-element.55), channel_id=1, source_target_pairs={{0,1},{1,0},{2,3},{3,2},{4,5},{5,4},{6,7},{7,6},{8,9},{9,8},{10,11... | collective-permute-start | bytes 331784 | tf_op jit(solution)/shard_map/ppermute | solution.py:411
  12.0 1.0 %collective-permute-done.2.from_core = f32[16,512]{1,0:T(8,128)S(1)} collective-permute-done((f32[16,512]{1,0:T(8,128)S(1)}, f32[16,512]{1,0:T(8,128)S(1)}, u32[]{:S(2)}, u32[]{:S(2)}) %collective-permute-start.2) | collective-permute-done | bytes 32800 | tf_op jit(solution)/shard_map/ppermute | solution.py:416
  13.0 0.8 %collective-permute-done.3.from_y = f32[24,512]{1,0:T(8,128)S(1)} collective-permute-done((f32[24,512]{1,0:T(8,128)S(1)}, f32[24,512]{1,0:T(8,128)S(1)}, u32[]{:S(2)}, u32[]{:S(2)}) %collective-permute-start.3) | collective-permute-done | bytes 49184 | tf_op jit(solution)/shard_map/ppermute | solution.py:417
  14.2 3.0 %collective-permute-start.4 = (f32[4,512]{1,0:T(4,128)S(1)}, f32[4,512]{1,0:T(4,128)S(1)}, u32[]{:S(2)}, u32[]{:S(2)}) collective-permute-start(f32[4,512]{1,0:T(4,128)S(1)} %get-tuple-element.44), channel_id=1, source_target_pairs={{0,1},{1,0},{2,3},{3,2},{4,5},{5,4},{6,7},{7,6},{8,9},{9,8},{10,11... | collective-permute-start | bytes 24584 | tf_op jit(solution)/shard_map/ppermute | solution.py:411
  17.2 1.6 %collective-permute-done.4.from_x = f32[4,512]{1,0:T(4,128)S(1)} collective-permute-done((f32[4,512]{1,0:T(4,128)S(1)}, f32[4,512]{1,0:T(4,128)S(1)}, u32[]{:S(2)}, u32[]{:S(2)}) %collective-permute-start.4) | collective-permute-done | bytes 8224 | tf_op jit(solution)/shard_map/ppermute | solution.py:411
  18.9 1.1 %collective-permute-start.6 = (f32[16,512]{1,0:T(8,128)S(1)}, f32[16,512]{1,0:T(8,128)S(1)}, u32[]{:S(2)}, u32[]{:S(2)}) collective-permute-start(f32[16,512]{1,0:T(8,128)S(1)} %get-tuple-element.46), channel_id=1, source_target_pairs={{0,8},{8,0},{16,24},{24,16},{1,9},{9,1},{17,25},{25,17},{2,10},{10... | collective-permute-start | bytes 98312 | tf_op jit(solution)/shard_map/ppermute | solution.py:416
  20.0 0.9 %collective-permute-done.6.from_core.refs_5_ = f32[16,512]{1,0:T(8,128)S(1)} collective-permute-done((f32[16,512]{1,0:T(8,128)S(1)}, f32[16,512]{1,0:T(8,128)S(1)}, u32[]{:S(2)}, u32[]{:S(2)}) %collective-permute-start.6) | collective-permute-done | bytes 32800 | tf_op jit(solution)/shard_map/ppermute | solution.py:416
  20.8 1.6 %collective-permute-done.7.from_y.refs_6_ = f32[24,512]{1,0:T(8,128)S(1)} collective-permute-done((f32[24,512]{1,0:T(8,128)S(1)}, f32[24,512]{1,0:T(8,128)S(1)}, u32[]{:S(2)}, u32[]{:S(2)}) %collective-permute-start.7) | collective-permute-done | bytes 49184 | tf_op jit(solution)/shard_map/ppermute | solution.py:417
  23.7 3.6 %collective-permute-start.8 = (f32[4,512]{1,0:T(4,128)S(1)}, f32[4,512]{1,0:T(4,128)S(1)}, u32[]{:S(2)}, u32[]{:S(2)}) collective-permute-start(f32[4,512]{1,0:T(4,128)S(1)} %get-tuple-element.49), channel_id=1, source_target_pairs={{0,1},{1,0},{2,3},{3,2},{4,5},{5,4},{6,7},{7,6},{8,9},{9,8},{10,11... | collective-permute-start | bytes 24584 | tf_op jit(solution)/shard_map/ppermute | solution.py:411
  27.2 1.6 %collective-permute-done.8.from_x = f32[4,512]{1,0:T(4,128)S(1)} collective-permute-done((f32[4,512]{1,0:T(4,128)S(1)}, f32[4,512]{1,0:T(4,128)S(1)}, u32[]{:S(2)}, u32[]{:S(2)}) %collective-permute-start.8) | collective-permute-done | bytes 8224 | tf_op jit(solution)/shard_map/ppermute | solution.py:411
  29.0 1.0 %collective-permute-start.10 = (f32[16,512]{1,0:T(8,128)S(1)}, f32[16,512]{1,0:T(8,128)S(1)}, u32[]{:S(2)}, u32[]{:S(2)}) collective-permute-start(f32[16,512]{1,0:T(8,128)S(1)} %get-tuple-element.51), channel_id=1, source_target_pairs={{0,8},{8,0},{16,24},{24,16},{1,9},{9,1},{17,25},{25,17},{2,10},{10... | collective-permute-start | bytes 98312 | tf_op jit(solution)/shard_map/ppermute | solution.py:416
  30.9 1.7 %collective-permute-done.11.from_y = f32[24,512]{1,0:T(8,128)S(1)} collective-permute-done((f32[24,512]{1,0:T(8,128)S(1)}, f32[24,512]{1,0:T(8,128)S(1)}, u32[]{:S(2)}, u32[]{:S(2)}) %collective-permute-start.11) | collective-permute-done | bytes 49184 | tf_op jit(solution)/shard_map/ppermute | solution.py:417
  34.3 2.7 %collective-permute-start.16 = (f32[8,256]{1,0:T(8,128)S(1)}, f32[8,256]{1,0:T(8,128)S(1)}, u32[]{:S(2)}, u32[]{:S(2)}) collective-permute-start(f32[8,256]{1,0:T(8,128)S(1)} %get-tuple-element.59), channel_id=1, source_target_pairs={{0,1},{1,0},{2,3},{3,2},{4,5},{5,4},{6,7},{7,6},{8,9},{9,8},{10,11... | collective-permute-start | bytes 24584 | tf_op jit(solution)/shard_map/ppermute | solution.py:411
  37.0 1.5 %collective-permute-done.16.from_x = f32[8,256]{1,0:T(8,128)S(1)} collective-permute-done((f32[8,256]{1,0:T(8,128)S(1)}, f32[8,256]{1,0:T(8,128)S(1)}, u32[]{:S(2)}, u32[]{:S(2)}) %collective-permute-start.16) | collective-permute-done | bytes 8224 | tf_op jit(solution)/shard_map/ppermute | solution.py:411
  38.6 1.2 %collective-permute-start.20 = (f32[24,256]{1,0:T(8,128)S(1)}, f32[24,256]{1,0:T(8,128)S(1)}, u32[]{:S(2)}, u32[]{:S(2)}) collective-permute-start(f32[24,256]{1,0:T(8,128)S(1)} %shard_map.78.packed), channel_id=1, source_target_pairs={{0,16},{16,0},{8,24},{24,8},{1,17},{17,1},{9,25},{25,9},{2,18},{18... | collective-permute-start | bytes 73736 | tf_op jit(solution)/shard_map/ppermute | solution.py:482
  39.8 1.0 %collective-permute-start.18 = (f32[24,256]{1,0:T(8,128)S(1)}, f32[24,256]{1,0:T(8,128)S(1)}, u32[]{:S(2)}, u32[]{:S(2)}) collective-permute-start(f32[24,256]{1,0:T(8,128)S(1)} %shard_map.78.packed), channel_id=1, source_target_pairs={{0,8},{8,0},{16,24},{24,16},{1,9},{9,1},{17,25},{25,17},{2,10},{10... | collective-permute-start | bytes 73736 | tf_op jit(solution)/shard_map/ppermute | solution.py:480
  40.8 1.5 %collective-permute-done.22.late = f32[9,32,128]{2,1,0:T(8,128)S(1)} collective-permute-done((f32[9,32,128]{2,1,0:T(8,128)S(1)}, f32[9,32,128]{2,1,0:T(8,128)S(1)}, u32[]{:S(2)}, u32[]{:S(2)}) %collective-permute-start.22) | collective-permute-done | bytes 147488 | tf_op jit(solution)/shard_map/ppermute | solution.py:461
  42.3 0.9 %collective-permute-done.20.far_below.far_above = f32[24,256]{1,0:T(8,128)S(1)} collective-permute-done((f32[24,256]{1,0:T(8,128)S(1)}, f32[24,256]{1,0:T(8,128)S(1)}, u32[]{:S(2)}, u32[]{:S(2)}) %collective-permute-start.20) | collective-permute-done | bytes 24608 | tf_op jit(solution)/shard_map/ppermute | solution.py:482
  44.0 11.3 %all_to_all.5.gathered = f32[32,1,2,128]{3,2,1,0:T(2,128)S(1)} all-to-all(f32[32,1,2,128]{3,2,1,0:T(2,128)S(1)} %get-tuple-element.64), channel_id=1, replica_groups=mesh['grp'=4,'sub'=8] {'grp','sub'}, dimensions={0} | all-to-all | bytes 65536 | tf_op jit(solution)/shard_map/all_to_all | solution.py:498
  55.3 2.2 %shard_map.80 = (f32[1,16,128]{2,1,0:T(8,128)}, f32[4,8,512]{2,1,0:T(8,128)}, f32[2,4,256]{2,1,0:T(4,128)}) custom-call(f32[32,1,2,128]{3,2,1,0:T(2,128)S(1)} %all_to_all.5.gathered, f32[4,27,16,128]{3,2,1,0:T(8,128)S(1)} %shard_map.77.c, f32[4,8,512]{2,1,0:T(8,128)S(1)} %get-tuple-element.48.v.fine, f32[2,4,256]{2,1,0:T(4,128)S(1)} %get-tuple-element.65.middle), custom_call_target="tpu_custom_call" | custom-call | tf_op jit(solution)/shard_map/pallas_call | solution.py:25
  (45 shorter events, 7.0 us)
Async XLA Ops:
  1.5 20.9 %collective-permute-start.12 = (f32[27,1,16,128]{3,2,1,0:T(8,128)}, f32[27,1,16,128]{3,2,1,0:T(8,128)S(1)}, u32[]{:S(2)}, u32[]{:S(2)}) collective-permute-start(f32[27,1,16,128]{3,2,1,0:T(8,128)} %refs_0_), channel_id=1, source_target_pairs={{0,16},{8,24},{16,0},{24,8},{1,17},{9,25},{17,1},{25,9},{2,18},{10... | collective-permute-start | bytes 663560 | tf_op jit(solution)/shard_map/ppermute | solution.py:445
  4.6 5.6 %collective-permute-start.1 = (f32[8,512]{1,0:T(8,128)S(1)}, f32[8,512]{1,0:T(8,128)S(1)}, u32[]{:S(2)}, u32[]{:S(2)}) collective-permute-start(f32[8,512]{1,0:T(8,128)S(1)} %get-tuple-element.37), channel_id=1, source_target_pairs={{1,2},{2,1},{3,4},{4,3},{5,6},{6,5},{9,10},{10,9},{11,12},{12,11},... | collective-permute-start | bytes 49160 | tf_op jit(solution)/shard_map/ppermute | solution.py:412
  4.6 5.5 %collective-permute-start = (f32[4,512]{1,0:T(4,128)S(1)}, f32[4,512]{1,0:T(4,128)S(1)}, u32[]{:S(2)}, u32[]{:S(2)}) collective-permute-start(f32[4,512]{1,0:T(4,128)S(1)} %get-tuple-element.36), channel_id=1, source_target_pairs={{0,1},{1,0},{2,3},{3,2},{4,5},{5,4},{6,7},{7,6},{8,9},{9,8},{10,11... | collective-permute-start | bytes 24584 | tf_op jit(solution)/shard_map/ppermute | solution.py:411
  10.1 12.4 %copy-start.2 = (f32[27,1,16,128]{3,2,1,0:T(8,128)S(1)}, f32[27,1,16,128]{3,2,1,0:T(8,128)}, u32[]{:S(2)}) copy-start(f32[27,1,16,128]{3,2,1,0:T(8,128)} %refs_0_) | copy-start | bytes 663556
  10.2 3.6 %collective-permute-start.3 = (f32[24,512]{1,0:T(8,128)S(1)}, f32[24,512]{1,0:T(8,128)S(1)}, u32[]{:S(2)}, u32[]{:S(2)}) collective-permute-start(f32[24,512]{1,0:T(8,128)S(1)} %get-tuple-element.42), channel_id=1, source_target_pairs={{8,16},{16,8},{24,0},{0,24},{9,17},{17,9},{25,1},{1,25},{10,18},{1... | collective-permute-start | bytes 147464 | tf_op jit(solution)/shard_map/ppermute | solution.py:417
  10.3 10.5 %collective-permute-start.13 = (f32[27,2,2,256]{3,2,1,0:T(2,128)S(1)}, f32[27,2,2,256]{3,2,1,0:T(2,128)S(1)}, u32[]{:S(2)}, u32[]{:S(2)}) collective-permute-start(f32[27,2,2,256]{3,2,1,0:T(2,128)S(1)} %get-tuple-element.55), channel_id=1, source_target_pairs={{0,1},{1,0},{2,3},{3,2},{4,5},{5,4},{6,7},{7,6},{8,9},{9,8},{10,11... | collective-permute-start | bytes 331784 | tf_op jit(solution)/shard_map/ppermute | solution.py:411
  11.5 9.4 %collective-permute-start.14 = (f32[27,2,2,256]{3,2,1,0:T(2,128)S(1)}, f32[27,2,2,256]{3,2,1,0:T(2,128)S(1)}, u32[]{:S(2)}, u32[]{:S(2)}) collective-permute-start(f32[27,2,2,256]{3,2,1,0:T(2,128)S(1)} %get-tuple-element.56), channel_id=1, source_target_pairs={{1,2},{2,1},{3,4},{4,3},{5,6},{6,5},{9,10},{10,9},{11,12},{12,11},... | collective-permute-start | bytes 331784 | tf_op jit(solution)/shard_map/ppermute | solution.py:412
  11.8 1.2 %collective-permute-start.2 = (f32[16,512]{1,0:T(8,128)S(1)}, f32[16,512]{1,0:T(8,128)S(1)}, u32[]{:S(2)}, u32[]{:S(2)}) collective-permute-start(f32[16,512]{1,0:T(8,128)S(1)} %get-tuple-element.41), channel_id=1, source_target_pairs={{0,8},{8,0},{16,24},{24,16},{1,9},{9,1},{17,25},{25,17},{2,10},{10... | collective-permute-start | bytes 98312 | tf_op jit(solution)/shard_map/ppermute | solution.py:416
  14.1 4.7 %collective-permute-start.5 = (f32[8,512]{1,0:T(8,128)S(1)}, f32[8,512]{1,0:T(8,128)S(1)}, u32[]{:S(2)}, u32[]{:S(2)}) collective-permute-start(f32[8,512]{1,0:T(8,128)S(1)} %get-tuple-element.45), channel_id=1, source_target_pairs={{1,2},{2,1},{3,4},{4,3},{5,6},{6,5},{9,10},{10,9},{11,12},{12,11},... | collective-permute-start | bytes 49160 | tf_op jit(solution)/shard_map/ppermute | solution.py:412
  14.2 4.7 %collective-permute-start.4 = (f32[4,512]{1,0:T(4,128)S(1)}, f32[4,512]{1,0:T(4,128)S(1)}, u32[]{:S(2)}, u32[]{:S(2)}) collective-permute-start(f32[4,512]{1,0:T(4,128)S(1)} %get-tuple-element.44), channel_id=1, source_target_pairs={{0,1},{1,0},{2,3},{3,2},{4,5},{5,4},{6,7},{7,6},{8,9},{9,8},{10,11... | collective-permute-start | bytes 24584 | tf_op jit(solution)/shard_map/ppermute | solution.py:411
  18.8 3.6 %collective-permute-start.7 = (f32[24,512]{1,0:T(8,128)S(1)}, f32[24,512]{1,0:T(8,128)S(1)}, u32[]{:S(2)}, u32[]{:S(2)}) collective-permute-start(f32[24,512]{1,0:T(8,128)S(1)} %get-tuple-element.47), channel_id=1, source_target_pairs={{8,16},{16,8},{24,0},{0,24},{9,17},{17,9},{25,1},{1,25},{10,18},{1... | collective-permute-start | bytes 147464 | tf_op jit(solution)/shard_map/ppermute | solution.py:417
  18.9 1.9 %collective-permute-start.6 = (f32[16,512]{1,0:T(8,128)S(1)}, f32[16,512]{1,0:T(8,128)S(1)}, u32[]{:S(2)}, u32[]{:S(2)}) collective-permute-start(f32[16,512]{1,0:T(8,128)S(1)} %get-tuple-element.46), channel_id=1, source_target_pairs={{0,8},{8,0},{16,24},{24,16},{1,9},{9,1},{17,25},{25,17},{2,10},{10... | collective-permute-start | bytes 98312 | tf_op jit(solution)/shard_map/ppermute | solution.py:416
  22.8 14.2 %collective-permute-start.15 = (f32[27,64,128]{2,1,0:T(8,128)S(1)}, f32[27,64,128]{2,1,0:T(8,128)S(1)}, u32[]{:S(2)}, u32[]{:S(2)}) collective-permute-start(f32[27,64,128]{2,1,0:T(8,128)S(1)} %get-tuple-element.57.own), channel_id=1, source_target_pairs={{0,8},{8,0},{16,24},{24,16},{1,9},{9,1},{17,25},{25,17},{2,10},{10... | collective-permute-start | bytes 2654216 | tf_op jit(solution)/shard_map/ppermute | solution.py:456
  23.1 5.7 %collective-permute-start.9 = (f32[8,512]{1,0:T(8,128)S(1)}, f32[8,512]{1,0:T(8,128)S(1)}, u32[]{:S(2)}, u32[]{:S(2)}) collective-permute-start(f32[8,512]{1,0:T(8,128)S(1)} %get-tuple-element.50), channel_id=1, source_target_pairs={{1,2},{2,1},{3,4},{4,3},{5,6},{6,5},{9,10},{10,9},{11,12},{12,11},... | collective-permute-start | bytes 49160 | tf_op jit(solution)/shard_map/ppermute | solution.py:412
  23.7 5.2 %collective-permute-start.8 = (f32[4,512]{1,0:T(4,128)S(1)}, f32[4,512]{1,0:T(4,128)S(1)}, u32[]{:S(2)}, u32[]{:S(2)}) collective-permute-start(f32[4,512]{1,0:T(4,128)S(1)} %get-tuple-element.49), channel_id=1, source_target_pairs={{0,1},{1,0},{2,3},{3,2},{4,5},{5,4},{6,7},{7,6},{8,9},{9,8},{10,11... | collective-permute-start | bytes 24584 | tf_op jit(solution)/shard_map/ppermute | solution.py:411
  28.9 3.6 %collective-permute-start.11 = (f32[24,512]{1,0:T(8,128)S(1)}, f32[24,512]{1,0:T(8,128)S(1)}, u32[]{:S(2)}, u32[]{:S(2)}) collective-permute-start(f32[24,512]{1,0:T(8,128)S(1)} %get-tuple-element.52), channel_id=1, source_target_pairs={{8,16},{16,8},{24,0},{0,24},{9,17},{17,9},{25,1},{1,25},{10,18},{1... | collective-permute-start | bytes 147464 | tf_op jit(solution)/shard_map/ppermute | solution.py:417
  29.0 1.9 %collective-permute-start.10 = (f32[16,512]{1,0:T(8,128)S(1)}, f32[16,512]{1,0:T(8,128)S(1)}, u32[]{:S(2)}, u32[]{:S(2)}) collective-permute-start(f32[16,512]{1,0:T(8,128)S(1)} %get-tuple-element.51), channel_id=1, source_target_pairs={{0,8},{8,0},{16,24},{24,16},{1,9},{9,1},{17,25},{25,17},{2,10},{10... | collective-permute-start | bytes 98312 | tf_op jit(solution)/shard_map/ppermute | solution.py:416
  30.0 12.3 %collective-permute-start.21 = (f32[18,32,128]{2,1,0:T(8,128)S(1)}, f32[18,32,128]{2,1,0:T(8,128)S(1)}, u32[]{:S(2)}, u32[]{:S(2)}) collective-permute-start(f32[18,32,128]{2,1,0:T(8,128)S(1)} %get-tuple-element.61), channel_id=1, source_target_pairs={{8,16},{16,8},{24,0},{0,24},{9,17},{17,9},{25,1},{1,25},{10,18},{1... | collective-permute-start | bytes 884744 | tf_op jit(solution)/shard_map/ppermute | solution.py:457
  32.5 9.8 %collective-permute-start.22 = (f32[9,32,128]{2,1,0:T(8,128)S(1)}, f32[9,32,128]{2,1,0:T(8,128)S(1)}, u32[]{:S(2)}, u32[]{:S(2)}) collective-permute-start(f32[9,32,128]{2,1,0:T(8,128)S(1)} %get-tuple-element.63), channel_id=1, source_target_pairs={{8,16},{16,8},{24,0},{0,24},{9,17},{17,9},{25,1},{1,25},{10,18},{1... | collective-permute-start | bytes 442376 | tf_op jit(solution)/shard_map/ppermute | solution.py:461
  33.5 5.1 %collective-permute-start.17 = (f32[16,256]{1,0:T(8,128)S(1)}, f32[16,256]{1,0:T(8,128)S(1)}, u32[]{:S(2)}, u32[]{:S(2)}) collective-permute-start(f32[16,256]{1,0:T(8,128)S(1)} %get-tuple-element.60), channel_id=1, source_target_pairs={{1,2},{2,1},{3,4},{4,3},{5,6},{6,5},{9,10},{10,9},{11,12},{12,11},... | collective-permute-start | bytes 49160 | tf_op jit(solution)/shard_map/ppermute | solution.py:412
  34.3 4.3 %collective-permute-start.16 = (f32[8,256]{1,0:T(8,128)S(1)}, f32[8,256]{1,0:T(8,128)S(1)}, u32[]{:S(2)}, u32[]{:S(2)}) collective-permute-start(f32[8,256]{1,0:T(8,128)S(1)} %get-tuple-element.59), channel_id=1, source_target_pairs={{0,1},{1,0},{2,3},{3,2},{4,5},{5,4},{6,7},{7,6},{8,9},{9,8},{10,11... | collective-permute-start | bytes 24584 | tf_op jit(solution)/shard_map/ppermute | solution.py:411
  38.6 4.6 %collective-permute-start.20 = (f32[24,256]{1,0:T(8,128)S(1)}, f32[24,256]{1,0:T(8,128)S(1)}, u32[]{:S(2)}, u32[]{:S(2)}) collective-permute-start(f32[24,256]{1,0:T(8,128)S(1)} %shard_map.78.packed), channel_id=1, source_target_pairs={{0,16},{16,0},{8,24},{24,8},{1,17},{17,1},{9,25},{25,9},{2,18},{18... | collective-permute-start | bytes 73736 | tf_op jit(solution)/shard_map/ppermute | solution.py:482
  39.8 3.6 %collective-permute-start.19 = (f32[24,256]{1,0:T(8,128)S(1)}, f32[24,256]{1,0:T(8,128)S(1)}, u32[]{:S(2)}, u32[]{:S(2)}) collective-permute-start(f32[24,256]{1,0:T(8,128)S(1)} %shard_map.78.packed), channel_id=1, source_target_pairs={{8,16},{16,8},{24,0},{0,24},{9,17},{17,9},{25,1},{1,25},{10,18},{1... | collective-permute-start | bytes 73736 | tf_op jit(solution)/shard_map/ppermute | solution.py:483
  39.8 3.6 %collective-permute-start.18 = (f32[24,256]{1,0:T(8,128)S(1)}, f32[24,256]{1,0:T(8,128)S(1)}, u32[]{:S(2)}, u32[]{:S(2)}) collective-permute-start(f32[24,256]{1,0:T(8,128)S(1)} %shard_map.78.packed), channel_id=1, source_target_pairs={{0,8},{8,0},{16,24},{24,16},{1,9},{9,1},{17,25},{25,17},{2,10},{10... | collective-permute-start | bytes 73736 | tf_op jit(solution)/shard_map/ppermute | solution.py:480
  (2 other events, 2.4 us)

commit v9 on v8

--- a/solution.py
+++ b/solution.py
@@ -11,7 +11,7 @@
 NB = 16
 WEIGHT = 0.8
 CENTER = 13
-EARLY = 18
+EARLY = 19
 LANES = 128
 ROWS = 8
 

time: 57.7 us -> 57.4 us (level)
    ppermute x3, waiting for transfers between devices: 4.12 us -> 3.06 us  [along_grp(): from_y = lax.ppermute(to_y, 'grp', y_ring)]
    ppermute x3, waiting for transfers between devices: 1.97 us -> 3.03 us  [along_grp(): from_core = lax.ppermute(to_core, 'grp', core_pairs)]
    ppermute x3, starting transfers between devices: 2.33 us -> 1.31 us  [along_grp(): from_core = lax.ppermute(to_core, 'grp', core_pairs)]
    ppermute x1, starting transfers between devices: 0.71 us -> 1.73 us  [body(): early = lax.ppermute(early, 'grp', y_ring)]
    ppermute x1, waiting for transfers between devices: 1.5 us -> 0.54 us  [body(): late = lax.ppermute(after(late, *halo[2:]), 'grp', y_ring)]
where the time goes in v9:
time: 57.4 us; the launch traced here: 57.2 us
  starting transfers between devices  24.2 us (42%)
  waiting for transfers between devices  13.2 us (23%)
  blocking collectives  11.2 us (20%)
  Pallas kernels  4.66 us (8%)
  local copies, waits for them, and re-layouts  2.21 us (4%)
  other arithmetic  0.89 us (2%)
  between operations  0.77 us (1%)
    ppermute x5, starting transfers between devices, along_sub(): from_x = lax.ppermute(to_x, 'sub', x_pairs)  13.5 us
    all_to_all x1, blocking collectives, body(): gathered = lax.all_to_all(coarse_source, ('grp', 'sub'), 0, 0, tiled=True)  11.2 us
    ppermute x5, waiting for transfers between devices, along_sub(): from_x = lax.ppermute(to_x, 'sub', x_pairs)  4.8 us
    pallas_call x14, Pallas kernels, call(): pl.pallas_call(kernel, out_shape=outs, in_specs=[vmem] * len(args), out_s...  4.66 us
    ppermute x3, waiting for transfers between devices, along_grp(): from_y = lax.ppermute(to_y, 'grp', y_ring)  3.06 us
    ppermute x1, starting transfers between devices, body(): lax.ppermute(known[offset], 'grp', [(i, i ^ bit) for i in range(groups)])  3.03 us
    ppermute x3, waiting for transfers between devices, along_grp(): from_core = lax.ppermute(to_core, 'grp', core_pairs)  3.03 us
    unnamed x6, local copies, waits for them, and re-layouts  2.21 us
  transfers between devices with their start and end apart: 23, of which 12 were waited for; matrix products, arithmetic and copies ran while one was open for 0% of the time, Pallas kernels for 3%

profile of v9, /device:TPU:0, one launch (start us, length us, event | category | flops | bytes accessed | tf_op | source)
XLA Modules:
  0.0 57.2 jit_solution(13401575771094398956)
XLA Ops:
  0.6 0.9 %bitcast_divide_fusion.v.first = f32[4,8,512]{2,1,0:T(8,128)S(1)} fusion(f32[27,4,8,512]{3,2,1,0:T(8,128)} %c.2, f32[4,8,512]{2,1,0:T(8,128)} %param.4), kind=kLoop, calls=%fused_computation | loop fusion | flops 32768 | bytes 196608 | tf_op jit(solution)/shard_map/div | solution.py:421
  1.5 3.0 %collective-permute-start.12 = (f32[27,1,16,128]{3,2,1,0:T(8,128)}, f32[27,1,16,128]{3,2,1,0:T(8,128)S(1)}, u32[]{:S(2)}, u32[]{:S(2)}) collective-permute-start(f32[27,1,16,128]{3,2,1,0:T(8,128)} %refs_0_), channel_id=1, source_target_pairs={{0,16},{8,24},{16,0},{24,8},{1,17},{9,25},{17,1},{25,9},{2,18},{10... | collective-permute-start | bytes 663560 | tf_op jit(solution)/shard_map/ppermute | solution.py:445
  4.6 3.0 %collective-permute-start = (f32[4,512]{1,0:T(4,128)S(1)}, f32[4,512]{1,0:T(4,128)S(1)}, u32[]{:S(2)}, u32[]{:S(2)}) collective-permute-start(f32[4,512]{1,0:T(4,128)S(1)} %get-tuple-element.36), channel_id=1, source_target_pairs={{0,1},{1,0},{2,3},{3,2},{4,5},{5,4},{6,7},{7,6},{8,9},{9,8},{10,11... | collective-permute-start | bytes 24584 | tf_op jit(solution)/shard_map/ppermute | solution.py:411
  7.7 1.5 %copy-done = f32[27,4,8,512]{3,2,1,0:T(8,128)S(1)} copy-done((f32[27,4,8,512]{3,2,1,0:T(8,128)S(1)}, f32[27,4,8,512]{3,2,1,0:T(8,128)}, u32[]{:S(2)}) %copy-start) | copy-done | bytes 1769496
  10.3 1.2 %collective-permute-start.13 = (f32[27,2,2,256]{3,2,1,0:T(2,128)S(1)}, f32[27,2,2,256]{3,2,1,0:T(2,128)S(1)}, u32[]{:S(2)}, u32[]{:S(2)}) collective-permute-start(f32[27,2,2,256]{3,2,1,0:T(2,128)S(1)} %get-tuple-element.55), channel_id=1, source_target_pairs={{0,1},{1,0},{2,3},{3,2},{4,5},{5,4},{6,7},{7,6},{8,9},{9,8},{10,11... | collective-permute-start | bytes 331784 | tf_op jit(solution)/shard_map/ppermute | solution.py:411
  12.0 1.0 %collective-permute-done.2.from_core = f32[16,512]{1,0:T(8,128)S(1)} collective-permute-done((f32[16,512]{1,0:T(8,128)S(1)}, f32[16,512]{1,0:T(8,128)S(1)}, u32[]{:S(2)}, u32[]{:S(2)}) %collective-permute-start.2) | collective-permute-done | bytes 32800 | tf_op jit(solution)/shard_map/ppermute | solution.py:416
  13.0 0.8 %collective-permute-done.3.from_y = f32[24,512]{1,0:T(8,128)S(1)} collective-permute-done((f32[24,512]{1,0:T(8,128)S(1)}, f32[24,512]{1,0:T(8,128)S(1)}, u32[]{:S(2)}, u32[]{:S(2)}) %collective-permute-start.3) | collective-permute-done | bytes 49184 | tf_op jit(solution)/shard_map/ppermute | solution.py:417
  14.2 3.0 %collective-permute-start.4 = (f32[4,512]{1,0:T(4,128)S(1)}, f32[4,512]{1,0:T(4,128)S(1)}, u32[]{:S(2)}, u32[]{:S(2)}) collective-permute-start(f32[4,512]{1,0:T(4,128)S(1)} %get-tuple-element.44), channel_id=1, source_target_pairs={{0,1},{1,0},{2,3},{3,2},{4,5},{5,4},{6,7},{7,6},{8,9},{9,8},{10,11... | collective-permute-start | bytes 24584 | tf_op jit(solution)/shard_map/ppermute | solution.py:411
  17.2 1.6 %collective-permute-done.4.from_x = f32[4,512]{1,0:T(4,128)S(1)} collective-permute-done((f32[4,512]{1,0:T(4,128)S(1)}, f32[4,512]{1,0:T(4,128)S(1)}, u32[]{:S(2)}, u32[]{:S(2)}) %collective-permute-start.4) | collective-permute-done | bytes 8224 | tf_op jit(solution)/shard_map/ppermute | solution.py:411
  18.9 1.1 %collective-permute-start.6 = (f32[16,512]{1,0:T(8,128)S(1)}, f32[16,512]{1,0:T(8,128)S(1)}, u32[]{:S(2)}, u32[]{:S(2)}) collective-permute-start(f32[16,512]{1,0:T(8,128)S(1)} %get-tuple-element.46), channel_id=1, source_target_pairs={{0,8},{8,0},{16,24},{24,16},{1,9},{9,1},{17,25},{25,17},{2,10},{10... | collective-permute-start | bytes 98312 | tf_op jit(solution)/shard_map/ppermute | solution.py:416
  20.0 0.9 %collective-permute-done.6.from_core.refs_5_ = f32[16,512]{1,0:T(8,128)S(1)} collective-permute-done((f32[16,512]{1,0:T(8,128)S(1)}, f32[16,512]{1,0:T(8,128)S(1)}, u32[]{:S(2)}, u32[]{:S(2)}) %collective-permute-start.6) | collective-permute-done | bytes 32800 | tf_op jit(solution)/shard_map/ppermute | solution.py:416
  20.8 1.6 %collective-permute-done.7.from_y.refs_6_ = f32[24,512]{1,0:T(8,128)S(1)} collective-permute-done((f32[24,512]{1,0:T(8,128)S(1)}, f32[24,512]{1,0:T(8,128)S(1)}, u32[]{:S(2)}, u32[]{:S(2)}) %collective-permute-start.7) | collective-permute-done | bytes 49184 | tf_op jit(solution)/shard_map/ppermute | solution.py:417
  23.7 3.6 %collective-permute-start.8 = (f32[4,512]{1,0:T(4,128)S(1)}, f32[4,512]{1,0:T(4,128)S(1)}, u32[]{:S(2)}, u32[]{:S(2)}) collective-permute-start(f32[4,512]{1,0:T(4,128)S(1)} %get-tuple-element.49), channel_id=1, source_target_pairs={{0,1},{1,0},{2,3},{3,2},{4,5},{5,4},{6,7},{7,6},{8,9},{9,8},{10,11... | collective-permute-start | bytes 24584 | tf_op jit(solution)/shard_map/ppermute | solution.py:411
  27.2 1.6 %collective-permute-done.8.from_x = f32[4,512]{1,0:T(4,128)S(1)} collective-permute-done((f32[4,512]{1,0:T(4,128)S(1)}, f32[4,512]{1,0:T(4,128)S(1)}, u32[]{:S(2)}, u32[]{:S(2)}) %collective-permute-start.8) | collective-permute-done | bytes 8224 | tf_op jit(solution)/shard_map/ppermute | solution.py:411
  29.0 1.7 %collective-permute-start.21 = (f32[19,32,128]{2,1,0:T(8,128)S(1)}, f32[19,32,128]{2,1,0:T(8,128)S(1)}, u32[]{:S(2)}, u32[]{:S(2)}) collective-permute-start(f32[19,32,128]{2,1,0:T(8,128)S(1)} %get-tuple-element.61), channel_id=1, source_target_pairs={{8,16},{16,8},{24,0},{0,24},{9,17},{17,9},{25,1},{1,25},{10,18},{1... | collective-permute-start | bytes 933896 | tf_op jit(solution)/shard_map/ppermute | solution.py:457
  30.7 1.2 %collective-permute-done.10.from_core = f32[16,512]{1,0:T(8,128)S(1)} collective-permute-done((f32[16,512]{1,0:T(8,128)S(1)}, f32[16,512]{1,0:T(8,128)S(1)}, u32[]{:S(2)}, u32[]{:S(2)}) %collective-permute-start.10) | collective-permute-done | bytes 32800 | tf_op jit(solution)/shard_map/ppermute | solution.py:416
  33.5 0.8 %collective-permute-start.17 = (f32[16,256]{1,0:T(8,128)S(1)}, f32[16,256]{1,0:T(8,128)S(1)}, u32[]{:S(2)}, u32[]{:S(2)}) collective-permute-start(f32[16,256]{1,0:T(8,128)S(1)} %get-tuple-element.60), channel_id=1, source_target_pairs={{1,2},{2,1},{3,4},{4,3},{5,6},{6,5},{9,10},{10,9},{11,12},{12,11},... | collective-permute-start | bytes 49160 | tf_op jit(solution)/shard_map/ppermute | solution.py:412
  34.3 2.7 %collective-permute-start.16 = (f32[8,256]{1,0:T(8,128)S(1)}, f32[8,256]{1,0:T(8,128)S(1)}, u32[]{:S(2)}, u32[]{:S(2)}) collective-permute-start(f32[8,256]{1,0:T(8,128)S(1)} %get-tuple-element.59), channel_id=1, source_target_pairs={{0,1},{1,0},{2,3},{3,2},{4,5},{5,4},{6,7},{7,6},{8,9},{9,8},{10,11... | collective-permute-start | bytes 24584 | tf_op jit(solution)/shard_map/ppermute | solution.py:411
  37.0 1.5 %collective-permute-done.16.from_x = f32[8,256]{1,0:T(8,128)S(1)} collective-permute-done((f32[8,256]{1,0:T(8,128)S(1)}, f32[8,256]{1,0:T(8,128)S(1)}, u32[]{:S(2)}, u32[]{:S(2)}) %collective-permute-start.16) | collective-permute-done | bytes 8224 | tf_op jit(solution)/shard_map/ppermute | solution.py:411
  38.6 1.2 %collective-permute-start.20 = (f32[24,256]{1,0:T(8,128)S(1)}, f32[24,256]{1,0:T(8,128)S(1)}, u32[]{:S(2)}, u32[]{:S(2)}) collective-permute-start(f32[24,256]{1,0:T(8,128)S(1)} %shard_map.78.packed), channel_id=1, source_target_pairs={{0,16},{16,0},{8,24},{24,8},{1,17},{17,1},{9,25},{25,9},{2,18},{18... | collective-permute-start | bytes 73736 | tf_op jit(solution)/shard_map/ppermute | solution.py:482
  39.8 1.0 %collective-permute-start.18 = (f32[24,256]{1,0:T(8,128)S(1)}, f32[24,256]{1,0:T(8,128)S(1)}, u32[]{:S(2)}, u32[]{:S(2)}) collective-permute-start(f32[24,256]{1,0:T(8,128)S(1)} %shard_map.78.packed), channel_id=1, source_target_pairs={{0,8},{8,0},{16,24},{24,16},{1,9},{9,1},{17,25},{25,17},{2,10},{10... | collective-permute-start | bytes 73736 | tf_op jit(solution)/shard_map/ppermute | solution.py:480
  41.3 1.2 %collective-permute-done.20.far_below.far_above = f32[24,256]{1,0:T(8,128)S(1)} collective-permute-done((f32[24,256]{1,0:T(8,128)S(1)}, f32[24,256]{1,0:T(8,128)S(1)}, u32[]{:S(2)}, u32[]{:S(2)}) %collective-permute-start.20) | collective-permute-done | bytes 24608 | tf_op jit(solution)/shard_map/ppermute | solution.py:482
  43.7 11.2 %all_to_all.5.gathered = f32[32,1,2,128]{3,2,1,0:T(2,128)S(1)} all-to-all(f32[32,1,2,128]{3,2,1,0:T(2,128)S(1)} %get-tuple-element.64), channel_id=1, replica_groups=mesh['grp'=4,'sub'=8] {'grp','sub'}, dimensions={0} | all-to-all | bytes 65536 | tf_op jit(solution)/shard_map/all_to_all | solution.py:498
  54.9 2.2 %shard_map.80 = (f32[1,16,128]{2,1,0:T(8,128)}, f32[4,8,512]{2,1,0:T(8,128)}, f32[2,4,256]{2,1,0:T(4,128)}) custom-call(f32[32,1,2,128]{3,2,1,0:T(2,128)S(1)} %all_to_all.5.gathered, f32[4,27,16,128]{3,2,1,0:T(8,128)S(1)} %shard_map.77.c, f32[4,8,512]{2,1,0:T(8,128)S(1)} %get-tuple-element.48.v.fine, f32[2,4,256]{2,1,0:T(4,128)S(1)} %get-tuple-element.65.middle), custom_call_target="tpu_custom_call" | custom-call | tf_op jit(solution)/shard_map/pallas_call | solution.py:25
  (45 shorter events, 6.8 us)
Async XLA Ops:
  1.5 20.9 %collective-permute-start.12 = (f32[27,1,16,128]{3,2,1,0:T(8,128)}, f32[27,1,16,128]{3,2,1,0:T(8,128)S(1)}, u32[]{:S(2)}, u32[]{:S(2)}) collective-permute-start(f32[27,1,16,128]{3,2,1,0:T(8,128)} %refs_0_), channel_id=1, source_target_pairs={{0,16},{8,24},{16,0},{24,8},{1,17},{9,25},{17,1},{25,9},{2,18},{10... | collective-permute-start | bytes 663560 | tf_op jit(solution)/shard_map/ppermute | solution.py:445
  4.6 5.6 %collective-permute-start.1 = (f32[8,512]{1,0:T(8,128)S(1)}, f32[8,512]{1,0:T(8,128)S(1)}, u32[]{:S(2)}, u32[]{:S(2)}) collective-permute-start(f32[8,512]{1,0:T(8,128)S(1)} %get-tuple-element.37), channel_id=1, source_target_pairs={{1,2},{2,1},{3,4},{4,3},{5,6},{6,5},{9,10},{10,9},{11,12},{12,11},... | collective-permute-start | bytes 49160 | tf_op jit(solution)/shard_map/ppermute | solution.py:412
  4.6 5.5 %collective-permute-start = (f32[4,512]{1,0:T(4,128)S(1)}, f32[4,512]{1,0:T(4,128)S(1)}, u32[]{:S(2)}, u32[]{:S(2)}) collective-permute-start(f32[4,512]{1,0:T(4,128)S(1)} %get-tuple-element.36), channel_id=1, source_target_pairs={{0,1},{1,0},{2,3},{3,2},{4,5},{5,4},{6,7},{7,6},{8,9},{9,8},{10,11... | collective-permute-start | bytes 24584 | tf_op jit(solution)/shard_map/ppermute | solution.py:411
  10.1 12.4 %copy-start.2 = (f32[27,1,16,128]{3,2,1,0:T(8,128)S(1)}, f32[27,1,16,128]{3,2,1,0:T(8,128)}, u32[]{:S(2)}) copy-start(f32[27,1,16,128]{3,2,1,0:T(8,128)} %refs_0_) | copy-start | bytes 663556
  10.2 3.6 %collective-permute-start.3 = (f32[24,512]{1,0:T(8,128)S(1)}, f32[24,512]{1,0:T(8,128)S(1)}, u32[]{:S(2)}, u32[]{:S(2)}) collective-permute-start(f32[24,512]{1,0:T(8,128)S(1)} %get-tuple-element.42), channel_id=1, source_target_pairs={{8,16},{16,8},{24,0},{0,24},{9,17},{17,9},{25,1},{1,25},{10,18},{1... | collective-permute-start | bytes 147464 | tf_op jit(solution)/shard_map/ppermute | solution.py:417
  10.3 10.5 %collective-permute-start.13 = (f32[27,2,2,256]{3,2,1,0:T(2,128)S(1)}, f32[27,2,2,256]{3,2,1,0:T(2,128)S(1)}, u32[]{:S(2)}, u32[]{:S(2)}) collective-permute-start(f32[27,2,2,256]{3,2,1,0:T(2,128)S(1)} %get-tuple-element.55), channel_id=1, source_target_pairs={{0,1},{1,0},{2,3},{3,2},{4,5},{5,4},{6,7},{7,6},{8,9},{9,8},{10,11... | collective-permute-start | bytes 331784 | tf_op jit(solution)/shard_map/ppermute | solution.py:411
  11.5 9.4 %collective-permute-start.14 = (f32[27,2,2,256]{3,2,1,0:T(2,128)S(1)}, f32[27,2,2,256]{3,2,1,0:T(2,128)S(1)}, u32[]{:S(2)}, u32[]{:S(2)}) collective-permute-start(f32[27,2,2,256]{3,2,1,0:T(2,128)S(1)} %get-tuple-element.56), channel_id=1, source_target_pairs={{1,2},{2,1},{3,4},{4,3},{5,6},{6,5},{9,10},{10,9},{11,12},{12,11},... | collective-permute-start | bytes 331784 | tf_op jit(solution)/shard_map/ppermute | solution.py:412
  11.8 1.2 %collective-permute-start.2 = (f32[16,512]{1,0:T(8,128)S(1)}, f32[16,512]{1,0:T(8,128)S(1)}, u32[]{:S(2)}, u32[]{:S(2)}) collective-permute-start(f32[16,512]{1,0:T(8,128)S(1)} %get-tuple-element.41), channel_id=1, source_target_pairs={{0,8},{8,0},{16,24},{24,16},{1,9},{9,1},{17,25},{25,17},{2,10},{10... | collective-permute-start | bytes 98312 | tf_op jit(solution)/shard_map/ppermute | solution.py:416
  14.1 4.7 %collective-permute-start.5 = (f32[8,512]{1,0:T(8,128)S(1)}, f32[8,512]{1,0:T(8,128)S(1)}, u32[]{:S(2)}, u32[]{:S(2)}) collective-permute-start(f32[8,512]{1,0:T(8,128)S(1)} %get-tuple-element.45), channel_id=1, source_target_pairs={{1,2},{2,1},{3,4},{4,3},{5,6},{6,5},{9,10},{10,9},{11,12},{12,11},... | collective-permute-start | bytes 49160 | tf_op jit(solution)/shard_map/ppermute | solution.py:412
  14.2 4.7 %collective-permute-start.4 = (f32[4,512]{1,0:T(4,128)S(1)}, f32[4,512]{1,0:T(4,128)S(1)}, u32[]{:S(2)}, u32[]{:S(2)}) collective-permute-start(f32[4,512]{1,0:T(4,128)S(1)} %get-tuple-element.44), channel_id=1, source_target_pairs={{0,1},{1,0},{2,3},{3,2},{4,5},{5,4},{6,7},{7,6},{8,9},{9,8},{10,11... | collective-permute-start | bytes 24584 | tf_op jit(solution)/shard_map/ppermute | solution.py:411
  18.8 3.6 %collective-permute-start.7 = (f32[24,512]{1,0:T(8,128)S(1)}, f32[24,512]{1,0:T(8,128)S(1)}, u32[]{:S(2)}, u32[]{:S(2)}) collective-permute-start(f32[24,512]{1,0:T(8,128)S(1)} %get-tuple-element.47), channel_id=1, source_target_pairs={{8,16},{16,8},{24,0},{0,24},{9,17},{17,9},{25,1},{1,25},{10,18},{1... | collective-permute-start | bytes 147464 | tf_op jit(solution)/shard_map/ppermute | solution.py:417
  18.9 1.9 %collective-permute-start.6 = (f32[16,512]{1,0:T(8,128)S(1)}, f32[16,512]{1,0:T(8,128)S(1)}, u32[]{:S(2)}, u32[]{:S(2)}) collective-permute-start(f32[16,512]{1,0:T(8,128)S(1)} %get-tuple-element.46), channel_id=1, source_target_pairs={{0,8},{8,0},{16,24},{24,16},{1,9},{9,1},{17,25},{25,17},{2,10},{10... | collective-permute-start | bytes 98312 | tf_op jit(solution)/shard_map/ppermute | solution.py:416
  22.8 14.2 %collective-permute-start.15 = (f32[27,64,128]{2,1,0:T(8,128)S(1)}, f32[27,64,128]{2,1,0:T(8,128)S(1)}, u32[]{:S(2)}, u32[]{:S(2)}) collective-permute-start(f32[27,64,128]{2,1,0:T(8,128)S(1)} %get-tuple-element.57.own), channel_id=1, source_target_pairs={{0,8},{8,0},{16,24},{24,16},{1,9},{9,1},{17,25},{25,17},{2,10},{10... | collective-permute-start | bytes 2654216 | tf_op jit(solution)/shard_map/ppermute | solution.py:456
  23.1 5.7 %collective-permute-start.9 = (f32[8,512]{1,0:T(8,128)S(1)}, f32[8,512]{1,0:T(8,128)S(1)}, u32[]{:S(2)}, u32[]{:S(2)}) collective-permute-start(f32[8,512]{1,0:T(8,128)S(1)} %get-tuple-element.50), channel_id=1, source_target_pairs={{1,2},{2,1},{3,4},{4,3},{5,6},{6,5},{9,10},{10,9},{11,12},{12,11},... | collective-permute-start | bytes 49160 | tf_op jit(solution)/shard_map/ppermute | solution.py:412
  23.7 5.2 %collective-permute-start.8 = (f32[4,512]{1,0:T(4,128)S(1)}, f32[4,512]{1,0:T(4,128)S(1)}, u32[]{:S(2)}, u32[]{:S(2)}) collective-permute-start(f32[4,512]{1,0:T(4,128)S(1)} %get-tuple-element.49), channel_id=1, source_target_pairs={{0,1},{1,0},{2,3},{3,2},{4,5},{5,4},{6,7},{7,6},{8,9},{9,8},{10,11... | collective-permute-start | bytes 24584 | tf_op jit(solution)/shard_map/ppermute | solution.py:411
  28.9 3.6 %collective-permute-start.11 = (f32[24,512]{1,0:T(8,128)S(1)}, f32[24,512]{1,0:T(8,128)S(1)}, u32[]{:S(2)}, u32[]{:S(2)}) collective-permute-start(f32[24,512]{1,0:T(8,128)S(1)} %get-tuple-element.52), channel_id=1, source_target_pairs={{8,16},{16,8},{24,0},{0,24},{9,17},{17,9},{25,1},{1,25},{10,18},{1... | collective-permute-start | bytes 147464 | tf_op jit(solution)/shard_map/ppermute | solution.py:417
  29.0 12.4 %collective-permute-start.21 = (f32[19,32,128]{2,1,0:T(8,128)S(1)}, f32[19,32,128]{2,1,0:T(8,128)S(1)}, u32[]{:S(2)}, u32[]{:S(2)}) collective-permute-start(f32[19,32,128]{2,1,0:T(8,128)S(1)} %get-tuple-element.61), channel_id=1, source_target_pairs={{8,16},{16,8},{24,0},{0,24},{9,17},{17,9},{25,1},{1,25},{10,18},{1... | collective-permute-start | bytes 933896 | tf_op jit(solution)/shard_map/ppermute | solution.py:457
  30.7 1.2 %collective-permute-start.10 = (f32[16,512]{1,0:T(8,128)S(1)}, f32[16,512]{1,0:T(8,128)S(1)}, u32[]{:S(2)}, u32[]{:S(2)}) collective-permute-start(f32[16,512]{1,0:T(8,128)S(1)} %get-tuple-element.51), channel_id=1, source_target_pairs={{0,8},{8,0},{16,24},{24,16},{1,9},{9,1},{17,25},{25,17},{2,10},{10... | collective-permute-start | bytes 98312 | tf_op jit(solution)/shard_map/ppermute | solution.py:416
  32.5 8.8 %collective-permute-start.22 = (f32[8,32,128]{2,1,0:T(8,128)S(1)}, f32[8,32,128]{2,1,0:T(8,128)S(1)}, u32[]{:S(2)}, u32[]{:S(2)}) collective-permute-start(f32[8,32,128]{2,1,0:T(8,128)S(1)} %get-tuple-element.63), channel_id=1, source_target_pairs={{8,16},{16,8},{24,0},{0,24},{9,17},{17,9},{25,1},{1,25},{10,18},{1... | collective-permute-start | bytes 393224 | tf_op jit(solution)/shard_map/ppermute | solution.py:461
  33.5 5.1 %collective-permute-start.17 = (f32[16,256]{1,0:T(8,128)S(1)}, f32[16,256]{1,0:T(8,128)S(1)}, u32[]{:S(2)}, u32[]{:S(2)}) collective-permute-start(f32[16,256]{1,0:T(8,128)S(1)} %get-tuple-element.60), channel_id=1, source_target_pairs={{1,2},{2,1},{3,4},{4,3},{5,6},{6,5},{9,10},{10,9},{11,12},{12,11},... | collective-permute-start | bytes 49160 | tf_op jit(solution)/shard_map/ppermute | solution.py:412
  34.3 4.3 %collective-permute-start.16 = (f32[8,256]{1,0:T(8,128)S(1)}, f32[8,256]{1,0:T(8,128)S(1)}, u32[]{:S(2)}, u32[]{:S(2)}) collective-permute-start(f32[8,256]{1,0:T(8,128)S(1)} %get-tuple-element.59), channel_id=1, source_target_pairs={{0,1},{1,0},{2,3},{3,2},{4,5},{5,4},{6,7},{7,6},{8,9},{9,8},{10,11... | collective-permute-start | bytes 24584 | tf_op jit(solution)/shard_map/ppermute | solution.py:411
  38.6 3.9 %collective-permute-start.20 = (f32[24,256]{1,0:T(8,128)S(1)}, f32[24,256]{1,0:T(8,128)S(1)}, u32[]{:S(2)}, u32[]{:S(2)}) collective-permute-start(f32[24,256]{1,0:T(8,128)S(1)} %shard_map.78.packed), channel_id=1, source_target_pairs={{0,16},{16,0},{8,24},{24,8},{1,17},{17,1},{9,25},{25,9},{2,18},{18... | collective-permute-start | bytes 73736 | tf_op jit(solution)/shard_map/ppermute | solution.py:482
  39.8 3.3 %collective-permute-start.19 = (f32[24,256]{1,0:T(8,128)S(1)}, f32[24,256]{1,0:T(8,128)S(1)}, u32[]{:S(2)}, u32[]{:S(2)}) collective-permute-start(f32[24,256]{1,0:T(8,128)S(1)} %shard_map.78.packed), channel_id=1, source_target_pairs={{8,16},{16,8},{24,0},{0,24},{9,17},{17,9},{25,1},{1,25},{10,18},{1... | collective-permute-start | bytes 73736 | tf_op jit(solution)/shard_map/ppermute | solution.py:483
  39.8 3.3 %collective-permute-start.18 = (f32[24,256]{1,0:T(8,128)S(1)}, f32[24,256]{1,0:T(8,128)S(1)}, u32[]{:S(2)}, u32[]{:S(2)}) collective-permute-start(f32[24,256]{1,0:T(8,128)S(1)} %shard_map.78.packed), channel_id=1, source_target_pairs={{0,8},{8,0},{16,24},{24,16},{1,9},{9,1},{17,25},{25,17},{2,10},{10... | collective-permute-start | bytes 73736 | tf_op jit(solution)/shard_map/ppermute | solution.py:480
  (2 other events, 2.4 us)

commit v10 on v9

--- a/solution.py
+++ b/solution.py
@@ -420,12 +420,12 @@
     weights = call(coefficient_scale_kernel, shape(*fine.shape), [fine])
     v = WEIGHT * source / fine[CENTER]
     first = v
-    to_x, to_zx = call(edges_kernel, [shape(planes, extent), shape(2 * planes, extent)], [v])
+    to_x, to_zx = call(edges_kernel, [shape(planes, extent), shape(3 * planes, extent)], [v])
 
     def sweep(v, halo):
         v, *edges = call(
             functools.partial(sweep_kernel, groups),
-            [shape(planes, rows, extent), shape(planes, extent), shape(2 * planes, extent)],
+            [shape(planes, rows, extent), shape(planes, extent), shape(3 * planes, extent)],
             [v, first, weights, *halo],
         )
         return v, along_sub(edges)
@@ -451,8 +451,9 @@
     early, late, own = call(
         functools.partial(coefficient_pack_kernel, len(known)),
         [shape(EARLY, start, LANES), shape(27 - EARLY, start, LANES), shape(27, start + len(known) * coarse_planes * coarse_rows, LANES)],
-        [*(known[o] for o in offsets), middle, *halo_c, *halo[2:]],
-    )
+        [*(known[o] for o in offsets), middle, *halo_c, *halo[:2]],
+    )
+    early, own = after_all((early, own), *halo[2:])
     core = lax.ppermute(own, "grp", core_pairs)
     early = lax.ppermute(early, "grp", y_ring)
     v, halo = sweep(v, halo)

time: 57.4 us -> 57.2 us (level)
  no operation moved by 1% of the time
where the time goes in v10:
time: 57.2 us; the launch traced here: 57 us
  starting transfers between devices  24.3 us (42%)
  waiting for transfers between devices  12.8 us (22%)
  blocking collectives  11.2 us (20%)
  Pallas kernels  4.8 us (8%)
  local copies, waits for them, and re-layouts  2.21 us (4%)
  other arithmetic  0.89 us (2%)
  between operations  0.78 us (1%)
    ppermute x5, starting transfers between devices, along_sub(): from_x = lax.ppermute(to_x, 'sub', x_pairs)  13.6 us
    all_to_all x1, blocking collectives, body(): gathered = lax.all_to_all(coarse_source, ('grp', 'sub'), 0, 0, tiled=True)  11.2 us
    ppermute x5, waiting for transfers between devices, along_sub(): from_x = lax.ppermute(to_x, 'sub', x_pairs)  4.8 us
    pallas_call x14, Pallas kernels, call(): pl.pallas_call(kernel, out_shape=outs, in_specs=[vmem] * len(args), out_s...  4.8 us
    ppermute x3, waiting for transfers between devices, along_grp(): from_y = lax.ppermute(to_y, 'grp', y_ring)  3.08 us
    ppermute x1, starting transfers between devices, body(): lax.ppermute(known[offset], 'grp', [(i, i ^ bit) for i in range(groups)])  3.03 us
    ppermute x3, waiting for transfers between devices, along_grp(): from_core = lax.ppermute(to_core, 'grp', core_pairs)  2.68 us
    unnamed x6, local copies, waits for them, and re-layouts  2.21 us
  transfers between devices with their start and end apart: 23, of which 12 were waited for; matrix products, arithmetic and copies ran while one was open for 0% of the time, Pallas kernels for 3%

profile of v10, /device:TPU:0, one launch (start us, length us, event | category | flops | bytes accessed | tf_op | source)
XLA Modules:
  0.0 57.0 jit_solution(11714919087162111994)
XLA Ops:
  0.6 0.9 %bitcast_divide_fusion.v.first = f32[4,8,512]{2,1,0:T(8,128)S(1)} fusion(f32[27,4,8,512]{3,2,1,0:T(8,128)} %c.2, f32[4,8,512]{2,1,0:T(8,128)} %param.4), kind=kLoop, calls=%fused_computation | loop fusion | flops 32768 | bytes 196608 | tf_op jit(solution)/shard_map/div | solution.py:421
  1.5 3.0 %collective-permute-start.12 = (f32[27,1,16,128]{3,2,1,0:T(8,128)}, f32[27,1,16,128]{3,2,1,0:T(8,128)S(1)}, u32[]{:S(2)}, u32[]{:S(2)}) collective-permute-start(f32[27,1,16,128]{3,2,1,0:T(8,128)} %refs_0_), channel_id=1, source_target_pairs={{0,16},{8,24},{16,0},{24,8},{1,17},{9,25},{17,1},{25,9},{2,18},{10... | collective-permute-start | bytes 663560 | tf_op jit(solution)/shard_map/ppermute | solution.py:445
  4.6 3.0 %collective-permute-start = (f32[4,512]{1,0:T(4,128)S(1)}, f32[4,512]{1,0:T(4,128)S(1)}, u32[]{:S(2)}, u32[]{:S(2)}) collective-permute-start(f32[4,512]{1,0:T(4,128)S(1)} %get-tuple-element.38), channel_id=1, source_target_pairs={{0,1},{1,0},{2,3},{3,2},{4,5},{5,4},{6,7},{7,6},{8,9},{9,8},{10,11... | collective-permute-start | bytes 24584 | tf_op jit(solution)/shard_map/ppermute | solution.py:411
  7.7 1.5 %copy-done = f32[27,4,8,512]{3,2,1,0:T(8,128)S(1)} copy-done((f32[27,4,8,512]{3,2,1,0:T(8,128)S(1)}, f32[27,4,8,512]{3,2,1,0:T(8,128)}, u32[]{:S(2)}) %copy-start) | copy-done | bytes 1769496
  9.3 0.7 %copy-done.1 = f32[27,2,4,256]{3,2,1,0:T(4,128)S(1)} copy-done((f32[27,2,4,256]{3,2,1,0:T(4,128)S(1)}, f32[27,2,4,256]{3,2,1,0:T(4,128)}, u32[]{:S(2)}) %copy-start.1) | copy-done | bytes 221208
  10.3 1.2 %collective-permute-start.13 = (f32[27,2,2,256]{3,2,1,0:T(2,128)S(1)}, f32[27,2,2,256]{3,2,1,0:T(2,128)S(1)}, u32[]{:S(2)}, u32[]{:S(2)}) collective-permute-start(f32[27,2,2,256]{3,2,1,0:T(2,128)S(1)} %get-tuple-element.57), channel_id=1, source_target_pairs={{0,1},{1,0},{2,3},{3,2},{4,5},{5,4},{6,7},{7,6},{8,9},{9,8},{10,11... | collective-permute-start | bytes 331784 | tf_op jit(solution)/shard_map/ppermute | solution.py:411
  12.0 1.0 %collective-permute-done.2.from_core = f32[16,512]{1,0:T(8,128)S(1)} collective-permute-done((f32[16,512]{1,0:T(8,128)S(1)}, f32[16,512]{1,0:T(8,128)S(1)}, u32[]{:S(2)}, u32[]{:S(2)}) %collective-permute-start.2) | collective-permute-done | bytes 32800 | tf_op jit(solution)/shard_map/ppermute | solution.py:416
  13.0 0.8 %collective-permute-done.3.from_y = f32[24,512]{1,0:T(8,128)S(1)} collective-permute-done((f32[24,512]{1,0:T(8,128)S(1)}, f32[24,512]{1,0:T(8,128)S(1)}, u32[]{:S(2)}, u32[]{:S(2)}) %collective-permute-start.3) | collective-permute-done | bytes 49184 | tf_op jit(solution)/shard_map/ppermute | solution.py:417
  14.2 3.0 %collective-permute-start.4 = (f32[4,512]{1,0:T(4,128)S(1)}, f32[4,512]{1,0:T(4,128)S(1)}, u32[]{:S(2)}, u32[]{:S(2)}) collective-permute-start(f32[4,512]{1,0:T(4,128)S(1)} %get-tuple-element.46), channel_id=1, source_target_pairs={{0,1},{1,0},{2,3},{3,2},{4,5},{5,4},{6,7},{7,6},{8,9},{9,8},{10,11... | collective-permute-start | bytes 24584 | tf_op jit(solution)/shard_map/ppermute | solution.py:411
  17.2 1.6 %collective-permute-done.4.from_x.refs_5_ = f32[4,512]{1,0:T(4,128)S(1)} collective-permute-done((f32[4,512]{1,0:T(4,128)S(1)}, f32[4,512]{1,0:T(4,128)S(1)}, u32[]{:S(2)}, u32[]{:S(2)}) %collective-permute-start.4) | collective-permute-done | bytes 8224 | tf_op jit(solution)/shard_map/ppermute | solution.py:411
  19.0 1.1 %collective-permute-start.6 = (f32[16,512]{1,0:T(8,128)S(1)}, f32[16,512]{1,0:T(8,128)S(1)}, u32[]{:S(2)}, u32[]{:S(2)}) collective-permute-start(f32[16,512]{1,0:T(8,128)S(1)} %get-tuple-element.48), channel_id=1, source_target_pairs={{0,8},{8,0},{16,24},{24,16},{1,9},{9,1},{17,25},{25,17},{2,10},{10... | collective-permute-start | bytes 98312 | tf_op jit(solution)/shard_map/ppermute | solution.py:416
  20.9 1.6 %collective-permute-done.7.from_y = f32[24,512]{1,0:T(8,128)S(1)} collective-permute-done((f32[24,512]{1,0:T(8,128)S(1)}, f32[24,512]{1,0:T(8,128)S(1)}, u32[]{:S(2)}, u32[]{:S(2)}) %collective-permute-start.7) | collective-permute-done | bytes 49184 | tf_op jit(solution)/shard_map/ppermute | solution.py:417
  23.4 3.5 %collective-permute-start.8 = (f32[4,512]{1,0:T(4,128)S(1)}, f32[4,512]{1,0:T(4,128)S(1)}, u32[]{:S(2)}, u32[]{:S(2)}) collective-permute-start(f32[4,512]{1,0:T(4,128)S(1)} %get-tuple-element.51), channel_id=1, source_target_pairs={{0,1},{1,0},{2,3},{3,2},{4,5},{5,4},{6,7},{7,6},{8,9},{9,8},{10,11... | collective-permute-start | bytes 24584 | tf_op jit(solution)/shard_map/ppermute | solution.py:411
  26.9 1.6 %collective-permute-done.8.from_x = f32[4,512]{1,0:T(4,128)S(1)} collective-permute-done((f32[4,512]{1,0:T(4,128)S(1)}, f32[4,512]{1,0:T(4,128)S(1)}, u32[]{:S(2)}, u32[]{:S(2)}) %collective-permute-start.8) | collective-permute-done | bytes 8224 | tf_op jit(solution)/shard_map/ppermute | solution.py:411
  28.7 1.7 %collective-permute-start.21 = (f32[19,32,128]{2,1,0:T(8,128)S(1)}, f32[19,32,128]{2,1,0:T(8,128)S(1)}, u32[]{:S(2)}, u32[]{:S(2)}) collective-permute-start(f32[19,32,128]{2,1,0:T(8,128)S(1)} %get-tuple-element.65), channel_id=1, source_target_pairs={{8,16},{16,8},{24,0},{0,24},{9,17},{17,9},{25,1},{1,25},{10,18},{1... | collective-permute-start | bytes 933896 | tf_op jit(solution)/shard_map/ppermute | solution.py:458
  30.4 1.2 %collective-permute-done.10.from_core = f32[16,512]{1,0:T(8,128)S(1)} collective-permute-done((f32[16,512]{1,0:T(8,128)S(1)}, f32[16,512]{1,0:T(8,128)S(1)}, u32[]{:S(2)}, u32[]{:S(2)}) %collective-permute-start.10) | collective-permute-done | bytes 32800 | tf_op jit(solution)/shard_map/ppermute | solution.py:416
  33.2 0.8 %collective-permute-start.17 = (f32[16,256]{1,0:T(8,128)S(1)}, f32[16,256]{1,0:T(8,128)S(1)}, u32[]{:S(2)}, u32[]{:S(2)}) collective-permute-start(f32[16,256]{1,0:T(8,128)S(1)} %get-tuple-element.64), channel_id=1, source_target_pairs={{1,2},{2,1},{3,4},{4,3},{5,6},{6,5},{9,10},{10,9},{11,12},{12,11},... | collective-permute-start | bytes 49160 | tf_op jit(solution)/shard_map/ppermute | solution.py:412
  34.0 2.9 %collective-permute-start.16 = (f32[8,256]{1,0:T(8,128)S(1)}, f32[8,256]{1,0:T(8,128)S(1)}, u32[]{:S(2)}, u32[]{:S(2)}) collective-permute-start(f32[8,256]{1,0:T(8,128)S(1)} %get-tuple-element.63), channel_id=1, source_target_pairs={{0,1},{1,0},{2,3},{3,2},{4,5},{5,4},{6,7},{7,6},{8,9},{9,8},{10,11... | collective-permute-start | bytes 24584 | tf_op jit(solution)/shard_map/ppermute | solution.py:411
  36.9 1.5 %collective-permute-done.16.from_x = f32[8,256]{1,0:T(8,128)S(1)} collective-permute-done((f32[8,256]{1,0:T(8,128)S(1)}, f32[8,256]{1,0:T(8,128)S(1)}, u32[]{:S(2)}, u32[]{:S(2)}) %collective-permute-start.16) | collective-permute-done | bytes 8224 | tf_op jit(solution)/shard_map/ppermute | solution.py:411
  38.5 1.2 %collective-permute-start.20 = (f32[24,256]{1,0:T(8,128)S(1)}, f32[24,256]{1,0:T(8,128)S(1)}, u32[]{:S(2)}, u32[]{:S(2)}) collective-permute-start(f32[24,256]{1,0:T(8,128)S(1)} %shard_map.78.packed), channel_id=1, source_target_pairs={{0,16},{16,0},{8,24},{24,8},{1,17},{17,1},{9,25},{25,9},{2,18},{18... | collective-permute-start | bytes 73736 | tf_op jit(solution)/shard_map/ppermute | solution.py:483
  39.7 1.0 %collective-permute-start.18 = (f32[24,256]{1,0:T(8,128)S(1)}, f32[24,256]{1,0:T(8,128)S(1)}, u32[]{:S(2)}, u32[]{:S(2)}) collective-permute-start(f32[24,256]{1,0:T(8,128)S(1)} %shard_map.78.packed), channel_id=1, source_target_pairs={{0,8},{8,0},{16,24},{24,16},{1,9},{9,1},{17,25},{25,17},{2,10},{10... | collective-permute-start | bytes 73736 | tf_op jit(solution)/shard_map/ppermute | solution.py:481
  41.1 1.3 %collective-permute-done.20.far_below.far_above = f32[24,256]{1,0:T(8,128)S(1)} collective-permute-done((f32[24,256]{1,0:T(8,128)S(1)}, f32[24,256]{1,0:T(8,128)S(1)}, u32[]{:S(2)}, u32[]{:S(2)}) %collective-permute-start.20) | collective-permute-done | bytes 24608 | tf_op jit(solution)/shard_map/ppermute | solution.py:483
  43.6 11.2 %all_to_all.5.gathered = f32[32,1,2,128]{3,2,1,0:T(2,128)S(1)} all-to-all(f32[32,1,2,128]{3,2,1,0:T(2,128)S(1)} %get-tuple-element.68), channel_id=1, replica_groups=mesh['grp'=4,'sub'=8] {'grp','sub'}, dimensions={0} | all-to-all | bytes 65536 | tf_op jit(solution)/shard_map/all_to_all | solution.py:499
  54.8 2.2 %shard_map.80 = (f32[1,16,128]{2,1,0:T(8,128)}, f32[4,8,512]{2,1,0:T(8,128)}, f32[2,4,256]{2,1,0:T(4,128)}) custom-call(f32[32,1,2,128]{3,2,1,0:T(2,128)S(1)} %all_to_all.5.gathered, f32[4,27,16,128]{3,2,1,0:T(8,128)S(1)} %shard_map.77.c, f32[4,8,512]{2,1,0:T(8,128)S(1)} %get-tuple-element.50.v.fine, f32[2,4,256]{2,1,0:T(4,128)S(1)} %get-tuple-element.69.middle), custom_call_target="tpu_custom_call" | custom-call | tf_op jit(solution)/shard_map/pallas_call | solution.py:25
  (45 shorter events, 6.5 us)
Async XLA Ops:
  1.5 18.5 %collective-permute-start.12 = (f32[27,1,16,128]{3,2,1,0:T(8,128)}, f32[27,1,16,128]{3,2,1,0:T(8,128)S(1)}, u32[]{:S(2)}, u32[]{:S(2)}) collective-permute-start(f32[27,1,16,128]{3,2,1,0:T(8,128)} %refs_0_), channel_id=1, source_target_pairs={{0,16},{8,24},{16,0},{24,8},{1,17},{9,25},{17,1},{25,9},{2,18},{10... | collective-permute-start | bytes 663560 | tf_op jit(solution)/shard_map/ppermute | solution.py:445
  4.6 5.6 %collective-permute-start.1 = (f32[12,512]{1,0:T(8,128)S(1)}, f32[12,512]{1,0:T(8,128)S(1)}, u32[]{:S(2)}, u32[]{:S(2)}) collective-permute-start(f32[12,512]{1,0:T(8,128)S(1)} %get-tuple-element.39), channel_id=1, source_target_pairs={{1,2},{2,1},{3,4},{4,3},{5,6},{6,5},{9,10},{10,9},{11,12},{12,11},... | collective-permute-start | bytes 73736 | tf_op jit(solution)/shard_map/ppermute | solution.py:412
  4.6 5.5 %collective-permute-start = (f32[4,512]{1,0:T(4,128)S(1)}, f32[4,512]{1,0:T(4,128)S(1)}, u32[]{:S(2)}, u32[]{:S(2)}) collective-permute-start(f32[4,512]{1,0:T(4,128)S(1)} %get-tuple-element.38), channel_id=1, source_target_pairs={{0,1},{1,0},{2,3},{3,2},{4,5},{5,4},{6,7},{7,6},{8,9},{9,8},{10,11... | collective-permute-start | bytes 24584 | tf_op jit(solution)/shard_map/ppermute | solution.py:411
  10.1 10.0 %copy-start.2 = (f32[27,1,16,128]{3,2,1,0:T(8,128)S(1)}, f32[27,1,16,128]{3,2,1,0:T(8,128)}, u32[]{:S(2)}) copy-start(f32[27,1,16,128]{3,2,1,0:T(8,128)} %refs_0_) | copy-start | bytes 663556
  10.2 3.6 %collective-permute-start.3 = (f32[24,512]{1,0:T(8,128)S(1)}, f32[24,512]{1,0:T(8,128)S(1)}, u32[]{:S(2)}, u32[]{:S(2)}) collective-permute-start(f32[24,512]{1,0:T(8,128)S(1)} %get-tuple-element.44), channel_id=1, source_target_pairs={{8,16},{16,8},{24,0},{0,24},{9,17},{17,9},{25,1},{1,25},{10,18},{1... | collective-permute-start | bytes 147464 | tf_op jit(solution)/shard_map/ppermute | solution.py:417
  10.3 9.7 %collective-permute-start.13 = (f32[27,2,2,256]{3,2,1,0:T(2,128)S(1)}, f32[27,2,2,256]{3,2,1,0:T(2,128)S(1)}, u32[]{:S(2)}, u32[]{:S(2)}) collective-permute-start(f32[27,2,2,256]{3,2,1,0:T(2,128)S(1)} %get-tuple-element.57), channel_id=1, source_target_pairs={{0,1},{1,0},{2,3},{3,2},{4,5},{5,4},{6,7},{7,6},{8,9},{9,8},{10,11... | collective-permute-start | bytes 331784 | tf_op jit(solution)/shard_map/ppermute | solution.py:411
  11.5 8.5 %collective-permute-start.14 = (f32[27,2,2,256]{3,2,1,0:T(2,128)S(1)}, f32[27,2,2,256]{3,2,1,0:T(2,128)S(1)}, u32[]{:S(2)}, u32[]{:S(2)}) collective-permute-start(f32[27,2,2,256]{3,2,1,0:T(2,128)S(1)} %get-tuple-element.58), channel_id=1, source_target_pairs={{1,2},{2,1},{3,4},{4,3},{5,6},{6,5},{9,10},{10,9},{11,12},{12,11},... | collective-permute-start | bytes 331784 | tf_op jit(solution)/shard_map/ppermute | solution.py:412
  11.8 1.2 %collective-permute-start.2 = (f32[16,512]{1,0:T(8,128)S(1)}, f32[16,512]{1,0:T(8,128)S(1)}, u32[]{:S(2)}, u32[]{:S(2)}) collective-permute-start(f32[16,512]{1,0:T(8,128)S(1)} %get-tuple-element.43), channel_id=1, source_target_pairs={{0,8},{8,0},{16,24},{24,16},{1,9},{9,1},{17,25},{25,17},{2,10},{10... | collective-permute-start | bytes 98312 | tf_op jit(solution)/shard_map/ppermute | solution.py:416
  14.1 4.7 %collective-permute-start.5 = (f32[12,512]{1,0:T(8,128)S(1)}, f32[12,512]{1,0:T(8,128)S(1)}, u32[]{:S(2)}, u32[]{:S(2)}) collective-permute-start(f32[12,512]{1,0:T(8,128)S(1)} %get-tuple-element.47), channel_id=1, source_target_pairs={{1,2},{2,1},{3,4},{4,3},{5,6},{6,5},{9,10},{10,9},{11,12},{12,11},... | collective-permute-start | bytes 73736 | tf_op jit(solution)/shard_map/ppermute | solution.py:412
  14.2 4.7 %collective-permute-start.4 = (f32[4,512]{1,0:T(4,128)S(1)}, f32[4,512]{1,0:T(4,128)S(1)}, u32[]{:S(2)}, u32[]{:S(2)}) collective-permute-start(f32[4,512]{1,0:T(4,128)S(1)} %get-tuple-element.46), channel_id=1, source_target_pairs={{0,1},{1,0},{2,3},{3,2},{4,5},{5,4},{6,7},{7,6},{8,9},{9,8},{10,11... | collective-permute-start | bytes 24584 | tf_op jit(solution)/shard_map/ppermute | solution.py:411
  18.9 3.6 %collective-permute-start.7 = (f32[24,512]{1,0:T(8,128)S(1)}, f32[24,512]{1,0:T(8,128)S(1)}, u32[]{:S(2)}, u32[]{:S(2)}) collective-permute-start(f32[24,512]{1,0:T(8,128)S(1)} %get-tuple-element.49), channel_id=1, source_target_pairs={{8,16},{16,8},{24,0},{0,24},{9,17},{17,9},{25,1},{1,25},{10,18},{1... | collective-permute-start | bytes 147464 | tf_op jit(solution)/shard_map/ppermute | solution.py:417
  19.0 1.9 %collective-permute-start.6 = (f32[16,512]{1,0:T(8,128)S(1)}, f32[16,512]{1,0:T(8,128)S(1)}, u32[]{:S(2)}, u32[]{:S(2)}) collective-permute-start(f32[16,512]{1,0:T(8,128)S(1)} %get-tuple-element.48), channel_id=1, source_target_pairs={{0,8},{8,0},{16,24},{24,16},{1,9},{9,1},{17,25},{25,17},{2,10},{10... | collective-permute-start | bytes 98312 | tf_op jit(solution)/shard_map/ppermute | solution.py:416
  22.5 14.4 %collective-permute-start.15 = (f32[27,64,128]{2,1,0:T(8,128)S(1)}, f32[27,64,128]{2,1,0:T(8,128)S(1)}, u32[]{:S(2)}, u32[]{:S(2)}) collective-permute-start(f32[27,64,128]{2,1,0:T(8,128)S(1)} %get-tuple-element.61.own), channel_id=1, source_target_pairs={{0,8},{8,0},{16,24},{24,16},{1,9},{9,1},{17,25},{25,17},{2,10},{10... | collective-permute-start | bytes 2654216 | tf_op jit(solution)/shard_map/ppermute | solution.py:457
  22.8 5.7 %collective-permute-start.9 = (f32[12,512]{1,0:T(8,128)S(1)}, f32[12,512]{1,0:T(8,128)S(1)}, u32[]{:S(2)}, u32[]{:S(2)}) collective-permute-start(f32[12,512]{1,0:T(8,128)S(1)} %get-tuple-element.52), channel_id=1, source_target_pairs={{1,2},{2,1},{3,4},{4,3},{5,6},{6,5},{9,10},{10,9},{11,12},{12,11},... | collective-permute-start | bytes 73736 | tf_op jit(solution)/shard_map/ppermute | solution.py:412
  23.4 5.2 %collective-permute-start.8 = (f32[4,512]{1,0:T(4,128)S(1)}, f32[4,512]{1,0:T(4,128)S(1)}, u32[]{:S(2)}, u32[]{:S(2)}) collective-permute-start(f32[4,512]{1,0:T(4,128)S(1)} %get-tuple-element.51), channel_id=1, source_target_pairs={{0,1},{1,0},{2,3},{3,2},{4,5},{5,4},{6,7},{7,6},{8,9},{9,8},{10,11... | collective-permute-start | bytes 24584 | tf_op jit(solution)/shard_map/ppermute | solution.py:411
  28.6 3.6 %collective-permute-start.11 = (f32[24,512]{1,0:T(8,128)S(1)}, f32[24,512]{1,0:T(8,128)S(1)}, u32[]{:S(2)}, u32[]{:S(2)}) collective-permute-start(f32[24,512]{1,0:T(8,128)S(1)} %get-tuple-element.54), channel_id=1, source_target_pairs={{8,16},{16,8},{24,0},{0,24},{9,17},{17,9},{25,1},{1,25},{10,18},{1... | collective-permute-start | bytes 147464 | tf_op jit(solution)/shard_map/ppermute | solution.py:417
  28.7 12.4 %collective-permute-start.21 = (f32[19,32,128]{2,1,0:T(8,128)S(1)}, f32[19,32,128]{2,1,0:T(8,128)S(1)}, u32[]{:S(2)}, u32[]{:S(2)}) collective-permute-start(f32[19,32,128]{2,1,0:T(8,128)S(1)} %get-tuple-element.65), channel_id=1, source_target_pairs={{8,16},{16,8},{24,0},{0,24},{9,17},{17,9},{25,1},{1,25},{10,18},{1... | collective-permute-start | bytes 933896 | tf_op jit(solution)/shard_map/ppermute | solution.py:458
  30.4 1.2 %collective-permute-start.10 = (f32[16,512]{1,0:T(8,128)S(1)}, f32[16,512]{1,0:T(8,128)S(1)}, u32[]{:S(2)}, u32[]{:S(2)}) collective-permute-start(f32[16,512]{1,0:T(8,128)S(1)} %get-tuple-element.53), channel_id=1, source_target_pairs={{0,8},{8,0},{16,24},{24,16},{1,9},{9,1},{17,25},{25,17},{2,10},{10... | collective-permute-start | bytes 98312 | tf_op jit(solution)/shard_map/ppermute | solution.py:416
  32.2 8.8 %collective-permute-start.22 = (f32[8,32,128]{2,1,0:T(8,128)S(1)}, f32[8,32,128]{2,1,0:T(8,128)S(1)}, u32[]{:S(2)}, u32[]{:S(2)}) collective-permute-start(f32[8,32,128]{2,1,0:T(8,128)S(1)} %get-tuple-element.67), channel_id=1, source_target_pairs={{8,16},{16,8},{24,0},{0,24},{9,17},{17,9},{25,1},{1,25},{10,18},{1... | collective-permute-start | bytes 393224 | tf_op jit(solution)/shard_map/ppermute | solution.py:462
  33.2 5.3 %collective-permute-start.17 = (f32[16,256]{1,0:T(8,128)S(1)}, f32[16,256]{1,0:T(8,128)S(1)}, u32[]{:S(2)}, u32[]{:S(2)}) collective-permute-start(f32[16,256]{1,0:T(8,128)S(1)} %get-tuple-element.64), channel_id=1, source_target_pairs={{1,2},{2,1},{3,4},{4,3},{5,6},{6,5},{9,10},{10,9},{11,12},{12,11},... | collective-permute-start | bytes 49160 | tf_op jit(solution)/shard_map/ppermute | solution.py:412
  34.0 4.5 %collective-permute-start.16 = (f32[8,256]{1,0:T(8,128)S(1)}, f32[8,256]{1,0:T(8,128)S(1)}, u32[]{:S(2)}, u32[]{:S(2)}) collective-permute-start(f32[8,256]{1,0:T(8,128)S(1)} %get-tuple-element.63), channel_id=1, source_target_pairs={{0,1},{1,0},{2,3},{3,2},{4,5},{5,4},{6,7},{7,6},{8,9},{9,8},{10,11... | collective-permute-start | bytes 24584 | tf_op jit(solution)/shard_map/ppermute | solution.py:411
  38.5 3.9 %collective-permute-start.20 = (f32[24,256]{1,0:T(8,128)S(1)}, f32[24,256]{1,0:T(8,128)S(1)}, u32[]{:S(2)}, u32[]{:S(2)}) collective-permute-start(f32[24,256]{1,0:T(8,128)S(1)} %shard_map.78.packed), channel_id=1, source_target_pairs={{0,16},{16,0},{8,24},{24,8},{1,17},{17,1},{9,25},{25,9},{2,18},{18... | collective-permute-start | bytes 73736 | tf_op jit(solution)/shard_map/ppermute | solution.py:483
  39.7 3.3 %collective-permute-start.19 = (f32[24,256]{1,0:T(8,128)S(1)}, f32[24,256]{1,0:T(8,128)S(1)}, u32[]{:S(2)}, u32[]{:S(2)}) collective-permute-start(f32[24,256]{1,0:T(8,128)S(1)} %shard_map.78.packed), channel_id=1, source_target_pairs={{8,16},{16,8},{24,0},{0,24},{9,17},{17,9},{25,1},{1,25},{10,18},{1... | collective-permute-start | bytes 73736 | tf_op jit(solution)/shard_map/ppermute | solution.py:484
  39.7 3.3 %collective-permute-start.18 = (f32[24,256]{1,0:T(8,128)S(1)}, f32[24,256]{1,0:T(8,128)S(1)}, u32[]{:S(2)}, u32[]{:S(2)}) collective-permute-start(f32[24,256]{1,0:T(8,128)S(1)} %shard_map.78.packed), channel_id=1, source_target_pairs={{0,8},{8,0},{16,24},{24,16},{1,9},{9,1},{17,25},{25,17},{2,10},{10... | collective-permute-start | bytes 73736 | tf_op jit(solution)/shard_map/ppermute | solution.py:481
  (2 other events, 2.4 us)

commit v11 on v10

--- a/solution.py
+++ b/solution.py
@@ -187,7 +187,7 @@
         to_zx[4 * x : 4 * x + 3, :] = pick(even("sub"), first_rows, last_rows)
 
 
-def middle_faces_kernel(mine, from_x, from_zx, out):
+def middle_faces_kernel(mine, from_x, from_zx, out, larger):
     planes, half, _ = mine.shape
     before, after = sides(from_x[...], from_zx[0 : 4 * planes, :])
     for x in range(planes):
@@ -198,6 +198,7 @@
         extra = planes * ROWS + 2 * x
         out[extra : extra + 1, :] = before[4 * x : 4 * x + 1]
         out[extra + 1 : extra + 2, :] = after[4 * x + 2 : 4 * x + 3]
+    larger[0 : out.shape[0], :] = out[...]
 
 
 def coefficient_edges_kernel(c, to_x, to_zx):
@@ -259,8 +260,8 @@
     group = lax.axis_index("grp")
     window = 3 * planes
 
-    below = pick(even("grp"), near_y[...], near_core[...])
-    above = pick(even("grp"), near_core[...], near_y[...])
+    below = pick(even("grp"), near_y[...], near_core[0 : near_y.shape[0], :])
+    above = pick(even("grp"), near_core[0 : near_y.shape[0], :], near_y[...])
     blocks = {-2: far_below[...], -1: below, 0: packed[...], 1: above, 2: far_above[...]}
     for away in (-2, -1, 1, 2):
         inside = (group + away >= 0) & (group + away < groups)
@@ -451,9 +452,8 @@
     early, late, own = call(
         functools.partial(coefficient_pack_kernel, len(known)),
         [shape(EARLY, start, LANES), shape(27 - EARLY, start, LANES), shape(27, start + len(known) * coarse_planes * coarse_rows, LANES)],
-        [*(known[o] for o in offsets), middle, *halo_c, *halo[:2]],
-    )
-    early, own = after_all((early, own), *halo[2:])
+        [*(known[o] for o in offsets), middle, *halo_c, *halo[2:]],
+    )
     core = lax.ppermute(own, "grp", core_pairs)
     early = lax.ppermute(early, "grp", y_ring)
     v, halo = sweep(v, halo)
@@ -473,12 +473,12 @@
         shape(total, 27, coarse_rows, coarse_extent),
         [own, core],
     )
-    packed = call(
+    packed, larger = call(
         middle_faces_kernel,
-        shape(middle_planes * ROWS + 8, middle_extent),
+        [shape(middle_planes * ROWS + 8, middle_extent), shape(middle_planes * ROWS + 16, middle_extent)],
         [after(iterate, ordered), *along_sub(edges)],
     )
-    near_core = lax.ppermute(packed, "grp", core_pairs)
+    near_core = lax.ppermute(larger, "grp", core_pairs)
     if groups == 4:
         far_below = far_above = lax.ppermute(packed, "grp", swaps([(0, 2), (1, 3)]))
         near_y = lax.ppermute(packed, "grp", y_ring)

time: 57.2 us -> 57.4 us (level)
  waiting for transfers between devices: 12.8 us -> 13.5 us
    ppermute x1, starting transfers between devices: 1.03 us -> 0.07 us  [body(): near_core = lax.ppermute(larger, 'grp', core_pairs)]
    ppermute x1, starting transfers between devices: 0.01 us -> 0.69 us  [body(): near_y = lax.ppermute(packed, 'grp', y_ring)]
where the time goes in v11:
time: 57.4 us; the launch traced here: 57.1 us
  starting transfers between devices  24.1 us (42%)
  waiting for transfers between devices  13.5 us (24%)
  blocking collectives  11 us (19%)
  Pallas kernels  4.66 us (8%)
  local copies, waits for them, and re-layouts  2.21 us (4%)
  other arithmetic  0.89 us (2%)
  between operations  0.78 us (1%)
    ppermute x5, starting transfers between devices, along_sub(): from_x = lax.ppermute(to_x, 'sub', x_pairs)  13.6 us
    all_to_all x1, blocking collectives, body(): gathered = lax.all_to_all(coarse_source, ('grp', 'sub'), 0, 0, tiled=True)  11 us
    ppermute x5, waiting for transfers between devices, along_sub(): from_x = lax.ppermute(to_x, 'sub', x_pairs)  4.8 us
    pallas_call x14, Pallas kernels, call(): pl.pallas_call(kernel, out_shape=outs, in_specs=[vmem] * len(args), out_s...  4.66 us
    ppermute x3, waiting for transfers between devices, along_grp(): from_y = lax.ppermute(to_y, 'grp', y_ring)  3.06 us
    ppermute x1, starting transfers between devices, body(): lax.ppermute(known[offset], 'grp', [(i, i ^ bit) for i in range(groups)])  3.03 us
    ppermute x3, waiting for transfers between devices, along_grp(): from_core = lax.ppermute(to_core, 'grp', core_pairs)  3.03 us
    unnamed x6, local copies, waits for them, and re-layouts  2.21 us
  transfers between devices with their start and end apart: 23, of which 12 were waited for; matrix products, arithmetic and copies ran while one was open for 0% of the time, Pallas kernels for 3%

profile of v11, /device:TPU:0, one launch (start us, length us, event | category | flops | bytes accessed | tf_op | source)
XLA Modules:
  0.0 57.1 jit_solution(8417420564884160559)
XLA Ops:
  0.6 0.9 %bitcast_divide_fusion.v.first = f32[4,8,512]{2,1,0:T(8,128)S(1)} fusion(f32[27,4,8,512]{3,2,1,0:T(8,128)} %c.2, f32[4,8,512]{2,1,0:T(8,128)} %param.4), kind=kLoop, calls=%fused_computation | loop fusion | flops 32768 | bytes 196608 | tf_op jit(solution)/shard_map/div | solution.py:422
  1.5 3.0 %collective-permute-start.12 = (f32[27,1,16,128]{3,2,1,0:T(8,128)}, f32[27,1,16,128]{3,2,1,0:T(8,128)S(1)}, u32[]{:S(2)}, u32[]{:S(2)}) collective-permute-start(f32[27,1,16,128]{3,2,1,0:T(8,128)} %refs_0_), channel_id=1, source_target_pairs={{0,16},{8,24},{16,0},{24,8},{1,17},{9,25},{17,1},{25,9},{2,18},{10... | collective-permute-start | bytes 663560 | tf_op jit(solution)/shard_map/ppermute | solution.py:446
  4.6 3.0 %collective-permute-start = (f32[4,512]{1,0:T(4,128)S(1)}, f32[4,512]{1,0:T(4,128)S(1)}, u32[]{:S(2)}, u32[]{:S(2)}) collective-permute-start(f32[4,512]{1,0:T(4,128)S(1)} %get-tuple-element.38), channel_id=1, source_target_pairs={{0,1},{1,0},{2,3},{3,2},{4,5},{5,4},{6,7},{7,6},{8,9},{9,8},{10,11... | collective-permute-start | bytes 24584 | tf_op jit(solution)/shard_map/ppermute | solution.py:412
  7.7 1.5 %copy-done = f32[27,4,8,512]{3,2,1,0:T(8,128)S(1)} copy-done((f32[27,4,8,512]{3,2,1,0:T(8,128)S(1)}, f32[27,4,8,512]{3,2,1,0:T(8,128)}, u32[]{:S(2)}) %copy-start) | copy-done | bytes 1769496
  9.3 0.7 %copy-done.1 = f32[27,2,4,256]{3,2,1,0:T(4,128)S(1)} copy-done((f32[27,2,4,256]{3,2,1,0:T(4,128)S(1)}, f32[27,2,4,256]{3,2,1,0:T(4,128)}, u32[]{:S(2)}) %copy-start.1) | copy-done | bytes 221208
  10.3 1.2 %collective-permute-start.13 = (f32[27,2,2,256]{3,2,1,0:T(2,128)S(1)}, f32[27,2,2,256]{3,2,1,0:T(2,128)S(1)}, u32[]{:S(2)}, u32[]{:S(2)}) collective-permute-start(f32[27,2,2,256]{3,2,1,0:T(2,128)S(1)} %get-tuple-element.57), channel_id=1, source_target_pairs={{0,1},{1,0},{2,3},{3,2},{4,5},{5,4},{6,7},{7,6},{8,9},{9,8},{10,11... | collective-permute-start | bytes 331784 | tf_op jit(solution)/shard_map/ppermute | solution.py:412
  12.0 1.0 %collective-permute-done.2.from_core = f32[16,512]{1,0:T(8,128)S(1)} collective-permute-done((f32[16,512]{1,0:T(8,128)S(1)}, f32[16,512]{1,0:T(8,128)S(1)}, u32[]{:S(2)}, u32[]{:S(2)}) %collective-permute-start.2) | collective-permute-done | bytes 32800 | tf_op jit(solution)/shard_map/ppermute | solution.py:417
  13.0 0.8 %collective-permute-done.3.from_y = f32[24,512]{1,0:T(8,128)S(1)} collective-permute-done((f32[24,512]{1,0:T(8,128)S(1)}, f32[24,512]{1,0:T(8,128)S(1)}, u32[]{:S(2)}, u32[]{:S(2)}) %collective-permute-start.3) | collective-permute-done | bytes 49184 | tf_op jit(solution)/shard_map/ppermute | solution.py:418
  14.2 3.0 %collective-permute-start.4 = (f32[4,512]{1,0:T(4,128)S(1)}, f32[4,512]{1,0:T(4,128)S(1)}, u32[]{:S(2)}, u32[]{:S(2)}) collective-permute-start(f32[4,512]{1,0:T(4,128)S(1)} %get-tuple-element.46), channel_id=1, source_target_pairs={{0,1},{1,0},{2,3},{3,2},{4,5},{5,4},{6,7},{7,6},{8,9},{9,8},{10,11... | collective-permute-start | bytes 24584 | tf_op jit(solution)/shard_map/ppermute | solution.py:412
  17.2 1.6 %collective-permute-done.4.from_x = f32[4,512]{1,0:T(4,128)S(1)} collective-permute-done((f32[4,512]{1,0:T(4,128)S(1)}, f32[4,512]{1,0:T(4,128)S(1)}, u32[]{:S(2)}, u32[]{:S(2)}) %collective-permute-start.4) | collective-permute-done | bytes 8224 | tf_op jit(solution)/shard_map/ppermute | solution.py:412
  18.9 1.1 %collective-permute-start.6 = (f32[16,512]{1,0:T(8,128)S(1)}, f32[16,512]{1,0:T(8,128)S(1)}, u32[]{:S(2)}, u32[]{:S(2)}) collective-permute-start(f32[16,512]{1,0:T(8,128)S(1)} %get-tuple-element.48), channel_id=1, source_target_pairs={{0,8},{8,0},{16,24},{24,16},{1,9},{9,1},{17,25},{25,17},{2,10},{10... | collective-permute-start | bytes 98312 | tf_op jit(solution)/shard_map/ppermute | solution.py:417
  20.0 0.9 %collective-permute-done.6.from_core.refs_5_ = f32[16,512]{1,0:T(8,128)S(1)} collective-permute-done((f32[16,512]{1,0:T(8,128)S(1)}, f32[16,512]{1,0:T(8,128)S(1)}, u32[]{:S(2)}, u32[]{:S(2)}) %collective-permute-start.6) | collective-permute-done | bytes 32800 | tf_op jit(solution)/shard_map/ppermute | solution.py:417
  20.8 1.6 %collective-permute-done.7.from_y.refs_6_ = f32[24,512]{1,0:T(8,128)S(1)} collective-permute-done((f32[24,512]{1,0:T(8,128)S(1)}, f32[24,512]{1,0:T(8,128)S(1)}, u32[]{:S(2)}, u32[]{:S(2)}) %collective-permute-start.7) | collective-permute-done | bytes 49184 | tf_op jit(solution)/shard_map/ppermute | solution.py:418
  23.7 3.6 %collective-permute-start.8 = (f32[4,512]{1,0:T(4,128)S(1)}, f32[4,512]{1,0:T(4,128)S(1)}, u32[]{:S(2)}, u32[]{:S(2)}) collective-permute-start(f32[4,512]{1,0:T(4,128)S(1)} %get-tuple-element.51), channel_id=1, source_target_pairs={{0,1},{1,0},{2,3},{3,2},{4,5},{5,4},{6,7},{7,6},{8,9},{9,8},{10,11... | collective-permute-start | bytes 24584 | tf_op jit(solution)/shard_map/ppermute | solution.py:412
  27.2 1.6 %collective-permute-done.8.from_x = f32[4,512]{1,0:T(4,128)S(1)} collective-permute-done((f32[4,512]{1,0:T(4,128)S(1)}, f32[4,512]{1,0:T(4,128)S(1)}, u32[]{:S(2)}, u32[]{:S(2)}) %collective-permute-start.8) | collective-permute-done | bytes 8224 | tf_op jit(solution)/shard_map/ppermute | solution.py:412
  29.0 1.7 %collective-permute-start.21 = (f32[19,32,128]{2,1,0:T(8,128)S(1)}, f32[19,32,128]{2,1,0:T(8,128)S(1)}, u32[]{:S(2)}, u32[]{:S(2)}) collective-permute-start(f32[19,32,128]{2,1,0:T(8,128)S(1)} %get-tuple-element.65), channel_id=1, source_target_pairs={{8,16},{16,8},{24,0},{0,24},{9,17},{17,9},{25,1},{1,25},{10,18},{1... | collective-permute-start | bytes 933896 | tf_op jit(solution)/shard_map/ppermute | solution.py:458
  30.7 1.2 %collective-permute-done.10.from_core = f32[16,512]{1,0:T(8,128)S(1)} collective-permute-done((f32[16,512]{1,0:T(8,128)S(1)}, f32[16,512]{1,0:T(8,128)S(1)}, u32[]{:S(2)}, u32[]{:S(2)}) %collective-permute-start.10) | collective-permute-done | bytes 32800 | tf_op jit(solution)/shard_map/ppermute | solution.py:417
  33.5 0.8 %collective-permute-start.17 = (f32[16,256]{1,0:T(8,128)S(1)}, f32[16,256]{1,0:T(8,128)S(1)}, u32[]{:S(2)}, u32[]{:S(2)}) collective-permute-start(f32[16,256]{1,0:T(8,128)S(1)} %get-tuple-element.62), channel_id=1, source_target_pairs={{1,2},{2,1},{3,4},{4,3},{5,6},{6,5},{9,10},{10,9},{11,12},{12,11},... | collective-permute-start | bytes 49160 | tf_op jit(solution)/shard_map/ppermute | solution.py:413
  34.3 2.8 %collective-permute-start.16 = (f32[8,256]{1,0:T(8,128)S(1)}, f32[8,256]{1,0:T(8,128)S(1)}, u32[]{:S(2)}, u32[]{:S(2)}) collective-permute-start(f32[8,256]{1,0:T(8,128)S(1)} %get-tuple-element.61), channel_id=1, source_target_pairs={{0,1},{1,0},{2,3},{3,2},{4,5},{5,4},{6,7},{7,6},{8,9},{9,8},{10,11... | collective-permute-start | bytes 24584 | tf_op jit(solution)/shard_map/ppermute | solution.py:412
  37.2 1.5 %collective-permute-done.16.from_x = f32[8,256]{1,0:T(8,128)S(1)} collective-permute-done((f32[8,256]{1,0:T(8,128)S(1)}, f32[8,256]{1,0:T(8,128)S(1)}, u32[]{:S(2)}, u32[]{:S(2)}) %collective-permute-start.16) | collective-permute-done | bytes 8224 | tf_op jit(solution)/shard_map/ppermute | solution.py:412
  38.8 1.2 %collective-permute-start.20 = (f32[24,256]{1,0:T(8,128)S(1)}, f32[24,256]{1,0:T(8,128)S(1)}, u32[]{:S(2)}, u32[]{:S(2)}) collective-permute-start(f32[24,256]{1,0:T(8,128)S(1)} %get-tuple-element.63.packed), channel_id=1, source_target_pairs={{0,16},{16,0},{8,24},{24,8},{1,17},{17,1},{9,25},{25,9},{2,18},{18... | collective-permute-start | bytes 73736 | tf_op jit(solution)/shard_map/ppermute | solution.py:483
  41.3 1.4 %collective-permute-done.20.far_below.far_above = f32[24,256]{1,0:T(8,128)S(1)} collective-permute-done((f32[24,256]{1,0:T(8,128)S(1)}, f32[24,256]{1,0:T(8,128)S(1)}, u32[]{:S(2)}, u32[]{:S(2)}) %collective-permute-start.20) | collective-permute-done | bytes 24608 | tf_op jit(solution)/shard_map/ppermute | solution.py:483
  43.9 11.0 %all_to_all.5.gathered = f32[32,1,2,128]{3,2,1,0:T(2,128)S(1)} all-to-all(f32[32,1,2,128]{3,2,1,0:T(2,128)S(1)} %get-tuple-element.68), channel_id=1, replica_groups=mesh['grp'=4,'sub'=8] {'grp','sub'}, dimensions={0} | all-to-all | bytes 65536 | tf_op jit(solution)/shard_map/all_to_all | solution.py:499
  54.9 2.2 %shard_map.80 = (f32[1,16,128]{2,1,0:T(8,128)}, f32[4,8,512]{2,1,0:T(8,128)}, f32[2,4,256]{2,1,0:T(4,128)}) custom-call(f32[32,1,2,128]{3,2,1,0:T(2,128)S(1)} %all_to_all.5.gathered, f32[4,27,16,128]{3,2,1,0:T(8,128)S(1)} %shard_map.77.c, f32[4,8,512]{2,1,0:T(8,128)S(1)} %get-tuple-element.50.v.fine, f32[2,4,256]{2,1,0:T(4,128)S(1)} %get-tuple-element.69.middle), custom_call_target="tpu_custom_call" | custom-call | tf_op jit(solution)/shard_map/pallas_call | solution.py:25
  (45 shorter events, 6.9 us)
Async XLA Ops:
  1.5 20.9 %collective-permute-start.12 = (f32[27,1,16,128]{3,2,1,0:T(8,128)}, f32[27,1,16,128]{3,2,1,0:T(8,128)S(1)}, u32[]{:S(2)}, u32[]{:S(2)}) collective-permute-start(f32[27,1,16,128]{3,2,1,0:T(8,128)} %refs_0_), channel_id=1, source_target_pairs={{0,16},{8,24},{16,0},{24,8},{1,17},{9,25},{17,1},{25,9},{2,18},{10... | collective-permute-start | bytes 663560 | tf_op jit(solution)/shard_map/ppermute | solution.py:446
  4.6 5.6 %collective-permute-start.1 = (f32[12,512]{1,0:T(8,128)S(1)}, f32[12,512]{1,0:T(8,128)S(1)}, u32[]{:S(2)}, u32[]{:S(2)}) collective-permute-start(f32[12,512]{1,0:T(8,128)S(1)} %get-tuple-element.39), channel_id=1, source_target_pairs={{1,2},{2,1},{3,4},{4,3},{5,6},{6,5},{9,10},{10,9},{11,12},{12,11},... | collective-permute-start | bytes 73736 | tf_op jit(solution)/shard_map/ppermute | solution.py:413
  4.6 5.5 %collective-permute-start = (f32[4,512]{1,0:T(4,128)S(1)}, f32[4,512]{1,0:T(4,128)S(1)}, u32[]{:S(2)}, u32[]{:S(2)}) collective-permute-start(f32[4,512]{1,0:T(4,128)S(1)} %get-tuple-element.38), channel_id=1, source_target_pairs={{0,1},{1,0},{2,3},{3,2},{4,5},{5,4},{6,7},{7,6},{8,9},{9,8},{10,11... | collective-permute-start | bytes 24584 | tf_op jit(solution)/shard_map/ppermute | solution.py:412
  10.1 12.4 %copy-start.2 = (f32[27,1,16,128]{3,2,1,0:T(8,128)S(1)}, f32[27,1,16,128]{3,2,1,0:T(8,128)}, u32[]{:S(2)}) copy-start(f32[27,1,16,128]{3,2,1,0:T(8,128)} %refs_0_) | copy-start | bytes 663556
  10.2 3.6 %collective-permute-start.3 = (f32[24,512]{1,0:T(8,128)S(1)}, f32[24,512]{1,0:T(8,128)S(1)}, u32[]{:S(2)}, u32[]{:S(2)}) collective-permute-start(f32[24,512]{1,0:T(8,128)S(1)} %get-tuple-element.44), channel_id=1, source_target_pairs={{8,16},{16,8},{24,0},{0,24},{9,17},{17,9},{25,1},{1,25},{10,18},{1... | collective-permute-start | bytes 147464 | tf_op jit(solution)/shard_map/ppermute | solution.py:418
  10.3 10.5 %collective-permute-start.13 = (f32[27,2,2,256]{3,2,1,0:T(2,128)S(1)}, f32[27,2,2,256]{3,2,1,0:T(2,128)S(1)}, u32[]{:S(2)}, u32[]{:S(2)}) collective-permute-start(f32[27,2,2,256]{3,2,1,0:T(2,128)S(1)} %get-tuple-element.57), channel_id=1, source_target_pairs={{0,1},{1,0},{2,3},{3,2},{4,5},{5,4},{6,7},{7,6},{8,9},{9,8},{10,11... | collective-permute-start | bytes 331784 | tf_op jit(solution)/shard_map/ppermute | solution.py:412
  11.5 9.4 %collective-permute-start.14 = (f32[27,2,2,256]{3,2,1,0:T(2,128)S(1)}, f32[27,2,2,256]{3,2,1,0:T(2,128)S(1)}, u32[]{:S(2)}, u32[]{:S(2)}) collective-permute-start(f32[27,2,2,256]{3,2,1,0:T(2,128)S(1)} %get-tuple-element.58), channel_id=1, source_target_pairs={{1,2},{2,1},{3,4},{4,3},{5,6},{6,5},{9,10},{10,9},{11,12},{12,11},... | collective-permute-start | bytes 331784 | tf_op jit(solution)/shard_map/ppermute | solution.py:413
  11.8 1.2 %collective-permute-start.2 = (f32[16,512]{1,0:T(8,128)S(1)}, f32[16,512]{1,0:T(8,128)S(1)}, u32[]{:S(2)}, u32[]{:S(2)}) collective-permute-start(f32[16,512]{1,0:T(8,128)S(1)} %get-tuple-element.43), channel_id=1, source_target_pairs={{0,8},{8,0},{16,24},{24,16},{1,9},{9,1},{17,25},{25,17},{2,10},{10... | collective-permute-start | bytes 98312 | tf_op jit(solution)/shard_map/ppermute | solution.py:417
  14.1 4.7 %collective-permute-start.5 = (f32[12,512]{1,0:T(8,128)S(1)}, f32[12,512]{1,0:T(8,128)S(1)}, u32[]{:S(2)}, u32[]{:S(2)}) collective-permute-start(f32[12,512]{1,0:T(8,128)S(1)} %get-tuple-element.47), channel_id=1, source_target_pairs={{1,2},{2,1},{3,4},{4,3},{5,6},{6,5},{9,10},{10,9},{11,12},{12,11},... | collective-permute-start | bytes 73736 | tf_op jit(solution)/shard_map/ppermute | solution.py:413
  14.2 4.7 %collective-permute-start.4 = (f32[4,512]{1,0:T(4,128)S(1)}, f32[4,512]{1,0:T(4,128)S(1)}, u32[]{:S(2)}, u32[]{:S(2)}) collective-permute-start(f32[4,512]{1,0:T(4,128)S(1)} %get-tuple-element.46), channel_id=1, source_target_pairs={{0,1},{1,0},{2,3},{3,2},{4,5},{5,4},{6,7},{7,6},{8,9},{9,8},{10,11... | collective-permute-start | bytes 24584 | tf_op jit(solution)/shard_map/ppermute | solution.py:412
  18.8 3.6 %collective-permute-start.7 = (f32[24,512]{1,0:T(8,128)S(1)}, f32[24,512]{1,0:T(8,128)S(1)}, u32[]{:S(2)}, u32[]{:S(2)}) collective-permute-start(f32[24,512]{1,0:T(8,128)S(1)} %get-tuple-element.49), channel_id=1, source_target_pairs={{8,16},{16,8},{24,0},{0,24},{9,17},{17,9},{25,1},{1,25},{10,18},{1... | collective-permute-start | bytes 147464 | tf_op jit(solution)/shard_map/ppermute | solution.py:418
  18.9 1.9 %collective-permute-start.6 = (f32[16,512]{1,0:T(8,128)S(1)}, f32[16,512]{1,0:T(8,128)S(1)}, u32[]{:S(2)}, u32[]{:S(2)}) collective-permute-start(f32[16,512]{1,0:T(8,128)S(1)} %get-tuple-element.48), channel_id=1, source_target_pairs={{0,8},{8,0},{16,24},{24,16},{1,9},{9,1},{17,25},{25,17},{2,10},{10... | collective-permute-start | bytes 98312 | tf_op jit(solution)/shard_map/ppermute | solution.py:417
  22.8 14.3 %collective-permute-start.15 = (f32[27,64,128]{2,1,0:T(8,128)S(1)}, f32[27,64,128]{2,1,0:T(8,128)S(1)}, u32[]{:S(2)}, u32[]{:S(2)}) collective-permute-start(f32[27,64,128]{2,1,0:T(8,128)S(1)} %get-tuple-element.59.own), channel_id=1, source_target_pairs={{0,8},{8,0},{16,24},{24,16},{1,9},{9,1},{17,25},{25,17},{2,10},{10... | collective-permute-start | bytes 2654216 | tf_op jit(solution)/shard_map/ppermute | solution.py:457
  23.1 5.7 %collective-permute-start.9 = (f32[12,512]{1,0:T(8,128)S(1)}, f32[12,512]{1,0:T(8,128)S(1)}, u32[]{:S(2)}, u32[]{:S(2)}) collective-permute-start(f32[12,512]{1,0:T(8,128)S(1)} %get-tuple-element.52), channel_id=1, source_target_pairs={{1,2},{2,1},{3,4},{4,3},{5,6},{6,5},{9,10},{10,9},{11,12},{12,11},... | collective-permute-start | bytes 73736 | tf_op jit(solution)/shard_map/ppermute | solution.py:413
  23.7 5.2 %collective-permute-start.8 = (f32[4,512]{1,0:T(4,128)S(1)}, f32[4,512]{1,0:T(4,128)S(1)}, u32[]{:S(2)}, u32[]{:S(2)}) collective-permute-start(f32[4,512]{1,0:T(4,128)S(1)} %get-tuple-element.51), channel_id=1, source_target_pairs={{0,1},{1,0},{2,3},{3,2},{4,5},{5,4},{6,7},{7,6},{8,9},{9,8},{10,11... | collective-permute-start | bytes 24584 | tf_op jit(solution)/shard_map/ppermute | solution.py:412
  28.9 3.6 %collective-permute-start.11 = (f32[24,512]{1,0:T(8,128)S(1)}, f32[24,512]{1,0:T(8,128)S(1)}, u32[]{:S(2)}, u32[]{:S(2)}) collective-permute-start(f32[24,512]{1,0:T(8,128)S(1)} %get-tuple-element.54), channel_id=1, source_target_pairs={{8,16},{16,8},{24,0},{0,24},{9,17},{17,9},{25,1},{1,25},{10,18},{1... | collective-permute-start | bytes 147464 | tf_op jit(solution)/shard_map/ppermute | solution.py:418
  29.0 12.4 %collective-permute-start.21 = (f32[19,32,128]{2,1,0:T(8,128)S(1)}, f32[19,32,128]{2,1,0:T(8,128)S(1)}, u32[]{:S(2)}, u32[]{:S(2)}) collective-permute-start(f32[19,32,128]{2,1,0:T(8,128)S(1)} %get-tuple-element.65), channel_id=1, source_target_pairs={{8,16},{16,8},{24,0},{0,24},{9,17},{17,9},{25,1},{1,25},{10,18},{1... | collective-permute-start | bytes 933896 | tf_op jit(solution)/shard_map/ppermute | solution.py:458
  30.7 1.2 %collective-permute-start.10 = (f32[16,512]{1,0:T(8,128)S(1)}, f32[16,512]{1,0:T(8,128)S(1)}, u32[]{:S(2)}, u32[]{:S(2)}) collective-permute-start(f32[16,512]{1,0:T(8,128)S(1)} %get-tuple-element.53), channel_id=1, source_target_pairs={{0,8},{8,0},{16,24},{24,16},{1,9},{9,1},{17,25},{25,17},{2,10},{10... | collective-permute-start | bytes 98312 | tf_op jit(solution)/shard_map/ppermute | solution.py:417
  32.5 8.8 %collective-permute-start.22 = (f32[8,32,128]{2,1,0:T(8,128)S(1)}, f32[8,32,128]{2,1,0:T(8,128)S(1)}, u32[]{:S(2)}, u32[]{:S(2)}) collective-permute-start(f32[8,32,128]{2,1,0:T(8,128)S(1)} %get-tuple-element.67), channel_id=1, source_target_pairs={{8,16},{16,8},{24,0},{0,24},{9,17},{17,9},{25,1},{1,25},{10,18},{1... | collective-permute-start | bytes 393224 | tf_op jit(solution)/shard_map/ppermute | solution.py:462
  33.5 5.3 %collective-permute-start.17 = (f32[16,256]{1,0:T(8,128)S(1)}, f32[16,256]{1,0:T(8,128)S(1)}, u32[]{:S(2)}, u32[]{:S(2)}) collective-permute-start(f32[16,256]{1,0:T(8,128)S(1)} %get-tuple-element.62), channel_id=1, source_target_pairs={{1,2},{2,1},{3,4},{4,3},{5,6},{6,5},{9,10},{10,9},{11,12},{12,11},... | collective-permute-start | bytes 49160 | tf_op jit(solution)/shard_map/ppermute | solution.py:413
  34.3 4.5 %collective-permute-start.16 = (f32[8,256]{1,0:T(8,128)S(1)}, f32[8,256]{1,0:T(8,128)S(1)}, u32[]{:S(2)}, u32[]{:S(2)}) collective-permute-start(f32[8,256]{1,0:T(8,128)S(1)} %get-tuple-element.61), channel_id=1, source_target_pairs={{0,1},{1,0},{2,3},{3,2},{4,5},{5,4},{6,7},{7,6},{8,9},{9,8},{10,11... | collective-permute-start | bytes 24584 | tf_op jit(solution)/shard_map/ppermute | solution.py:412
  38.8 4.5 %collective-permute-start.18 = (f32[32,256]{1,0:T(8,128)S(1)}, f32[32,256]{1,0:T(8,128)S(1)}, u32[]{:S(2)}, u32[]{:S(2)}) collective-permute-start(f32[32,256]{1,0:T(8,128)S(1)} %get-tuple-element.64), channel_id=1, source_target_pairs={{0,8},{8,0},{16,24},{24,16},{1,9},{9,1},{17,25},{25,17},{2,10},{10... | collective-permute-start | bytes 98312 | tf_op jit(solution)/shard_map/ppermute | solution.py:481
  38.8 3.9 %collective-permute-start.20 = (f32[24,256]{1,0:T(8,128)S(1)}, f32[24,256]{1,0:T(8,128)S(1)}, u32[]{:S(2)}, u32[]{:S(2)}) collective-permute-start(f32[24,256]{1,0:T(8,128)S(1)} %get-tuple-element.63.packed), channel_id=1, source_target_pairs={{0,16},{16,0},{8,24},{24,8},{1,17},{17,1},{9,25},{25,9},{2,18},{18... | collective-permute-start | bytes 73736 | tf_op jit(solution)/shard_map/ppermute | solution.py:483
  40.0 3.3 %collective-permute-start.19 = (f32[24,256]{1,0:T(8,128)S(1)}, f32[24,256]{1,0:T(8,128)S(1)}, u32[]{:S(2)}, u32[]{:S(2)}) collective-permute-start(f32[24,256]{1,0:T(8,128)S(1)} %get-tuple-element.63.packed), channel_id=1, source_target_pairs={{8,16},{16,8},{24,0},{0,24},{9,17},{17,9},{25,1},{1,25},{10,18},{1... | collective-permute-start | bytes 73736 | tf_op jit(solution)/shard_map/ppermute | solution.py:484
  (2 other events, 2.4 us)
